TPU v7x, 128 devices: a whole 4x4x4 slice. The times are simulated.
128 devices in a mesh: ia: 16 (over z, x_hi, core), ja: 8 (over y, x_lo).
Axes of the slice: x: 4 (x_hi: 2, x_lo: 2; x = x_hi * 2 + x_lo), y: 4, z: 4, core: 2. Of those that a mesh axis runs over, the one named last changes fastest.
Arguments:
- pair: bfloat16 [512, 512, 128], P('ia', 'ja'), may hold values from -9 to 9
- cotangent: bfloat16 [512, 512, 128], P('ia', 'ja'), may hold values from -6 to 6
- norm_gain: float32 [128], replicated, may hold values from 0.25 to 1.75
- norm_shift: float32 [128], replicated, may hold values from -3 to 3
- query_weight: bfloat16 [128, 128], replicated, may hold values from -2 to 2
- key_weight: bfloat16 [128, 128], replicated, may hold values from -2 to 2
- value_weight: bfloat16 [128, 128], replicated, may hold values from -0.5 to 0.5
- gate_weight: bfloat16 [128, 128], replicated, may hold values from -0.5 to 0.5
- bias_weight: bfloat16 [128, 4], replicated, may hold values from -0.5 to 0.5
- out_weight: bfloat16 [128, 128], replicated, may hold values from -0.5 to 0.5
Outputs:
- update: bfloat16 [512, 512, 128], P('ia', 'ja')
- pair_grad: float32 [512, 512, 128], P('ia', 'ja')
All inputs are finite; a program needn't handle non-finite values.
Results may differ from a plain program's by a relative error of at most 0.04.
The roundings to bfloat16 on the way count: a program that leaves them out, or rounds other values in their place, can miss the bound.
Values may be sent and summed in bfloat16 or wider, within the bound.
No kernel may reach another device: no remote copies, remote signals or barrier semaphores. Data moves between devices by JAX's collectives and lax.ppermute only.
A program may use at most 128 MiB of HBM per device.

v0:
```python
import math

import jax
import jax.numpy as jnp
from jax import lax
from jax.sharding import PartitionSpec as P

EPSILON = 1e-05


def from_root(block, axis, owner):
    block = jnp.where(lax.axis_index(axis) == owner, block, jnp.zeros_like(block))
    return lax.psum(block, axis)


def normalize(values, norm_gain, norm_shift):
    mean_val = jnp.mean(values, axis=-1, keepdims=True)
    centred = values - mean_val
    variance = jnp.mean(centred * centred, axis=-1, keepdims=True)
    return centred * lax.rsqrt(variance + EPSILON) * norm_gain + norm_shift


def project(rows, weight):
    return jnp.dot(rows, weight, preferred_element_type=jnp.float32)


def shards(
    pair,
    cotangent,
    norm_gain,
    norm_shift,
    query_weight,
    key_weight,
    value_weight,
    gate_weight,
    bias_weight,
    out_weight,
):
    rows_i, rows_j, channels = pair.shape
    head_count = bias_weight.shape[1]
    inner_width = query_weight.shape[1]
    head_dim = inner_width // head_count
    row_ratio = lax.axis_size("ia") // lax.axis_size("ja")
    key_count = rows_j * lax.axis_size("ja")
    block_len = min(128, key_count)
    block_total = key_count // block_len
    score_scale = 1.0 / math.sqrt(head_dim)
    column = lax.axis_index("ja")
    row_index = lax.axis_index("ia")
    flat_pair = pair.astype(jnp.float32).reshape(rows_i * rows_j, channels)
    normed, norm_back = jax.vjp(lambda rows: normalize(rows, norm_gain, norm_shift), flat_pair)
    normed_b = normed.astype(jnp.bfloat16)
    queries = (
        project(normed_b, query_weight)
        .astype(jnp.bfloat16)
        .reshape(rows_i, rows_j, head_count, head_dim)
    )
    gate_act = jax.nn.sigmoid(project(normed_b, gate_weight)).reshape(rows_i, rows_j, inner_width)
    bias_tile = (
        project(normed_b, bias_weight)
        .astype(jnp.bfloat16)
        .reshape(rows_i, rows_j, head_count)
        .transpose(0, 2, 1)
    )
    keys_local = (
        project(normed_b, key_weight).astype(jnp.bfloat16).reshape(rows_i, rows_j, inner_width)
    )
    values_local = (
        project(normed_b, value_weight).astype(jnp.bfloat16).reshape(rows_i, rows_j, inner_width)
    )
    keys_all, values_all = (
        lax.all_gather(keys_local, "ja", axis=1, tiled=True),
        lax.all_gather(values_local, "ja", axis=1, tiled=True),
    )
    keys_all = keys_all.reshape(rows_i, key_count, head_count, head_dim)
    values_all = values_all.reshape(rows_i, key_count, head_count, head_dim)
    bias_rows = lax.all_gather(bias_tile, "ja", axis=2, tiled=True)
    whole_bias = lax.all_gather(bias_rows, "ia", axis=0, tiled=True)
    bias_need = lax.dynamic_slice_in_dim(whole_bias, column * rows_j, rows_j, 0)

    def block_scores(anchor, span_len):
        key_block = lax.dynamic_slice_in_dim(keys_all, anchor, span_len, 1)
        bias_block = lax.dynamic_slice_in_dim(bias_need, anchor, span_len, 2)
        raw = jnp.einsum("ijhd,ikhd->ijhk", queries, key_block, preferred_element_type=jnp.float32)
        return raw * score_scale + bias_block.astype(jnp.float32)[None]

    def max_step(position, state):
        running_max, running_sum = state
        scores = block_scores(position * block_len, block_len)
        new_max = jnp.maximum(running_max, jnp.max(scores, axis=-1))
        running_sum = running_sum * jnp.exp(running_max - new_max) + jnp.sum(
            jnp.exp(scores - new_max[..., None]), axis=-1
        )
        return (new_max, running_sum)

    start_max = jnp.full((rows_i, rows_j, head_count), -1e30, jnp.float32)
    start_sum = jnp.zeros((rows_i, rows_j, head_count), jnp.float32)
    final_max, final_sum = lax.fori_loop(0, block_total, max_step, (start_max, start_sum))
    log_total = final_max + jnp.log(final_sum)

    def out_step(position, accumulated):
        anchor = position * block_len
        probs_b = jnp.exp(block_scores(anchor, block_len) - log_total[..., None]).astype(
            jnp.bfloat16
        )
        value_block = lax.dynamic_slice_in_dim(values_all, anchor, block_len, 1)
        return accumulated + jnp.einsum(
            "ijhk,ikhd->ijhd", probs_b, value_block, preferred_element_type=jnp.float32
        )

    zero_heads = jnp.zeros((rows_i, rows_j, head_count, head_dim), jnp.float32)
    attended4 = lax.fori_loop(0, block_total, out_step, zero_heads)
    attended = attended4.reshape(rows_i, rows_j, inner_width)
    gated = (gate_act * attended).astype(jnp.bfloat16)
    update = jnp.einsum(
        "ijd,dc->ijc", gated, out_weight, preferred_element_type=jnp.float32
    ).astype(jnp.bfloat16)
    d_gated = jnp.einsum("ijc,dc->ijd", cotangent, out_weight, preferred_element_type=jnp.float32)
    d_att = (d_gated * gate_act).astype(jnp.bfloat16)
    d_gate_pre = (d_gated * attended * gate_act * (1.0 - gate_act)).astype(jnp.bfloat16)
    d_att4 = d_att.reshape(rows_i, rows_j, head_count, head_dim)
    diag_term = jnp.sum(d_att4.astype(jnp.float32) * attended4, axis=-1)

    def block_terms(anchor, span_len):
        key_block = lax.dynamic_slice_in_dim(keys_all, anchor, span_len, 1)
        value_block = lax.dynamic_slice_in_dim(values_all, anchor, span_len, 1)
        probs = jnp.exp(block_scores(anchor, span_len) - log_total[..., None])
        probs_b = probs.astype(jnp.bfloat16)
        d_probs = jnp.einsum(
            "ijhd,ikhd->ijhk", d_att4, value_block, preferred_element_type=jnp.float32
        )
        d_scores = (probs * (d_probs - diag_term[..., None])).astype(jnp.bfloat16)
        query_term = jnp.einsum(
            "ijhk,ikhd->ijhd", d_scores, key_block, preferred_element_type=jnp.float32
        )
        key_term = (
            jnp.einsum("ijhk,ijhd->ikhd", d_scores, queries, preferred_element_type=jnp.float32)
            * score_scale
        )
        value_term = jnp.einsum(
            "ijhk,ijhd->ikhd", probs_b, d_att4, preferred_element_type=jnp.float32
        )
        bias_term = jnp.sum(d_scores, axis=0, dtype=jnp.float32)
        return (query_term, key_term, value_term, bias_term)

    zero_bias = jnp.zeros((rows_j, head_count, key_count), jnp.float32)

    def grad_step(position, state):
        grad_query, grad_key, grad_value, grad_bias = state
        anchor = position * block_len
        query_term, key_term, value_term, bias_term = block_terms(anchor, block_len)
        grad_key = lax.dynamic_update_slice_in_dim(grad_key, key_term, anchor, 1)
        grad_value = lax.dynamic_update_slice_in_dim(grad_value, value_term, anchor, 1)
        grad_bias = lax.dynamic_update_slice_in_dim(grad_bias, bias_term, anchor, 2)
        return (grad_query + query_term, grad_key, grad_value, grad_bias)

    zero_keys = jnp.zeros((rows_i, key_count, head_count, head_dim), jnp.float32)
    query_sum, key_part, value_part, bias_part = lax.fori_loop(
        0, block_total, grad_step, (zero_heads, zero_keys, zero_keys, zero_bias)
    )
    key_sum, value_sum = (
        lax.psum_scatter(
            key_part.reshape(rows_i, key_count, inner_width).astype(jnp.bfloat16),
            "ja",
            scatter_dimension=1,
            tiled=True,
        ).astype(jnp.float32),
        lax.psum_scatter(
            value_part.reshape(rows_i, key_count, inner_width).astype(jnp.bfloat16),
            "ja",
            scatter_dimension=1,
            tiled=True,
        ).astype(jnp.float32),
    )
    grad_query_b = (
        (query_sum * score_scale).astype(jnp.bfloat16).reshape(rows_i * rows_j, inner_width)
    )
    grad_key_b = key_sum.astype(jnp.bfloat16).reshape(rows_i * rows_j, inner_width)
    grad_value_b = value_sum.astype(jnp.bfloat16).reshape(rows_i * rows_j, inner_width)
    bias_total = lax.psum(bias_part.astype(jnp.bfloat16), "ia").astype(jnp.float32)
    own_rows = lax.dynamic_slice_in_dim(bias_total, row_index % row_ratio * rows_i, rows_i, 0)
    owner_rows = from_root(own_rows.astype(jnp.bfloat16), "ja", row_index // row_ratio).astype(
        own_rows.dtype
    )
    bias_grad_tile = lax.dynamic_slice_in_dim(owner_rows, column * rows_j, rows_j, 2).astype(
        jnp.bfloat16
    )
    d_normed = jnp.einsum(
        "nd,cd->nc", grad_query_b, query_weight, preferred_element_type=jnp.float32
    )
    d_normed = d_normed + jnp.einsum(
        "nd,cd->nc", grad_key_b, key_weight, preferred_element_type=jnp.float32
    )
    d_normed = d_normed + jnp.einsum(
        "nd,cd->nc", grad_value_b, value_weight, preferred_element_type=jnp.float32
    )
    d_normed = d_normed + jnp.einsum(
        "nd,cd->nc",
        d_gate_pre.reshape(rows_i * rows_j, inner_width),
        gate_weight,
        preferred_element_type=jnp.float32,
    )
    bias_back = jnp.einsum(
        "ihj,ch->ijc", bias_grad_tile, bias_weight, preferred_element_type=jnp.float32
    )
    d_normed = d_normed + bias_back.reshape(rows_i * rows_j, channels)
    pair_grad = norm_back(d_normed)[0].reshape(rows_i, rows_j, channels)
    return (update, pair_grad)


def solution(mesh):
    in_specs = (P("ia", "ja", None), P("ia", "ja", None), P(), P(), P(), P(), P(), P(), P(), P())
    out_specs = (P("ia", "ja", None), P("ia", "ja", None))
    return jax.shard_map(shards, mesh=mesh, in_specs=in_specs, out_specs=out_specs, check_vma=False)
```

profile of v0, /device:TPU:0, one launch (start us, length us, event | category | flops | bytes accessed | tf_op | source)
XLA Modules:
  0.0 799.0 jit_solution(4232289838402924321)
XLA Ops:
  7.3 1.4 convert_reduce_fusion.1
  8.8 1.7 multiply_reduce_fusion.2
  10.6 1.7 add_convert_fusion
  13.4 30.4 %all_gather.14 = bf16[32,4,512]{0,1,2:T(4,128)(2,1)S(1)} all-gather(bf16[32,4,64]{0,1,2:T(4,128)(2,1)S(1)} %bitcast.171), channel_id=1, replica_groups=mesh['ia'=16,'ja'=8] {'ja'}, dimensions={2}, use_global_device_ids=true | all-gather | bytes 147456 | tf_op jit(solution)/shard_map/all_gather | solution.py:77
  49.4 1.4 fusion.39
  50.8 43.3 %all-gather.8.cloned.1.call-done = bf16[512,4,512]{2,1,0:T(4,128)(2,1)} async-done(((bf16[32,4,512]{2,1,0:T(4,128)(2,1)}), bf16[512,4,512]{2,1,0:T(4,128)(2,1)}) %all-gather.8.cloned.1.call-update) | async-done | bytes 2097168 | tf_op jit(solution)/shard_map/all_gather | solution.py:78
  95.3 90.1 %all-gather.6.cloned.1.call-done = bf16[32,512,128]{2,1,0:T(8,128)(2,1)} async-done(((bf16[32,64,128]{2,1,0:T(8,128)(2,1)}), bf16[32,512,128]{2,1,0:T(8,128)(2,1)}) %all-gather.6.cloned.1.call-update) | async-done | bytes 4194320 | tf_op jit(solution)/shard_map/all_gather | solution.py:72
  185.4 6.5 copy.65
  191.8 22.3 %while.50 = (s32[]{:T(128)}, f32[32,64,4]{1,2,0:T(4,128)S(1)}, f32[32,64,4]{1,2,0:T(4,128)S(1)}, bf16[32,512,4,32]{1,3,2,0:T(8,128)(2,1)}, bf16[32,64,4,32]{1,3,...) while((s32[]{:T(128)}, f32[32,64,4]{1,2,0:T(4,128)S(1)}, ...), condition=%wide.region_5.0_spmd.clone, body=%wide.region_2.0_spmd.clone.sunk | while | flops 74522632 | bytes 10846382 | solution.py:98
  191.9 3.0 fusion.94
  194.9 2.4 exponential_reduce_fusion.2
  197.4 3.0 fusion.94
  200.5 2.4 exponential_reduce_fusion.2
  203.0 3.0 fusion.94
  206.0 2.4 exponential_reduce_fusion.2
  208.6 3.0 fusion.94
  211.6 2.4 exponential_reduce_fusion.2
  214.2 64.1 %all-gather.4.cloned.1.call-done = bf16[32,512,128]{2,1,0:T(8,128)(2,1)} async-done(((bf16[32,64,128]{2,1,0:T(8,128)(2,1)}), bf16[32,512,128]{2,1,0:T(8,128)(2,1)}) %all-gather.4.cloned.1.call-update) | async-done | bytes 4194320 | tf_op jit(solution)/shard_map/all_gather | solution.py:73
  278.3 6.5 copy.64
  284.8 24.4 %while.51 = (s32[]{:T(128)}, f32[32,64,4,32]{1,3,2,0:T(8,128)}, bf16[32,512,4,32]{1,3,2,0:T(8,128)(2,1)}, bf16[32,512,4,32]{1,3,2,0:T(8,128)(2,1)}, bf16[32,64,4...) while((s32[]{:T(128)}, f32[32,64,4,32]{1,3,2,0:T(8,128)}, ...), condition=%wide.region_7.0_spmd.clone, body=%wide.region_6.0_spmd.clone.sunk | while | flops 138969088 | bytes 6129328 | solution.py:112
  284.8 5.6 bitcast_add_fusion.7
  290.4 6.3 bitcast_add_fusion.7
  296.7 6.3 bitcast_add_fusion.7
  303.0 6.3 bitcast_add_fusion.7
  309.2 2.2 copy.73
  311.4 2.8 multiply_convert_fusion.1
  314.7 2.1 multiply_reduce_fusion
  316.9 2.5 broadcast_in_dim.52.clone
  319.4 2.5 broadcast_in_dim.52
  321.8 62.6 %while.52 = (s32[]{:T(128)}, f32[32,64,4,32]{1,3,2,0:T(8,128)}, bf16[32,512,4,32]{1,3,2,0:T(8,128)(2,1)}, bf16[32,512,4,32]{1,3,2,0:T(8,128)(2,1)}, bf16[64,4,51...) while((s32[]{:T(128)}, f32[32,64,4,32]{1,3,2,0:T(8,128)}, ...), condition=%wide.region_11.0_spmd.clone, body=%wide.region_9.0_spmd.clone.sunk | while | flops 349175808 | bytes 107741592 | solution.py:158
  321.9 2.0 fusion.108
  323.9 4.3 convert_reduce_fusion.3
  328.2 2.0 bitcast_dynamic-update-slice_fusion.5
  330.3 3.7 bitcast_add_fusion.8
  335.6 1.9 copy-done.9
  337.5 2.0 fusion.108
  339.5 4.3 convert_reduce_fusion.3
  343.8 2.0 bitcast_dynamic-update-slice_fusion.5
  345.9 3.7 bitcast_add_fusion.8
  351.2 1.9 copy-done.9
  353.1 2.0 fusion.108
  355.1 4.3 convert_reduce_fusion.3
  359.4 2.0 bitcast_dynamic-update-slice_fusion.5
  361.6 3.7 bitcast_add_fusion.8
  366.8 1.9 copy-done.9
  368.8 2.0 fusion.108
  370.8 4.3 convert_reduce_fusion.3
  375.1 2.0 bitcast_dynamic-update-slice_fusion.5
  377.2 3.7 bitcast_add_fusion.8
  382.5 1.9 copy-done.9
  385.2 137.3 %all-reduce.3.cloned.1.call-done = bf16[64,4,512]{2,1,0:T(4,128)(2,1)} async-done(((bf16[64,4,512]{2,1,0:T(4,128)(2,1)}), bf16[64,4,512]{2,1,0:T(4,128)(2,1)}) %all-reduce.3.cloned.1.call-update) | async-done | bytes 262160 | tf_op jit(solution)/shard_map/psum | solution.py:180
  522.5 1.6 fusion.40
  524.2 7.9 copy.78
  532.2 7.9 copy.80
  540.1 1.6 copy-done.4
  542.0 1.7 copy.77
  543.6 2.1 reshape.118
  548.1 50.9 %all-reduce.5.cloned.1.call-done = bf16[32,4,512]{2,1,0:T(4,128)(2,1)} async-done(((bf16[32,4,512]{2,1,0:T(4,128)(2,1)}), bf16[32,4,512]{2,1,0:T(4,128)(2,1)}) %all-reduce.5.cloned.1.call-update) | async-done | bytes 131088 | tf_op jit(solution)/shard_map/psum | solution.py:13
  599.0 1.4 fusion.41
  600.4 91.3 %reduce-scatter.3.cloned.1.call-done = bf16[32,64,128]{2,0,1:T(8,128)(2,1)} async-done(((bf16[32,512,128]{2,0,1:T(8,128)(2,1)}), bf16[32,64,128]{2,0,1:T(8,128)(2,1)}) %reduce-scatter.3.cloned.1.call-update) | async-done | bytes 524304 | tf_op jit(solution)/shard_map/reduce_scatter | solution.py:162
  693.0 1.5 convolution_add_fusion.2
  694.6 90.8 %reduce-scatter.5.cloned.1.call-done = bf16[32,64,128]{2,0,1:T(8,128)(2,1)} async-done(((bf16[32,512,128]{2,0,1:T(8,128)(2,1)}), bf16[32,64,128]{2,0,1:T(8,128)(2,1)}) %reduce-scatter.5.cloned.1.call-update) | async-done | bytes 524304 | tf_op jit(solution)/shard_map/reduce_scatter | solution.py:168
  787.0 1.8 multiply_reduce_fusion.1
  790.1 2.0 broadcast_add_fusion
  (162 shorter events, 23.3 us)
Async XLA Ops:
  7.2 304.2 %copy-start = (bf16[32,64,128]{2,1,0:T(8,128)(2,1)S(1)}, bf16[32,64,128]{2,1,0:T(8,128)(2,1)}, u32[]{:S(2)}) copy-start(bf16[32,64,128]{2,1,0:T(8,128)(2,1)} %param.17) | copy-start | bytes 1572868
  7.2 37.7 %copy-start.16 = (bf16[128,128]{1,0:T(8,128)(2,1)S(1)}, bf16[128,128]{1,0:T(8,128)(2,1)}, u32[]{:S(2)}) copy-start(bf16[128,128]{1,0:T(8,128)(2,1)} %param.21) | copy-start | bytes 98308
  7.2 38.8 %copy-start.18 = (bf16[128,128]{1,0:T(8,128)(2,1)S(1)}, bf16[128,128]{1,0:T(8,128)(2,1)}, u32[]{:S(2)}) copy-start(bf16[128,128]{1,0:T(8,128)(2,1)} %param.22) | copy-start | bytes 98308
  7.2 40.2 %copy-start.14 = (bf16[128,128]{1,0:T(8,128)(2,1)S(1)}, bf16[128,128]{1,0:T(8,128)(2,1)}, u32[]{:S(2)}) copy-start(bf16[128,128]{1,0:T(8,128)(2,1)} %param.20) | copy-start | bytes 98308
  7.2 87.0 %all-gather.8.cloned.1.call-start = ((), (), s32[]{:S(2)}) async-start(), calls=%async_computation.4 | async-start | bytes 2228224 | tf_op jit(solution)/shard_map/all_gather | solution.py:78
  10.6 37.4 %copy-start.20 = (f32[2048]{0:T(1024)}, f32[2048]{0:T(1024)S(1)}, u32[]{:S(2)}) copy-start(f32[2048]{0:T(1024)S(1)} %add.223) | copy-start | bytes 24580
  44.8 140.6 %all-gather.6.cloned.1.call-start = ((), (), s32[]{:S(2)}) async-start(), calls=%async_computation.3 | async-start | bytes 4718592 | tf_op jit(solution)/shard_map/all_gather | solution.py:72
  45.9 3.5 copy-start.22
  46.0 232.3 %all-gather.4.cloned.1.call-start = ((), (), s32[]{:S(2)}) async-start(), calls=%async_computation.2 | async-start | bytes 4718592 | tf_op jit(solution)/shard_map/all_gather | solution.py:73
  47.1 475.4 %all-reduce.3.cloned.1.call-start = ((), (), s32[]{:S(2)}) async-start(), calls=%async_computation.7 | async-start | bytes 524288 | tf_op jit(solution)/shard_map/psum | solution.py:180
  284.8 26.6 %copy-start.15 = (bf16[128,128]{1,0:T(8,128)(2,1)S(1)}, bf16[128,128]{1,0:T(8,128)(2,1)}, u32[]{:S(2)}) copy-start(bf16[128,128]{1,0:T(8,128)(2,1)} %param.25) | copy-start | bytes 98308
  311.4 2.8 copy-start.10
  323.9 4.3 copy-start.6
  328.1 2.1 copy-start.2
  330.2 4.8 copy-start.7
  330.2 4.0 copy-start.8
  334.2 1.3 copy-start.3
  335.6 1.9 copy-start.9
  339.5 4.3 copy-start.6
  343.8 2.1 copy-start.2
  345.8 4.8 copy-start.7
  345.8 4.0 copy-start.8
  349.9 1.3 copy-start.3
  351.2 1.9 copy-start.9
  355.1 4.3 copy-start.6
  359.4 2.1 copy-start.2
  361.4 4.8 copy-start.7
  361.5 4.0 copy-start.8
  365.5 1.3 copy-start.3
  366.8 1.9 copy-start.9
  370.8 4.3 copy-start.6
  375.1 2.1 copy-start.2
  377.1 4.8 copy-start.7
  377.1 4.0 copy-start.8
  381.1 1.3 copy-start.3
  382.5 1.9 copy-start.9
  384.4 0.7 copy-start.13
  385.1 213.9 %all-reduce.5.cloned.1.call-start = ((), (), s32[]{:S(2)}) async-start(), calls=%async_computation.8 | async-start | bytes 262144 | tf_op jit(solution)/shard_map/psum | solution.py:13
  524.2 167.6 %reduce-scatter.3.cloned.1.call-start = ((), (), s32[]{:S(2)}) async-start(), calls=%async_computation.5 | async-start | bytes 4718592 | tf_op jit(solution)/shard_map/reduce_scatter | solution.py:162
  532.1 253.3 %reduce-scatter.5.cloned.1.call-start = ((), (), s32[]{:S(2)}) async-start(), calls=%async_computation.6 | async-start | bytes 4718592 | tf_op jit(solution)/shard_map/reduce_scatter | solution.py:168
  540.0 1.6 copy-start.4
  541.9 5.1 copy-start.11
  542.0 5.1 copy-start.12
  542.0 57.1 %copy-start.24 = (bf16[128,4]{0,1:T(4,128)(2,1)S(1)}, bf16[128,4]{0,1:T(4,128)(2,1)}, u32[]{:S(2)}) copy-start(bf16[128,4]{0,1:T(4,128)(2,1)} %param.24) | copy-start | bytes 3076
  543.6 149.4 %copy-start.17 = (bf16[128,128]{1,0:T(8,128)(2,1)S(1)}, bf16[128,128]{1,0:T(8,128)(2,1)}, u32[]{:S(2)}) copy-start(bf16[128,128]{1,0:T(8,128)(2,1)} %param.21) | copy-start | bytes 98308
  547.0 239.6 %copy-start.19 = (bf16[128,128]{1,0:T(8,128)(2,1)S(1)}, bf16[128,128]{1,0:T(8,128)(2,1)}, u32[]{:S(2)}) copy-start(bf16[128,128]{1,0:T(8,128)(2,1)} %param.22) | copy-start | bytes 98308
  548.1 238.8 %copy-start.5 = (bf16[32,64,128]{2,1,0:T(8,128)(2,1)S(1)}, bf16[32,64,128]{2,1,0:T(8,128)(2,1)}, u32[]{:S(2)}) copy-start(bf16[32,64,128]{2,1,0:T(8,128)(2,1)} %param.16) | copy-start | bytes 1572868
  548.1 238.8 %copy-start.23 = (bf16[128,128]{1,0:T(8,128)(2,1)S(1)}, bf16[128,128]{1,0:T(8,128)(2,1)}, u32[]{:S(2)}) copy-start(bf16[128,128]{1,0:T(8,128)(2,1)} %param.23) | copy-start | bytes 98308
  548.1 238.8 %copy-start.25 = (f32[128]{0:T(128)S(1)}, f32[128]{0:T(128)}, u32[]{:S(2)}) copy-start(f32[128]{0:T(128)} %param.18) | copy-start | bytes 1540
  694.5 94.2 %copy-start.21 = (f32[2048]{0:T(1024)S(1)}, f32[2048]{0:T(1024)}, u32[]{:S(2)}) copy-start(f32[2048]{0:T(1024)} %copy-done.20) | copy-start | bytes 24580
  786.9 5.2 copy-start.1
Sparse Core Ops, SparseCore 0:
  44.9 49.2 all-gather.7
  95.8 89.4 all-gather.5
  187.6 90.6 all-gather.3
  385.3 137.1 all-reduce.2
  524.9 74.0 all-reduce.4
  601.3 90.4 reduce-scatter.2
  694.2 91.1 reduce-scatter.4
where the time goes:
time: 801 us; the launch traced here: 799 us
  waiting for transfers between devices  568 us (71%)
  matrix products  102 us (13%)
  local copies, waits for them, and re-layouts  60.2 us (8%)
  blocking collectives  30.4 us (4%)
  other arithmetic  22.5 us (3%)
  between operations  14.6 us (2%)
    psum x1, waiting for transfers between devices, shards(): lax.psum(bias_part.astype(jnp.bfloat16), 'ia').astype(jnp.float32)  137 us
    reduce_scatter x1, waiting for transfers between devices, shards(): lax.psum_scatter(key_part.reshape(rows_i, key_count, inner_width).astype(...  91.3 us
    reduce_scatter x1, waiting for transfers between devices, shards(): lax.psum_scatter(value_part.reshape(rows_i, key_count, inner_width).astyp...  90.8 us
    all_gather x1, waiting for transfers between devices, shards(): lax.all_gather(keys_local, 'ja', axis=1, tiled=True)  90.1 us
    all_gather x1, waiting for transfers between devices, shards(): lax.all_gather(values_local, 'ja', axis=1, tiled=True)  64.1 us
    psum x1, waiting for transfers between devices, from_root(): return lax.psum(block, axis)  50.9 us
    all_gather x1, waiting for transfers between devices, shards(): whole_bias = lax.all_gather(bias_rows, 'ia', axis=0, tiled=True)  43.3 us
    all_gather x1, blocking collectives, shards(): bias_rows = lax.all_gather(bias_tile, 'ja', axis=2, tiled=True)  30.4 us
  transfers between devices with their start and end apart: 7, of which 7 were waited for; matrix products, arithmetic and copies ran while one was open for 8% of the time, Pallas kernels for 0%

commit v1 on v0

v1 whole, which is shorter than its diff:
```python
import math

import jax
import jax.numpy as jnp
from jax import lax
from jax.experimental import pallas as pl
from jax.experimental.pallas import tpu as pltpu
from jax.sharding import Mesh, PartitionSpec as P

EPSILON = 1e-05
LOG2E = math.log2(math.e)
IA = ("z", "xh", "core")
JA = ("y", "xl")
F32 = jnp.float32
BF16 = jnp.bfloat16


def normalize(values, norm_gain, norm_shift):
    mean_val = jnp.mean(values, axis=-1, keepdims=True)
    centred = values - mean_val
    variance = jnp.mean(centred * centred, axis=-1, keepdims=True)
    return centred * lax.rsqrt(variance + EPSILON) * norm_gain + norm_shift


def mm(a, b):
    return lax.dot_general(a, b, (((1,), (0,)), ((), ())), preferred_element_type=F32)


def mm_nt(a, b):
    return lax.dot_general(a, b, (((1,), (1,)), ((), ())), preferred_element_type=F32)


def mm_tn(a, b):
    return lax.dot_general(a, b, (((0,), (0,)), ((), ())), preferred_element_type=F32)


def attention_kernel(
    heads,
    pair_ref,
    cot_ref,
    gain_ref,
    shift_ref,
    w_n_ref,
    w_t_ref,
    w_o_ref,
    bias0_ref,
    bias1_ref,
    update_ref,
    dn_ref,
    gb0_ref,
    gb1_ref,
    bias_s,
    gb_s,
    s_s,
    dp_s,
    p_s,
    ds_s,
    qt_s,
    kt_s,
    vt_s,
    dat_s,
    att_s,
    dq_s,
    dk_s,
    dv_s,
):
    row = pl.program_id(0)
    n_blocks, _, block, channels = pair_ref.shape
    n = n_blocks * block
    inner = w_o_ref.shape[0]
    head_dim = inner // heads
    scale = 1.0 / math.sqrt(head_dim)
    lanes = 128
    chunks = n // lanes
    half = heads // 2

    @pl.when(row == 0)
    def _():
        for h in range(heads):
            src = bias0_ref if h < half else bias1_ref
            hh = h % half
            for z in range(chunks):
                for b in range(n_blocks):
                    tile = src[z, b, hh * block : (hh + 1) * block, :].astype(F32)
                    bias_s[h, b * block : (b + 1) * block, z * lanes : (z + 1) * lanes] = (
                        tile * LOG2E
                    )

    x = pair_ref[...].reshape(n, channels).astype(F32)
    normed = normalize(x, gain_ref[...], shift_ref[...]).astype(BF16)
    proj = mm(normed, w_n_ref[...])
    q_n = proj[:, :inner].astype(BF16)
    k_n = proj[:, inner : 2 * inner].astype(BF16)
    v_n = proj[:, 2 * inner :].astype(BF16)
    proj_t = mm_nt(w_t_ref[...], normed)
    qt_s[...] = proj_t[:inner].astype(BF16)
    gate = jax.nn.sigmoid(proj_t[inner : 2 * inner])
    kt_s[...] = proj_t[2 * inner : 3 * inner].astype(BF16)
    vt_s[...] = proj_t[3 * inner :].astype(BF16)
    d_gated = mm_nt(w_o_ref[...], cot_ref[...].reshape(n, channels))
    dat = (d_gated * gate).astype(BF16)
    dat_s[...] = dat
    da_n = dat.T
    dk_s[...] = jnp.zeros_like(dk_s)
    dv_s[...] = jnp.zeros_like(dv_s)
    row_head = lax.broadcasted_iota(jnp.int32, (inner, n), 0) // head_dim
    lane_head = lax.broadcasted_iota(jnp.int32, (n, inner), 1) // head_dim
    step = 16

    def head_body(h, carry):
        rows = pl.ds(pl.multiple_of(h * head_dim, head_dim), head_dim)
        q_mask = jnp.where(row_head == h, qt_s[...], jnp.zeros((), BF16))
        a_mask = jnp.where(row_head == h, dat_s[...], jnp.zeros((), BF16))
        s_s[...] = mm(k_n, q_mask)
        top = jnp.full((8, n), -jnp.inf, F32)
        for k in range(0, n, step):
            t = s_s[k : k + step, :] * (scale * LOG2E) + bias_s[h, k : k + step, :]
            s_s[k : k + step, :] = t
            top = jnp.maximum(top, jnp.maximum(t[:8], t[8:]))
        top = jnp.max(top, axis=0, keepdims=True)
        total = jnp.zeros((8, n), F32)
        for k in range(0, n, step):
            p = jnp.exp2(s_s[k : k + step, :] - top)
            s_s[k : k + step, :] = p
            total = total + (p[:8] + p[8:])
        inv = 1.0 / jnp.sum(total, axis=0, keepdims=True)
        for k in range(0, n, step):
            p_s[k : k + step, :] = (s_s[k : k + step, :] * inv).astype(BF16)
        att = mm(vt_s[rows, :], p_s[...])
        att_s[rows, :] = att
        diag = jnp.sum(dat_s[rows, :].astype(F32) * att, axis=0, keepdims=True)
        dp_s[...] = mm(v_n, a_mask)
        for k in range(0, n, step):
            ds = (s_s[k : k + step, :] * inv) * (dp_s[k : k + step, :] - diag)
            gb_s[h, k : k + step, :] += ds
            ds_s[k : k + step, :] = ds.astype(BF16)
        dq_s[rows, :] = mm(kt_s[rows, :], ds_s[...])
        dk_s[...] += mm(ds_s[...], jnp.where(lane_head == h, q_n, jnp.zeros((), BF16)))
        dv_s[...] += mm(p_s[...], jnp.where(lane_head == h, da_n, jnp.zeros((), BF16)))
        return carry

    @pl.when(row == 0)
    def _():
        gb_s[...] = jnp.zeros_like(gb_s)

    lax.fori_loop(0, heads, head_body, 0)

    att = att_s[...]
    gated = (gate * att).astype(BF16)
    update = mm_tn(gated, w_o_ref[...])
    update_ref[...] = update.astype(BF16).reshape(update_ref.shape)
    d_gate = (d_gated * att * gate * (1.0 - gate)).astype(BF16)
    left_t = jnp.concatenate([(dq_s[...] * scale).astype(BF16), d_gate], axis=0)
    left = jnp.concatenate(
        [(dk_s[...] * scale).astype(BF16), dv_s[...].astype(BF16)], axis=1
    )
    dn = mm_tn(left_t, w_t_ref[: 2 * inner]) + mm(left, w_t_ref[2 * inner :])
    dn_ref[...] = dn.astype(BF16).reshape(dn_ref.shape)

    @pl.when(row == pl.num_programs(0) - 1)
    def _():
        for h in range(heads):
            dst = gb0_ref if h < half else gb1_ref
            hh = h % half
            for z in range(chunks):
                for b in range(n_blocks):
                    dst[z, b, hh * block : (hh + 1) * block, :] = gb_s[
                        h, b * block : (b + 1) * block, z * lanes : (z + 1) * lanes
                    ].astype(BF16)


def attention(heads, pair, cot, gain, shift, w_n, w_t, w_o, bias0, bias1):
    n_blocks, rows, block, channels = pair.shape
    n = n_blocks * block
    inner = w_o.shape[0]
    row_spec = pl.BlockSpec((n_blocks, 1, block, channels), lambda i: (0, i, 0, 0))

    def whole(a):
        return pl.BlockSpec(a.shape, lambda i: (0,) * len(a.shape))

    flops = 2 * 6 * rows * n * n * inner
    return pl.pallas_call(
        lambda *refs: attention_kernel(heads, *refs),
        grid=(rows,),
        in_specs=[row_spec, row_spec]
        + [whole(a) for a in (gain, shift, w_n, w_t, w_o, bias0, bias1)],
        out_specs=[row_spec, row_spec, whole(bias0), whole(bias1)],
        out_shape=[
            jax.ShapeDtypeStruct(pair.shape, BF16),
            jax.ShapeDtypeStruct(pair.shape, BF16),
            jax.ShapeDtypeStruct(bias0.shape, BF16),
            jax.ShapeDtypeStruct(bias1.shape, BF16),
        ],
        scratch_shapes=[
            pltpu.VMEM((heads, n, n), F32),
            pltpu.VMEM((heads, n, n), F32),
            pltpu.VMEM((n, n), F32),
            pltpu.VMEM((n, n), F32),
            pltpu.VMEM((n, n), BF16),
            pltpu.VMEM((n, n), BF16),
            pltpu.VMEM((inner, n), BF16),
            pltpu.VMEM((inner, n), BF16),
            pltpu.VMEM((inner, n), BF16),
            pltpu.VMEM((inner, n), BF16),
            pltpu.VMEM((inner, n), F32),
            pltpu.VMEM((inner, n), F32),
            pltpu.VMEM((n, inner), F32),
            pltpu.VMEM((n, inner), F32),
        ],
        compiler_params=pltpu.CompilerParams(vmem_limit_bytes=48 * 1024 * 1024),
        cost_estimate=pl.CostEstimate(
            flops=flops, bytes_accessed=8 * 2**20, transcendentals=rows * n * n * heads
        ),
    )(pair, cot, gain, shift, w_n, w_t, w_o, bias0, bias1)


def swap(a):
    return lax.ppermute(a, "core", [(0, 1), (1, 0)])


def shards(
    pair,
    cotangent,
    norm_gain,
    norm_shift,
    query_weight,
    key_weight,
    value_weight,
    gate_weight,
    bias_weight,
    out_weight,
):
    rows_i, rows_j, channels = pair.shape
    heads = bias_weight.shape[1]
    inner = query_weight.shape[1]
    n_ja = lax.axis_size(JA)
    n_z = lax.axis_size("z")
    n_xh = lax.axis_size("xh")
    n_core = lax.axis_size("core")
    own_i = rows_i // n_ja
    core = lax.axis_index("core")
    width = (heads // n_core) * rows_j

    pair_rows = lax.all_to_all(
        pair.reshape(n_ja, own_i, rows_j, channels), JA, 0, 0, tiled=True
    )
    cot_rows = lax.all_to_all(
        cotangent.reshape(n_ja, own_i, rows_j, channels), JA, 0, 0, tiled=True
    )

    flat_pair = pair.astype(F32).reshape(rows_i * rows_j, channels)
    normed, norm_back = jax.vjp(lambda rows: normalize(rows, norm_gain, norm_shift), flat_pair)
    bias_tile = (
        jnp.dot(normed.astype(BF16), bias_weight, preferred_element_type=F32)
        .astype(BF16)
        .reshape(rows_i, rows_j, heads)
        .transpose(0, 2, 1)
        .reshape(rows_i, n_core, width)
        .transpose(1, 0, 2)
    )
    near = lax.all_to_all(
        jnp.broadcast_to(
            bias_tile[None, :, None], (n_xh, n_core, n_ja, rows_i, width)
        ).reshape(n_xh * n_core * n_ja, rows_i, width),
        ("xh", "core", "y", "xl"),
        0,
        0,
        tiled=True,
    )
    near = (
        near.reshape(n_xh * n_core, n_ja, rows_i, width)
        .transpose(1, 3, 0, 2)
        .reshape(n_ja, width, n_xh * n_core * rows_i)
    )
    bias_own = lax.all_to_all(
        jnp.broadcast_to(near[None], (n_z,) + near.shape), "z", 0, 0, tiled=True
    )
    bias_other = swap(bias_own)

    turn = core * (inner // n_core)

    def turned(w, axis):
        return jnp.where(core == 0, w, jnp.roll(w, inner // n_core, axis))

    del turn
    w_q, w_k, w_v, w_g = (
        turned(w, 1) for w in (query_weight, key_weight, value_weight, gate_weight)
    )
    w_o = turned(out_weight, 0)
    w_n = jnp.concatenate([w_q, w_k, w_v], axis=1)
    w_t = jnp.concatenate([w_q.T, w_g.T, w_k.T, w_v.T], axis=0)

    update_rows, dn_rows, gb_own, gb_other = attention(
        heads,
        pair_rows,
        cot_rows,
        norm_gain.reshape(1, channels),
        norm_shift.reshape(1, channels),
        w_n,
        w_t,
        w_o,
        bias_own,
        bias_other,
    )

    update = lax.all_to_all(update_rows, JA, 0, 0, tiled=True).reshape(pair.shape)
    dn = lax.all_to_all(dn_rows, JA, 0, 0, tiled=True).reshape(rows_i * rows_j, channels)

    gb = (gb_own.astype(F32) + swap(gb_other).astype(F32)).astype(BF16)
    gb = lax.all_to_all(gb, "z", 0, 0, tiled=True)
    gb = jnp.sum(gb.astype(F32), axis=0).astype(BF16)
    gb = (
        gb.transpose(2, 0, 1)
        .reshape(n_xh * n_core, rows_i, n_ja, width)
        .transpose(0, 2, 1, 3)
        .reshape(n_xh * n_core * n_ja, rows_i, width)
    )
    gb = lax.all_to_all(gb, ("xh", "core", "y", "xl"), 0, 0, tiled=True)
    gb = jnp.sum(
        gb.reshape(n_xh, n_core, n_ja, rows_i, width).astype(F32), axis=(0, 2)
    ).astype(BF16)
    gb = gb.transpose(1, 0, 2).reshape(rows_i, heads, rows_j)
    bias_back = jnp.einsum("ihj,ch->ijc", gb, bias_weight, preferred_element_type=F32)
    d_normed = dn.astype(F32) + bias_back.reshape(rows_i * rows_j, channels)
    pair_grad = norm_back(d_normed)[0].reshape(rows_i, rows_j, channels)
    return (update, pair_grad)


def solution(mesh):
    fine = Mesh(mesh.devices.reshape(4, 2, 2, 4, 2), IA + JA)
    spec = P(IA, JA, None)
    in_specs = (spec, spec) + (P(),) * 8
    return jax.shard_map(
        shards, mesh=fine, in_specs=in_specs, out_specs=(spec, spec), check_vma=False
    )
```

time: 801 us -> 166 us (0.21)
  waiting for transfers between devices: 568 us -> 54.9 us
  matrix products: 102 us -> 2.15 us
  local copies, waits for them, and re-layouts: 60.2 us -> 3.56 us
  Pallas kernels: 0 us -> 28 us
  starting transfers between devices: 0.47 us -> 19.5 us
  blocking collectives: 30.4 us -> 47.4 us
  between operations: 14.6 us -> 0.92 us
  other arithmetic: 22.5 us -> 9.26 us
    all_gather x3 -> x0, waiting for transfers between devices: 198 us -> none  [the longest x1 90.1 us: shards(): lax.all_gather(keys_local, 'ja', axis=1, tiled=True)]
    psum x2 -> x0, waiting for transfers between devices: 188 us -> none  [the longest x1 137 us: shards(): lax.psum(bias_part.astype(jnp.bfloat16), 'ia').astype(jnp.float32)]
    reduce_scatter x2 -> x0, waiting for transfers between devices: 182 us -> none  [the longest x1 91.3 us: shards(): lax.psum_scatter(key_part.reshape(rows_i, key_count, inner_width).astype(...]
    dot_general x40 -> x2, matrix products: 102 us -> 2.15 us  [the longest x1 1.92 us: shards(): jnp.einsum('ihj,ch->ijc', gb, bias_weight, preferred_element_type=F32)]
    all_to_all x0 -> x5, waiting for transfers between devices: none -> 52.2 us  [the longest x1 15.1 us: shards(): lax.all_to_all(jnp.broadcast_to(near[None], (n_z,) + near.shape), 'z', 0,...]
    all_to_all x0 -> x3, blocking collectives: none -> 47.4 us  [the longest x1 18.1 us: shards(): gb = lax.all_to_all(gb, 'z', 0, 0, tiled=True)]
    all_gather x1 -> x0, blocking collectives: 30.4 us -> none  [shards(): bias_rows = lax.all_gather(bias_tile, 'ja', axis=2, tiled=True)]
    pallas_call x0 -> x1, Pallas kernels: none -> 28 us  [attention(): pl.pallas_call(lambda *refs: attention_kernel(heads, *refs), grid=(rows,)...]
  transfers between devices with their start and end apart: 7 -> 7, of which waited for: 7 -> 6; matrix products, arithmetic and copies ran while one was open for 8% -> 1% of each run, Pallas kernels for 0% -> 0%
where the time goes in v1:
time: 166 us
  waiting for transfers between devices  54.9 us (33%)
  blocking collectives  47.4 us (29%)
  Pallas kernels  28 us (17%)
  starting transfers between devices  19.5 us (12%)
  other arithmetic  9.26 us (6%)
  local copies, waits for them, and re-layouts  3.56 us (2%)
  matrix products  2.15 us (1%)
    pallas_call x1, Pallas kernels, attention(): pl.pallas_call(lambda *refs: attention_kernel(heads, *refs), grid=(rows,)...  28 us
    all_to_all x1, blocking collectives, shards(): gb = lax.all_to_all(gb, 'z', 0, 0, tiled=True)  18.1 us
    all_to_all x1, blocking collectives, shards(): lax.all_to_all(jnp.broadcast_to(bias_tile[None, :, None], (n_xh, n_core,...  16.1 us
    all_to_all x1, waiting for transfers between devices, shards(): lax.all_to_all(jnp.broadcast_to(near[None], (n_z,) + near.shape), 'z', 0,...  15.1 us
    all_to_all x1, blocking collectives, shards(): gb = lax.all_to_all(gb, ('xh', 'core', 'y', 'xl'), 0, 0, tiled=True)  13.2 us
    all_to_all x1, waiting for transfers between devices, shards(): lax.all_to_all(dn_rows, JA, 0, 0, tiled=True)  10.3 us
    all_to_all x1, waiting for transfers between devices, shards(): lax.all_to_all(update_rows, JA, 0, 0, tiled=True).reshape(pair.shape)  9.31 us
    all_to_all x1, waiting for transfers between devices, shards(): lax.all_to_all(cotangent.reshape(n_ja, own_i, rows_j, channels), JA, 0, 0...  9.08 us
  transfers between devices with their start and end apart: 7, of which 6 were waited for; matrix products, arithmetic and copies ran while one was open for 1% of the time, Pallas kernels for 0%

profile of v1, /device:TPU:0, one launch (start us, length us, event | category | flops | bytes accessed | tf_op | source)
XLA Modules:
  0.0 165.6 jit_solution(11649685275408491791)
XLA Ops:
  0.6 0.0 copy-start
  0.6 0.0 copy-start.1
  0.7 0.0 copy-start.2
  0.7 1.4 convert_reduce_fusion
  2.1 0.1 div.21
  2.2 1.7 %multiply_reduce_fusion.1 = f32[32,64]{1,0:T(8,128)S(1)} fusion(bf16[32,64,128]{2,1,0:T(8,128)(2,1)} %param.10, f32[32,64]{1,0:T(8,128)S(1)} %broadcast_multiply_fusion), kind=kLoop, calls=%fused_computation.8 | loop fusion | flops 1046528 | bytes 540672 | tf_op jit(solution)/shard_map/jvp()/reduce_sum | solution.py:21
  3.9 0.1 add.32
  3.9 0.0 copy-done.1
  3.9 0.0 copy-done.2
  3.9 1.7 add_convert_fusion.1
  5.6 0.0 copy-done
  5.6 0.2 convolution_convert_fusion
  5.8 0.1 reshape.106
  6.0 0.1 reshape.107
  6.1 16.1 %all_to_all.40 = bf16[32,32,128]{2,1,0:T(8,128)(2,1)S(1)} all-to-all(bf16[32,32,128]{2,1,0:T(8,128)(2,1)S(1)} %bitcast.57), channel_id=1, replica_groups=mesh['z'=4,'xh'=2,'core'=2,'y'=4,'xl'=2] {'xh','core','y','xl'}, dimensions={0} | all-to-all | bytes 524288 | tf_op jit(solution)/shard_map/all_to_all | solution.py:261
  22.3 0.2 copy.24
  22.5 1.2 broadcast_in_dim.12
  23.7 0.0 copy-start.5
  23.7 0.0 copy-start.6
  23.7 0.0 copy-start.3
  23.7 5.4 %all-to-all-start.3 = ((bf16[4,8,128,128]{3,2,1,0:T(8,128)(2,1)}), bf16[4,8,128,128]{3,2,1,0:T(8,128)(2,1)S(1)}, u32[]{:S(2)}, u32[]{:S(2)}) async-start(bf16[4,8,128,128]{3,2,1,0:T(8,128)(2,1)} %broadcast_in_dim.12), calls=%async_computation.3 | async-start | bytes 2097152 | tf_op jit(solution)/shard_map/all_to_all | solution.py:275
  29.1 0.0 copy-done.5
  29.1 0.0 copy-start.4
  29.1 0.1 fusion.5
  29.2 0.0 copy-done.6
  29.2 0.1 fusion.6
  29.3 0.0 copy-done.3
  29.3 0.1 fusion.7
  29.4 15.1 %all-to-all-done.3.refs_7_ = bf16[4,8,128,128]{3,2,1,0:T(8,128)(2,1)S(1)} async-done(((bf16[4,8,128,128]{3,2,1,0:T(8,128)(2,1)}), bf16[4,8,128,128]{3,2,1,0:T(8,128)(2,1)S(1)}, u32[]{:S(2)}, u32[]{:S(2)}) %all-to-all-start.3) | async-done | bytes 1048608 | tf_op jit(solution)/shard_map/all_to_all | solution.py:275
  44.5 3.5 %all-to-all-start.1 = ((bf16[8,4,64,128]{3,2,1,0:T(8,128)(2,1)}), bf16[8,4,64,128]{3,2,1,0:T(8,128)(2,1)S(1)}, u32[]{:S(2)}, u32[]{:S(2)}) async-start(bf16[8,4,64,128]{3,2,1,0:T(8,128)(2,1)} %bitcast.1), calls=%async_computation.1 | async-start | bytes 1048576 | tf_op jit(solution)/shard_map/all_to_all | solution.py:247
  48.0 0.0 copy-done.4
  48.0 0.0 copy-start.7
  48.0 0.1 fusion.4
  48.1 0.0 collective-permute-start
  48.2 0.1 fusion.1
  48.3 0.1 maximum_select_fusion
  48.4 9.1 %all-to-all-done.1.refs_1_ = bf16[8,4,64,128]{3,2,1,0:T(8,128)(2,1)S(1)} async-done(((bf16[8,4,64,128]{3,2,1,0:T(8,128)(2,1)}), bf16[8,4,64,128]{3,2,1,0:T(8,128)(2,1)S(1)}, u32[]{:S(2)}, u32[]{:S(2)}) %all-to-all-start.1) | async-done | bytes 524320 | tf_op jit(solution)/shard_map/all_to_all | solution.py:247
  57.4 3.5 %all-to-all-start = ((bf16[8,4,64,128]{3,2,1,0:T(8,128)(2,1)}), bf16[8,4,64,128]{3,2,1,0:T(8,128)(2,1)S(1)}, u32[]{:S(2)}, u32[]{:S(2)}) async-start(bf16[8,4,64,128]{3,2,1,0:T(8,128)(2,1)} %bitcast), calls=%async_computation | async-start | bytes 1048576 | tf_op jit(solution)/shard_map/all_to_all | solution.py:244
  60.9 0.0 copy-done.7
  61.0 0.1 maximum_select_fusion.2
  61.1 0.1 copy.25.refs_5_
  61.2 8.4 %all-to-all-done.refs_0_ = bf16[8,4,64,128]{3,2,1,0:T(8,128)(2,1)S(1)} async-done(((bf16[8,4,64,128]{3,2,1,0:T(8,128)(2,1)}), bf16[8,4,64,128]{3,2,1,0:T(8,128)(2,1)S(1)}, u32[]{:S(2)}, u32[]{:S(2)}) %all-to-all-start) | async-done | bytes 524320 | tf_op jit(solution)/shard_map/all_to_all | solution.py:244
  69.6 0.0 collective-permute-done.refs_8_
  69.6 28.0 %shard_map.113 = (bf16[8,4,64,128]{3,2,1,0:T(8,128)(2,1)}, bf16[8,4,64,128]{3,2,1,0:T(8,128)(2,1)}, bf16[4,8,128,128]{3,2,1,0:T(8,128)(2,1)S(1)}, bf16[4,8,128,128]{3,2,1,0:T(8,128)(2,1)S(1)}) custom-call(bf16[8,4,64,128]{3,2,1,0:T(8,128)(2,1)S(1)} %all-to-all-done.refs_0_, bf16[8,4,64,128]{3,2,1,0:T(8,128)(2,1)S(1)} %all-to-all-done.1.refs_1_, ...), custom_call_target="tpu_custom_call" | custom-call | flops 1610612736 | bytes 8388608 | tf_op jit(solution)/shard_map/pallas_call | solution.py:182
  97.6 0.0 collective-permute-start.1
  97.6 2.7 %collective-permute-done.1 = bf16[4,8,128,128]{3,2,1,0:T(8,128)(2,1)S(1)} collective-permute-done((bf16[4,8,128,128]{3,2,1,0:T(8,128)(2,1)S(1)}, bf16[4,8,128,128]{3,2,1,0:T(8,128)(2,1)S(1)}, u32[]{:S(2)}, u32[]{:S(2)}) %collective-permute-start.1) | collective-permute-done | bytes 1048608 | tf_op jit(solution)/shard_map/ppermute | solution.py:218
  100.3 0.4 add_convert_fusion
  100.7 18.1 %all_to_all.41 = bf16[4,8,128,128]{3,2,1,0:T(8,128)(2,1)S(1)} all-to-all(bf16[4,8,128,128]{3,2,1,0:T(8,128)(2,1)S(1)} %add_convert_fusion), channel_id=1, replica_groups=mesh['z'=4,'xh'=2,'core'=2,'y'=4,'xl'=2] {'z'}, dimensions={0} | all-to-all | bytes 2097152 | tf_op jit(solution)/shard_map/all_to_all | solution.py:310
  118.8 3.5 %all-to-all-start.4 = ((bf16[8,4,64,128]{3,2,1,0:T(8,128)(2,1)}), bf16[8,4,64,128]{3,2,1,0:T(8,128)(2,1)S(1)}, u32[]{:S(2)}, u32[]{:S(2)}) async-start(bf16[8,4,64,128]{3,2,1,0:T(8,128)(2,1)} %get-tuple-element.6), calls=%async_computation.4 | async-start | bytes 1048576 | tf_op jit(solution)/shard_map/all_to_all | solution.py:306
  122.3 0.2 reduce_sum.70
  122.5 0.2 copy.26
  122.7 9.3 %all-to-all-done.4 = bf16[8,4,64,128]{3,2,1,0:T(8,128)(2,1)S(1)} async-done(((bf16[8,4,64,128]{3,2,1,0:T(8,128)(2,1)}), bf16[8,4,64,128]{3,2,1,0:T(8,128)(2,1)S(1)}, u32[]{:S(2)}, u32[]{:S(2)}) %all-to-all-start.4) | async-done | bytes 524320 | tf_op jit(solution)/shard_map/all_to_all | solution.py:306
  132.0 13.2 %all_to_all.42 = bf16[32,32,128]{2,1,0:T(8,128)(2,1)S(1)} all-to-all(bf16[32,32,128]{2,1,0:T(8,128)(2,1)S(1)} %bitcast.56), channel_id=1, replica_groups=mesh['z'=4,'xh'=2,'core'=2,'y'=4,'xl'=2] {'xh','core','y','xl'}, dimensions={0} | all-to-all | bytes 524288 | tf_op jit(solution)/shard_map/all_to_all | solution.py:318
  145.2 3.5 %all-to-all-start.5 = ((bf16[8,4,64,128]{3,2,1,0:T(8,128)(2,1)}), bf16[8,4,64,128]{3,2,1,0:T(8,128)(2,1)S(1)}, u32[]{:S(2)}, u32[]{:S(2)}) async-start(bf16[8,4,64,128]{3,2,1,0:T(8,128)(2,1)} %get-tuple-element.7), calls=%async_computation.5 | async-start | bytes 1048576 | tf_op jit(solution)/shard_map/all_to_all | solution.py:307
  148.8 0.1 reshape.114
  148.9 0.1 dot_general.12
  149.0 10.3 %all-to-all-done.5 = bf16[8,4,64,128]{3,2,1,0:T(8,128)(2,1)S(1)} async-done(((bf16[8,4,64,128]{3,2,1,0:T(8,128)(2,1)}), bf16[8,4,64,128]{3,2,1,0:T(8,128)(2,1)S(1)}, u32[]{:S(2)}, u32[]{:S(2)}) %all-to-all-start.5) | async-done | bytes 524320 | tf_op jit(solution)/shard_map/all_to_all | solution.py:307
  159.3 1.9 %multiply_reduce_fusion = (f32[2048]{0:T(1024)S(1)}, f32[2048,128]{1,0:T(8,128)S(1)}) fusion(bf16[32,64,128]{2,1,0:T(8,128)(2,1)} %param.10, bf16[8,4,64,128]{3,2,1,0:T(8,128)(2,1)S(1)} %all-to-all-done.5, f32[128]{0:T(128)S(1)} %copy-done.1, f32[2048]{0:T(1024)S(1)} %div.21, bf16[2048,4]{0,1:T(4,128)(2,1)S(1)} %dot_general.12, bf16[128,4]{0,1:T(4,128)(2,1)S(1)} %copy-done), kind=kOutput, calls=%fused_computation.6 | convolution fusion | flops 3930112 | bytes 2131456 | tf_op jit(solution)/shard_map/ihj,ch->ijc/dot_general | solution.py:323
  161.2 2.3 %fusion.2 = (f32[2048]{0:T(1024)S(1)}, f32[2048,128]{1,0:T(8,128)S(1)}) fusion(f32[2048]{0:T(1024)S(1)} %multiply_multiply_fusion, f32[2048]{0:T(1024)S(1)} %div.21, bf16[32,64,128]{2,1,0:T(8,128)(2,1)} %param.10, f32[2048]{0:T(1024)S(1)} %rsqrt.10, f32[128]{0:T(128)S(1)} %copy-done.1, f32[2048,128]{1,0:T(8,128)S(1)} %get-tuple-element.23, ...), kind=kLoop, calls=%fused_computation.24 | loop fusion | flops 2619392 | bytes 3179008 | tf_op jit(solution)/shard_map/transpose(jvp())/reduce_sum | solution.py:20
  163.5 1.3 broadcast_add_fusion
  164.8 0.8 copy.33
  (16 shorter events, 0.3 us)
Async XLA Ops:
  0.6 5.0 %copy-start = (bf16[128,4]{0,1:T(4,128)(2,1)S(1)}, bf16[128,4]{0,1:T(4,128)(2,1)}, u32[]{:S(2)}) copy-start(bf16[128,4]{0,1:T(4,128)(2,1)} %param.18) | copy-start | bytes 3076
  0.6 3.3 %copy-start.1 = (f32[128]{0:T(128)S(1)}, f32[128]{0:T(128)}, u32[]{:S(2)}) copy-start(f32[128]{0:T(128)} %param.12) | copy-start | bytes 1540
  0.7 3.3 %copy-start.2 = (f32[128]{0:T(128)S(1)}, f32[128]{0:T(128)}, u32[]{:S(2)}) copy-start(f32[128]{0:T(128)} %param.13) | copy-start | bytes 1540
  23.7 5.4 %copy-start.5 = (bf16[128,128]{1,0:T(8,128)(2,1)S(1)}, bf16[128,128]{1,0:T(8,128)(2,1)}, u32[]{:S(2)}) copy-start(bf16[128,128]{1,0:T(8,128)(2,1)} %param.14) | copy-start | bytes 98308
  23.7 5.5 %copy-start.6 = (bf16[128,128]{1,0:T(8,128)(2,1)S(1)}, bf16[128,128]{1,0:T(8,128)(2,1)}, u32[]{:S(2)}) copy-start(bf16[128,128]{1,0:T(8,128)(2,1)} %param.15) | copy-start | bytes 98308
  23.7 5.6 %copy-start.3 = (bf16[128,128]{1,0:T(8,128)(2,1)S(1)}, bf16[128,128]{1,0:T(8,128)(2,1)}, u32[]{:S(2)}) copy-start(bf16[128,128]{1,0:T(8,128)(2,1)} %param.16) | copy-start | bytes 98308
  23.7 20.8 %all-to-all-start.3 = ((bf16[4,8,128,128]{3,2,1,0:T(8,128)(2,1)}), bf16[4,8,128,128]{3,2,1,0:T(8,128)(2,1)S(1)}, u32[]{:S(2)}, u32[]{:S(2)}) async-start(bf16[4,8,128,128]{3,2,1,0:T(8,128)(2,1)} %broadcast_in_dim.12), calls=%async_computation.3 | async-start | bytes 2097152 | tf_op jit(solution)/shard_map/all_to_all | solution.py:275
  29.1 18.9 %copy-start.4 = (bf16[128,128]{1,0:T(8,128)(2,1)S(1)}, bf16[128,128]{1,0:T(8,128)(2,1)}, u32[]{:S(2)}) copy-start(bf16[128,128]{1,0:T(8,128)(2,1)} %param.17) | copy-start | bytes 98308
  44.5 12.9 %all-to-all-start.1 = ((bf16[8,4,64,128]{3,2,1,0:T(8,128)(2,1)}), bf16[8,4,64,128]{3,2,1,0:T(8,128)(2,1)S(1)}, u32[]{:S(2)}, u32[]{:S(2)}) async-start(bf16[8,4,64,128]{3,2,1,0:T(8,128)(2,1)} %bitcast.1), calls=%async_computation.1 | async-start | bytes 1048576 | tf_op jit(solution)/shard_map/all_to_all | solution.py:247
  48.0 12.9 %copy-start.7 = (bf16[128,128]{1,0:T(8,128)(2,1)S(1)}, bf16[128,128]{1,0:T(8,128)(2,1)}, u32[]{:S(2)}) copy-start(bf16[128,128]{1,0:T(8,128)(2,1)} %param.19) | copy-start | bytes 98308
  48.1 21.5 %collective-permute-start = (bf16[4,8,128,128]{3,2,1,0:T(8,128)(2,1)S(1)}, bf16[4,8,128,128]{3,2,1,0:T(8,128)(2,1)}, u32[]{:S(2)}, u32[]{:S(2)}) collective-permute-start(bf16[4,8,128,128]{3,2,1,0:T(8,128)(2,1)S(1)} %all-to-all-done.3.refs_7_), channel_id=1, source_target_pairs={{0,8},{8,0},{1,9},{9,1},{2,10},{10,2},{3,11},{11,3},{4,12},{12,4},... | collective-permute-start | bytes 3145736 | tf_op jit(solution)/shard_map/ppermute | solution.py:218
  57.4 12.2 %all-to-all-start = ((bf16[8,4,64,128]{3,2,1,0:T(8,128)(2,1)}), bf16[8,4,64,128]{3,2,1,0:T(8,128)(2,1)S(1)}, u32[]{:S(2)}, u32[]{:S(2)}) async-start(bf16[8,4,64,128]{3,2,1,0:T(8,128)(2,1)} %bitcast), calls=%async_computation | async-start | bytes 1048576 | tf_op jit(solution)/shard_map/all_to_all | solution.py:244
  97.6 2.7 %collective-permute-start.1 = (bf16[4,8,128,128]{3,2,1,0:T(8,128)(2,1)S(1)}, bf16[4,8,128,128]{3,2,1,0:T(8,128)(2,1)S(1)}, u32[]{:S(2)}, u32[]{:S(2)}) collective-permute-start(bf16[4,8,128,128]{3,2,1,0:T(8,128)(2,1)S(1)} %get-tuple-element.9), channel_id=1, source_target_pairs={{0,8},{8,0},{1,9},{9,1},{2,10},{10,2},{3,11},{11,3},{4,12},{12,4},... | collective-permute-start | bytes 3145736 | tf_op jit(solution)/shard_map/ppermute | solution.py:218
  118.8 13.3 %all-to-all-start.4 = ((bf16[8,4,64,128]{3,2,1,0:T(8,128)(2,1)}), bf16[8,4,64,128]{3,2,1,0:T(8,128)(2,1)S(1)}, u32[]{:S(2)}, u32[]{:S(2)}) async-start(bf16[8,4,64,128]{3,2,1,0:T(8,128)(2,1)} %get-tuple-element.6), calls=%async_computation.4 | async-start | bytes 1048576 | tf_op jit(solution)/shard_map/all_to_all | solution.py:306
  145.2 14.1 %all-to-all-start.5 = ((bf16[8,4,64,128]{3,2,1,0:T(8,128)(2,1)}), bf16[8,4,64,128]{3,2,1,0:T(8,128)(2,1)S(1)}, u32[]{:S(2)}, u32[]{:S(2)}) async-start(bf16[8,4,64,128]{3,2,1,0:T(8,128)(2,1)} %get-tuple-element.7), calls=%async_computation.5 | async-start | bytes 1048576 | tf_op jit(solution)/shard_map/all_to_all | solution.py:307

commit v2 on v1

--- a/solution.py
+++ b/solution.py
@@ -32,6 +32,121 @@
 
 def mm_tn(a, b):
     return lax.dot_general(a, b, (((0,), (0,)), ((), ())), preferred_element_type=F32)
+
+
+def swap(a):
+    return lax.ppermute(a, "core", [(0, 1), (1, 0)])
+
+
+def cross(a, bits):
+    return lax.ppermute(a, ("xh", "core"), [(s, s ^ bits) for s in range(4)])
+
+
+def shift(a, axis, by):
+    size = lax.axis_size(axis)
+    return lax.ppermute(a, axis, [(s, (s + by) % size) for s in range(size)])
+
+
+def prep_kernel(pair_ref, gain_ref, shift_ref, w_ref, mine_ref, theirs_ref, tile_s):
+    rows, block, channels = pair_ref.shape
+    x = pair_ref[...].reshape(rows * block, channels).astype(F32)
+    normed = normalize(x, gain_ref[...], shift_ref[...]).astype(BF16)
+    every = mm(normed, w_ref[...])
+    width = every.shape[1]
+    half = width // 2
+    sub = block // 2
+    lane = lax.broadcasted_iota(jnp.int32, (block, width), 1)
+    column = lane // half * sub + lane % sub
+    keep = lax.broadcasted_iota(jnp.int32, (block, width), 0) == column
+    lines = []
+    for i in range(rows):
+        part = jnp.where(keep, every[i * block : (i + 1) * block], 0.0)
+        lines.append(jnp.sum(part, axis=0, keepdims=True))
+    tile = jnp.concatenate(lines, axis=0).astype(BF16)
+    tile_s[0] = tile[:, :half]
+    tile_s[1] = tile[:, half:]
+    core = lax.axis_index("core")
+    mine_ref[...] = tile_s[core]
+    theirs_ref[...] = tile_s[1 - core]
+
+
+def prep(pair, gain, shift_row, w_spread):
+    rows = pair.shape[0]
+    half = w_spread.shape[1] // 2
+    tile = jax.ShapeDtypeStruct((rows, half), BF16)
+    return pl.pallas_call(
+        prep_kernel,
+        out_shape=[tile, tile],
+        scratch_shapes=[pltpu.VMEM((2, rows, half), BF16)],
+        compiler_params=pltpu.CompilerParams(vmem_limit_bytes=32 * 1024 * 1024),
+        cost_estimate=pl.CostEstimate(
+            flops=2**27, bytes_accessed=2**19, transcendentals=2**12
+        ),
+    )(pair, gain, shift_row, w_spread)
+
+
+def assemble_kernel(own_ref, core_ref, far_ref, both_ref, out_ref, rows_s):
+    rows = own_ref.shape[0]
+    me = lax.axis_index("xh") * 2 + lax.axis_index("core")
+    for bits, ref in enumerate((own_ref, core_ref, far_ref, both_ref)):
+        start = pl.multiple_of((me ^ bits) * rows, rows)
+        rows_s[pl.ds(start, rows), :] = ref[...]
+    out_ref[...] = rows_s[...].astype(F32).T.astype(BF16)
+
+
+def assemble(own, core, far, both):
+    rows, width = own.shape
+    return pl.pallas_call(
+        assemble_kernel,
+        out_shape=jax.ShapeDtypeStruct((width, 4 * rows), BF16),
+        scratch_shapes=[pltpu.VMEM((4 * rows, width), BF16)],
+        cost_estimate=pl.CostEstimate(flops=2**16, bytes_accessed=2**16, transcendentals=0),
+    )(own, core, far, both)
+
+
+def final_kernel(
+    pair_ref, dn_ref, gain_ref, shift_ref, w_ref, g0_ref, g1_ref, g2_ref, g3_ref, out_ref, tile_s
+):
+    rows, block, channels = pair_ref.shape
+    core = lax.axis_index("core")
+    tile_s[core] = g0_ref[...].astype(F32) + g2_ref[...].astype(F32)
+    tile_s[1 - core] = g1_ref[...].astype(F32) + g3_ref[...].astype(F32)
+    tile = jnp.concatenate([tile_s[0], tile_s[1]], axis=1)
+    width = tile.shape[1]
+    half = width // 2
+    sub = block // 2
+    lane = lax.broadcasted_iota(jnp.int32, (block, width), 1)
+    column = lane // half * sub + lane % sub
+    keep = lax.broadcasted_iota(jnp.int32, (block, width), 0) == column
+    spread = jnp.concatenate(
+        [
+            jnp.where(keep, jnp.broadcast_to(tile[i : i + 1], keep.shape), 0.0).astype(BF16)
+            for i in range(rows)
+        ],
+        axis=0,
+    )
+    dn = dn_ref[...].reshape(rows * block, channels).astype(F32) + mm(spread, w_ref[...])
+    x = pair_ref[...].reshape(rows * block, channels).astype(F32)
+    centred = x - jnp.mean(x, axis=-1, keepdims=True)
+    rstd = lax.rsqrt(jnp.mean(centred * centred, axis=-1, keepdims=True) + EPSILON)
+    unit = centred * rstd
+    push = dn * gain_ref[...]
+    along = jnp.mean(push * unit, axis=-1, keepdims=True)
+    level = jnp.mean(push, axis=-1, keepdims=True)
+    out_ref[...] = ((push - level - unit * along) * rstd).reshape(out_ref.shape)
+
+
+def final(pair, dn, gain, shift_row, w_spread, tiles):
+    rows, half = tiles[0].shape
+    return pl.pallas_call(
+        final_kernel,
+        out_shape=jax.ShapeDtypeStruct(pair.shape, F32),
+        scratch_shapes=[pltpu.VMEM((2, rows, half), F32)],
+        compiler_params=pltpu.CompilerParams(vmem_limit_bytes=32 * 1024 * 1024),
+        cost_estimate=pl.CostEstimate(
+            flops=2**27, bytes_accessed=2**21, transcendentals=2**12
+        ),
+    )(pair, dn, gain, shift_row, w_spread, *tiles)
 
 
 def attention_kernel(
@@ -43,12 +158,26 @@
     w_n_ref,
     w_t_ref,
     w_o_ref,
-    bias0_ref,
-    bias1_ref,
+    own_ref,
+    prev_ref,
+    next_ref,
+    opp0_ref,
+    opp1_ref,
+    own_ref2,
+    prev_ref2,
+    next_ref2,
+    opp0_ref2,
+    opp1_ref2,
     update_ref,
     dn_ref,
-    gb0_ref,
-    gb1_ref,
+    gb_own_ref,
+    gb_next_ref,
+    gb_prev_ref,
+    gb_opp_ref,
+    gb_own_ref2,
+    gb_next_ref2,
+    gb_prev_ref2,
+    gb_opp_ref2,
     bias_s,
     gb_s,
     s_s,
@@ -72,19 +201,36 @@
     scale = 1.0 / math.sqrt(head_dim)
     lanes = 128
     chunks = n // lanes
-    half = heads // 2
+    sub = block // 2
+    core = lax.axis_index("core")
+    z = lax.axis_index("z")
+    y = lax.axis_index("y")
+    xl = lax.axis_index("xl")
+
+    def lanes_of(ahead):
+        start = lax.rem(z + ahead, chunks) * lanes
+        return pl.ds(pl.multiple_of(start, lanes), lanes)
+
+    def rows_of(owner, which):
+        return pl.ds(pl.multiple_of(owner * block + which * sub, sub), sub)
 
     @pl.when(row == 0)
     def _():
-        for h in range(heads):
-            src = bias0_ref if h < half else bias1_ref
-            hh = h % half
-            for z in range(chunks):
-                for b in range(n_blocks):
-                    tile = src[z, b, hh * block : (hh + 1) * block, :].astype(F32)
-                    bias_s[h, b * block : (b + 1) * block, z * lanes : (z + 1) * lanes] = (
-                        tile * LOG2E
-                    )
+        gb_s[...] = jnp.zeros_like(gb_s)
+        for which, refs in (
+            (core, (own_ref, prev_ref, next_ref, opp0_ref, opp1_ref)),
+            (1 - core, (own_ref2, prev_ref2, next_ref2, opp0_ref2, opp1_ref2)),
+        ):
+            for ahead, ref in ((0, refs[0]), (3, refs[1]), (1, refs[2]), (2, None)):
+                for far in range(2):
+                    for back in range(4):
+                        owner = lax.rem(y + 4 - back, 4) * 2 + (xl ^ far)
+                        tile = refs[3 + far][back] if ref is None else ref[far, back]
+                        tile = tile.astype(F32) * LOG2E
+                        for h in range(heads):
+                            bias_s[h, rows_of(owner, which), lanes_of(ahead)] = tile[
+                                h * sub : (h + 1) * sub
+                            ]
 
     x = pair_ref[...].reshape(n, channels).astype(F32)
     normed = normalize(x, gain_ref[...], shift_ref[...]).astype(BF16)
@@ -139,10 +285,6 @@
         dv_s[...] += mm(p_s[...], jnp.where(lane_head == h, da_n, jnp.zeros((), BF16)))
         return carry
 
-    @pl.when(row == 0)
-    def _():
-        gb_s[...] = jnp.zeros_like(gb_s)
-
     lax.fori_loop(0, heads, head_body, 0)
 
     att = att_s[...]
@@ -159,17 +301,19 @@
 
     @pl.when(row == pl.num_programs(0) - 1)
     def _():
-        for h in range(heads):
-            dst = gb0_ref if h < half else gb1_ref
-            hh = h % half
-            for z in range(chunks):
-                for b in range(n_blocks):
-                    dst[z, b, hh * block : (hh + 1) * block, :] = gb_s[
-                        h, b * block : (b + 1) * block, z * lanes : (z + 1) * lanes
-                    ].astype(BF16)
-
-
-def attention(heads, pair, cot, gain, shift, w_n, w_t, w_o, bias0, bias1):
+        for which, refs in (
+            (core, (gb_own_ref, gb_next_ref, gb_opp_ref, gb_prev_ref)),
+            (1 - core, (gb_own_ref2, gb_next_ref2, gb_opp_ref2, gb_prev_ref2)),
+        ):
+            for ahead, ref in enumerate(refs):
+                for owner in range(n_blocks):
+                    for h in range(heads):
+                        ref[owner, h * sub : (h + 1) * sub, :] = gb_s[
+                            h, rows_of(owner, which), lanes_of(ahead)
+                        ].astype(BF16)
+
+
+def attention(heads, pair, cot, gain, shift_row, w_n, w_t, w_o, bias):
     n_blocks, rows, block, channels = pair.shape
     n = n_blocks * block
     inner = w_o.shape[0]
@@ -178,19 +322,19 @@
     def whole(a):
         return pl.BlockSpec(a.shape, lambda i: (0,) * len(a.shape))
 
+    chunk = jax.ShapeDtypeStruct((n_blocks, heads * block // 2, 128), BF16)
     flops = 2 * 6 * rows * n * n * inner
     return pl.pallas_call(
         lambda *refs: attention_kernel(heads, *refs),
         grid=(rows,),
         in_specs=[row_spec, row_spec]
-        + [whole(a) for a in (gain, shift, w_n, w_t, w_o, bias0, bias1)],
-        out_specs=[row_spec, row_spec, whole(bias0), whole(bias1)],
+        + [whole(a) for a in (gain, shift_row, w_n, w_t, w_o, *bias)],
+        out_specs=[row_spec, row_spec] + [whole(chunk)] * 8,
         out_shape=[
             jax.ShapeDtypeStruct(pair.shape, BF16),
             jax.ShapeDtypeStruct(pair.shape, BF16),
-            jax.ShapeDtypeStruct(bias0.shape, BF16),
-            jax.ShapeDtypeStruct(bias1.shape, BF16),
-        ],
+        ]
+        + [chunk] * 8,
         scratch_shapes=[
             pltpu.VMEM((heads, n, n), F32),
             pltpu.VMEM((heads, n, n), F32),
@@ -211,11 +355,7 @@
         cost_estimate=pl.CostEstimate(
             flops=flops, bytes_accessed=8 * 2**20, transcendentals=rows * n * n * heads
         ),
-    )(pair, cot, gain, shift, w_n, w_t, w_o, bias0, bias1)
-
-
-def swap(a):
-    return lax.ppermute(a, "core", [(0, 1), (1, 0)])
+    )(pair, cot, gain, shift_row, w_n, w_t, w_o, *bias)
 
 
 def shards(
@@ -232,14 +372,13 @@
 ):
     rows_i, rows_j, channels = pair.shape
     heads = bias_weight.shape[1]
-    inner = query_weight.shape[1]
     n_ja = lax.axis_size(JA)
-    n_z = lax.axis_size("z")
-    n_xh = lax.axis_size("xh")
-    n_core = lax.axis_size("core")
     own_i = rows_i // n_ja
-    core = lax.axis_index("core")
-    width = (heads // n_core) * rows_j
+    sub = rows_j // 2
+    gain = norm_gain.reshape(1, channels)
+    shift_row = norm_shift.reshape(1, channels)
+    head_of = jnp.tile(jnp.repeat(jnp.arange(heads), sub), 2)
+    w_spread = bias_weight[:, head_of]
 
     pair_rows = lax.all_to_all(
         pair.reshape(n_ja, own_i, rows_j, channels), JA, 0, 0, tiled=True
@@ -248,81 +387,55 @@
         cotangent.reshape(n_ja, own_i, rows_j, channels), JA, 0, 0, tiled=True
     )
 
-    flat_pair = pair.astype(F32).reshape(rows_i * rows_j, channels)
-    normed, norm_back = jax.vjp(lambda rows: normalize(rows, norm_gain, norm_shift), flat_pair)
-    bias_tile = (
-        jnp.dot(normed.astype(BF16), bias_weight, preferred_element_type=F32)
-        .astype(BF16)
-        .reshape(rows_i, rows_j, heads)
-        .transpose(0, 2, 1)
-        .reshape(rows_i, n_core, width)
-        .transpose(1, 0, 2)
-    )
-    near = lax.all_to_all(
-        jnp.broadcast_to(
-            bias_tile[None, :, None], (n_xh, n_core, n_ja, rows_i, width)
-        ).reshape(n_xh * n_core * n_ja, rows_i, width),
-        ("xh", "core", "y", "xl"),
-        0,
-        0,
-        tiled=True,
-    )
-    near = (
-        near.reshape(n_xh * n_core, n_ja, rows_i, width)
-        .transpose(1, 3, 0, 2)
-        .reshape(n_ja, width, n_xh * n_core * rows_i)
-    )
-    bias_own = lax.all_to_all(
-        jnp.broadcast_to(near[None], (n_z,) + near.shape), "z", 0, 0, tiled=True
-    )
-    bias_other = swap(bias_own)
-
-    turn = core * (inner // n_core)
-
-    def turned(w, axis):
-        return jnp.where(core == 0, w, jnp.roll(w, inner // n_core, axis))
-
-    del turn
-    w_q, w_k, w_v, w_g = (
-        turned(w, 1) for w in (query_weight, key_weight, value_weight, gate_weight)
-    )
-    w_o = turned(out_weight, 0)
-    w_n = jnp.concatenate([w_q, w_k, w_v], axis=1)
-    w_t = jnp.concatenate([w_q.T, w_g.T, w_k.T, w_v.T], axis=0)
-
-    update_rows, dn_rows, gb_own, gb_other = attention(
-        heads,
-        pair_rows,
-        cot_rows,
-        norm_gain.reshape(1, channels),
-        norm_shift.reshape(1, channels),
-        w_n,
-        w_t,
-        w_o,
-        bias_own,
-        bias_other,
-    )
+    mine, theirs = prep(pair, gain, shift_row, w_spread)
+    tile = assemble(mine, cross(theirs, 1), cross(mine, 2), cross(theirs, 3))
+    near = jnp.stack([tile] + [shift(tile, "y", d) for d in (1, 2, 3)])
+    near = jnp.stack([near, lax.ppermute(near, "xl", [(0, 1), (1, 0)])])
+    prev, after = shift(near, "z", 1), shift(near, "z", 3)
+    opp0, opp1 = shift(prev[0], "z", 1), shift(after[1], "z", 3)
+    bias = [near, prev, after, opp0, opp1]
+    bias = bias + [swap(a) for a in bias]
+
+    w_n = jnp.concatenate([query_weight, key_weight, value_weight], axis=1)
+    w_t = jnp.concatenate([query_weight.T, gate_weight.T, key_weight.T, value_weight.T], axis=0)
+
+    update_rows, dn_rows, *gb = attention(
+        heads, pair_rows, cot_rows, gain, shift_row, w_n, w_t, out_weight, bias
+    )
+
+    def joined(a, b):
+        return a.astype(F32) + b.astype(F32)
+
+    opp = joined(gb[3], swap(gb[7])).astype(BF16)
+    half = n_ja // 2
+    via_next = shift(opp[:half], "z", 1)
+    via_prev = shift(opp[half:], "z", 3)
+    ahead = joined(gb[1], swap(gb[5]))
+    back = joined(gb[2], swap(gb[6]))
+    own = joined(gb[0], swap(gb[4]))
+    zeros = jnp.zeros_like(via_next)
+    ahead = ahead + jnp.concatenate([via_next, zeros], axis=0).astype(F32)
+    back = back + jnp.concatenate([zeros, via_prev], axis=0).astype(F32)
+    own = own + joined(shift(ahead.astype(BF16), "z", 1), shift(back.astype(BF16), "z", 3))
+    own = own.astype(BF16).reshape((4, 2) + own.shape[1:])
+    y = lax.axis_index("y")
+    xl = lax.axis_index("xl")
+
+    def pick(a, at):
+        return lax.dynamic_index_in_dim(a, at, 0, keepdims=False)
+
+    near = pick(own, y).astype(F32)
+    for d in (1, 2, 3):
+        near = near + shift(pick(own, (y + d) % 4), "y", d).astype(F32)
+    near = near.astype(BF16)
+    tile = joined(pick(near, xl), lax.ppermute(pick(near, 1 - xl), "xl", [(0, 1), (1, 0)]))
+    tile = tile.T.astype(BF16).reshape(4, rows_i, -1)
+    me = lax.axis_index("xh") * 2 + lax.axis_index("core")
+    tiles = [pick(tile, me)] + [cross(pick(tile, me ^ bits), bits) for bits in (1, 2, 3)]
 
     update = lax.all_to_all(update_rows, JA, 0, 0, tiled=True).reshape(pair.shape)
-    dn = lax.all_to_all(dn_rows, JA, 0, 0, tiled=True).reshape(rows_i * rows_j, channels)
-
-    gb = (gb_own.astype(F32) + swap(gb_other).astype(F32)).astype(BF16)
-    gb = lax.all_to_all(gb, "z", 0, 0, tiled=True)
-    gb = jnp.sum(gb.astype(F32), axis=0).astype(BF16)
-    gb = (
-        gb.transpose(2, 0, 1)
-        .reshape(n_xh * n_core, rows_i, n_ja, width)
-        .transpose(0, 2, 1, 3)
-        .reshape(n_xh * n_core * n_ja, rows_i, width)
-    )
-    gb = lax.all_to_all(gb, ("xh", "core", "y", "xl"), 0, 0, tiled=True)
-    gb = jnp.sum(
-        gb.reshape(n_xh, n_core, n_ja, rows_i, width).astype(F32), axis=(0, 2)
-    ).astype(BF16)
-    gb = gb.transpose(1, 0, 2).reshape(rows_i, heads, rows_j)
-    bias_back = jnp.einsum("ihj,ch->ijc", gb, bias_weight, preferred_element_type=F32)
-    d_normed = dn.astype(F32) + bias_back.reshape(rows_i * rows_j, channels)
-    pair_grad = norm_back(d_normed)[0].reshape(rows_i, rows_j, channels)
+    dn = lax.all_to_all(dn_rows, JA, 0, 0, tiled=True).reshape(pair.shape)
+    pair_grad = final(pair, dn, gain, shift_row, w_spread.T, tiles)
     return (update, pair_grad)
 
 

time: 166 us -> 139 us (0.84); the launches traced: 166 us -> 137 us
  blocking collectives: 47.4 us -> 0 us
  starting transfers between devices: 19.5 us -> 52.4 us
  waiting for transfers between devices: 54.9 us -> 41.6 us
  other arithmetic: 9.26 us -> 1.3 us
  Pallas kernels: 28 us -> 35.6 us
  matrix products: 2.15 us -> 0 us
    all_to_all x3 -> x0, blocking collectives: 47.4 us -> none  [the longest x1 18.1 us: shards(): gb = lax.all_to_all(gb, 'z', 0, 0, tiled=True)]
    ppermute x0 -> x22, starting transfers between devices: none -> 34.2 us  [the longest x14 24.8 us: shift(): return lax.ppermute(a, axis, [(s, (s + by) % size) for s in range(size)])]
    ppermute x0 -> x22, waiting for transfers between devices: none -> 32.3 us  [the longest x14 14 us: shift(): return lax.ppermute(a, axis, [(s, (s + by) % size) for s in range(size)])]
    all_to_all x2 -> x1, waiting for transfers between devices: 25.4 us -> 0.01 us  [shards(): dn = lax.all_to_all(dn_rows, JA, 0, 0, tiled=True).reshape(pair.shape)]
    all_to_all x1, waiting for transfers between devices: 9.31 us -> 0.01 us  [shards(): lax.all_to_all(update_rows, JA, 0, 0, tiled=True).reshape(pair.shape)]
    all_to_all x1, waiting for transfers between devices: 9.08 us -> 2.39 us  [shards(): lax.all_to_all(cotangent.reshape(n_ja, own_i, rows_j, channels), JA, 0, 0...]
    pallas_call x0 -> x3, Pallas kernels: none -> 6.66 us  [the longest x1 3.22 us: final(): pl.pallas_call(final_kernel, out_shape=jax.ShapeDtypeStruct(pair.shape, F...]
    reduce_sum x5 -> x0, other arithmetic: 5.6 us -> none  [the longest x1 2.26 us: normalize(): centred = values - mean_val]
  transfers between devices with their start and end apart: 7 -> 35, of which waited for: 6 -> 18; matrix products, arithmetic and copies ran while one was open for 1% -> 1% of each run, Pallas kernels for 0% -> 0%
where the time goes in v2:
time: 139 us; the launch traced here: 137 us
  starting transfers between devices  52.4 us (38%)
  waiting for transfers between devices  41.6 us (30%)
  Pallas kernels  35.6 us (26%)
  local copies, waits for them, and re-layouts  4.99 us (4%)
    pallas_call x1, Pallas kernels, attention(): pl.pallas_call(lambda *refs: attention_kernel(heads, *refs), grid=(rows,)...  29 us
    ppermute x14, starting transfers between devices, shift(): return lax.ppermute(a, axis, [(s, (s + by) % size) for s in range(size)])  24.8 us
    ppermute x14, waiting for transfers between devices, shift(): return lax.ppermute(a, axis, [(s, (s + by) % size) for s in range(size)])  14 us
    ppermute x6, waiting for transfers between devices, cross(): return lax.ppermute(a, ('xh', 'core'), [(s, s ^ bits) for s in range(4)])  7.72 us
    ppermute x6, starting transfers between devices, cross(): return lax.ppermute(a, ('xh', 'core'), [(s, s ^ bits) for s in range(4)])  6.9 us
    ppermute x1, waiting for transfers between devices, shards(): lax.ppermute(pick(near, 1 - xl), 'xl', [(0, 1), (1, 0)])  6.27 us
    all_to_all x1, waiting for transfers between devices, shards(): lax.all_to_all(pair.reshape(n_ja, own_i, rows_j, channels), JA, 0, 0, til...  5.82 us
    all_to_all x1, starting transfers between devices, shards(): lax.all_to_all(update_rows, JA, 0, 0, tiled=True).reshape(pair.shape)  4.55 us
  transfers between devices with their start and end apart: 35, of which 18 were waited for; matrix products, arithmetic and copies ran while one was open for 1% of the time, Pallas kernels for 0%

profile of v2, /device:TPU:0, one launch (start us, length us, event | category | flops | bytes accessed | tf_op | source)
XLA Modules:
  0.0 136.8 jit_solution(12367041541109211922)
XLA Ops:
  0.8 0.6 copy-done
  1.3 0.9 gather_fusion
  2.2 0.1 copy.16
  2.3 0.6 copy-done.2
  3.0 2.0 %shard_map.113 = (bf16[32,128]{1,0:T(8,128)(2,1)S(1)}, bf16[32,128]{1,0:T(8,128)(2,1)S(1)}) custom-call(bf16[32,64,128]{2,1,0:T(8,128)(2,1)} %pair_ref.3, f32[1,128]{1,0:T(1,128)S(1)} %bitcast.52, f32[1,128]{1,0:T(1,128)S(1)} %bitcast.55, bf16[128,256]{1,0:T(8,128)(2,1)S(1)} %bitcast.51), custom_call_target="tpu_custom_call" | custom-call | flops 134217728 | bytes 524288 | tf_op jit(solution)/shard_map/pallas_call | solution.py:77
  5.0 3.2 %collective-permute-start.1 = (bf16[32,128]{1,0:T(8,128)(2,1)S(1)}, bf16[32,128]{1,0:T(8,128)(2,1)S(1)}, u32[]{:S(2)}, u32[]{:S(2)}) collective-permute-start(bf16[32,128]{1,0:T(8,128)(2,1)S(1)} %get-tuple-element.14.own_ref), channel_id=1, source_target_pairs={{0,16},{8,24},{16,0},{24,8},{1,17},{9,25},{17,1},{25,9},{2,18},{10... | collective-permute-start | bytes 24584 | tf_op jit(solution)/shard_map/ppermute | solution.py:42
  8.2 0.2 collective-permute-start.2
  8.4 1.9 %collective-permute-done.1.far_ref = bf16[32,128]{1,0:T(8,128)(2,1)S(1)} collective-permute-done((bf16[32,128]{1,0:T(8,128)(2,1)S(1)}, bf16[32,128]{1,0:T(8,128)(2,1)S(1)}, u32[]{:S(2)}, u32[]{:S(2)}) %collective-permute-start.1) | collective-permute-done | bytes 8224 | tf_op jit(solution)/shard_map/ppermute | solution.py:42
  10.3 2.5 %collective-permute-done.2.both_ref = bf16[32,128]{1,0:T(8,128)(2,1)S(1)} collective-permute-done((bf16[32,128]{1,0:T(8,128)(2,1)S(1)}, bf16[32,128]{1,0:T(8,128)(2,1)S(1)}, u32[]{:S(2)}, u32[]{:S(2)}) %collective-permute-start.2) | collective-permute-done | bytes 8224 | tf_op jit(solution)/shard_map/ppermute | solution.py:42
  12.8 0.6 copy-done.11
  13.4 1.5 %shard_map.114 = bf16[128,128]{1,0:T(8,128)(2,1)} custom-call(bf16[32,128]{1,0:T(8,128)(2,1)} %copy-done.1, bf16[32,128]{1,0:T(8,128)(2,1)} %copy-done.9, bf16[32,128]{1,0:T(8,128)(2,1)} %copy-done.10, bf16[32,128]{1,0:T(8,128)(2,1)} %copy-done.11), custom_call_target="tpu_custom_call" | custom-call | flops 65536 | bytes 65536 | tf_op jit(solution)/shard_map/pallas_call | solution.py:99
  14.9 1.6 %collective-permute-start.3 = (bf16[128,128]{1,0:T(8,128)(2,1)}, bf16[128,128]{1,0:T(8,128)(2,1)S(1)}, u32[]{:S(2)}, u32[]{:S(2)}) collective-permute-start(bf16[128,128]{1,0:T(8,128)(2,1)} %shard_map.114), channel_id=1, source_target_pairs={{0,2},{2,4},{4,6},{6,0},{1,3},{3,5},{5,7},{7,1},{8,10},{10,12},{12... | collective-permute-start | bytes 98312 | tf_op jit(solution)/shard_map/ppermute | solution.py:47
  16.5 2.9 %collective-permute-start.4 = (bf16[128,128]{1,0:T(8,128)(2,1)}, bf16[128,128]{1,0:T(8,128)(2,1)S(1)}, u32[]{:S(2)}, u32[]{:S(2)}) collective-permute-start(bf16[128,128]{1,0:T(8,128)(2,1)} %shard_map.114), channel_id=1, source_target_pairs={{0,4},{2,6},{4,0},{6,2},{1,5},{3,7},{5,1},{7,3},{8,12},{10,14},{12... | collective-permute-start | bytes 98312 | tf_op jit(solution)/shard_map/ppermute | solution.py:47
  19.4 1.3 collective-permute-start.5
  20.7 1.4 %collective-permute-done.4 = bf16[128,128]{1,0:T(8,128)(2,1)S(1)} collective-permute-done((bf16[128,128]{1,0:T(8,128)(2,1)}, bf16[128,128]{1,0:T(8,128)(2,1)S(1)}, u32[]{:S(2)}, u32[]{:S(2)}) %collective-permute-start.4) | collective-permute-done | bytes 32800 | tf_op jit(solution)/shard_map/ppermute | solution.py:47
  22.1 1.4 %collective-permute-done.5 = bf16[128,128]{1,0:T(8,128)(2,1)S(1)} collective-permute-done((bf16[128,128]{1,0:T(8,128)(2,1)}, bf16[128,128]{1,0:T(8,128)(2,1)S(1)}, u32[]{:S(2)}, u32[]{:S(2)}) %collective-permute-start.5) | collective-permute-done | bytes 32800 | tf_op jit(solution)/shard_map/ppermute | solution.py:47
  23.5 0.8 fusion.5
  24.3 0.7 collective-permute-start.6
  24.9 4.4 %collective-permute-done.6 = bf16[4,128,128]{2,1,0:T(8,128)(2,1)S(1)} collective-permute-done((bf16[4,128,128]{2,1,0:T(8,128)(2,1)S(1)}, bf16[4,128,128]{2,1,0:T(8,128)(2,1)S(1)}, u32[]{:S(2)}, u32[]{:S(2)}) %collective-permute-start.6) | collective-permute-done | bytes 131104 | tf_op jit(solution)/shard_map/ppermute | solution.py:393
  29.3 2.0 %collective-permute-start.7 = (bf16[2,4,128,128]{3,2,1,0:T(8,128)(2,1)S(1)}, bf16[2,4,128,128]{3,2,1,0:T(8,128)(2,1)S(1)}, u32[]{:S(2)}, u32[]{:S(2)}) collective-permute-start(bf16[2,4,128,128]{3,2,1,0:T(8,128)(2,1)S(1)} %pad_maximum_fusion.refs_7_), channel_id=1, source_target_pairs={{0,32},{32,64},{64,96},{96,0},{1,33},{33,65},{65,97},{97,1},{2,34}... | collective-permute-start | bytes 786440 | tf_op jit(solution)/shard_map/ppermute | solution.py:47
  31.3 3.9 %all-to-all-start = ((bf16[8,4,64,128]{3,2,1,0:T(8,128)(2,1)}), bf16[8,4,64,128]{3,2,1,0:T(8,128)(2,1)S(1)}, u32[]{:S(2)}, u32[]{:S(2)}) async-start(bf16[8,4,64,128]{3,2,1,0:T(8,128)(2,1)} %bitcast), calls=%async_computation | async-start | bytes 1048576 | tf_op jit(solution)/shard_map/all_to_all | solution.py:383
  35.2 2.1 %collective-permute-start.8 = (bf16[2,4,128,128]{3,2,1,0:T(8,128)(2,1)S(1)}, bf16[2,4,128,128]{3,2,1,0:T(8,128)(2,1)S(1)}, u32[]{:S(2)}, u32[]{:S(2)}) collective-permute-start(bf16[2,4,128,128]{3,2,1,0:T(8,128)(2,1)S(1)} %pad_maximum_fusion.refs_7_), channel_id=1, source_target_pairs={{0,96},{32,0},{64,32},{96,64},{1,97},{33,1},{65,33},{97,65},{2,98}... | collective-permute-start | bytes 786440 | tf_op jit(solution)/shard_map/ppermute | solution.py:47
  37.3 0.5 collective-permute-done.7.refs_8_
  37.8 0.2 collective-permute-start.9
  38.1 5.8 %all-to-all-done.refs_0_ = bf16[8,4,64,128]{3,2,1,0:T(8,128)(2,1)S(1)} async-done(((bf16[8,4,64,128]{3,2,1,0:T(8,128)(2,1)}), bf16[8,4,64,128]{3,2,1,0:T(8,128)(2,1)S(1)}, u32[]{:S(2)}, u32[]{:S(2)}) %all-to-all-start) | async-done | bytes 524320 | tf_op jit(solution)/shard_map/all_to_all | solution.py:383
  43.9 4.2 %all-to-all-start.1 = ((bf16[8,4,64,128]{3,2,1,0:T(8,128)(2,1)}), bf16[8,4,64,128]{3,2,1,0:T(8,128)(2,1)}, u32[]{:S(2)}, u32[]{:S(2)}) async-start(bf16[8,4,64,128]{3,2,1,0:T(8,128)(2,1)} %bitcast.1), calls=%async_computation.1 | async-start | bytes 1048576 | tf_op jit(solution)/shard_map/all_to_all | solution.py:386
  48.1 2.2 %collective-permute-start.10 = (bf16[4,128,128]{2,1,0:T(8,128)(2,1)S(1)}, bf16[4,128,128]{2,1,0:T(8,128)(2,1)S(1)}, u32[]{:S(2)}, u32[]{:S(2)}) collective-permute-start(bf16[4,128,128]{2,1,0:T(8,128)(2,1)S(1)} %slice_bitcast_fusion), channel_id=1, source_target_pairs={{0,96},{32,0},{64,32},{96,64},{1,97},{33,1},{65,33},{97,65},{2,98}... | collective-permute-start | bytes 393224 | tf_op jit(solution)/shard_map/ppermute | solution.py:47
  50.3 0.5 collective-permute-start.12
  50.8 0.5 collective-permute-start.14
  51.4 1.8 %collective-permute-done.10.refs_11_ = bf16[4,128,128]{2,1,0:T(8,128)(2,1)S(1)} collective-permute-done((bf16[4,128,128]{2,1,0:T(8,128)(2,1)S(1)}, bf16[4,128,128]{2,1,0:T(8,128)(2,1)S(1)}, u32[]{:S(2)}, u32[]{:S(2)}) %collective-permute-start.10) | collective-permute-done | bytes 131104 | tf_op jit(solution)/shard_map/ppermute | solution.py:47
  53.2 0.1 copy.12
  53.3 0.1 copy.14
  53.4 0.1 copy.15
  53.6 0.6 copy-done.8
  54.2 0.1 copy.13
  54.4 2.4 %all-to-all-done.1.refs_1_ = bf16[8,4,64,128]{3,2,1,0:T(8,128)(2,1)} async-done(((bf16[8,4,64,128]{3,2,1,0:T(8,128)(2,1)}), bf16[8,4,64,128]{3,2,1,0:T(8,128)(2,1)}, u32[]{:S(2)}, u32[]{:S(2)}) %all-to-all-start.1) | async-done | bytes 524320 | tf_op jit(solution)/shard_map/all_to_all | solution.py:386
  56.8 29.0 %shard_map.115 = (bf16[8,4,64,128]{3,2,1,0:T(8,128)(2,1)}, bf16[8,4,64,128]{3,2,1,0:T(8,128)(2,1)}, bf16[8,128,128]{2,1,0:T(8,128)(2,1)S(1)}, bf16[8,128,128]{2,...) custom-call(bf16[8,4,64,128]{3,2,1,0:T(8,128)(2,1)S(1)} %all-to-all-, ...), custom_call_target="tpu_custom_call" | custom-call | flops 1610612736 | bytes 8388608 | tf_op jit(solution)/shard_map/pallas_call | solution.py:327
  85.8 0.5 collective-permute-start.17
  86.3 1.0 collective-permute-done.18
  87.4 2.0 %collective-permute-start.19 = (bf16[4,128,128]{2,1,0:T(8,128)(2,1)S(1)}, bf16[4,128,128]{2,1,0:T(8,128)(2,1)S(1)}, u32[]{:S(2)}, u32[]{:S(2)}) collective-permute-start(bf16[4,128,128]{2,1,0:T(8,128)(2,1)S(1)} %get-tuple-element.29), channel_id=1, source_target_pairs={{0,32},{32,64},{64,96},{96,0},{1,33},{33,65},{65,97},{97,1},{2,34}... | collective-permute-start | bytes 393224 | tf_op jit(solution)/shard_map/ppermute | solution.py:47
  89.4 0.5 collective-permute-start.16
  89.9 1.3 collective-permute-start.22
  91.2 3.0 %collective-permute-done.19 = bf16[4,128,128]{2,1,0:T(8,128)(2,1)S(1)} collective-permute-done((bf16[4,128,128]{2,1,0:T(8,128)(2,1)S(1)}, bf16[4,128,128]{2,1,0:T(8,128)(2,1)S(1)}, u32[]{:S(2)}, u32[]{:S(2)}) %collective-permute-start.19) | collective-permute-done | bytes 131104 | tf_op jit(solution)/shard_map/ppermute | solution.py:47
  94.3 0.8 collective-permute-start.20
  95.1 0.2 collective-permute-done.22
  95.4 2.6 %collective-permute-start.23 = (bf16[8,128,128]{2,1,0:T(8,128)(2,1)S(1)}, bf16[8,128,128]{2,1,0:T(8,128)(2,1)S(1)}, u32[]{:S(2)}, u32[]{:S(2)}) collective-permute-start(bf16[8,128,128]{2,1,0:T(8,128)(2,1)S(1)} %add_convert_fusion.1), channel_id=1, source_target_pairs={{0,96},{32,0},{64,32},{96,64},{1,97},{33,1},{65,33},{97,65},{2,98}... | collective-permute-start | bytes 786440 | tf_op jit(solution)/shard_map/ppermute | solution.py:47
  98.0 4.5 %all-to-all-start.2 = ((bf16[8,4,64,128]{3,2,1,0:T(8,128)(2,1)}), bf16[8,4,64,128]{3,2,1,0:T(8,128)(2,1)S(1)}, u32[]{:S(2)}, u32[]{:S(2)}) async-start(bf16[8,4,64,128]{3,2,1,0:T(8,128)(2,1)} %get-tuple-element.16), calls=%async_computation.2 | async-start | bytes 1048576 | tf_op jit(solution)/shard_map/all_to_all | solution.py:436
  102.5 0.6 collective-permute-done.20
  103.1 0.1 add_convert_fusion
  103.3 1.5 %collective-permute-start.24 = (bf16[2,128,128]{2,1,0:T(8,128)(2,1)S(1)}, bf16[2,128,128]{2,1,0:T(8,128)(2,1)S(1)}, u32[]{:S(2)}, u32[]{:S(2)}) collective-permute-start(bf16[2,128,128]{2,1,0:T(8,128)(2,1)S(1)} %get-tuple-element.26), channel_id=1, source_target_pairs={{0,2},{2,4},{4,6},{6,0},{1,3},{3,5},{5,7},{7,1},{8,10},{10,12},{12... | collective-permute-start | bytes 196616 | tf_op jit(solution)/shard_map/ppermute | solution.py:47
  104.8 2.7 %collective-permute-start.25 = (bf16[2,128,128]{2,1,0:T(8,128)(2,1)S(1)}, bf16[2,128,128]{2,1,0:T(8,128)(2,1)S(1)}, u32[]{:S(2)}, u32[]{:S(2)}) collective-permute-start(bf16[2,128,128]{2,1,0:T(8,128)(2,1)S(1)} %get-tuple-element.28), channel_id=1, source_target_pairs={{0,4},{2,6},{4,0},{6,2},{1,5},{3,7},{5,1},{7,3},{8,12},{10,14},{12... | collective-permute-start | bytes 196616 | tf_op jit(solution)/shard_map/ppermute | solution.py:47
  107.5 1.5 %collective-permute-start.26 = (bf16[2,128,128]{2,1,0:T(8,128)(2,1)S(1)}, bf16[2,128,128]{2,1,0:T(8,128)(2,1)S(1)}, u32[]{:S(2)}, u32[]{:S(2)}) collective-permute-start(bf16[2,128,128]{2,1,0:T(8,128)(2,1)S(1)} %get-tuple-element.27), channel_id=1, source_target_pairs={{0,6},{2,0},{4,2},{6,4},{1,7},{3,1},{5,3},{7,5},{8,14},{10,8},{12,... | collective-permute-start | bytes 196616 | tf_op jit(solution)/shard_map/ppermute | solution.py:47
  109.0 4.2 %collective-permute-done.24 = bf16[2,128,128]{2,1,0:T(8,128)(2,1)S(1)} collective-permute-done((bf16[2,128,128]{2,1,0:T(8,128)(2,1)S(1)}, bf16[2,128,128]{2,1,0:T(8,128)(2,1)S(1)}, u32[]{:S(2)}, u32[]{:S(2)}) %collective-permute-start.24) | collective-permute-done | bytes 65568 | tf_op jit(solution)/shard_map/ppermute | solution.py:47
  113.1 1.0 collective-permute-done.25
  114.2 3.5 %all-to-all-start.3 = ((bf16[8,4,64,128]{3,2,1,0:T(8,128)(2,1)}), bf16[8,4,64,128]{3,2,1,0:T(8,128)(2,1)S(1)}, u32[]{:S(2)}, u32[]{:S(2)}) async-start(bf16[8,4,64,128]{3,2,1,0:T(8,128)(2,1)} %get-tuple-element.17), calls=%async_computation.3 | async-start | bytes 1048576 | tf_op jit(solution)/shard_map/all_to_all | solution.py:437
  117.7 1.9 %collective-permute-start.27 = (bf16[128,128]{1,0:T(8,128)(2,1)S(1)}, bf16[128,128]{1,0:T(8,128)(2,1)S(1)}, u32[]{:S(2)}, u32[]{:S(2)}) collective-permute-start(bf16[128,128]{1,0:T(8,128)(2,1)S(1)} %dynamic-slice_bitcast_fusion.3), channel_id=1, source_target_pairs={{0,1},{1,0},{2,3},{3,2},{4,5},{5,4},{6,7},{7,6},{8,9},{9,8},{10,11... | collective-permute-start | bytes 98312 | tf_op jit(solution)/shard_map/ppermute | solution.py:431
  119.6 6.3 %collective-permute-done.27 = bf16[128,128]{1,0:T(8,128)(2,1)S(1)} collective-permute-done((bf16[128,128]{1,0:T(8,128)(2,1)S(1)}, bf16[128,128]{1,0:T(8,128)(2,1)S(1)}, u32[]{:S(2)}, u32[]{:S(2)}) %collective-permute-start.27) | collective-permute-done | bytes 32800 | tf_op jit(solution)/shard_map/ppermute | solution.py:431
  125.9 0.1 copy.17
  126.1 2.1 %collective-permute-start.29 = (bf16[32,128]{1,0:T(8,128)(2,1)S(1)}, bf16[32,128]{1,0:T(8,128)(2,1)S(1)}, u32[]{:S(2)}, u32[]{:S(2)}) collective-permute-start(bf16[32,128]{1,0:T(8,128)(2,1)S(1)} %get-tuple-element.34), channel_id=1, source_target_pairs={{0,16},{8,24},{16,0},{24,8},{1,17},{9,25},{17,1},{25,9},{2,18},{10... | collective-permute-start | bytes 24584 | tf_op jit(solution)/shard_map/ppermute | solution.py:42
  128.3 1.3 collective-permute-start.30
  129.5 1.9 %collective-permute-done.29.g2_ref = bf16[32,128]{1,0:T(8,128)(2,1)S(1)} collective-permute-done((bf16[32,128]{1,0:T(8,128)(2,1)S(1)}, bf16[32,128]{1,0:T(8,128)(2,1)S(1)}, u32[]{:S(2)}, u32[]{:S(2)}) %collective-permute-start.29) | collective-permute-done | bytes 8224 | tf_op jit(solution)/shard_map/ppermute | solution.py:42
  131.4 1.5 %collective-permute-done.30.g3_ref = bf16[32,128]{1,0:T(8,128)(2,1)S(1)} collective-permute-done((bf16[32,128]{1,0:T(8,128)(2,1)S(1)}, bf16[32,128]{1,0:T(8,128)(2,1)S(1)}, u32[]{:S(2)}, u32[]{:S(2)}) %collective-permute-start.30) | collective-permute-done | bytes 8224 | tf_op jit(solution)/shard_map/ppermute | solution.py:42
  132.8 3.2 %shard_map.116 = f32[32,64,128]{2,1,0:T(8,128)} custom-call(bf16[32,64,128]{2,1,0:T(8,128)(2,1)} %pair_ref.3, bf16[32,64,128]{2,1,0:T(8,128)(2,1)S(1)} %bitcast.50, f32[1,128]{1,0:T(1,128)S(1)} %bitcast.54, f32[1,128]{1,0:T(1,128)S(1)} %bitcast.57, bf16[256,128]{1,0:T(8,128)(2,1)S(1)} %gather_fusion, bf16[32,128]{1,0:T(8,128)(2,1)S(1)} %get-tuple-element.36.g0_ref, ...), custom_call_target="tpu_custom_call" | custom-call | flops 134217728 | bytes 2097152 | tf_op jit(solution)/shard_map/pallas_call | solution.py:141
  136.1 0.8 copy.19
  (63 shorter events, 0.9 us)
Async XLA Ops:
  0.6 0.7 copy-start
  2.3 0.7 copy-start.2
  2.3 0.7 copy-start.3
  4.9 7.9 %copy-start.1 = (bf16[32,128]{1,0:T(8,128)(2,1)}, bf16[32,128]{1,0:T(8,128)(2,1)S(1)}, u32[]{:S(2)}) copy-start(bf16[32,128]{1,0:T(8,128)(2,1)S(1)} %get-tuple-element.14.own_ref) | copy-start | bytes 24580
  4.9 3.5 %collective-permute-start = (bf16[32,128]{1,0:T(8,128)(2,1)S(1)}, bf16[32,128]{1,0:T(8,128)(2,1)S(1)}, u32[]{:S(2)}, u32[]{:S(2)}) collective-permute-start(bf16[32,128]{1,0:T(8,128)(2,1)S(1)} %get-tuple-element.15), channel_id=1, source_target_pairs={{0,8},{8,0},{16,24},{24,16},{1,9},{9,1},{17,25},{25,17},{2,10},{10... | collective-permute-start | bytes 24584 | tf_op jit(solution)/shard_map/ppermute | solution.py:42
  5.0 5.2 %collective-permute-start.1 = (bf16[32,128]{1,0:T(8,128)(2,1)S(1)}, bf16[32,128]{1,0:T(8,128)(2,1)S(1)}, u32[]{:S(2)}, u32[]{:S(2)}) collective-permute-start(bf16[32,128]{1,0:T(8,128)(2,1)S(1)} %get-tuple-element.14.own_ref), channel_id=1, source_target_pairs={{0,16},{8,24},{16,0},{24,8},{1,17},{9,25},{17,1},{25,9},{2,18},{10... | collective-permute-start | bytes 24584 | tf_op jit(solution)/shard_map/ppermute | solution.py:42
  8.2 4.6 %collective-permute-start.2 = (bf16[32,128]{1,0:T(8,128)(2,1)S(1)}, bf16[32,128]{1,0:T(8,128)(2,1)S(1)}, u32[]{:S(2)}, u32[]{:S(2)}) collective-permute-start(bf16[32,128]{1,0:T(8,128)(2,1)S(1)} %get-tuple-element.15), channel_id=1, source_target_pairs={{0,24},{8,16},{16,8},{24,0},{1,25},{9,17},{17,9},{25,1},{2,26},{10... | collective-permute-start | bytes 24584 | tf_op jit(solution)/shard_map/ppermute | solution.py:42
  8.4 4.4 %copy-start.9 = (bf16[32,128]{1,0:T(8,128)(2,1)}, bf16[32,128]{1,0:T(8,128)(2,1)S(1)}, u32[]{:S(2)}) copy-start(bf16[32,128]{1,0:T(8,128)(2,1)S(1)} %collective-permute-done.core_ref) | copy-start | bytes 24580
  10.3 2.5 %copy-start.10 = (bf16[32,128]{1,0:T(8,128)(2,1)}, bf16[32,128]{1,0:T(8,128)(2,1)S(1)}, u32[]{:S(2)}) copy-start(bf16[32,128]{1,0:T(8,128)(2,1)S(1)} %collective-permute-done.1.far_ref) | copy-start | bytes 24580
  12.8 0.6 copy-start.11
  14.9 5.8 %collective-permute-start.3 = (bf16[128,128]{1,0:T(8,128)(2,1)}, bf16[128,128]{1,0:T(8,128)(2,1)S(1)}, u32[]{:S(2)}, u32[]{:S(2)}) collective-permute-start(bf16[128,128]{1,0:T(8,128)(2,1)} %shard_map.114), channel_id=1, source_target_pairs={{0,2},{2,4},{4,6},{6,0},{1,3},{3,5},{5,7},{7,1},{8,10},{10,12},{12... | collective-permute-start | bytes 98312 | tf_op jit(solution)/shard_map/ppermute | solution.py:47
  16.5 5.6 %collective-permute-start.4 = (bf16[128,128]{1,0:T(8,128)(2,1)}, bf16[128,128]{1,0:T(8,128)(2,1)S(1)}, u32[]{:S(2)}, u32[]{:S(2)}) collective-permute-start(bf16[128,128]{1,0:T(8,128)(2,1)} %shard_map.114), channel_id=1, source_target_pairs={{0,4},{2,6},{4,0},{6,2},{1,5},{3,7},{5,1},{7,3},{8,12},{10,14},{12... | collective-permute-start | bytes 98312 | tf_op jit(solution)/shard_map/ppermute | solution.py:47
  19.4 4.1 %collective-permute-start.5 = (bf16[128,128]{1,0:T(8,128)(2,1)}, bf16[128,128]{1,0:T(8,128)(2,1)S(1)}, u32[]{:S(2)}, u32[]{:S(2)}) collective-permute-start(bf16[128,128]{1,0:T(8,128)(2,1)} %shard_map.114), channel_id=1, source_target_pairs={{0,6},{2,0},{4,2},{6,4},{1,7},{3,1},{5,3},{7,5},{8,14},{10,8},{12,... | collective-permute-start | bytes 98312 | tf_op jit(solution)/shard_map/ppermute | solution.py:47
  24.3 5.0 %collective-permute-start.6 = (bf16[4,128,128]{2,1,0:T(8,128)(2,1)S(1)}, bf16[4,128,128]{2,1,0:T(8,128)(2,1)S(1)}, u32[]{:S(2)}, u32[]{:S(2)}) collective-permute-start(bf16[4,128,128]{2,1,0:T(8,128)(2,1)S(1)} %get-tuple-element.32), channel_id=1, source_target_pairs={{0,1},{1,0},{2,3},{3,2},{4,5},{5,4},{6,7},{7,6},{8,9},{9,8},{10,11... | collective-permute-start | bytes 393224 | tf_op jit(solution)/shard_map/ppermute | solution.py:393
  29.3 8.5 %collective-permute-start.7 = (bf16[2,4,128,128]{3,2,1,0:T(8,128)(2,1)S(1)}, bf16[2,4,128,128]{3,2,1,0:T(8,128)(2,1)S(1)}, u32[]{:S(2)}, u32[]{:S(2)}) collective-permute-start(bf16[2,4,128,128]{3,2,1,0:T(8,128)(2,1)S(1)} %pad_maximum_fusion.refs_7_), channel_id=1, source_target_pairs={{0,32},{32,64},{64,96},{96,0},{1,33},{33,65},{65,97},{97,1},{2,34}... | collective-permute-start | bytes 786440 | tf_op jit(solution)/shard_map/ppermute | solution.py:47
  31.3 12.6 %all-to-all-start = ((bf16[8,4,64,128]{3,2,1,0:T(8,128)(2,1)}), bf16[8,4,64,128]{3,2,1,0:T(8,128)(2,1)S(1)}, u32[]{:S(2)}, u32[]{:S(2)}) async-start(bf16[8,4,64,128]{3,2,1,0:T(8,128)(2,1)} %bitcast), calls=%async_computation | async-start | bytes 1048576 | tf_op jit(solution)/shard_map/all_to_all | solution.py:383
  35.2 12.9 %collective-permute-start.8 = (bf16[2,4,128,128]{3,2,1,0:T(8,128)(2,1)S(1)}, bf16[2,4,128,128]{3,2,1,0:T(8,128)(2,1)S(1)}, u32[]{:S(2)}, u32[]{:S(2)}) collective-permute-start(bf16[2,4,128,128]{3,2,1,0:T(8,128)(2,1)S(1)} %pad_maximum_fusion.refs_7_), channel_id=1, source_target_pairs={{0,96},{32,0},{64,32},{96,64},{1,97},{33,1},{65,33},{97,65},{2,98}... | collective-permute-start | bytes 786440 | tf_op jit(solution)/shard_map/ppermute | solution.py:47
  37.8 13.0 %collective-permute-start.9 = (bf16[4,128,128]{2,1,0:T(8,128)(2,1)S(1)}, bf16[4,128,128]{2,1,0:T(8,128)(2,1)S(1)}, u32[]{:S(2)}, u32[]{:S(2)}) collective-permute-start(bf16[4,128,128]{2,1,0:T(8,128)(2,1)S(1)} %slice_bitcast_fusion.1), channel_id=1, source_target_pairs={{0,32},{32,64},{64,96},{96,0},{1,33},{33,65},{65,97},{97,1},{2,34}... | collective-permute-start | bytes 393224 | tf_op jit(solution)/shard_map/ppermute | solution.py:47
  43.9 12.9 %all-to-all-start.1 = ((bf16[8,4,64,128]{3,2,1,0:T(8,128)(2,1)}), bf16[8,4,64,128]{3,2,1,0:T(8,128)(2,1)}, u32[]{:S(2)}, u32[]{:S(2)}) async-start(bf16[8,4,64,128]{3,2,1,0:T(8,128)(2,1)} %bitcast.1), calls=%async_computation.1 | async-start | bytes 1048576 | tf_op jit(solution)/shard_map/all_to_all | solution.py:386
  48.0 5.1 %copy-start.5 = (bf16[128,128]{1,0:T(8,128)(2,1)S(1)}, bf16[128,128]{1,0:T(8,128)(2,1)}, u32[]{:S(2)}) copy-start(bf16[128,128]{1,0:T(8,128)(2,1)} %param.14) | copy-start | bytes 98308
  48.1 5.1 %copy-start.6 = (bf16[128,128]{1,0:T(8,128)(2,1)S(1)}, bf16[128,128]{1,0:T(8,128)(2,1)}, u32[]{:S(2)}) copy-start(bf16[128,128]{1,0:T(8,128)(2,1)} %param.15) | copy-start | bytes 98308
  48.1 5.1 %copy-start.7 = (bf16[128,128]{1,0:T(8,128)(2,1)S(1)}, bf16[128,128]{1,0:T(8,128)(2,1)}, u32[]{:S(2)}) copy-start(bf16[128,128]{1,0:T(8,128)(2,1)} %param.16) | copy-start | bytes 98308
  48.1 5.0 %collective-permute-start.10 = (bf16[4,128,128]{2,1,0:T(8,128)(2,1)S(1)}, bf16[4,128,128]{2,1,0:T(8,128)(2,1)S(1)}, u32[]{:S(2)}, u32[]{:S(2)}) collective-permute-start(bf16[4,128,128]{2,1,0:T(8,128)(2,1)S(1)} %slice_bitcast_fusion), channel_id=1, source_target_pairs={{0,96},{32,0},{64,32},{96,64},{1,97},{33,1},{65,33},{97,65},{2,98}... | collective-permute-start | bytes 393224 | tf_op jit(solution)/shard_map/ppermute | solution.py:47
  50.3 4.0 %collective-permute-start.11 = (bf16[2,4,128,128]{3,2,1,0:T(8,128)(2,1)S(1)}, bf16[2,4,128,128]{3,2,1,0:T(8,128)(2,1)S(1)}, u32[]{:S(2)}, u32[]{:S(2)}) collective-permute-start(bf16[2,4,128,128]{3,2,1,0:T(8,128)(2,1)S(1)} %pad_maximum_fusion.refs_7_), channel_id=1, source_target_pairs={{0,8},{8,0},{1,9},{9,1},{2,10},{10,2},{3,11},{11,3},{4,12},{12,4},... | collective-permute-start | bytes 786440 | tf_op jit(solution)/shard_map/ppermute | solution.py:38
  50.3 6.4 %collective-permute-start.12 = (bf16[2,4,128,128]{3,2,1,0:T(8,128)(2,1)S(1)}, bf16[2,4,128,128]{3,2,1,0:T(8,128)(2,1)S(1)}, u32[]{:S(2)}, u32[]{:S(2)}) collective-permute-start(bf16[2,4,128,128]{3,2,1,0:T(8,128)(2,1)S(1)} %collective-permute-done.7.refs_8_), channel_id=1, source_target_pairs={{0,8},{8,0},{1,9},{9,1},{2,10},{10,2},{3,11},{11,3},{4,12},{12,4},... | collective-permute-start | bytes 786440 | tf_op jit(solution)/shard_map/ppermute | solution.py:38
  50.8 5.9 %collective-permute-start.13 = (bf16[2,4,128,128]{3,2,1,0:T(8,128)(2,1)S(1)}, bf16[2,4,128,128]{3,2,1,0:T(8,128)(2,1)S(1)}, u32[]{:S(2)}, u32[]{:S(2)}) collective-permute-start(bf16[2,4,128,128]{3,2,1,0:T(8,128)(2,1)S(1)} %collective-permute-done.8.refs_9_), channel_id=1, source_target_pairs={{0,8},{8,0},{1,9},{9,1},{2,10},{10,2},{3,11},{11,3},{4,12},{12,4},... | collective-permute-start | bytes 786440 | tf_op jit(solution)/shard_map/ppermute | solution.py:38
  50.8 5.9 %collective-permute-start.14 = (bf16[4,128,128]{2,1,0:T(8,128)(2,1)S(1)}, bf16[4,128,128]{2,1,0:T(8,128)(2,1)S(1)}, u32[]{:S(2)}, u32[]{:S(2)}) collective-permute-start(bf16[4,128,128]{2,1,0:T(8,128)(2,1)S(1)} %collective-permute-done.9.refs_10_), channel_id=1, source_target_pairs={{0,8},{8,0},{1,9},{9,1},{2,10},{10,2},{3,11},{11,3},{4,12},{12,4},... | collective-permute-start | bytes 393224 | tf_op jit(solution)/shard_map/ppermute | solution.py:38
  53.1 3.6 %collective-permute-start.15 = (bf16[4,128,128]{2,1,0:T(8,128)(2,1)S(1)}, bf16[4,128,128]{2,1,0:T(8,128)(2,1)S(1)}, u32[]{:S(2)}, u32[]{:S(2)}) collective-permute-start(bf16[4,128,128]{2,1,0:T(8,128)(2,1)S(1)} %collective-permute-done.10.refs_11_), channel_id=1, source_target_pairs={{0,8},{8,0},{1,9},{9,1},{2,10},{10,2},{3,11},{11,3},{4,12},{12,4},... | collective-permute-start | bytes 393224 | tf_op jit(solution)/shard_map/ppermute | solution.py:38
  53.4 0.8 copy-start.8
  54.3 2.5 %copy-start.4 = (bf16[128,128]{1,0:T(8,128)(2,1)S(1)}, bf16[128,128]{1,0:T(8,128)(2,1)}, u32[]{:S(2)}) copy-start(bf16[128,128]{1,0:T(8,128)(2,1)} %refs_6_.1) | copy-start | bytes 98308
  85.8 1.5 %collective-permute-start.18 = (bf16[8,128,128]{2,1,0:T(8,128)(2,1)S(1)}, bf16[8,128,128]{2,1,0:T(8,128)(2,1)S(1)}, u32[]{:S(2)}, u32[]{:S(2)}) collective-permute-start(bf16[8,128,128]{2,1,0:T(8,128)(2,1)S(1)} %get-tuple-element.23), channel_id=1, source_target_pairs={{0,8},{8,0},{1,9},{9,1},{2,10},{10,2},{3,11},{11,3},{4,12},{12,4},... | collective-permute-start | bytes 786440 | tf_op jit(solution)/shard_map/ppermute | solution.py:38
  85.8 5.5 %collective-permute-start.17 = (bf16[8,128,128]{2,1,0:T(8,128)(2,1)S(1)}, bf16[8,128,128]{2,1,0:T(8,128)(2,1)S(1)}, u32[]{:S(2)}, u32[]{:S(2)}) collective-permute-start(bf16[8,128,128]{2,1,0:T(8,128)(2,1)S(1)} %get-tuple-element.21), channel_id=1, source_target_pairs={{0,8},{8,0},{1,9},{9,1},{2,10},{10,2},{3,11},{11,3},{4,12},{12,4},... | collective-permute-start | bytes 786440 | tf_op jit(solution)/shard_map/ppermute | solution.py:38
  87.4 6.8 %collective-permute-start.19 = (bf16[4,128,128]{2,1,0:T(8,128)(2,1)S(1)}, bf16[4,128,128]{2,1,0:T(8,128)(2,1)S(1)}, u32[]{:S(2)}, u32[]{:S(2)}) collective-permute-start(bf16[4,128,128]{2,1,0:T(8,128)(2,1)S(1)} %get-tuple-element.29), channel_id=1, source_target_pairs={{0,32},{32,64},{64,96},{96,0},{1,33},{33,65},{65,97},{97,1},{2,34}... | collective-permute-start | bytes 393224 | tf_op jit(solution)/shard_map/ppermute | solution.py:47
  89.4 5.7 %collective-permute-start.21 = (bf16[8,128,128]{2,1,0:T(8,128)(2,1)S(1)}, bf16[8,128,128]{2,1,0:T(8,128)(2,1)S(1)}, u32[]{:S(2)}, u32[]{:S(2)}) collective-permute-start(bf16[8,128,128]{2,1,0:T(8,128)(2,1)S(1)} %get-tuple-element.25), channel_id=1, source_target_pairs={{0,8},{8,0},{1,9},{9,1},{2,10},{10,2},{3,11},{11,3},{4,12},{12,4},... | collective-permute-start | bytes 786440 | tf_op jit(solution)/shard_map/ppermute | solution.py:38
  89.4 13.2 %collective-permute-start.16 = (bf16[8,128,128]{2,1,0:T(8,128)(2,1)S(1)}, bf16[8,128,128]{2,1,0:T(8,128)(2,1)S(1)}, u32[]{:S(2)}, u32[]{:S(2)}) collective-permute-start(bf16[8,128,128]{2,1,0:T(8,128)(2,1)S(1)} %get-tuple-element.19), channel_id=1, source_target_pairs={{0,8},{8,0},{1,9},{9,1},{2,10},{10,2},{3,11},{11,3},{4,12},{12,4},... | collective-permute-start | bytes 786440 | tf_op jit(solution)/shard_map/ppermute | solution.py:38
  89.9 5.4 %collective-permute-start.22 = (bf16[4,128,128]{2,1,0:T(8,128)(2,1)S(1)}, bf16[4,128,128]{2,1,0:T(8,128)(2,1)S(1)}, u32[]{:S(2)}, u32[]{:S(2)}) collective-permute-start(bf16[4,128,128]{2,1,0:T(8,128)(2,1)S(1)} %get-tuple-element.30), channel_id=1, source_target_pairs={{0,96},{32,0},{64,32},{96,64},{1,97},{33,1},{65,33},{97,65},{2,98}... | collective-permute-start | bytes 393224 | tf_op jit(solution)/shard_map/ppermute | solution.py:47
  94.3 8.8 %collective-permute-start.20 = (bf16[8,128,128]{2,1,0:T(8,128)(2,1)S(1)}, bf16[8,128,128]{2,1,0:T(8,128)(2,1)S(1)}, u32[]{:S(2)}, u32[]{:S(2)}) collective-permute-start(bf16[8,128,128]{2,1,0:T(8,128)(2,1)S(1)} %add_convert_fusion.2), channel_id=1, source_target_pairs={{0,32},{32,64},{64,96},{96,0},{1,33},{33,65},{65,97},{97,1},{2,34}... | collective-permute-start | bytes 786440 | tf_op jit(solution)/shard_map/ppermute | solution.py:47
  95.4 7.7 %collective-permute-start.23 = (bf16[8,128,128]{2,1,0:T(8,128)(2,1)S(1)}, bf16[8,128,128]{2,1,0:T(8,128)(2,1)S(1)}, u32[]{:S(2)}, u32[]{:S(2)}) collective-permute-start(bf16[8,128,128]{2,1,0:T(8,128)(2,1)S(1)} %add_convert_fusion.1), channel_id=1, source_target_pairs={{0,96},{32,0},{64,32},{96,64},{1,97},{33,1},{65,33},{97,65},{2,98}... | collective-permute-start | bytes 786440 | tf_op jit(solution)/shard_map/ppermute | solution.py:47
  98.0 16.2 %all-to-all-start.2 = ((bf16[8,4,64,128]{3,2,1,0:T(8,128)(2,1)}), bf16[8,4,64,128]{3,2,1,0:T(8,128)(2,1)S(1)}, u32[]{:S(2)}, u32[]{:S(2)}) async-start(bf16[8,4,64,128]{3,2,1,0:T(8,128)(2,1)} %get-tuple-element.16), calls=%async_computation.2 | async-start | bytes 1048576 | tf_op jit(solution)/shard_map/all_to_all | solution.py:436
  103.3 9.8 %collective-permute-start.24 = (bf16[2,128,128]{2,1,0:T(8,128)(2,1)S(1)}, bf16[2,128,128]{2,1,0:T(8,128)(2,1)S(1)}, u32[]{:S(2)}, u32[]{:S(2)}) collective-permute-start(bf16[2,128,128]{2,1,0:T(8,128)(2,1)S(1)} %get-tuple-element.26), channel_id=1, source_target_pairs={{0,2},{2,4},{4,6},{6,0},{1,3},{3,5},{5,7},{7,1},{8,10},{10,12},{12... | collective-permute-start | bytes 196616 | tf_op jit(solution)/shard_map/ppermute | solution.py:47
  104.8 9.3 %collective-permute-start.25 = (bf16[2,128,128]{2,1,0:T(8,128)(2,1)S(1)}, bf16[2,128,128]{2,1,0:T(8,128)(2,1)S(1)}, u32[]{:S(2)}, u32[]{:S(2)}) collective-permute-start(bf16[2,128,128]{2,1,0:T(8,128)(2,1)S(1)} %get-tuple-element.28), channel_id=1, source_target_pairs={{0,4},{2,6},{4,0},{6,2},{1,5},{3,7},{5,1},{7,3},{8,12},{10,14},{12... | collective-permute-start | bytes 196616 | tf_op jit(solution)/shard_map/ppermute | solution.py:47
  107.5 6.6 %collective-permute-start.26 = (bf16[2,128,128]{2,1,0:T(8,128)(2,1)S(1)}, bf16[2,128,128]{2,1,0:T(8,128)(2,1)S(1)}, u32[]{:S(2)}, u32[]{:S(2)}) collective-permute-start(bf16[2,128,128]{2,1,0:T(8,128)(2,1)S(1)} %get-tuple-element.27), channel_id=1, source_target_pairs={{0,6},{2,0},{4,2},{6,4},{1,7},{3,1},{5,3},{7,5},{8,14},{10,8},{12,... | collective-permute-start | bytes 196616 | tf_op jit(solution)/shard_map/ppermute | solution.py:47
  114.2 15.3 %all-to-all-start.3 = ((bf16[8,4,64,128]{3,2,1,0:T(8,128)(2,1)}), bf16[8,4,64,128]{3,2,1,0:T(8,128)(2,1)S(1)}, u32[]{:S(2)}, u32[]{:S(2)}) async-start(bf16[8,4,64,128]{3,2,1,0:T(8,128)(2,1)} %get-tuple-element.17), calls=%async_computation.3 | async-start | bytes 1048576 | tf_op jit(solution)/shard_map/all_to_all | solution.py:437
  117.7 8.2 %collective-permute-start.27 = (bf16[128,128]{1,0:T(8,128)(2,1)S(1)}, bf16[128,128]{1,0:T(8,128)(2,1)S(1)}, u32[]{:S(2)}, u32[]{:S(2)}) collective-permute-start(bf16[128,128]{1,0:T(8,128)(2,1)S(1)} %dynamic-slice_bitcast_fusion.3), channel_id=1, source_target_pairs={{0,1},{1,0},{2,3},{3,2},{4,5},{5,4},{6,7},{7,6},{8,9},{9,8},{10,11... | collective-permute-start | bytes 98312 | tf_op jit(solution)/shard_map/ppermute | solution.py:431
  126.0 3.5 %collective-permute-start.28 = (bf16[32,128]{1,0:T(8,128)(2,1)S(1)}, bf16[32,128]{1,0:T(8,128)(2,1)S(1)}, u32[]{:S(2)}, u32[]{:S(2)}) collective-permute-start(bf16[32,128]{1,0:T(8,128)(2,1)S(1)} %get-tuple-element.35), channel_id=1, source_target_pairs={{0,8},{8,0},{16,24},{24,16},{1,9},{9,1},{17,25},{25,17},{2,10},{10... | collective-permute-start | bytes 24584 | tf_op jit(solution)/shard_map/ppermute | solution.py:42
  126.1 5.2 %collective-permute-start.29 = (bf16[32,128]{1,0:T(8,128)(2,1)S(1)}, bf16[32,128]{1,0:T(8,128)(2,1)S(1)}, u32[]{:S(2)}, u32[]{:S(2)}) collective-permute-start(bf16[32,128]{1,0:T(8,128)(2,1)S(1)} %get-tuple-element.34), channel_id=1, source_target_pairs={{0,16},{8,24},{16,0},{24,8},{1,17},{9,25},{17,1},{25,9},{2,18},{10... | collective-permute-start | bytes 24584 | tf_op jit(solution)/shard_map/ppermute | solution.py:42
  128.3 4.6 %collective-permute-start.30 = (bf16[32,128]{1,0:T(8,128)(2,1)S(1)}, bf16[32,128]{1,0:T(8,128)(2,1)S(1)}, u32[]{:S(2)}, u32[]{:S(2)}) collective-permute-start(bf16[32,128]{1,0:T(8,128)(2,1)S(1)} %get-tuple-element.33), channel_id=1, source_target_pairs={{0,24},{8,16},{16,8},{24,0},{1,25},{9,17},{17,9},{25,1},{2,26},{10... | collective-permute-start | bytes 24584 | tf_op jit(solution)/shard_map/ppermute | solution.py:42

commit v3 on v0

v3 whole, which is shorter than its diff:
```python
import math

import jax
import jax.numpy as jnp
from jax import lax
from jax.experimental import pallas as pl
from jax.experimental.pallas import tpu as pltpu
from jax.sharding import Mesh, PartitionSpec as P

EPSILON = 1e-05
LOG2E = math.log2(math.e)
IA = ("z", "xh", "core")
JA = ("y", "xl")
F32 = jnp.float32
BF16 = jnp.bfloat16
LANES = 128
PARAMS = pltpu.CompilerParams(vmem_limit_bytes=48 * 1024 * 1024)


def normalize(values, norm_gain, norm_shift):
    mean_val = jnp.mean(values, axis=-1, keepdims=True)
    centred = values - mean_val
    variance = jnp.mean(centred * centred, axis=-1, keepdims=True)
    return centred * lax.rsqrt(variance + EPSILON) * norm_gain + norm_shift


def mm(a, b):
    return lax.dot_general(a, b, (((1,), (0,)), ((), ())), preferred_element_type=F32)


def mm_nt(a, b):
    return lax.dot_general(a, b, (((1,), (1,)), ((), ())), preferred_element_type=F32)


def mm_tn(a, b):
    return lax.dot_general(a, b, (((0,), (0,)), ((), ())), preferred_element_type=F32)


def swap(a):
    return lax.ppermute(a, "core", [(0, 1), (1, 0)])


def cross(a, bits):
    return lax.ppermute(a, ("xh", "xl"), [(s, s ^ bits) for s in range(4)])


def shift(a, axis, by):
    size = lax.axis_size(axis)
    return lax.ppermute(a, axis, [(s, (s + by) % size) for s in range(size)])


def whole(a):
    return pl.BlockSpec(a.shape, lambda *_: (0,) * len(a.shape))


def line_mask(block, width):
    lane = lax.broadcasted_iota(jnp.int32, (block, width), 1)
    return lax.broadcasted_iota(jnp.int32, (block, width), 0) == lane % block


def prep_kernel(pair_ref, gain_ref, shift_ref, w_ref, tile_ref):
    rows, block, channels = pair_ref.shape
    x = pair_ref[...].reshape(rows * block, channels).astype(F32)
    normed = normalize(x, gain_ref[...], shift_ref[...]).astype(BF16)
    every = mm(normed, w_ref[...])
    keep = line_mask(block, every.shape[1])
    lines = []
    for i in range(rows):
        part = jnp.where(keep, every[i * block : (i + 1) * block], 0.0)
        lines.append(jnp.sum(part, axis=0, keepdims=True))
    tile_ref[...] = jnp.concatenate(lines, axis=0).astype(BF16)


def prep(pair, gain, shift_row, w_spread):
    return pl.pallas_call(
        prep_kernel,
        out_shape=jax.ShapeDtypeStruct((pair.shape[0], w_spread.shape[1]), BF16),
        compiler_params=PARAMS,
        cost_estimate=pl.CostEstimate(
            flops=2**27, bytes_accessed=2**19, transcendentals=2**12
        ),
    )(pair, gain, shift_row, w_spread)


def project_kernel(
    rows_ref, gain_ref, shift_ref, w_n_ref, w_t_ref, w_o_ref, out_n_ref, out_t_ref, out_f_ref
):
    n_blocks, _, _, block, channels = rows_ref.shape
    n = n_blocks * block
    inner = w_o_ref.shape[0]
    x = rows_ref[:, 0].reshape(n, channels).astype(F32)
    normed = normalize(x, gain_ref[...], shift_ref[...]).astype(BF16)
    out_n_ref[0, :, : 3 * inner] = mm(normed, w_n_ref[...]).astype(BF16)
    proj_t = mm_nt(w_t_ref[...], normed)
    gate = jax.nn.sigmoid(proj_t[inner : 2 * inner])
    d_gated = mm_nt(w_o_ref[...], rows_ref[:, 1].reshape(n, channels))
    d_att = (d_gated * gate).astype(BF16)
    out_t_ref[0, :inner] = proj_t[:inner].astype(BF16)
    out_t_ref[0, inner : 3 * inner] = proj_t[2 * inner :].astype(BF16)
    out_t_ref[0, 3 * inner :] = d_att
    out_n_ref[0, :, 3 * inner :] = d_att.T
    out_f_ref[0, :inner] = gate
    out_f_ref[0, inner:] = d_gated


def project(both, gain, shift_row, w_n, w_t, w_o):
    n_blocks, kinds, rows, block, channels = both.shape
    n = n_blocks * block
    inner = w_o.shape[0]
    out_n = jax.ShapeDtypeStruct((rows, n, 4 * inner), BF16)
    out_t = jax.ShapeDtypeStruct((rows, 4 * inner, n), BF16)
    out_f = jax.ShapeDtypeStruct((rows, 2 * inner, n), F32)
    return pl.pallas_call(
        project_kernel,
        grid=(rows,),
        in_specs=[
            pl.BlockSpec((n_blocks, kinds, 1, block, channels), lambda i: (0, 0, i, 0, 0))
        ]
        + [whole(a) for a in (gain, shift_row, w_n, w_t, w_o)],
        out_specs=[
            pl.BlockSpec((1,) + a.shape[1:], lambda i: (i, 0, 0)) for a in (out_n, out_t, out_f)
        ],
        out_shape=[out_n, out_t, out_f],
        compiler_params=PARAMS,
        cost_estimate=pl.CostEstimate(
            flops=2**31, bytes_accessed=8 * 2**20, transcendentals=2**18
        ),
    )(both, gain, shift_row, w_n, w_t, w_o)


def z_lanes(ahead):
    at = lax.rem(lax.axis_index("z") + ahead, lax.axis_size("z"))
    return pl.ds(pl.multiple_of(at * LANES, LANES), LANES)


def attend_kernel(heads, aheads, n_own, *refs):
    n_ref, t_ref = refs[:2]
    bias_refs = refs[2 : 2 + n_own * 2]
    refs = refs[2 + n_own * 2 :]
    count = len(aheads)
    att_refs = refs[:count]
    dq_refs = refs[count : 2 * count]
    dk_ref, dv_ref = refs[2 * count : 2 * count + 2]
    mine_refs = refs[2 * count + 2 : 3 * count + 2]
    theirs_refs = refs[3 * count + 2 : 4 * count + 2]
    bias_s, gb_s, s_s, dp_s, p_s, ds_s, tile_s, line_s = refs[4 * count + 2 :]
    row = pl.program_id(0)
    n = n_ref.shape[1]
    inner = n_ref.shape[2] // 4
    head_dim = inner // heads
    scale = 1.0 / math.sqrt(head_dim)
    n_ja, _, lines = tile_s.shape
    block = n // n_ja
    rows_i = LANES // 4
    pairs = heads // 2
    core = lax.axis_index("core")
    xh = lax.axis_index("xh")
    xl = lax.axis_index("xl")
    y = lax.axis_index("y")

    @pl.when(row == 0)
    def _():
        gb_s[...] = jnp.zeros_like(gb_s)
        parts = n_own // count
        for c in range(count):
            for which in range(2):
                base = which * n_own + c * parts
                d = 0
                for ref in bias_refs[base : base + parts]:
                    for e in range(ref.shape[0]):
                        for bits in range(4):
                            owner = lax.rem(y + 4 - d, 4) * 2 + (xl ^ (bits & 1))
                            at = (xh ^ (bits >> 1)) * 2 + (core ^ which)
                            at = pl.ds(pl.multiple_of(at * rows_i, rows_i), rows_i)
                            tile_s[owner, at, :] = ref[e, bits]
                        d += 1
            for owner in range(n_ja):
                for p in range(pairs):
                    t = tile_s[owner, :, p * LANES : (p + 1) * LANES].astype(F32).T * LOG2E
                    for e in range(2):
                        h = p * 2 + e
                        bias_s[
                            c, owner * block : (owner + 1) * block, h * LANES : (h + 1) * LANES
                        ] = t[e * block : (e + 1) * block]

    k_n = n_ref[0, :, inner : 2 * inner]
    v_n = n_ref[0, :, 2 * inner : 3 * inner]
    row_head = lax.broadcasted_iota(jnp.int32, (inner, LANES), 0) // head_dim
    lane_head = lax.broadcasted_iota(jnp.int32, (LANES, inner), 1) // head_dim
    nil = jnp.zeros((), BF16)
    step = 16
    wide = heads * LANES
    for c, ahead in enumerate(aheads):
        at = z_lanes(ahead)
        q_t = t_ref[0, :inner, at]
        a_t = t_ref[0, 3 * inner :, at]
        q_n = n_ref[0, at, :inner]
        a_n = n_ref[0, at, 3 * inner :]
        q_blk = jnp.concatenate([jnp.where(row_head == h, q_t, nil) for h in range(heads)], 1)
        a_blk = jnp.concatenate([jnp.where(row_head == h, a_t, nil) for h in range(heads)], 1)
        q_row = jnp.concatenate([jnp.where(lane_head == h, q_n, nil) for h in range(heads)], 0)
        a_row = jnp.concatenate([jnp.where(lane_head == h, a_n, nil) for h in range(heads)], 0)
        s_s[...] = mm(k_n, q_blk)
        top = jnp.full((8, wide), -jnp.inf, F32)
        for k in range(0, n, step):
            t = s_s[k : k + step, :] * (scale * LOG2E) + bias_s[c, k : k + step, :]
            s_s[k : k + step, :] = t
            top = jnp.maximum(top, jnp.maximum(t[:8], t[8:]))
        top = jnp.max(top, axis=0, keepdims=True)
        total = jnp.zeros((8, wide), F32)
        for k in range(0, n, step):
            p = jnp.exp2(s_s[k : k + step, :] - top)
            s_s[k : k + step, :] = p
            total = total + (p[:8] + p[8:])
        inv = 1.0 / jnp.sum(total, axis=0, keepdims=True)
        for k in range(0, n, step):
            p_s[k : k + step, :] = (s_s[k : k + step, :] * inv).astype(BF16)
        diag = []
        for p in range(pairs):
            rows = slice(p * 2 * head_dim, (p + 1) * 2 * head_dim)
            cols = slice(p * 2 * LANES, (p + 1) * 2 * LANES)
            att = mm(t_ref[0, 2 * inner + rows.start : 2 * inner + rows.stop, :], p_s[:, cols])
            diag.append(
                jnp.sum(a_blk[rows, cols].astype(F32) * att, axis=0, keepdims=True)
            )
            for e in range(2):
                h = p * 2 + e
                att_refs[c][0, h * head_dim : (h + 1) * head_dim, :] = att[
                    e * head_dim : (e + 1) * head_dim, e * LANES : (e + 1) * LANES
                ]
        diag = jnp.concatenate(diag, axis=1)
        dp_s[...] = mm(v_n, a_blk)
        for k in range(0, n, step):
            ds = (s_s[k : k + step, :] * inv) * (dp_s[k : k + step, :] - diag)
            gb_s[c, k : k + step, :] += ds
            ds_s[k : k + step, :] = ds.astype(BF16)
        for p in range(pairs):
            cols = slice(p * 2 * LANES, (p + 1) * 2 * LANES)
            first = inner + p * 2 * head_dim
            dq = mm(t_ref[0, first : first + 2 * head_dim, :], ds_s[:, cols]) * scale
            for e in range(2):
                h = p * 2 + e
                dq_refs[c][0, h * head_dim : (h + 1) * head_dim, :] = dq[
                    e * head_dim : (e + 1) * head_dim, e * LANES : (e + 1) * LANES
                ].astype(BF16)
        dk_c = mm(ds_s[...], q_row)
        dv_c = mm(p_s[...], a_row)
        dk = dk_c if c == 0 else dk + dk_c
        dv = dv_c if c == 0 else dv + dv_c
    dk_ref[0] = (dk * scale).astype(BF16)
    dv_ref[0] = dv.astype(BF16)

    @pl.when(row == pl.num_programs(0) - 1)
    def _():
        for c in range(count):
            for owner in range(n_ja):
                for p in range(pairs):
                    t = jnp.concatenate(
                        [
                            gb_s[
                                c,
                                owner * block : (owner + 1) * block,
                                h * LANES : (h + 1) * LANES,
                            ]
                            for h in (2 * p, 2 * p + 1)
                        ],
                        axis=0,
                    )
                    line_s[:, p * LANES : (p + 1) * LANES] = t.T.astype(BF16)
                for far in range(2):
                    for ref, which in ((mine_refs[c], core), (theirs_refs[c], 1 - core)):
                        at = pl.multiple_of((far * 2 + which) * rows_i, rows_i)
                        ref[far, owner] = line_s[pl.ds(at, rows_i), :]


def attend(heads, aheads, by_n, by_t, own, other):
    rows, n, wide = by_n.shape
    inner = wide // 4
    count = len(aheads)
    rows_i, lines = own[0].shape[2:]
    n_ja = n // (lines // heads)
    att = jax.ShapeDtypeStruct((rows, inner, LANES), F32)
    dq = jax.ShapeDtypeStruct((rows, inner, LANES), BF16)
    grad = jax.ShapeDtypeStruct((rows, n, inner), BF16)
    gb = jax.ShapeDtypeStruct((2, n_ja, rows_i, lines), BF16)

    def by_row(a):
        return pl.BlockSpec((1,) + a.shape[1:], lambda i: (i, 0, 0))

    out_shape = [att] * count + [dq] * count + [grad] * 2 + [gb] * (2 * count)
    out = pl.pallas_call(
        lambda *refs: attend_kernel(heads, aheads, len(own), *refs),
        grid=(rows,),
        in_specs=[by_row(by_n), by_row(by_t)] + [whole(a) for a in (*own, *other)],
        out_specs=[by_row(a) for a in out_shape[: 2 * count + 2]] + [whole(gb)] * (2 * count),
        out_shape=out_shape,
        scratch_shapes=[
            pltpu.VMEM((count, n, heads * LANES), F32),
            pltpu.VMEM((count, n, heads * LANES), F32),
            pltpu.VMEM((n, heads * LANES), F32),
            pltpu.VMEM((n, heads * LANES), F32),
            pltpu.VMEM((n, heads * LANES), BF16),
            pltpu.VMEM((n, heads * LANES), BF16),
            pltpu.VMEM((n_ja, LANES, lines), BF16),
            pltpu.VMEM((LANES, lines), BF16),
        ],
        compiler_params=PARAMS,
        cost_estimate=pl.CostEstimate(
            flops=count * 2**32, bytes_accessed=2**23, transcendentals=count * 2**20
        ),
    )(by_n, by_t, *own, *other)
    return (
        out[:count],
        out[count : 2 * count],
        out[2 * count],
        out[2 * count + 1],
        out[2 * count + 2 : 3 * count + 2],
        out[3 * count + 2 :],
    )


def finish_kernel(aheads, n_parts, f_ref, w_t_ref, w_o_ref, *refs):
    count = len(aheads)
    att_refs, dq_refs = refs[:count], refs[count : 2 * count]
    dk_refs = refs[2 * count : 2 * count + n_parts]
    dv_refs = refs[2 * count + n_parts : 2 * count + 2 * n_parts]
    out_ref, att_s, dq_s = refs[2 * count + 2 * n_parts :]
    inner = w_o_ref.shape[0]
    for ahead, att_ref, dq_ref in zip(aheads, att_refs, dq_refs):
        at = z_lanes(ahead)
        att_s[:, at] = att_ref[0]
        dq_s[:, at] = dq_ref[0]
    gate = f_ref[0, :inner]
    d_gated = f_ref[0, inner:]
    att = att_s[...]
    half = (out_ref.shape[0],) + out_ref.shape[2:]
    update = mm_tn((gate * att).astype(BF16), w_o_ref[...])
    out_ref[:, 0] = update.astype(BF16).reshape(half)
    d_gate = (d_gated * att * gate * (1.0 - gate)).astype(BF16)
    left_t = jnp.concatenate([dq_s[...], d_gate], axis=0)
    dk = sum(ref[0].astype(F32) for ref in dk_refs).astype(BF16)
    dv = sum(ref[0].astype(F32) for ref in dv_refs).astype(BF16)
    dn = mm_tn(left_t, w_t_ref[: 2 * inner])
    dn = dn + mm(jnp.concatenate([dk, dv], axis=1), w_t_ref[2 * inner :])
    out_ref[:, 1] = dn.astype(BF16).reshape(half)


def finish(like, aheads, by_f, w_t, w_o, att, dq, dk, dv):
    n_blocks, kinds, rows, block, channels = like.shape
    inner = w_o.shape[0]
    arrays = (*att, *dq, *dk, *dv)

    def by_row(a):
        return pl.BlockSpec((1,) + a.shape[1:], lambda i: (i, 0, 0))

    return pl.pallas_call(
        lambda *refs: finish_kernel(aheads, len(dk), *refs),
        grid=(rows,),
        in_specs=[by_row(by_f), whole(w_t), whole(w_o)] + [by_row(a) for a in arrays],
        out_specs=pl.BlockSpec(
            (n_blocks, kinds, 1, block, channels), lambda i: (0, 0, i, 0, 0)
        ),
        out_shape=jax.ShapeDtypeStruct(like.shape, BF16),
        scratch_shapes=[
            pltpu.VMEM((inner, n_blocks * block), F32),
            pltpu.VMEM((inner, n_blocks * block), BF16),
        ],
        compiler_params=PARAMS,
        cost_estimate=pl.CostEstimate(flops=2**31, bytes_accessed=2**23, transcendentals=0),
    )(by_f, w_t, w_o, *arrays)


def final_kernel(pair_ref, both_ref, gain_ref, shift_ref, w_ref, gb_ref, out_ref):
    rows, block, channels = pair_ref.shape
    tile = jnp.sum(gb_ref[...].astype(F32), axis=0).astype(BF16).astype(F32)
    keep = line_mask(block, tile.shape[1])
    spread = jnp.concatenate(
        [
            jnp.where(keep, jnp.broadcast_to(tile[i : i + 1], keep.shape), 0.0).astype(BF16)
            for i in range(rows)
        ],
        axis=0,
    )
    dn = both_ref[:, 1].reshape(rows * block, channels).astype(F32) + mm(spread, w_ref[...])
    x = pair_ref[...].reshape(rows * block, channels).astype(F32)
    centred = x - jnp.mean(x, axis=-1, keepdims=True)
    rstd = lax.rsqrt(jnp.mean(centred * centred, axis=-1, keepdims=True) + EPSILON)
    unit = centred * rstd
    push = dn * gain_ref[...]
    along = jnp.mean(push * unit, axis=-1, keepdims=True)
    level = jnp.mean(push, axis=-1, keepdims=True)
    out_ref[...] = ((push - level - unit * along) * rstd).reshape(out_ref.shape)


def final(pair, both, gain, shift_row, w_spread, gb):
    return pl.pallas_call(
        final_kernel,
        out_shape=jax.ShapeDtypeStruct(pair.shape, F32),
        compiler_params=PARAMS,
        cost_estimate=pl.CostEstimate(
            flops=2**27, bytes_accessed=2**21, transcendentals=2**12
        ),
    )(pair, both, gain, shift_row, w_spread, gb)


def shards(
    pair,
    cotangent,
    norm_gain,
    norm_shift,
    query_weight,
    key_weight,
    value_weight,
    gate_weight,
    bias_weight,
    out_weight,
):
    rows_i, rows_j, channels = pair.shape
    heads = bias_weight.shape[1]
    n_ja = lax.axis_size(JA)
    own_i = rows_i // n_ja
    gain = norm_gain.reshape(1, channels)
    shift_row = norm_shift.reshape(1, channels)
    w_spread = jnp.repeat(bias_weight, rows_j, axis=1)
    w_n = jnp.concatenate([query_weight, key_weight, value_weight], axis=1)
    w_t = jnp.concatenate([query_weight.T, gate_weight.T, key_weight.T, value_weight.T], axis=0)

    parts = (n_ja, 1, own_i, rows_j, channels)
    both = jnp.concatenate([pair.reshape(parts), cotangent.reshape(parts)], axis=1)
    both = lax.all_to_all(both, JA, 0, 0, tiled=True)

    tile = prep(pair, gain, shift_row, w_spread)
    near = jnp.stack([tile] + [cross(tile, bits) for bits in (1, 2, 3)])
    near = jnp.stack([near] + [shift(near, "y", d) for d in (1, 2, 3)])
    prev, after = shift(near, "z", 1), shift(near, "z", 3)
    opp0, opp1 = shift(prev[:2], "z", 1), shift(after[2:], "z", 3)

    by_n, by_t, by_f = project(both, gain, shift_row, w_n, w_t, out_weight)
    att0, dq0, dk0, dv0, mine0, theirs0 = attend(
        heads, (0,), by_n, by_t, [near], [swap(near)]
    )
    att1, dq1, dk1, dv1, mine1, theirs1 = attend(
        heads, (3, 1), by_n, by_t, [prev, after], [swap(prev), swap(after)]
    )
    att2, dq2, dk2, dv2, mine2, theirs2 = attend(
        heads, (2,), by_n, by_t, [opp0, opp1], [swap(opp0), swap(opp1)]
    )
    done = finish(
        both,
        (0, 3, 1, 2),
        by_f,
        w_t,
        out_weight,
        (*att0, *att1, *att2),
        (*dq0, *dq1, *dq2),
        (dk0, dk1, dk2),
        (dv0, dv1, dv2),
    )

    def joined(a, b):
        return (a.astype(F32) + b.astype(F32)).astype(BF16)

    own = joined(mine0[0], swap(theirs0[0]))
    back = shift(joined(mine1[0], swap(theirs1[0])), "z", 3)
    ahead = shift(joined(mine1[1], swap(theirs1[1])), "z", 1)
    opp = shift(joined(mine2[0], swap(theirs2[0])), "z", 2)
    gb = (own.astype(F32) + back.astype(F32) + ahead.astype(F32) + opp.astype(F32)).astype(BF16)
    gb = lax.all_to_all(
        gb.reshape((2 * n_ja,) + gb.shape[2:]), ("xh",) + JA, 0, 0, tiled=True
    )

    done = lax.all_to_all(done, JA, 0, 0, tiled=True)
    update = done[:, 0].reshape(pair.shape)
    pair_grad = final(pair, done, gain, shift_row, w_spread.T, gb)
    return (update, pair_grad)


def solution(mesh):
    fine = Mesh(mesh.devices.reshape(4, 2, 2, 4, 2), IA + JA)
    spec = P(IA, JA, None)
    in_specs = (spec, spec) + (P(),) * 8
    return jax.shard_map(
        shards, mesh=fine, in_specs=in_specs, out_specs=(spec, spec), check_vma=False
    )
```

time: 801 us -> 134 us (0.17)
  waiting for transfers between devices: 568 us -> 37.9 us
  matrix products: 102 us -> 0 us
  local copies, waits for them, and re-layouts: 60.2 us -> 6.11 us
  starting transfers between devices: 0.47 us -> 42.2 us
  Pallas kernels: 0 us -> 39.5 us
  blocking collectives: 30.4 us -> 0 us
  other arithmetic: 22.5 us -> 6.42 us
  between operations: 14.6 us -> 0.88 us
    all_gather x3 -> x0, waiting for transfers between devices: 198 us -> none  [the longest x1 90.1 us: shards(): lax.all_gather(keys_local, 'ja', axis=1, tiled=True)]
    psum x2 -> x0, waiting for transfers between devices: 188 us -> none  [the longest x1 137 us: shards(): lax.psum(bias_part.astype(jnp.bfloat16), 'ia').astype(jnp.float32)]
    reduce_scatter x2 -> x0, waiting for transfers between devices: 182 us -> none  [the longest x1 91.3 us: shards(): lax.psum_scatter(key_part.reshape(rows_i, key_count, inner_width).astype(...]
    dot_general x40 -> x0, matrix products: 102 us -> none  [the longest x4 24.3 us: out_step(): jnp.einsum('ijhk,ikhd->ijhd', probs_b, value_block, preferred_element_typ...]
    pallas_call x0 -> x7, Pallas kernels: none -> 39.5 us  [the longest x3 28.3 us: attend(): pl.pallas_call(lambda *refs: attend_kernel(heads, aheads, len(own), *refs...]
    all_gather x1 -> x0, blocking collectives: 30.4 us -> none  [shards(): bias_rows = lax.all_gather(bias_tile, 'ja', axis=2, tiled=True)]
    ppermute x0 -> x22, waiting for transfers between devices: none -> 30 us  [the longest x10 20.6 us: shift(): return lax.ppermute(a, axis, [(s, (s + by) % size) for s in range(size)])]
    ppermute x0 -> x22, starting transfers between devices: none -> 26.1 us  [the longest x10 18.9 us: shift(): return lax.ppermute(a, axis, [(s, (s + by) % size) for s in range(size)])]
  transfers between devices with their start and end apart: 7 -> 25, of which waited for: 7 -> 10; matrix products, arithmetic and copies ran while one was open for 8% -> 4% of each run, Pallas kernels for 0% -> 28%
where the time goes in v3:
time: 134 us; the launch traced here: 133 us
  starting transfers between devices  42.2 us (31%)
  Pallas kernels  39.5 us (29%)
  waiting for transfers between devices  37.9 us (28%)
  other arithmetic  6.42 us (5%)
  local copies, waits for them, and re-layouts  6.11 us (5%)
    pallas_call x3, Pallas kernels, attend(): pl.pallas_call(lambda *refs: attend_kernel(heads, aheads, len(own), *refs...  28.3 us
    ppermute x10, waiting for transfers between devices, shift(): return lax.ppermute(a, axis, [(s, (s + by) % size) for s in range(size)])  20.6 us
    ppermute x10, starting transfers between devices, shift(): return lax.ppermute(a, axis, [(s, (s + by) % size) for s in range(size)])  18.9 us
    ppermute x3, waiting for transfers between devices, cross(): return lax.ppermute(a, ('xh', 'xl'), [(s, s ^ bits) for s in range(4)])  9.37 us
    all_to_all x1, waiting for transfers between devices, shards(): lax.all_to_all(gb.reshape((2 * n_ja,) + gb.shape[2:]), ('xh',) + JA, 0, 0...  7.84 us
    all_to_all x1, starting transfers between devices, shards(): lax.all_to_all(gb.reshape((2 * n_ja,) + gb.shape[2:]), ('xh',) + JA, 0, 0...  6.12 us
    all_to_all x1, starting transfers between devices, shards(): both = lax.all_to_all(both, JA, 0, 0, tiled=True)  5.62 us
    unnamed x32, local copies, waits for them, and re-layouts  5.12 us
  transfers between devices with their start and end apart: 25, of which 10 were waited for; matrix products, arithmetic and copies ran while one was open for 4% of the time, Pallas kernels for 28%

profile of v3, /device:TPU:0, one launch (start us, length us, event | category | flops | bytes accessed | tf_op | source)
XLA Modules:
  0.0 132.9 jit_solution(14503328537461989135)
XLA Ops:
  0.7 2.3 %pad_maximum_fusion = bf16[8,2,4,64,128]{4,3,2,1,0:T(8,128)(2,1)} fusion(bf16[8,1,4,64,128]{4,3,2,1,0:T(8,128)(2,1)} %bitcast.33, bf16[8,1,4,64,128]{4,3,2,1,0:T(8,128)(2,1)} %bitcast.22), kind=kLoop, calls=%fused_computation | loop fusion | flops 524288 | bytes 2097152 | tf_op jit(solution)/shard_map/concatenate | solution.py:429
  3.0 0.0 copy-start.1
  3.0 5.6 %all-to-all-start = ((bf16[8,2,4,64,128]{4,3,2,1,0:T(8,128)(2,1)}), bf16[8,2,4,64,128]{4,3,2,1,0:T(8,128)(2,1)S(1)}, u32[]{:S(2)}, u32[]{:S(2)}) async-start(bf16[8,2,4,64,128]{4,3,2,1,0:T(8,128)(2,1)} %pad_maximum_fusion), calls=%async_computation | async-start | bytes 2097152 | tf_op jit(solution)/shard_map/all_to_all | solution.py:430
  8.7 0.1 copy.16.w_ref
  8.8 0.9 shard_map.114
  9.7 2.1 %collective-permute-start = (bf16[32,256]{1,0:T(8,128)(2,1)S(1)}, bf16[32,256]{1,0:T(8,128)(2,1)S(1)}, u32[]{:S(2)}, u32[]{:S(2)}) collective-permute-start(bf16[32,256]{1,0:T(8,128)(2,1)S(1)} %shard_map.114), channel_id=1, source_target_pairs={{0,1},{1,0},{16,17},{17,16},{2,3},{3,2},{18,19},{19,18},{4,5},{5,4... | collective-permute-start | bytes 49160 | tf_op jit(solution)/shard_map/ppermute | solution.py:44
  11.8 2.7 %collective-permute-start.1 = (bf16[32,256]{1,0:T(8,128)(2,1)S(1)}, bf16[32,256]{1,0:T(8,128)(2,1)S(1)}, u32[]{:S(2)}, u32[]{:S(2)}) collective-permute-start(bf16[32,256]{1,0:T(8,128)(2,1)S(1)} %shard_map.114), channel_id=1, source_target_pairs={{0,16},{1,17},{16,0},{17,1},{2,18},{3,19},{18,2},{19,3},{4,20},{5,... | collective-permute-start | bytes 49160 | tf_op jit(solution)/shard_map/ppermute | solution.py:44
  14.6 0.0 collective-permute-start.2
  14.6 8.2 %collective-permute-done = bf16[32,256]{1,0:T(8,128)(2,1)S(1)} collective-permute-done((bf16[32,256]{1,0:T(8,128)(2,1)S(1)}, bf16[32,256]{1,0:T(8,128)(2,1)S(1)}, u32[]{:S(2)}, u32[]{:S(2)}) %collective-permute-start) | collective-permute-done | bytes 16416 | tf_op jit(solution)/shard_map/ppermute | solution.py:44
  22.8 1.2 collective-permute-done.1
  24.0 1.8 %collective-permute-start.3 = (bf16[4,32,256]{2,1,0:T(8,128)(2,1)S(1)}, bf16[4,32,256]{2,1,0:T(8,128)(2,1)S(1)}, u32[]{:S(2)}, u32[]{:S(2)}) collective-permute-start(bf16[4,32,256]{2,1,0:T(8,128)(2,1)S(1)} %get-tuple-element.53), channel_id=1, source_target_pairs={{0,2},{2,4},{4,6},{6,0},{1,3},{3,5},{5,7},{7,1},{8,10},{10,12},{12... | collective-permute-start | bytes 196616 | tf_op jit(solution)/shard_map/ppermute | solution.py:49
  25.8 2.7 %collective-permute-start.4 = (bf16[4,32,256]{2,1,0:T(8,128)(2,1)S(1)}, bf16[4,32,256]{2,1,0:T(8,128)(2,1)S(1)}, u32[]{:S(2)}, u32[]{:S(2)}) collective-permute-start(bf16[4,32,256]{2,1,0:T(8,128)(2,1)S(1)} %get-tuple-element.53), channel_id=1, source_target_pairs={{0,4},{2,6},{4,0},{6,2},{1,5},{3,7},{5,1},{7,3},{8,12},{10,14},{12... | collective-permute-start | bytes 196616 | tf_op jit(solution)/shard_map/ppermute | solution.py:49
  28.4 1.5 %collective-permute-start.5 = (bf16[4,32,256]{2,1,0:T(8,128)(2,1)S(1)}, bf16[4,32,256]{2,1,0:T(8,128)(2,1)S(1)}, u32[]{:S(2)}, u32[]{:S(2)}) collective-permute-start(bf16[4,32,256]{2,1,0:T(8,128)(2,1)S(1)} %get-tuple-element.53), channel_id=1, source_target_pairs={{0,6},{2,0},{4,2},{6,4},{1,7},{3,1},{5,3},{7,5},{8,14},{10,8},{12,... | collective-permute-start | bytes 196616 | tf_op jit(solution)/shard_map/ppermute | solution.py:49
  29.9 1.6 %collective-permute-done.4 = bf16[4,32,256]{2,1,0:T(8,128)(2,1)S(1)} collective-permute-done((bf16[4,32,256]{2,1,0:T(8,128)(2,1)S(1)}, bf16[4,32,256]{2,1,0:T(8,128)(2,1)S(1)}, u32[]{:S(2)}, u32[]{:S(2)}) %collective-permute-start.4) | collective-permute-done | bytes 65568 | tf_op jit(solution)/shard_map/ppermute | solution.py:49
  31.5 1.2 collective-permute-done.5
  32.7 2.0 %collective-permute-start.7 = (bf16[4,4,32,256]{3,2,1,0:T(8,128)(2,1)S(1)}, bf16[4,4,32,256]{3,2,1,0:T(8,128)(2,1)S(1)}, u32[]{:S(2)}, u32[]{:S(2)}) collective-permute-start(bf16[4,4,32,256]{3,2,1,0:T(8,128)(2,1)S(1)} %pad_maximum_fusion.1.refs_2_), channel_id=1, source_target_pairs={{0,32},{32,64},{64,96},{96,0},{1,33},{33,65},{65,97},{97,1},{2,34}... | collective-permute-start | bytes 786440 | tf_op jit(solution)/shard_map/ppermute | solution.py:49
  34.7 2.2 %collective-permute-start.8 = (bf16[4,4,32,256]{3,2,1,0:T(8,128)(2,1)S(1)}, bf16[4,4,32,256]{3,2,1,0:T(8,128)(2,1)S(1)}, u32[]{:S(2)}, u32[]{:S(2)}) collective-permute-start(bf16[4,4,32,256]{3,2,1,0:T(8,128)(2,1)S(1)} %pad_maximum_fusion.1.refs_2_), channel_id=1, source_target_pairs={{0,96},{32,0},{64,32},{96,64},{1,97},{33,1},{65,33},{97,65},{2,98}... | collective-permute-start | bytes 786440 | tf_op jit(solution)/shard_map/ppermute | solution.py:49
  36.9 0.1 copy.12
  37.1 0.1 copy.13
  37.2 0.1 copy.14
  37.3 0.1 copy.15
  37.4 3.8 %collective-permute-done.7.refs_2_ = bf16[4,4,32,256]{3,2,1,0:T(8,128)(2,1)S(1)} collective-permute-done((bf16[4,4,32,256]{3,2,1,0:T(8,128)(2,1)S(1)}, bf16[4,4,32,256]{3,2,1,0:T(8,128)(2,1)S(1)}, u32[]{:S(2)}, u32[]{:S(2)}) %collective-permute-start.7) | collective-permute-done | bytes 262176 | tf_op jit(solution)/shard_map/ppermute | solution.py:49
  41.2 0.8 collective-permute-start.11
  42.0 0.1 collective-permute-done.8.refs_3_
  42.1 2.8 %collective-permute-start.12 = (bf16[2,4,32,256]{3,2,1,0:T(8,128)(2,1)S(1)}, bf16[2,4,32,256]{3,2,1,0:T(8,128)(2,1)}, u32[]{:S(2)}, u32[]{:S(2)}) collective-permute-start(bf16[2,4,32,256]{3,2,1,0:T(8,128)(2,1)S(1)} %slice.13), channel_id=1, source_target_pairs={{0,96},{32,0},{64,32},{96,64},{1,97},{33,1},{65,33},{97,65},{2,98}... | collective-permute-start | bytes 393224 | tf_op jit(solution)/shard_map/ppermute | solution.py:49
  44.9 0.1 collective-permute-start.10
  44.9 0.5 collective-permute-start.9
  45.5 0.2 collective-permute-start.6
  45.6 2.1 %collective-permute-done.11.refs_2_ = bf16[2,4,32,256]{3,2,1,0:T(8,128)(2,1)} collective-permute-done((bf16[2,4,32,256]{3,2,1,0:T(8,128)(2,1)S(1)}, bf16[2,4,32,256]{3,2,1,0:T(8,128)(2,1)}, u32[]{:S(2)}, u32[]{:S(2)}) %collective-permute-start.11) | collective-permute-done | bytes 131104 | tf_op jit(solution)/shard_map/ppermute | solution.py:49
  47.8 0.0 collective-permute-start.13
  47.8 0.0 collective-permute-done.12.refs_3_
  47.8 0.5 collective-permute-start.14
  48.3 0.0 all-to-all-done.rows_ref
  48.3 3.6 %shard_map.113 = (bf16[4,512,512]{2,1,0:T(8,128)(2,1)S(1)}, bf16[4,512,512]{2,1,0:T(8,128)(2,1)S(1)}, f32[4,256,512]{2,1,0:T(8,128)}) custom-call(bf16[8,2,4,64,128]{4,3,2,1,0:T(8,128)(2,1)S(1)} %all-to-all-done.rows_ref, f32[1,128]{1,0:T(1,128)S(1)} %bitcast.27, f32[1,128]{1,0:T(1,128)S(1)} %bitcast.30, bf16[128,384]{1,0:T(8,128)(2,1)S(1)} %pad_maximum_fusion.3.w_n_ref, ...), custom_call_target="tpu_custom_call" | custom-call | flops 2147483648 | bytes 8388608 | tf_op jit(solution)/shard_map/pallas_call | solution.py:113
  51.9 1.3 copy-done.8
  53.2 0.0 collective-permute-done.10.refs_5_
  53.2 0.7 copy-done.4
  53.9 0.0 collective-permute-done.9.refs_4_
  53.9 0.7 copy-done.6
  54.6 0.9 copy-done.5
  55.6 0.9 copy-done.7
  56.5 12.7 %shard_map.116 = (f32[4,128,128]{2,1,0:T(8,128)S(1)}, f32[4,128,128]{2,1,0:T(8,128)S(1)}, bf16[4,128,128]{2,1,0:T(8,128)(2,1)S(1)}, bf16[4,128,128]{2,1,0:T(8,12...) custom-call(bf16[4,512,512]{2,1,0:T(8,128)(2,1)S(1)} %get-tuple-elem, ...), custom_call_target="tpu_custom_call" | custom-call | flops 8589934592 | bytes 8388608 | tf_op jit(solution)/shard_map/pallas_call | solution.py:291
  69.2 0.0 collective-permute-start.16
  69.3 0.5 collective-permute-start.18
  69.8 0.0 collective-permute-done.13.refs_4_
  69.8 7.9 %shard_map.117 = (f32[4,128,128]{2,1,0:T(8,128)S(1)}, bf16[4,128,128]{2,1,0:T(8,128)(2,1)S(1)}, bf16[4,512,128]{2,1,0:T(8,128)(2,1)S(1)}, bf16[4,512,128]{2,1,0:...) custom-call(bf16[4,512,512]{2,1,0:T(8,128)(2,1)S(1)} %get-tuple-element.28.refs_0_, ...), custom_call_target="tpu_custom_call" | custom-call | flops 4294967296 | bytes 8388608 | tf_op jit(solution)/shard_map/pallas_call | solution.py:291
  77.7 0.1 collective-permute-start.20
  77.8 7.7 %shard_map.115 = (f32[4,128,128]{2,1,0:T(8,128)S(1)}, bf16[4,128,128]{2,1,0:T(8,128)(2,1)S(1)}, bf16[4,512,128]{2,1,0:T(8,128)(2,1)S(1)}, bf16[4,512,128]{2,1,0:...) custom-call(bf16[4,512,512]{2,1,0:T(8,128)(2,1)S(1)} %get-tuple-element.28.refs_0_, ...), custom_call_target="tpu_custom_call" | custom-call | flops 4294967296 | bytes 8388608 | tf_op jit(solution)/shard_map/pallas_call | solution.py:291
  85.5 0.5 collective-permute-start.15
  85.9 4.4 %shard_map.118 = bf16[8,2,4,64,128]{4,3,2,1,0:T(8,128)(2,1)} custom-call(f32[4,256,512]{2,1,0:T(8,128)} %get-tuple-element.27.refs_0_, bf16[512,128]{1,0:T(8,128)(2,1)S(1)} %pad_maximum_fusion.2.w_t_ref.refs_1_, bf16[128,128]{1,0:T(8,128)(2,1)S(1)} %copy-done.1, f32[4,128,128]{2,1,0:T(8,128)S(1)} %get-tuple-element.30.refs_3_, ...), custom_call_target="tpu_custom_call" | custom-call | flops 2147483648 | bytes 8388608 | tf_op jit(solution)/shard_map/pallas_call | solution.py:356
  90.4 4.3 %all-to-all-start.1 = ((bf16[8,2,4,64,128]{4,3,2,1,0:T(8,128)(2,1)}), bf16[8,2,4,64,128]{4,3,2,1,0:T(8,128)(2,1)S(1)}, u32[]{:S(2)}, u32[]{:S(2)}) async-start(bf16[8,2,4,64,128]{4,3,2,1,0:T(8,128)(2,1)} %shard_map.118), calls=%async_computation.1 | async-start | bytes 2097152 | tf_op jit(solution)/shard_map/all_to_all | solution.py:472
  94.7 1.0 add_convert_fusion.3
  95.7 3.2 %collective-permute-start.17 = (bf16[2,8,32,256]{3,2,1,0:T(8,128)(2,1)S(1)}, bf16[2,8,32,256]{3,2,1,0:T(8,128)(2,1)S(1)}, u32[]{:S(2)}, u32[]{:S(2)}) collective-permute-start(bf16[2,8,32,256]{3,2,1,0:T(8,128)(2,1)S(1)} %add_convert_fusion.3), channel_id=1, source_target_pairs={{0,96},{32,0},{64,32},{96,64},{1,97},{33,1},{65,33},{97,65},{2,98}... | collective-permute-start | bytes 786440 | tf_op jit(solution)/shard_map/ppermute | solution.py:49
  98.9 1.0 add_convert_fusion.2
  100.0 0.1 collective-permute-start.19
  100.1 1.0 add_convert_fusion.1
  101.1 2.0 %collective-permute-start.21 = (bf16[2,8,32,256]{3,2,1,0:T(8,128)(2,1)S(1)}, bf16[2,8,32,256]{3,2,1,0:T(8,128)(2,1)S(1)}, u32[]{:S(2)}, u32[]{:S(2)}) collective-permute-start(bf16[2,8,32,256]{3,2,1,0:T(8,128)(2,1)S(1)} %add_convert_fusion.1), channel_id=1, source_target_pairs={{0,64},{32,96},{64,0},{96,32},{1,65},{33,97},{65,1},{97,33},{2,66}... | collective-permute-start | bytes 786440 | tf_op jit(solution)/shard_map/ppermute | solution.py:49
  103.1 7.4 %collective-permute-done.17 = bf16[2,8,32,256]{3,2,1,0:T(8,128)(2,1)S(1)} collective-permute-done((bf16[2,8,32,256]{3,2,1,0:T(8,128)(2,1)S(1)}, bf16[2,8,32,256]{3,2,1,0:T(8,128)(2,1)S(1)}, u32[]{:S(2)}, u32[]{:S(2)}) %collective-permute-start.17) | collective-permute-done | bytes 262176 | tf_op jit(solution)/shard_map/ppermute | solution.py:49
  110.5 4.5 %collective-permute-done.19 = bf16[2,8,32,256]{3,2,1,0:T(8,128)(2,1)S(1)} collective-permute-done((bf16[2,8,32,256]{3,2,1,0:T(8,128)(2,1)S(1)}, bf16[2,8,32,256]{3,2,1,0:T(8,128)(2,1)S(1)}, u32[]{:S(2)}, u32[]{:S(2)}) %collective-permute-start.19) | collective-permute-done | bytes 262176 | tf_op jit(solution)/shard_map/ppermute | solution.py:49
  115.0 0.9 add_convert_fusion
  115.9 6.1 %all-to-all-start.2 = ((bf16[16,32,256]{2,1,0:T(8,128)(2,1)}), bf16[16,32,256]{2,1,0:T(8,128)(2,1)S(1)}, u32[]{:S(2)}, u32[]{:S(2)}) async-start(bf16[16,32,256]{2,1,0:T(8,128)(2,1)} %bitcast.19), calls=%async_computation.2 | async-start | bytes 524288 | tf_op jit(solution)/shard_map/all_to_all | solution.py:468
  122.0 0.8 slice.14
  122.9 7.8 %all-to-all-done.2.gb_ref = bf16[16,32,256]{2,1,0:T(8,128)(2,1)S(1)} async-done(((bf16[16,32,256]{2,1,0:T(8,128)(2,1)}), bf16[16,32,256]{2,1,0:T(8,128)(2,1)S(1)}, u32[]{:S(2)}, u32[]{:S(2)}) %all-to-all-start.2) | async-done | bytes 262176 | tf_op jit(solution)/shard_map/all_to_all | solution.py:468
  130.7 2.1 %shard_map.119 = f32[32,64,128]{2,1,0:T(8,128)} custom-call(bf16[32,64,128]{2,1,0:T(8,128)(2,1)S(1)} %copy-done, bf16[8,2,4,64,128]{4,3,2,1,0:T(8,128)(2,1)S(1)} %all-to-all-done.1.both_ref, f32[1,128]{1,0:T(1,128)S(1)} %bitcast.28, f32[1,128]{1,0:T(1,128)S(1)} %bitcast.31, bf16[256,128]{1,0:T(8,128)(2,1)S(1)} %bitcast.24, ...), custom_call_target="tpu_custom_call" | custom-call | flops 134217728 | bytes 2097152 | tf_op jit(solution)/shard_map/pallas_call | solution.py:396
  (39 shorter events, 0.2 us)
Async XLA Ops:
  0.6 8.0 %copy-start.13 = (bf16[128,4]{0,1:T(4,128)(2,1)S(1)}, bf16[128,4]{0,1:T(4,128)(2,1)}, u32[]{:S(2)}) copy-start(bf16[128,4]{0,1:T(4,128)(2,1)} %param.18) | copy-start | bytes 3076
  0.6 8.1 %copy-start = (bf16[32,64,128]{2,1,0:T(8,128)(2,1)S(1)}, bf16[32,64,128]{2,1,0:T(8,128)(2,1)}, u32[]{:S(2)}) copy-start(bf16[32,64,128]{2,1,0:T(8,128)(2,1)} %pair_ref.3) | copy-start | bytes 1572868
  0.7 8.1 %copy-start.2 = (f32[128]{0:T(128)S(1)}, f32[128]{0:T(128)}, u32[]{:S(2)}) copy-start(f32[128]{0:T(128)} %param.12) | copy-start | bytes 1540
  0.7 8.1 %copy-start.3 = (f32[128]{0:T(128)S(1)}, f32[128]{0:T(128)}, u32[]{:S(2)}) copy-start(f32[128]{0:T(128)} %param.13) | copy-start | bytes 1540
  3.0 33.9 %copy-start.11 = (bf16[128,128]{1,0:T(8,128)(2,1)S(1)}, bf16[128,128]{1,0:T(8,128)(2,1)}, u32[]{:S(2)}) copy-start(bf16[128,128]{1,0:T(8,128)(2,1)} %param.14) | copy-start | bytes 98308
  3.0 34.0 %copy-start.12 = (bf16[128,128]{1,0:T(8,128)(2,1)S(1)}, bf16[128,128]{1,0:T(8,128)(2,1)}, u32[]{:S(2)}) copy-start(bf16[128,128]{1,0:T(8,128)(2,1)} %param.17) | copy-start | bytes 98308
  3.0 34.2 %copy-start.10 = (bf16[128,128]{1,0:T(8,128)(2,1)S(1)}, bf16[128,128]{1,0:T(8,128)(2,1)}, u32[]{:S(2)}) copy-start(bf16[128,128]{1,0:T(8,128)(2,1)} %param.15) | copy-start | bytes 98308
  3.0 34.3 %copy-start.9 = (bf16[128,128]{1,0:T(8,128)(2,1)S(1)}, bf16[128,128]{1,0:T(8,128)(2,1)}, u32[]{:S(2)}) copy-start(bf16[128,128]{1,0:T(8,128)(2,1)} %param.16) | copy-start | bytes 98308
  3.0 45.3 %copy-start.1 = (bf16[128,128]{1,0:T(8,128)(2,1)S(1)}, bf16[128,128]{1,0:T(8,128)(2,1)}, u32[]{:S(2)}) copy-start(bf16[128,128]{1,0:T(8,128)(2,1)} %refs_2_.1) | copy-start | bytes 98308
  3.0 45.3 %all-to-all-start = ((bf16[8,2,4,64,128]{4,3,2,1,0:T(8,128)(2,1)}), bf16[8,2,4,64,128]{4,3,2,1,0:T(8,128)(2,1)S(1)}, u32[]{:S(2)}, u32[]{:S(2)}) async-start(bf16[8,2,4,64,128]{4,3,2,1,0:T(8,128)(2,1)} %pad_maximum_fusion), calls=%async_computation | async-start | bytes 2097152 | tf_op jit(solution)/shard_map/all_to_all | solution.py:430
  9.7 13.0 %collective-permute-start = (bf16[32,256]{1,0:T(8,128)(2,1)S(1)}, bf16[32,256]{1,0:T(8,128)(2,1)S(1)}, u32[]{:S(2)}, u32[]{:S(2)}) collective-permute-start(bf16[32,256]{1,0:T(8,128)(2,1)S(1)} %shard_map.114), channel_id=1, source_target_pairs={{0,1},{1,0},{16,17},{17,16},{2,3},{3,2},{18,19},{19,18},{4,5},{5,4... | collective-permute-start | bytes 49160 | tf_op jit(solution)/shard_map/ppermute | solution.py:44
  11.8 12.1 %collective-permute-start.1 = (bf16[32,256]{1,0:T(8,128)(2,1)S(1)}, bf16[32,256]{1,0:T(8,128)(2,1)S(1)}, u32[]{:S(2)}, u32[]{:S(2)}) collective-permute-start(bf16[32,256]{1,0:T(8,128)(2,1)S(1)} %shard_map.114), channel_id=1, source_target_pairs={{0,16},{1,17},{16,0},{17,1},{2,18},{3,19},{18,2},{19,3},{4,20},{5,... | collective-permute-start | bytes 49160 | tf_op jit(solution)/shard_map/ppermute | solution.py:44
  14.6 9.4 %collective-permute-start.2 = (bf16[32,256]{1,0:T(8,128)(2,1)S(1)}, bf16[32,256]{1,0:T(8,128)(2,1)S(1)}, u32[]{:S(2)}, u32[]{:S(2)}) collective-permute-start(bf16[32,256]{1,0:T(8,128)(2,1)S(1)} %shard_map.114), channel_id=1, source_target_pairs={{0,17},{1,16},{16,1},{17,0},{2,19},{3,18},{18,3},{19,2},{4,21},{5,... | collective-permute-start | bytes 49160 | tf_op jit(solution)/shard_map/ppermute | solution.py:44
  24.0 5.9 %collective-permute-start.3 = (bf16[4,32,256]{2,1,0:T(8,128)(2,1)S(1)}, bf16[4,32,256]{2,1,0:T(8,128)(2,1)S(1)}, u32[]{:S(2)}, u32[]{:S(2)}) collective-permute-start(bf16[4,32,256]{2,1,0:T(8,128)(2,1)S(1)} %get-tuple-element.53), channel_id=1, source_target_pairs={{0,2},{2,4},{4,6},{6,0},{1,3},{3,5},{5,7},{7,1},{8,10},{10,12},{12... | collective-permute-start | bytes 196616 | tf_op jit(solution)/shard_map/ppermute | solution.py:49
  25.8 5.8 %collective-permute-start.4 = (bf16[4,32,256]{2,1,0:T(8,128)(2,1)S(1)}, bf16[4,32,256]{2,1,0:T(8,128)(2,1)S(1)}, u32[]{:S(2)}, u32[]{:S(2)}) collective-permute-start(bf16[4,32,256]{2,1,0:T(8,128)(2,1)S(1)} %get-tuple-element.53), channel_id=1, source_target_pairs={{0,4},{2,6},{4,0},{6,2},{1,5},{3,7},{5,1},{7,3},{8,12},{10,14},{12... | collective-permute-start | bytes 196616 | tf_op jit(solution)/shard_map/ppermute | solution.py:49
  28.4 4.3 %collective-permute-start.5 = (bf16[4,32,256]{2,1,0:T(8,128)(2,1)S(1)}, bf16[4,32,256]{2,1,0:T(8,128)(2,1)S(1)}, u32[]{:S(2)}, u32[]{:S(2)}) collective-permute-start(bf16[4,32,256]{2,1,0:T(8,128)(2,1)S(1)} %get-tuple-element.53), channel_id=1, source_target_pairs={{0,6},{2,0},{4,2},{6,4},{1,7},{3,1},{5,3},{7,5},{8,14},{10,8},{12,... | collective-permute-start | bytes 196616 | tf_op jit(solution)/shard_map/ppermute | solution.py:49
  32.7 8.5 %collective-permute-start.7 = (bf16[4,4,32,256]{3,2,1,0:T(8,128)(2,1)S(1)}, bf16[4,4,32,256]{3,2,1,0:T(8,128)(2,1)S(1)}, u32[]{:S(2)}, u32[]{:S(2)}) collective-permute-start(bf16[4,4,32,256]{3,2,1,0:T(8,128)(2,1)S(1)} %pad_maximum_fusion.1.refs_2_), channel_id=1, source_target_pairs={{0,32},{32,64},{64,96},{96,0},{1,33},{33,65},{65,97},{97,1},{2,34}... | collective-permute-start | bytes 786440 | tf_op jit(solution)/shard_map/ppermute | solution.py:49
  34.7 7.3 %collective-permute-start.8 = (bf16[4,4,32,256]{3,2,1,0:T(8,128)(2,1)S(1)}, bf16[4,4,32,256]{3,2,1,0:T(8,128)(2,1)S(1)}, u32[]{:S(2)}, u32[]{:S(2)}) collective-permute-start(bf16[4,4,32,256]{3,2,1,0:T(8,128)(2,1)S(1)} %pad_maximum_fusion.1.refs_2_), channel_id=1, source_target_pairs={{0,96},{32,0},{64,32},{96,64},{1,97},{33,1},{65,33},{97,65},{2,98}... | collective-permute-start | bytes 786440 | tf_op jit(solution)/shard_map/ppermute | solution.py:49
  41.2 6.5 %collective-permute-start.11 = (bf16[2,4,32,256]{3,2,1,0:T(8,128)(2,1)S(1)}, bf16[2,4,32,256]{3,2,1,0:T(8,128)(2,1)}, u32[]{:S(2)}, u32[]{:S(2)}) collective-permute-start(bf16[2,4,32,256]{3,2,1,0:T(8,128)(2,1)S(1)} %slice.12), channel_id=1, source_target_pairs={{0,32},{32,64},{64,96},{96,0},{1,33},{33,65},{65,97},{97,1},{2,34}... | collective-permute-start | bytes 393224 | tf_op jit(solution)/shard_map/ppermute | solution.py:49
  42.1 5.7 %collective-permute-start.12 = (bf16[2,4,32,256]{3,2,1,0:T(8,128)(2,1)S(1)}, bf16[2,4,32,256]{3,2,1,0:T(8,128)(2,1)}, u32[]{:S(2)}, u32[]{:S(2)}) collective-permute-start(bf16[2,4,32,256]{3,2,1,0:T(8,128)(2,1)S(1)} %slice.13), channel_id=1, source_target_pairs={{0,96},{32,0},{64,32},{96,64},{1,97},{33,1},{65,33},{97,65},{2,98}... | collective-permute-start | bytes 393224 | tf_op jit(solution)/shard_map/ppermute | solution.py:49
  44.9 8.4 %collective-permute-start.10 = (bf16[4,4,32,256]{3,2,1,0:T(8,128)(2,1)S(1)}, bf16[4,4,32,256]{3,2,1,0:T(8,128)(2,1)S(1)}, u32[]{:S(2)}, u32[]{:S(2)}) collective-permute-start(bf16[4,4,32,256]{3,2,1,0:T(8,128)(2,1)S(1)} %collective-permute-done.8.refs_3_), channel_id=1, source_target_pairs={{0,8},{8,0},{1,9},{9,1},{2,10},{10,2},{3,11},{11,3},{4,12},{12,4},... | collective-permute-start | bytes 786440 | tf_op jit(solution)/shard_map/ppermute | solution.py:40
  44.9 9.0 %collective-permute-start.9 = (bf16[4,4,32,256]{3,2,1,0:T(8,128)(2,1)S(1)}, bf16[4,4,32,256]{3,2,1,0:T(8,128)(2,1)S(1)}, u32[]{:S(2)}, u32[]{:S(2)}) collective-permute-start(bf16[4,4,32,256]{3,2,1,0:T(8,128)(2,1)S(1)} %collective-permute-done.7.refs_2_), channel_id=1, source_target_pairs={{0,8},{8,0},{1,9},{9,1},{2,10},{10,2},{3,11},{11,3},{4,12},{12,4},... | collective-permute-start | bytes 786440 | tf_op jit(solution)/shard_map/ppermute | solution.py:40
  45.5 32.3 %collective-permute-start.6 = (bf16[4,4,32,256]{3,2,1,0:T(8,128)(2,1)S(1)}, bf16[4,4,32,256]{3,2,1,0:T(8,128)(2,1)S(1)}, u32[]{:S(2)}, u32[]{:S(2)}) collective-permute-start(bf16[4,4,32,256]{3,2,1,0:T(8,128)(2,1)S(1)} %pad_maximum_fusion.1.refs_2_), channel_id=1, source_target_pairs={{0,8},{8,0},{1,9},{9,1},{2,10},{10,2},{3,11},{11,3},{4,12},{12,4},... | collective-permute-start | bytes 786440 | tf_op jit(solution)/shard_map/ppermute | solution.py:40
  47.8 22.0 %collective-permute-start.13 = (bf16[2,4,32,256]{3,2,1,0:T(8,128)(2,1)}, bf16[2,4,32,256]{3,2,1,0:T(8,128)(2,1)}, u32[]{:S(2)}, u32[]{:S(2)}) collective-permute-start(bf16[2,4,32,256]{3,2,1,0:T(8,128)(2,1)} %collective-permute-done.11.refs_2_), channel_id=1, source_target_pairs={{0,8},{8,0},{1,9},{9,1},{2,10},{10,2},{3,11},{11,3},{4,12},{12,4},... | collective-permute-start | bytes 393224 | tf_op jit(solution)/shard_map/ppermute | solution.py:40
  47.8 22.0 %collective-permute-start.14 = (bf16[2,4,32,256]{3,2,1,0:T(8,128)(2,1)}, bf16[2,4,32,256]{3,2,1,0:T(8,128)(2,1)}, u32[]{:S(2)}, u32[]{:S(2)}) collective-permute-start(bf16[2,4,32,256]{3,2,1,0:T(8,128)(2,1)} %collective-permute-done.12.refs_3_), channel_id=1, source_target_pairs={{0,8},{8,0},{1,9},{9,1},{2,10},{10,2},{3,11},{11,3},{4,12},{12,4},... | collective-permute-start | bytes 393224 | tf_op jit(solution)/shard_map/ppermute | solution.py:40
  51.9 1.3 copy-start.8
  53.2 0.7 copy-start.4
  53.9 0.7 copy-start.6
  54.6 0.9 copy-start.5
  55.6 0.9 copy-start.7
  69.2 25.5 %collective-permute-start.16 = (bf16[2,8,32,256]{3,2,1,0:T(8,128)(2,1)}, bf16[2,8,32,256]{3,2,1,0:T(8,128)(2,1)}, u32[]{:S(2)}, u32[]{:S(2)}) collective-permute-start(bf16[2,8,32,256]{3,2,1,0:T(8,128)(2,1)} %get-tuple-element.47), channel_id=1, source_target_pairs={{0,8},{8,0},{1,9},{9,1},{2,10},{10,2},{3,11},{11,3},{4,12},{12,4},... | collective-permute-start | bytes 786440 | tf_op jit(solution)/shard_map/ppermute | solution.py:40
  69.3 29.6 %collective-permute-start.18 = (bf16[2,8,32,256]{3,2,1,0:T(8,128)(2,1)}, bf16[2,8,32,256]{3,2,1,0:T(8,128)(2,1)}, u32[]{:S(2)}, u32[]{:S(2)}) collective-permute-start(bf16[2,8,32,256]{3,2,1,0:T(8,128)(2,1)} %get-tuple-element.49), channel_id=1, source_target_pairs={{0,8},{8,0},{1,9},{9,1},{2,10},{10,2},{3,11},{11,3},{4,12},{12,4},... | collective-permute-start | bytes 786440 | tf_op jit(solution)/shard_map/ppermute | solution.py:40
  77.7 22.3 %collective-permute-start.20 = (bf16[2,8,32,256]{3,2,1,0:T(8,128)(2,1)}, bf16[2,8,32,256]{3,2,1,0:T(8,128)(2,1)}, u32[]{:S(2)}, u32[]{:S(2)}) collective-permute-start(bf16[2,8,32,256]{3,2,1,0:T(8,128)(2,1)} %get-tuple-element.51), channel_id=1, source_target_pairs={{0,8},{8,0},{1,9},{9,1},{2,10},{10,2},{3,11},{11,3},{4,12},{12,4},... | collective-permute-start | bytes 786440 | tf_op jit(solution)/shard_map/ppermute | solution.py:40
  85.5 17.6 %collective-permute-start.15 = (bf16[2,8,32,256]{3,2,1,0:T(8,128)(2,1)}, bf16[2,8,32,256]{3,2,1,0:T(8,128)(2,1)S(1)}, u32[]{:S(2)}, u32[]{:S(2)}) collective-permute-start(bf16[2,8,32,256]{3,2,1,0:T(8,128)(2,1)} %get-tuple-element.45), channel_id=1, source_target_pairs={{0,8},{8,0},{1,9},{9,1},{2,10},{10,2},{3,11},{11,3},{4,12},{12,4},... | collective-permute-start | bytes 786440 | tf_op jit(solution)/shard_map/ppermute | solution.py:40
  90.4 25.5 %all-to-all-start.1 = ((bf16[8,2,4,64,128]{4,3,2,1,0:T(8,128)(2,1)}), bf16[8,2,4,64,128]{4,3,2,1,0:T(8,128)(2,1)S(1)}, u32[]{:S(2)}, u32[]{:S(2)}) async-start(bf16[8,2,4,64,128]{4,3,2,1,0:T(8,128)(2,1)} %shard_map.118), calls=%async_computation.1 | async-start | bytes 2097152 | tf_op jit(solution)/shard_map/all_to_all | solution.py:472
  95.7 14.7 %collective-permute-start.17 = (bf16[2,8,32,256]{3,2,1,0:T(8,128)(2,1)S(1)}, bf16[2,8,32,256]{3,2,1,0:T(8,128)(2,1)S(1)}, u32[]{:S(2)}, u32[]{:S(2)}) collective-permute-start(bf16[2,8,32,256]{3,2,1,0:T(8,128)(2,1)S(1)} %add_convert_fusion.3), channel_id=1, source_target_pairs={{0,96},{32,0},{64,32},{96,64},{1,97},{33,1},{65,33},{97,65},{2,98}... | collective-permute-start | bytes 786440 | tf_op jit(solution)/shard_map/ppermute | solution.py:49
  100.0 15.0 %collective-permute-start.19 = (bf16[2,8,32,256]{3,2,1,0:T(8,128)(2,1)S(1)}, bf16[2,8,32,256]{3,2,1,0:T(8,128)(2,1)S(1)}, u32[]{:S(2)}, u32[]{:S(2)}) collective-permute-start(bf16[2,8,32,256]{3,2,1,0:T(8,128)(2,1)S(1)} %add_convert_fusion.2), channel_id=1, source_target_pairs={{0,32},{32,64},{64,96},{96,0},{1,33},{33,65},{65,97},{97,1},{2,34}... | collective-permute-start | bytes 786440 | tf_op jit(solution)/shard_map/ppermute | solution.py:49
  101.1 13.9 %collective-permute-start.21 = (bf16[2,8,32,256]{3,2,1,0:T(8,128)(2,1)S(1)}, bf16[2,8,32,256]{3,2,1,0:T(8,128)(2,1)S(1)}, u32[]{:S(2)}, u32[]{:S(2)}) collective-permute-start(bf16[2,8,32,256]{3,2,1,0:T(8,128)(2,1)S(1)} %add_convert_fusion.1), channel_id=1, source_target_pairs={{0,64},{32,96},{64,0},{96,32},{1,65},{33,97},{65,1},{97,33},{2,66}... | collective-permute-start | bytes 786440 | tf_op jit(solution)/shard_map/ppermute | solution.py:49
  115.9 14.8 %all-to-all-start.2 = ((bf16[16,32,256]{2,1,0:T(8,128)(2,1)}), bf16[16,32,256]{2,1,0:T(8,128)(2,1)S(1)}, u32[]{:S(2)}, u32[]{:S(2)}) async-start(bf16[16,32,256]{2,1,0:T(8,128)(2,1)} %bitcast.19), calls=%async_computation.2 | async-start | bytes 524288 | tf_op jit(solution)/shard_map/all_to_all | solution.py:468

commit v4 on v3

--- a/solution.py
+++ b/solution.py
@@ -58,42 +58,53 @@
     return lax.broadcasted_iota(jnp.int32, (block, width), 0) == lane % block
 
 
-def prep_kernel(pair_ref, gain_ref, shift_ref, w_ref, tile_ref):
+def prep_kernel(pair_ref, cot_ref, gain_ref, shift_ref, w_ref, out_ref):
     rows, block, channels = pair_ref.shape
+    n_ja = out_ref.shape[0]
+    own = rows // n_ja
+    split = (n_ja, own, block, channels)
+    out_ref[:, :own] = pair_ref[...].reshape(split)
+    out_ref[:, own : 2 * own] = cot_ref[...].reshape(split)
     x = pair_ref[...].reshape(rows * block, channels).astype(F32)
     normed = normalize(x, gain_ref[...], shift_ref[...]).astype(BF16)
     every = mm(normed, w_ref[...])
-    keep = line_mask(block, every.shape[1])
+    width = every.shape[1]
+    keep = line_mask(block, width)
     lines = []
     for i in range(rows):
         part = jnp.where(keep, every[i * block : (i + 1) * block], 0.0)
         lines.append(jnp.sum(part, axis=0, keepdims=True))
-    tile_ref[...] = jnp.concatenate(lines, axis=0).astype(BF16)
-
-
-def prep(pair, gain, shift_row, w_spread):
+    tile = jnp.concatenate(lines, axis=0).astype(BF16)
+    tile = jnp.concatenate([tile[:, :LANES], tile[:, LANES:]], axis=0)
+    for d in range(n_ja):
+        out_ref[d, 2 * own] = tile
+
+
+def prep(pair, cot, gain, shift_row, w_spread, n_ja):
+    rows, block, channels = pair.shape
+    out = jax.ShapeDtypeStruct((n_ja, 2 * rows // n_ja + 1, block, channels), BF16)
     return pl.pallas_call(
         prep_kernel,
-        out_shape=jax.ShapeDtypeStruct((pair.shape[0], w_spread.shape[1]), BF16),
+        out_shape=out,
         compiler_params=PARAMS,
         cost_estimate=pl.CostEstimate(
-            flops=2**27, bytes_accessed=2**19, transcendentals=2**12
+            flops=2**27, bytes_accessed=2**21, transcendentals=2**12
         ),
-    )(pair, gain, shift_row, w_spread)
+    )(pair, cot, gain, shift_row, w_spread)
 
 
 def project_kernel(
-    rows_ref, gain_ref, shift_ref, w_n_ref, w_t_ref, w_o_ref, out_n_ref, out_t_ref, out_f_ref
+    pair_ref, cot_ref, gain_ref, shift_ref, w_n_ref, w_t_ref, w_o_ref, out_n_ref, out_t_ref, out_f_ref
 ):
-    n_blocks, _, _, block, channels = rows_ref.shape
+    n_blocks, _, block, channels = pair_ref.shape
     n = n_blocks * block
     inner = w_o_ref.shape[0]
-    x = rows_ref[:, 0].reshape(n, channels).astype(F32)
+    x = pair_ref[...].reshape(n, channels).astype(F32)
     normed = normalize(x, gain_ref[...], shift_ref[...]).astype(BF16)
     out_n_ref[0, :, : 3 * inner] = mm(normed, w_n_ref[...]).astype(BF16)
     proj_t = mm_nt(w_t_ref[...], normed)
     gate = jax.nn.sigmoid(proj_t[inner : 2 * inner])
-    d_gated = mm_nt(w_o_ref[...], rows_ref[:, 1].reshape(n, channels))
+    d_gated = mm_nt(w_o_ref[...], cot_ref[...].reshape(n, channels))
     d_att = (d_gated * gate).astype(BF16)
     out_t_ref[0, :inner] = proj_t[:inner].astype(BF16)
     out_t_ref[0, inner : 3 * inner] = proj_t[2 * inner :].astype(BF16)
@@ -104,7 +115,8 @@
 
 
 def project(both, gain, shift_row, w_n, w_t, w_o):
-    n_blocks, kinds, rows, block, channels = both.shape
+    n_blocks, slabs, block, channels = both.shape
+    rows = slabs // 2
     n = n_blocks * block
     inner = w_o.shape[0]
     out_n = jax.ShapeDtypeStruct((rows, n, 4 * inner), BF16)
@@ -114,7 +126,8 @@
         project_kernel,
         grid=(rows,),
         in_specs=[
-            pl.BlockSpec((n_blocks, kinds, 1, block, channels), lambda i: (0, 0, i, 0, 0))
+            pl.BlockSpec((n_blocks, 1, block, channels), lambda i: (0, i, 0, 0)),
+            pl.BlockSpec((n_blocks, 1, block, channels), lambda i: (0, rows + i, 0, 0)),
         ]
         + [whole(a) for a in (gain, shift_row, w_n, w_t, w_o)],
         out_specs=[
@@ -125,7 +138,7 @@
         cost_estimate=pl.CostEstimate(
             flops=2**31, bytes_accessed=8 * 2**20, transcendentals=2**18
         ),
-    )(both, gain, shift_row, w_n, w_t, w_o)
+    )(both, both, gain, shift_row, w_n, w_t, w_o)
 
 
 def z_lanes(ahead):
@@ -155,8 +168,6 @@
     pairs = heads // 2
     core = lax.axis_index("core")
     xh = lax.axis_index("xh")
-    xl = lax.axis_index("xl")
-    y = lax.axis_index("y")
 
     @pl.when(row == 0)
     def _():
@@ -165,15 +176,17 @@
         for c in range(count):
             for which in range(2):
                 base = which * n_own + c * parts
-                d = 0
+                far = 0
                 for ref in bias_refs[base : base + parts]:
                     for e in range(ref.shape[0]):
-                        for bits in range(4):
-                            owner = lax.rem(y + 4 - d, 4) * 2 + (xl ^ (bits & 1))
-                            at = (xh ^ (bits >> 1)) * 2 + (core ^ which)
-                            at = pl.ds(pl.multiple_of(at * rows_i, rows_i), rows_i)
-                            tile_s[owner, at, :] = ref[e, bits]
-                        d += 1
+                        at = (xh ^ far) * 2 + (core ^ which)
+                        at = pl.ds(pl.multiple_of(at * rows_i, rows_i), rows_i)
+                        for owner in range(n_ja):
+                            for p in range(pairs):
+                                tile_s[owner, at, p * LANES : (p + 1) * LANES] = ref[
+                                    e, owner, p * rows_i : (p + 1) * rows_i, :
+                                ]
+                        far += 1
             for owner in range(n_ja):
                 for p in range(pairs):
                     t = tile_s[owner, :, p * LANES : (p + 1) * LANES].astype(F32).T * LOG2E
@@ -270,19 +283,22 @@
                 for far in range(2):
                     for ref, which in ((mine_refs[c], core), (theirs_refs[c], 1 - core)):
                         at = pl.multiple_of((far * 2 + which) * rows_i, rows_i)
-                        ref[far, owner] = line_s[pl.ds(at, rows_i), :]
+                        for p in range(pairs):
+                            ref[far, owner, p * rows_i : (p + 1) * rows_i, :] = line_s[
+                                pl.ds(at, rows_i), p * LANES : (p + 1) * LANES
+                            ]
 
 
 def attend(heads, aheads, by_n, by_t, own, other):
     rows, n, wide = by_n.shape
     inner = wide // 4
     count = len(aheads)
-    rows_i, lines = own[0].shape[2:]
-    n_ja = n // (lines // heads)
+    n_ja, slab, _ = own[0].shape[1:]
+    lines = heads * n // n_ja
     att = jax.ShapeDtypeStruct((rows, inner, LANES), F32)
     dq = jax.ShapeDtypeStruct((rows, inner, LANES), BF16)
     grad = jax.ShapeDtypeStruct((rows, n, inner), BF16)
-    gb = jax.ShapeDtypeStruct((2, n_ja, rows_i, lines), BF16)
+    gb = jax.ShapeDtypeStruct((2, n_ja, slab, LANES), BF16)
 
     def by_row(a):
         return pl.BlockSpec((1,) + a.shape[1:], lambda i: (i, 0, 0))
@@ -345,9 +361,10 @@
     out_ref[:, 1] = dn.astype(BF16).reshape(half)
 
 
-def finish(like, aheads, by_f, w_t, w_o, att, dq, dk, dv):
-    n_blocks, kinds, rows, block, channels = like.shape
-    inner = w_o.shape[0]
+def finish(block, aheads, by_f, w_t, w_o, att, dq, dk, dv):
+    rows, _, n = by_f.shape
+    inner, channels = w_o.shape
+    n_blocks = n // block
     arrays = (*att, *dq, *dk, *dv)
 
     def by_row(a):
@@ -358,9 +375,9 @@
         grid=(rows,),
         in_specs=[by_row(by_f), whole(w_t), whole(w_o)] + [by_row(a) for a in arrays],
         out_specs=pl.BlockSpec(
-            (n_blocks, kinds, 1, block, channels), lambda i: (0, 0, i, 0, 0)
+            (n_blocks, 2, 1, block, channels), lambda i: (0, 0, i, 0, 0)
         ),
-        out_shape=jax.ShapeDtypeStruct(like.shape, BF16),
+        out_shape=jax.ShapeDtypeStruct((n_blocks, 2, rows, block, channels), BF16),
         scratch_shapes=[
             pltpu.VMEM((inner, n_blocks * block), F32),
             pltpu.VMEM((inner, n_blocks * block), BF16),
@@ -370,9 +387,40 @@
     )(by_f, w_t, w_o, *arrays)
 
 
-def final_kernel(pair_ref, both_ref, gain_ref, shift_ref, w_ref, gb_ref, out_ref):
+def arrange_x_kernel(*refs):
+    ins, outs = refs[:4], refs[4:]
+    xh = lax.axis_index("xh")
+    xl = lax.axis_index("xl")
+    for bits, out in enumerate(outs):
+        for y in range(out.shape[0]):
+            at = (xh ^ (bits >> 1), y * 2 + (xl ^ (bits & 1)))
+            out[y] = sum(ref[at].astype(F32) for ref in ins).astype(BF16)
+
+
+def arrange_y_kernel(*refs):
+    ins, outs = refs[:4], refs[4:]
+    size = ins[0].shape[0]
+    y = lax.axis_index("y")
+    for ahead, out in enumerate(outs):
+        at = lax.rem(y + ahead, size)
+        out[...] = sum(ref[at].astype(F32) for ref in ins).astype(BF16)
+
+
+def arrange(kernel, arrays, shape):
+    out = jax.ShapeDtypeStruct(shape, BF16)
+    return pl.pallas_call(
+        kernel,
+        out_shape=[out] * 4,
+        cost_estimate=pl.CostEstimate(flops=2**18, bytes_accessed=2**20, transcendentals=0),
+    )(*arrays)
+
+
+def final_kernel(
+    pair_ref, both_ref, gain_ref, shift_ref, w_ref, g0_ref, g1_ref, g2_ref, g3_ref, out_ref
+):
     rows, block, channels = pair_ref.shape
-    tile = jnp.sum(gb_ref[...].astype(F32), axis=0).astype(BF16).astype(F32)
+    tile = sum(ref[...].astype(F32) for ref in (g0_ref, g1_ref, g2_ref, g3_ref))
+    tile = jnp.concatenate([tile[:rows], tile[rows:]], axis=1).astype(BF16).astype(F32)
     keep = line_mask(block, tile.shape[1])
     spread = jnp.concatenate(
         [
@@ -400,7 +448,7 @@
         cost_estimate=pl.CostEstimate(
             flops=2**27, bytes_accessed=2**21, transcendentals=2**12
         ),
-    )(pair, both, gain, shift_row, w_spread, gb)
+    )(pair, both, gain, shift_row, w_spread, *gb)
 
 
 def shards(
@@ -425,53 +473,47 @@
     w_n = jnp.concatenate([query_weight, key_weight, value_weight], axis=1)
     w_t = jnp.concatenate([query_weight.T, gate_weight.T, key_weight.T, value_weight.T], axis=0)
 
-    parts = (n_ja, 1, own_i, rows_j, channels)
-    both = jnp.concatenate([pair.reshape(parts), cotangent.reshape(parts)], axis=1)
+    both = prep(pair, cotangent, gain, shift_row, w_spread, n_ja)
     both = lax.all_to_all(both, JA, 0, 0, tiled=True)
 
-    tile = prep(pair, gain, shift_row, w_spread)
-    near = jnp.stack([tile] + [cross(tile, bits) for bits in (1, 2, 3)])
-    near = jnp.stack([near] + [shift(near, "y", d) for d in (1, 2, 3)])
+    near = both[:, 2 * own_i]
+    near = jnp.stack([near, lax.ppermute(near, "xh", [(0, 1), (1, 0)])])
     prev, after = shift(near, "z", 1), shift(near, "z", 3)
-    opp0, opp1 = shift(prev[:2], "z", 1), shift(after[2:], "z", 3)
+    opp0, opp1 = shift(prev[0], "z", 1)[None], shift(after[1], "z", 3)[None]
 
     by_n, by_t, by_f = project(both, gain, shift_row, w_n, w_t, out_weight)
-    att0, dq0, dk0, dv0, mine0, theirs0 = attend(
-        heads, (0,), by_n, by_t, [near], [swap(near)]
+    slices = (
+        (0, [near], [swap(near)]),
+        (3, [prev], [swap(prev)]),
+        (1, [after], [swap(after)]),
+        (2, [opp0, opp1], [swap(opp0), swap(opp1)]),
     )
-    att1, dq1, dk1, dv1, mine1, theirs1 = attend(
-        heads, (3, 1), by_n, by_t, [prev, after], [swap(prev), swap(after)]
-    )
-    att2, dq2, dk2, dv2, mine2, theirs2 = attend(
-        heads, (2,), by_n, by_t, [opp0, opp1], [swap(opp0), swap(opp1)]
-    )
-    done = finish(
-        both,
-        (0, 3, 1, 2),
-        by_f,
-        w_t,
-        out_weight,
-        (*att0, *att1, *att2),
-        (*dq0, *dq1, *dq2),
-        (dk0, dk1, dk2),
-        (dv0, dv1, dv2),
-    )
-
-    def joined(a, b):
-        return (a.astype(F32) + b.astype(F32)).astype(BF16)
-
-    own = joined(mine0[0], swap(theirs0[0]))
-    back = shift(joined(mine1[0], swap(theirs1[0])), "z", 3)
-    ahead = shift(joined(mine1[1], swap(theirs1[1])), "z", 1)
-    opp = shift(joined(mine2[0], swap(theirs2[0])), "z", 2)
-    gb = (own.astype(F32) + back.astype(F32) + ahead.astype(F32) + opp.astype(F32)).astype(BF16)
-    gb = lax.all_to_all(
-        gb.reshape((2 * n_ja,) + gb.shape[2:]), ("xh",) + JA, 0, 0, tiled=True
-    )
-
+    att, dq, dk, dv, total = [], [], [], [], []
+    for ahead, own, other in slices:
+        if dk:
+            own, other, dk[-1] = lax.optimization_barrier((own, other, dk[-1]))
+        att_a, dq_a, dk_a, dv_a, mine, theirs = attend(
+            heads, (ahead,), by_n, by_t, own, other
+        )
+        att += att_a
+        dq += dq_a
+        dk.append(dk_a)
+        dv.append(dv_a)
+        part = (mine[0].astype(F32) + swap(theirs[0]).astype(F32)).astype(BF16)
+        if ahead == 2:
+            part, dk[-1] = lax.optimization_barrier((part, dk[-1]))
+        total.append(shift(part, "z", ahead) if ahead else part)
+    done = finish(rows_j, (0, 3, 1, 2), by_f, w_t, out_weight, att, dq, dk, dv)
     done = lax.all_to_all(done, JA, 0, 0, tiled=True)
+
+    slab = total[0].shape[2:]
+    by_x = arrange(arrange_x_kernel, total, (lax.axis_size("y"),) + slab)
+    by_x = [by_x[0]] + [cross(by_x[bits], bits) for bits in (1, 2, 3)]
+    by_y = arrange(arrange_y_kernel, by_x, slab)
+    by_y = [by_y[0]] + [shift(by_y[d], "y", d) for d in (1, 2, 3)]
+
     update = done[:, 0].reshape(pair.shape)
-    pair_grad = final(pair, done, gain, shift_row, w_spread.T, gb)
+    pair_grad = final(pair, done, gain, shift_row, w_spread.T, by_y)
     return (update, pair_grad)
 
 

time: 134 us -> 133 us (level)
  blocking collectives: 0 us -> 22.6 us
  waiting for transfers between devices: 37.9 us -> 23.7 us
  starting transfers between devices: 42.2 us -> 30.9 us
  other arithmetic: 6.42 us -> 1.06 us
  local copies, waits for them, and re-layouts: 6.11 us -> 9.74 us
  Pallas kernels: 39.5 us -> 43.1 us
    all_to_all x0 -> x1, blocking collectives: none -> 22.6 us  [shards(): both = lax.all_to_all(both, JA, 0, 0, tiled=True)]
    all_to_all x2 -> x0, starting transfers between devices: 11.7 us -> none  [the longest x1 6.12 us: shards(): lax.all_to_all(gb.reshape((2 * n_ja,) + gb.shape[2:]), ('xh',) + JA, 0, 0...]
    all_to_all x2 -> x0, waiting for transfers between devices: 7.84 us -> none  [the longest x1 7.84 us: shards(): lax.all_to_all(gb.reshape((2 * n_ja,) + gb.shape[2:]), ('xh',) + JA, 0, 0...]
    ppermute x10, waiting for transfers between devices: 20.6 us -> 14.1 us  [shift(): return lax.ppermute(a, axis, [(s, (s + by) % size) for s in range(size)])]
    ppermute x3, waiting for transfers between devices: 9.37 us -> 5.33 us  [cross(): return lax.ppermute(a, ('xh', 'xl'), [(s, s ^ bits) for s in range(4)])]
    pallas_call x1 -> x3, Pallas kernels: 0.92 us -> 4.48 us  [the longest x2 3.53 us: arrange(): pl.pallas_call(kernel, out_shape=[out] * 4, cost_estimate=pl.CostEstimate...]
    ppermute x0 -> x1, waiting for transfers between devices: none -> 3.21 us  [shards(): near = jnp.stack([near, lax.ppermute(near, 'xh', [(0, 1), (1, 0)])])]
    convert_element_type x4, other arithmetic: 4.02 us -> 1 us  [shards(): part = (mine[0].astype(F32) + swap(theirs[0]).astype(F32)).astype(BF16)]
  transfers between devices with their start and end apart: 25 -> 24, of which waited for: 10 -> 8; matrix products, arithmetic and copies ran while one was open for 4% -> 2% of each run, Pallas kernels for 28% -> 25%
where the time goes in v4:
time: 133 us; the launch traced here: 132 us
  Pallas kernels  43.1 us (32%)
  starting transfers between devices  30.9 us (23%)
  waiting for transfers between devices  23.7 us (18%)
  blocking collectives  22.6 us (17%)
  local copies, waits for them, and re-layouts  9.74 us (7%)
    pallas_call x4, Pallas kernels, attend(): pl.pallas_call(lambda *refs: attend_kernel(heads, aheads, len(own), *refs...  28.4 us
    all_to_all x1, blocking collectives, shards(): both = lax.all_to_all(both, JA, 0, 0, tiled=True)  22.6 us
    ppermute x10, starting transfers between devices, shift(): return lax.ppermute(a, axis, [(s, (s + by) % size) for s in range(size)])  17.4 us
    ppermute x10, waiting for transfers between devices, shift(): return lax.ppermute(a, axis, [(s, (s + by) % size) for s in range(size)])  14.1 us
    unnamed x44, local copies, waits for them, and re-layouts  8.03 us
    ppermute x3, waiting for transfers between devices, cross(): return lax.ppermute(a, ('xh', 'xl'), [(s, s ^ bits) for s in range(4)])  5.33 us
    ppermute x3, starting transfers between devices, cross(): return lax.ppermute(a, ('xh', 'xl'), [(s, s ^ bits) for s in range(4)])  4.7 us
    pallas_call x1, Pallas kernels, finish(): pl.pallas_call(lambda *refs: finish_kernel(aheads, len(dk), *refs), grid=...  4.48 us
  transfers between devices with their start and end apart: 24, of which 8 were waited for; matrix products, arithmetic and copies ran while one was open for 2% of the time, Pallas kernels for 25%

profile of v4, /device:TPU:0, one launch (start us, length us, event | category | flops | bytes accessed | tf_op | source)
XLA Modules:
  0.0 132.1 jit_solution(18033190099867264850)
XLA Ops:
  0.6 0.7 broadcast_in_dim.9
  1.3 0.1 copy.20.w_ref
  1.4 0.0 copy-start
  1.4 1.0 copy-done
  2.5 1.0 copy-done.2
  3.5 0.7 copy-done.5
  4.2 0.7 copy-done.7
  4.8 1.0 shard_map.113
  5.8 0.0 copy-start.3
  5.8 0.0 copy-start.8
  5.8 22.6 %all_to_all.10.pair_ref.cot_ref = bf16[8,9,64,128]{3,2,1,0:T(8,128)(2,1)S(1)} all-to-all(bf16[8,9,64,128]{3,2,1,0:T(8,128)(2,1)S(1)} %shard_map.113), channel_id=1, replica_groups=mesh['z'=4,'xh'=2,'core'=2,'y'=4,'xl'=2] {'y','xl'}, dimensions={0} | all-to-all | bytes 2359296 | tf_op jit(solution)/shard_map/all_to_all | solution.py:477
  28.5 2.8 %collective-permute-start = (bf16[8,64,128]{2,1,0:T(8,128)(2,1)S(1)}, bf16[8,64,128]{2,1,0:T(8,128)(2,1)S(1)}, u32[]{:S(2)}, u32[]{:S(2)}) collective-permute-start(bf16[8,64,128]{2,1,0:T(8,128)(2,1)S(1)} %get-tuple-element.99), channel_id=1, source_target_pairs={{0,16},{16,0},{1,17},{17,1},{2,18},{18,2},{3,19},{19,3},{4,20},{20... | collective-permute-start | bytes 393224 | tf_op jit(solution)/shard_map/ppermute | solution.py:480
  31.4 0.1 copy.22
  31.5 0.1 copy.21
  31.6 0.1 copy.23
  31.7 0.1 copy.24
  31.9 3.2 %collective-permute-done = bf16[8,64,128]{2,1,0:T(8,128)(2,1)S(1)} collective-permute-done((bf16[8,64,128]{2,1,0:T(8,128)(2,1)S(1)}, bf16[8,64,128]{2,1,0:T(8,128)(2,1)S(1)}, u32[]{:S(2)}, u32[]{:S(2)}) %collective-permute-start) | collective-permute-done | bytes 131104 | tf_op jit(solution)/shard_map/ppermute | solution.py:480
  35.1 4.1 %collective-permute-start.4 = (bf16[2,8,64,128]{3,2,1,0:T(8,128)(2,1)S(1)}, bf16[2,8,64,128]{3,2,1,0:T(8,128)(2,1)S(1)}, u32[]{:S(2)}, u32[]{:S(2)}) collective-permute-start(bf16[2,8,64,128]{3,2,1,0:T(8,128)(2,1)S(1)} %pad_maximum_fusion.refs_2_), channel_id=1, source_target_pairs={{0,96},{32,0},{64,32},{96,64},{1,97},{33,1},{65,33},{97,65},{2,98}... | collective-permute-start | bytes 786440 | tf_op jit(solution)/shard_map/ppermute | solution.py:49
  39.2 0.1 collective-permute-start.2
  39.4 3.6 %shard_map.114 = (bf16[4,512,512]{2,1,0:T(8,128)(2,1)S(1)}, bf16[4,512,512]{2,1,0:T(8,128)(2,1)S(1)}, f32[4,256,512]{2,1,0:T(8,128)}) custom-call(bf16[8,9,64,128]{3,2,1,0:T(8,128)(2,1)S(1)} %all_to_all.10.pair_ref.cot_ref, bf16[8,9,64,128]{3,2,1,0:T(8,128)(2,1)S(1)} %all_to_all.10.pair_ref.cot_ref, f32[1,128]{1,0:T(1,128)S(1)} %bitcast.27, ...), custom_call_target="tpu_custom_call" | custom-call | flops 2147483648 | bytes 8388608 | tf_op jit(solution)/shard_map/pallas_call | solution.py:125
  43.0 1.3 %copy-done.9 = bf16[4,512,512]{2,1,0:T(8,128)(2,1)} copy-done((bf16[4,512,512]{2,1,0:T(8,128)(2,1)}, bf16[4,512,512]{2,1,0:T(8,128)(2,1)S(1)}, u32[]{:S(2)}) %copy-start.9) | copy-done | bytes 2097176
  44.4 3.3 %collective-permute-start.7 = (bf16[8,64,128]{2,1,0:T(8,128)(2,1)S(1)}, bf16[8,64,128]{2,1,0:T(8,128)(2,1)S(1)}, u32[]{:S(2)}, u32[]{:S(2)}) collective-permute-start(bf16[8,64,128]{2,1,0:T(8,128)(2,1)S(1)} %slice_bitcast_fusion), channel_id=1, source_target_pairs={{0,96},{32,0},{64,32},{96,64},{1,97},{33,1},{65,33},{97,65},{2,98}... | collective-permute-start | bytes 393224 | tf_op jit(solution)/shard_map/ppermute | solution.py:49
  47.6 0.1 collective-permute-start.6
  47.7 0.3 collective-permute-start.5
  48.0 0.3 collective-permute-start.3
  48.3 7.1 %shard_map.115 = (f32[4,128,128]{2,1,0:T(8,128)S(1)}, bf16[4,128,128]{2,1,0:T(8,128)(2,1)S(1)}, bf16[4,512,128]{2,1,0:T(8,128)(2,1)S(1)}, bf16[4,512,128]{2,1,0:...) custom-call(bf16[4,512,512]{2,1,0:T(8,128)(2,1)S(1)} %get-tuple-element.51.refs_0_, ...), custom_call_target="tpu_custom_call" | custom-call | flops 4294967296 | bytes 8388608 | tf_op jit(solution)/shard_map/pallas_call | solution.py:307
  55.4 0.3 collective-permute-start.9
  55.7 0.3 collective-permute-start.8
  56.0 7.1 %shard_map.116 = (f32[4,128,128]{2,1,0:T(8,128)S(1)}, bf16[4,128,128]{2,1,0:T(8,128)(2,1)S(1)}, bf16[4,512,128]{2,1,0:T(8,128)(2,1)S(1)}, bf16[4,512,128]{2,1,0:...) custom-call(bf16[4,512,512]{2,1,0:T(8,128)(2,1)S(1)} %get-tuple-element.51.refs_0_, ...), custom_call_target="tpu_custom_call" | custom-call | flops 4294967296 | bytes 8388608 | tf_op jit(solution)/shard_map/pallas_call | solution.py:307
  63.1 7.1 %shard_map.117 = (f32[4,128,128]{2,1,0:T(8,128)S(1)}, bf16[4,128,128]{2,1,0:T(8,128)(2,1)S(1)}, bf16[4,512,128]{2,1,0:T(8,128)(2,1)S(1)}, bf16[4,512,128]{2,1,0:...) custom-call(bf16[4,512,512]{2,1,0:T(8,128)(2,1)S(1)} %get-tuple-element.51.refs_0_, ...), custom_call_target="tpu_custom_call" | custom-call | flops 4294967296 | bytes 8388608 | tf_op jit(solution)/shard_map/pallas_call | solution.py:307
  70.2 7.1 %shard_map.118 = (f32[4,128,128]{2,1,0:T(8,128)S(1)}, bf16[4,128,128]{2,1,0:T(8,128)(2,1)S(1)}, bf16[4,512,128]{2,1,0:T(8,128)(2,1)S(1)}, bf16[4,512,128]{2,1,0:...) custom-call(bf16[4,512,512]{2,1,0:T(8,128)(2,1)S(1)} %get-tuple-element.51.refs_0_, ...), custom_call_target="tpu_custom_call" | custom-call | flops 4294967296 | bytes 8388608 | tf_op jit(solution)/shard_map/pallas_call | solution.py:307
  77.4 0.4 collective-permute-start.10
  77.8 0.2 collective-permute-start.12
  78.0 1.0 collective-permute-done.10
  79.0 0.1 add_convert_fusion.3
  79.1 4.5 %shard_map.119 = bf16[8,2,4,64,128]{4,3,2,1,0:T(8,128)(2,1)} custom-call(f32[4,256,512]{2,1,0:T(8,128)} %get-tuple-element.50.refs_0_, bf16[512,128]{1,0:T(8,128)(2,1)S(1)} %pad_maximum_fusion.1.w_t_ref.refs_1_, bf16[128,128]{1,0:T(8,128)(2,1)S(1)} %copy-done.3, f32[4,128,128]{2,1,0:T(8,128)S(1)} %get-tuple-element.53.refs_3_, ...), custom_call_target="tpu_custom_call" | custom-call | flops 2147483648 | bytes 8388608 | tf_op jit(solution)/shard_map/pallas_call | solution.py:373
  83.5 3.6 %all-to-all-start.1 = ((bf16[8,2,4,64,128]{4,3,2,1,0:T(8,128)(2,1)}), bf16[8,2,4,64,128]{4,3,2,1,0:T(8,128)(2,1)S(1)}, u32[]{:S(2)}, u32[]{:S(2)}) async-start(bf16[8,2,4,64,128]{4,3,2,1,0:T(8,128)(2,1)} %shard_map.119), calls=%async_computation.1 | async-start | bytes 2097152 | tf_op jit(solution)/shard_map/all_to_all | solution.py:507
  87.1 0.4 collective-permute-start.14
  87.5 0.2 collective-permute-start.11
  87.7 0.1 add_convert_fusion.1
  87.8 3.3 %collective-permute-start.13 = (bf16[2,8,64,128]{3,2,1,0:T(8,128)(2,1)S(1)}, bf16[2,8,64,128]{3,2,1,0:T(8,128)(2,1)S(1)}, u32[]{:S(2)}, u32[]{:S(2)}) collective-permute-start(bf16[2,8,64,128]{3,2,1,0:T(8,128)(2,1)S(1)} %add_convert_fusion.1), channel_id=1, source_target_pairs={{0,96},{32,0},{64,32},{96,64},{1,97},{33,1},{65,33},{97,65},{2,98}... | collective-permute-start | bytes 786440 | tf_op jit(solution)/shard_map/ppermute | solution.py:49
  91.1 0.1 add_convert_fusion
  91.2 1.0 collective-permute-start.15
  92.2 0.8 add_convert_fusion.2.refs_0_
  92.9 9.7 %collective-permute-done.13.refs_1_ = bf16[2,8,64,128]{3,2,1,0:T(8,128)(2,1)S(1)} collective-permute-done((bf16[2,8,64,128]{3,2,1,0:T(8,128)(2,1)S(1)}, bf16[2,8,64,128]{3,2,1,0:T(8,128)(2,1)S(1)}, u32[]{:S(2)}, u32[]{:S(2)}) %collective-permute-start.13) | collective-permute-done | bytes 262176 | tf_op jit(solution)/shard_map/ppermute | solution.py:49
  102.6 0.8 copy-done.11
  103.4 2.8 %collective-permute-done.15.refs_2_ = bf16[2,8,64,128]{3,2,1,0:T(8,128)(2,1)S(1)} collective-permute-done((bf16[2,8,64,128]{3,2,1,0:T(8,128)(2,1)S(1)}, bf16[2,8,64,128]{3,2,1,0:T(8,128)(2,1)S(1)}, u32[]{:S(2)}, u32[]{:S(2)}) %collective-permute-start.15) | collective-permute-done | bytes 262176 | tf_op jit(solution)/shard_map/ppermute | solution.py:49
  106.2 0.7 copy-done.12
  106.9 1.9 %shard_map.120 = (bf16[4,64,128]{2,1,0:T(8,128)(2,1)}, bf16[4,64,128]{2,1,0:T(8,128)(2,1)}, bf16[4,64,128]{2,1,0:T(8,128)(2,1)}, bf16[4,64,128]{2,1,0:T(8,128)(2,1)}) custom-call(bf16[2,8,64,128]{3,2,1,0:T(8,128)(2,1)} %add_convert_fusion.2.refs_0_, bf16[2,8,64,128]{3,2,1,0:T(8,128)(2,1)} %copy-done.10, bf16[2,8,64,128]{3,2,1,0:T(8,128)(2,1)} %copy-done.12, ...), custom_call_target="tpu_custom_call" | custom-call | flops 262144 | bytes 1048576 | tf_op jit(solution)/shard_map/pallas_call | solution.py:411
  108.9 1.6 %collective-permute-start.17 = (bf16[4,64,128]{2,1,0:T(8,128)(2,1)}, bf16[4,64,128]{2,1,0:T(8,128)(2,1)S(1)}, u32[]{:S(2)}, u32[]{:S(2)}) collective-permute-start(bf16[4,64,128]{2,1,0:T(8,128)(2,1)} %get-tuple-element.91), channel_id=1, source_target_pairs={{0,1},{1,0},{16,17},{17,16},{2,3},{3,2},{18,19},{19,18},{4,5},{5,4... | collective-permute-start | bytes 196616 | tf_op jit(solution)/shard_map/ppermute | solution.py:44
  110.5 2.7 %collective-permute-start.18 = (bf16[4,64,128]{2,1,0:T(8,128)(2,1)}, bf16[4,64,128]{2,1,0:T(8,128)(2,1)S(1)}, u32[]{:S(2)}, u32[]{:S(2)}) collective-permute-start(bf16[4,64,128]{2,1,0:T(8,128)(2,1)} %get-tuple-element.92), channel_id=1, source_target_pairs={{0,16},{1,17},{16,0},{17,1},{2,18},{3,19},{18,2},{19,3},{4,20},{5,... | collective-permute-start | bytes 196616 | tf_op jit(solution)/shard_map/ppermute | solution.py:44
  113.2 0.4 collective-permute-start.19
  113.6 3.1 %collective-permute-done.18.refs_2_ = bf16[4,64,128]{2,1,0:T(8,128)(2,1)S(1)} collective-permute-done((bf16[4,64,128]{2,1,0:T(8,128)(2,1)}, bf16[4,64,128]{2,1,0:T(8,128)(2,1)S(1)}, u32[]{:S(2)}, u32[]{:S(2)}) %collective-permute-start.18) | collective-permute-done | bytes 65568 | tf_op jit(solution)/shard_map/ppermute | solution.py:44
  116.7 2.2 %collective-permute-done.19.refs_3_ = bf16[4,64,128]{2,1,0:T(8,128)(2,1)S(1)} collective-permute-done((bf16[4,64,128]{2,1,0:T(8,128)(2,1)}, bf16[4,64,128]{2,1,0:T(8,128)(2,1)S(1)}, u32[]{:S(2)}, u32[]{:S(2)}) %collective-permute-start.19) | collective-permute-done | bytes 65568 | tf_op jit(solution)/shard_map/ppermute | solution.py:44
  118.9 0.6 copy-done.18
  119.5 1.6 %shard_map.121 = (bf16[64,128]{1,0:T(8,128)(2,1)}, bf16[64,128]{1,0:T(8,128)(2,1)}, bf16[64,128]{1,0:T(8,128)(2,1)}, bf16[64,128]{1,0:T(8,128)(2,1)}) custom-call(bf16[4,64,128]{2,1,0:T(8,128)(2,1)} %get-tuple-element.90.refs_0_, bf16[4,64,128]{2,1,0:T(8,128)(2,1)} %copy-done.16, bf16[4,64,128]{2,1,0:T(8,128)(2,1)} %copy-done.17, bf16[4,64,128]{2,1,0:T(8,128)(2,1)} %copy-done.18), custom_call_target="tpu_custom_call" | custom-call | flops 262144 | bytes 1048576 | tf_op jit(solution)/shard_map/pallas_call | solution.py:411
  121.1 1.5 %collective-permute-start.20 = (bf16[64,128]{1,0:T(8,128)(2,1)}, bf16[64,128]{1,0:T(8,128)(2,1)S(1)}, u32[]{:S(2)}, u32[]{:S(2)}) collective-permute-start(bf16[64,128]{1,0:T(8,128)(2,1)} %get-tuple-element.95), channel_id=1, source_target_pairs={{0,2},{2,4},{4,6},{6,0},{1,3},{3,5},{5,7},{7,1},{8,10},{10,12},{12... | collective-permute-start | bytes 49160 | tf_op jit(solution)/shard_map/ppermute | solution.py:49
  122.6 2.7 %collective-permute-start.21 = (bf16[64,128]{1,0:T(8,128)(2,1)}, bf16[64,128]{1,0:T(8,128)(2,1)S(1)}, u32[]{:S(2)}, u32[]{:S(2)}) collective-permute-start(bf16[64,128]{1,0:T(8,128)(2,1)} %get-tuple-element.96), channel_id=1, source_target_pairs={{0,4},{2,6},{4,0},{6,2},{1,5},{3,7},{5,1},{7,3},{8,12},{10,14},{12... | collective-permute-start | bytes 49160 | tf_op jit(solution)/shard_map/ppermute | solution.py:49
  125.3 1.4 %collective-permute-start.22 = (bf16[64,128]{1,0:T(8,128)(2,1)}, bf16[64,128]{1,0:T(8,128)(2,1)S(1)}, u32[]{:S(2)}, u32[]{:S(2)}) collective-permute-start(bf16[64,128]{1,0:T(8,128)(2,1)} %get-tuple-element.97), channel_id=1, source_target_pairs={{0,6},{2,0},{4,2},{6,4},{1,7},{3,1},{5,3},{7,5},{8,14},{10,8},{12,... | collective-permute-start | bytes 49160 | tf_op jit(solution)/shard_map/ppermute | solution.py:49
  126.7 0.8 slice.19
  127.6 0.4 collective-permute-done.21.g2_ref
  128.0 1.2 collective-permute-done.22.g3_ref
  129.2 0.7 copy-done.4
  130.0 2.2 %shard_map.122 = f32[32,64,128]{2,1,0:T(8,128)} custom-call(bf16[32,64,128]{2,1,0:T(8,128)(2,1)S(1)} %copy-done.1, bf16[8,2,4,64,128]{4,3,2,1,0:T(8,128)(2,1)S(1)} %all-to-all-done.1.both_ref, f32[1,128]{1,0:T(1,128)S(1)} %bitcast.28, f32[1,128]{1,0:T(1,128)S(1)} %bitcast.31, bf16[256,128]{1,0:T(8,128)(2,1)S(1)} %bitcast.25, bf16[64,128]{1,0:T(8,128)(2,1)S(1)} %copy-done.4, ...), custom_call_target="tpu_custom_call" | custom-call | flops 134217728 | bytes 2097152 | tf_op jit(solution)/shard_map/pallas_call | solution.py:444
  (52 shorter events, 0.2 us)
Async XLA Ops:
  1.4 1.0 copy-start
  2.5 1.0 copy-start.2
  3.5 0.7 copy-start.5
  4.2 0.7 copy-start.7
  4.8 26.5 %copy-start.19 = (bf16[128,128]{1,0:T(8,128)(2,1)S(1)}, bf16[128,128]{1,0:T(8,128)(2,1)}, u32[]{:S(2)}) copy-start(bf16[128,128]{1,0:T(8,128)(2,1)} %param.17) | copy-start | bytes 98308
  4.8 26.6 %copy-start.15 = (bf16[128,128]{1,0:T(8,128)(2,1)S(1)}, bf16[128,128]{1,0:T(8,128)(2,1)}, u32[]{:S(2)}) copy-start(bf16[128,128]{1,0:T(8,128)(2,1)} %param.14) | copy-start | bytes 98308
  4.8 26.8 %copy-start.14 = (bf16[128,128]{1,0:T(8,128)(2,1)S(1)}, bf16[128,128]{1,0:T(8,128)(2,1)}, u32[]{:S(2)}) copy-start(bf16[128,128]{1,0:T(8,128)(2,1)} %param.15) | copy-start | bytes 98308
  4.8 26.9 %copy-start.13 = (bf16[128,128]{1,0:T(8,128)(2,1)S(1)}, bf16[128,128]{1,0:T(8,128)(2,1)}, u32[]{:S(2)}) copy-start(bf16[128,128]{1,0:T(8,128)(2,1)} %param.16) | copy-start | bytes 98308
  5.8 33.5 %copy-start.3 = (bf16[128,128]{1,0:T(8,128)(2,1)S(1)}, bf16[128,128]{1,0:T(8,128)(2,1)}, u32[]{:S(2)}) copy-start(bf16[128,128]{1,0:T(8,128)(2,1)} %refs_2_.1) | copy-start | bytes 98308
  5.8 33.5 %copy-start.6 = (f32[128]{0:T(128)S(1)}, f32[128]{0:T(128)}, u32[]{:S(2)}) copy-start(f32[128]{0:T(128)} %param.12) | copy-start | bytes 1540
  5.8 33.5 %copy-start.8 = (f32[128]{0:T(128)S(1)}, f32[128]{0:T(128)}, u32[]{:S(2)}) copy-start(f32[128]{0:T(128)} %param.13) | copy-start | bytes 1540
  28.5 6.6 %collective-permute-start = (bf16[8,64,128]{2,1,0:T(8,128)(2,1)S(1)}, bf16[8,64,128]{2,1,0:T(8,128)(2,1)S(1)}, u32[]{:S(2)}, u32[]{:S(2)}) collective-permute-start(bf16[8,64,128]{2,1,0:T(8,128)(2,1)S(1)} %get-tuple-element.99), channel_id=1, source_target_pairs={{0,16},{16,0},{1,17},{17,1},{2,18},{18,2},{3,19},{19,3},{4,20},{20... | collective-permute-start | bytes 393224 | tf_op jit(solution)/shard_map/ppermute | solution.py:480
  35.1 9.2 %collective-permute-start.4 = (bf16[2,8,64,128]{3,2,1,0:T(8,128)(2,1)S(1)}, bf16[2,8,64,128]{3,2,1,0:T(8,128)(2,1)S(1)}, u32[]{:S(2)}, u32[]{:S(2)}) collective-permute-start(bf16[2,8,64,128]{3,2,1,0:T(8,128)(2,1)S(1)} %pad_maximum_fusion.refs_2_), channel_id=1, source_target_pairs={{0,96},{32,0},{64,32},{96,64},{1,97},{33,1},{65,33},{97,65},{2,98}... | collective-permute-start | bytes 786440 | tf_op jit(solution)/shard_map/ppermute | solution.py:49
  39.2 8.4 %collective-permute-start.2 = (bf16[2,8,64,128]{3,2,1,0:T(8,128)(2,1)S(1)}, bf16[2,8,64,128]{3,2,1,0:T(8,128)(2,1)S(1)}, u32[]{:S(2)}, u32[]{:S(2)}) collective-permute-start(bf16[2,8,64,128]{3,2,1,0:T(8,128)(2,1)S(1)} %pad_maximum_fusion.refs_2_), channel_id=1, source_target_pairs={{0,32},{32,64},{64,96},{96,0},{1,33},{33,65},{65,97},{97,1},{2,34}... | collective-permute-start | bytes 786440 | tf_op jit(solution)/shard_map/ppermute | solution.py:49
  43.0 1.3 %copy-start.9 = (bf16[4,512,512]{2,1,0:T(8,128)(2,1)}, bf16[4,512,512]{2,1,0:T(8,128)(2,1)S(1)}, u32[]{:S(2)}) copy-start(bf16[4,512,512]{2,1,0:T(8,128)(2,1)S(1)} %get-tuple-element.52.refs_1_) | copy-start | bytes 6291460
  44.3 4.0 %collective-permute-start.1 = (bf16[2,8,64,128]{3,2,1,0:T(8,128)(2,1)S(1)}, bf16[2,8,64,128]{3,2,1,0:T(8,128)(2,1)S(1)}, u32[]{:S(2)}, u32[]{:S(2)}) collective-permute-start(bf16[2,8,64,128]{3,2,1,0:T(8,128)(2,1)S(1)} %pad_maximum_fusion.refs_2_), channel_id=1, source_target_pairs={{0,8},{8,0},{1,9},{9,1},{2,10},{10,2},{3,11},{11,3},{4,12},{12,4},... | collective-permute-start | bytes 786440 | tf_op jit(solution)/shard_map/ppermute | solution.py:40
  44.4 11.0 %collective-permute-start.7 = (bf16[8,64,128]{2,1,0:T(8,128)(2,1)S(1)}, bf16[8,64,128]{2,1,0:T(8,128)(2,1)S(1)}, u32[]{:S(2)}, u32[]{:S(2)}) collective-permute-start(bf16[8,64,128]{2,1,0:T(8,128)(2,1)S(1)} %slice_bitcast_fusion), channel_id=1, source_target_pairs={{0,96},{32,0},{64,32},{96,64},{1,97},{33,1},{65,33},{97,65},{2,98}... | collective-permute-start | bytes 393224 | tf_op jit(solution)/shard_map/ppermute | solution.py:49
  47.6 8.1 %collective-permute-start.6 = (bf16[8,64,128]{2,1,0:T(8,128)(2,1)S(1)}, bf16[8,64,128]{2,1,0:T(8,128)(2,1)S(1)}, u32[]{:S(2)}, u32[]{:S(2)}) collective-permute-start(bf16[8,64,128]{2,1,0:T(8,128)(2,1)S(1)} %slice_bitcast_fusion.1), channel_id=1, source_target_pairs={{0,32},{32,64},{64,96},{96,0},{1,33},{33,65},{65,97},{97,1},{2,34}... | collective-permute-start | bytes 393224 | tf_op jit(solution)/shard_map/ppermute | solution.py:49
  47.7 15.4 %collective-permute-start.5 = (bf16[2,8,64,128]{3,2,1,0:T(8,128)(2,1)S(1)}, bf16[2,8,64,128]{3,2,1,0:T(8,128)(2,1)S(1)}, u32[]{:S(2)}, u32[]{:S(2)}) collective-permute-start(bf16[2,8,64,128]{3,2,1,0:T(8,128)(2,1)S(1)} %collective-permute-done.4.refs_2_), channel_id=1, source_target_pairs={{0,8},{8,0},{1,9},{9,1},{2,10},{10,2},{3,11},{11,3},{4,12},{12,4},... | collective-permute-start | bytes 786440 | tf_op jit(solution)/shard_map/ppermute | solution.py:40
  48.0 8.0 %collective-permute-start.3 = (bf16[2,8,64,128]{3,2,1,0:T(8,128)(2,1)S(1)}, bf16[2,8,64,128]{3,2,1,0:T(8,128)(2,1)S(1)}, u32[]{:S(2)}, u32[]{:S(2)}) collective-permute-start(bf16[2,8,64,128]{3,2,1,0:T(8,128)(2,1)S(1)} %collective-permute-done.2.refs_2_), channel_id=1, source_target_pairs={{0,8},{8,0},{1,9},{9,1},{2,10},{10,2},{3,11},{11,3},{4,12},{12,4},... | collective-permute-start | bytes 786440 | tf_op jit(solution)/shard_map/ppermute | solution.py:40
  55.4 14.8 %collective-permute-start.9 = (bf16[1,8,64,128]{3,2,1,0:T(8,128)(2,1)S(1)}, bf16[1,8,64,128]{3,2,1,0:T(8,128)(2,1)S(1)}, u32[]{:S(2)}, u32[]{:S(2)}) collective-permute-start(bf16[1,8,64,128]{3,2,1,0:T(8,128)(2,1)S(1)} %bitcast.32), channel_id=1, source_target_pairs={{0,8},{8,0},{1,9},{9,1},{2,10},{10,2},{3,11},{11,3},{4,12},{12,4},... | collective-permute-start | bytes 393224 | tf_op jit(solution)/shard_map/ppermute | solution.py:40
  55.7 14.5 %collective-permute-start.8 = (bf16[1,8,64,128]{3,2,1,0:T(8,128)(2,1)S(1)}, bf16[1,8,64,128]{3,2,1,0:T(8,128)(2,1)S(1)}, u32[]{:S(2)}, u32[]{:S(2)}) collective-permute-start(bf16[1,8,64,128]{3,2,1,0:T(8,128)(2,1)S(1)} %bitcast.34), channel_id=1, source_target_pairs={{0,8},{8,0},{1,9},{9,1},{2,10},{10,2},{3,11},{11,3},{4,12},{12,4},... | collective-permute-start | bytes 393224 | tf_op jit(solution)/shard_map/ppermute | solution.py:40
  77.4 1.6 %collective-permute-start.10 = (bf16[2,8,64,128]{3,2,1,0:T(8,128)(2,1)S(1)}, bf16[2,8,64,128]{3,2,1,0:T(8,128)(2,1)S(1)}, u32[]{:S(2)}, u32[]{:S(2)}) collective-permute-start(bf16[2,8,64,128]{3,2,1,0:T(8,128)(2,1)S(1)} %get-tuple-element.76), channel_id=1, source_target_pairs={{0,8},{8,0},{1,9},{9,1},{2,10},{10,2},{3,11},{11,3},{4,12},{12,4},... | collective-permute-start | bytes 786440 | tf_op jit(solution)/shard_map/ppermute | solution.py:40
  77.8 10.0 %collective-permute-start.12 = (bf16[2,8,64,128]{3,2,1,0:T(8,128)(2,1)S(1)}, bf16[2,8,64,128]{3,2,1,0:T(8,128)(2,1)S(1)}, u32[]{:S(2)}, u32[]{:S(2)}) collective-permute-start(bf16[2,8,64,128]{3,2,1,0:T(8,128)(2,1)S(1)} %get-tuple-element.86), channel_id=1, source_target_pairs={{0,8},{8,0},{1,9},{9,1},{2,10},{10,2},{3,11},{11,3},{4,12},{12,4},... | collective-permute-start | bytes 786440 | tf_op jit(solution)/shard_map/ppermute | solution.py:40
  83.5 43.2 %all-to-all-start.1 = ((bf16[8,2,4,64,128]{4,3,2,1,0:T(8,128)(2,1)}), bf16[8,2,4,64,128]{4,3,2,1,0:T(8,128)(2,1)S(1)}, u32[]{:S(2)}, u32[]{:S(2)}) async-start(bf16[8,2,4,64,128]{4,3,2,1,0:T(8,128)(2,1)} %shard_map.119), calls=%async_computation.1 | async-start | bytes 2097152 | tf_op jit(solution)/shard_map/all_to_all | solution.py:507
  87.1 4.0 %collective-permute-start.14 = (bf16[2,8,64,128]{3,2,1,0:T(8,128)(2,1)S(1)}, bf16[2,8,64,128]{3,2,1,0:T(8,128)(2,1)S(1)}, u32[]{:S(2)}, u32[]{:S(2)}) collective-permute-start(bf16[2,8,64,128]{3,2,1,0:T(8,128)(2,1)S(1)} %get-tuple-element.88), channel_id=1, source_target_pairs={{0,8},{8,0},{1,9},{9,1},{2,10},{10,2},{3,11},{11,3},{4,12},{12,4},... | collective-permute-start | bytes 786440 | tf_op jit(solution)/shard_map/ppermute | solution.py:40
  87.5 4.7 %collective-permute-start.11 = (bf16[2,8,64,128]{3,2,1,0:T(8,128)(2,1)S(1)}, bf16[2,8,64,128]{3,2,1,0:T(8,128)(2,1)S(1)}, u32[]{:S(2)}, u32[]{:S(2)}) collective-permute-start(bf16[2,8,64,128]{3,2,1,0:T(8,128)(2,1)S(1)} %get-tuple-element.84), channel_id=1, source_target_pairs={{0,8},{8,0},{1,9},{9,1},{2,10},{10,2},{3,11},{11,3},{4,12},{12,4},... | collective-permute-start | bytes 786440 | tf_op jit(solution)/shard_map/ppermute | solution.py:40
  87.8 41.4 %copy-start.1 = (bf16[32,64,128]{2,1,0:T(8,128)(2,1)S(1)}, bf16[32,64,128]{2,1,0:T(8,128)(2,1)}, u32[]{:S(2)}) copy-start(bf16[32,64,128]{2,1,0:T(8,128)(2,1)} %pair_ref.3) | copy-start | bytes 1572868
  87.8 14.8 %collective-permute-start.13 = (bf16[2,8,64,128]{3,2,1,0:T(8,128)(2,1)S(1)}, bf16[2,8,64,128]{3,2,1,0:T(8,128)(2,1)S(1)}, u32[]{:S(2)}, u32[]{:S(2)}) collective-permute-start(bf16[2,8,64,128]{3,2,1,0:T(8,128)(2,1)S(1)} %add_convert_fusion.1), channel_id=1, source_target_pairs={{0,96},{32,0},{64,32},{96,64},{1,97},{33,1},{65,33},{97,65},{2,98}... | collective-permute-start | bytes 786440 | tf_op jit(solution)/shard_map/ppermute | solution.py:49
  91.1 11.6 %collective-permute-start.16 = (bf16[2,8,64,128]{3,2,1,0:T(8,128)(2,1)S(1)}, bf16[2,8,64,128]{3,2,1,0:T(8,128)(2,1)S(1)}, u32[]{:S(2)}, u32[]{:S(2)}) collective-permute-start(bf16[2,8,64,128]{3,2,1,0:T(8,128)(2,1)S(1)} %add_convert_fusion.3), channel_id=1, source_target_pairs={{0,64},{32,96},{64,0},{96,32},{1,65},{33,97},{65,1},{97,33},{2,66}... | collective-permute-start | bytes 786440 | tf_op jit(solution)/shard_map/ppermute | solution.py:49
  91.2 15.1 %collective-permute-start.15 = (bf16[2,8,64,128]{3,2,1,0:T(8,128)(2,1)S(1)}, bf16[2,8,64,128]{3,2,1,0:T(8,128)(2,1)S(1)}, u32[]{:S(2)}, u32[]{:S(2)}) collective-permute-start(bf16[2,8,64,128]{3,2,1,0:T(8,128)(2,1)S(1)} %add_convert_fusion), channel_id=1, source_target_pairs={{0,32},{32,64},{64,96},{96,0},{1,33},{33,65},{65,97},{97,1},{2,34}... | collective-permute-start | bytes 786440 | tf_op jit(solution)/shard_map/ppermute | solution.py:49
  102.6 3.6 %copy-start.10 = (bf16[2,8,64,128]{3,2,1,0:T(8,128)(2,1)}, bf16[2,8,64,128]{3,2,1,0:T(8,128)(2,1)S(1)}, u32[]{:S(2)}) copy-start(bf16[2,8,64,128]{3,2,1,0:T(8,128)(2,1)S(1)} %collective-permute-done.13.refs_1_) | copy-start | bytes 786436
  102.6 0.8 copy-start.11
  106.2 0.7 copy-start.12
  108.9 4.7 %collective-permute-start.17 = (bf16[4,64,128]{2,1,0:T(8,128)(2,1)}, bf16[4,64,128]{2,1,0:T(8,128)(2,1)S(1)}, u32[]{:S(2)}, u32[]{:S(2)}) collective-permute-start(bf16[4,64,128]{2,1,0:T(8,128)(2,1)} %get-tuple-element.91), channel_id=1, source_target_pairs={{0,1},{1,0},{16,17},{17,16},{2,3},{3,2},{18,19},{19,18},{4,5},{5,4... | collective-permute-start | bytes 196616 | tf_op jit(solution)/shard_map/ppermute | solution.py:44
  110.5 6.2 %collective-permute-start.18 = (bf16[4,64,128]{2,1,0:T(8,128)(2,1)}, bf16[4,64,128]{2,1,0:T(8,128)(2,1)S(1)}, u32[]{:S(2)}, u32[]{:S(2)}) collective-permute-start(bf16[4,64,128]{2,1,0:T(8,128)(2,1)} %get-tuple-element.92), channel_id=1, source_target_pairs={{0,16},{1,17},{16,0},{17,1},{2,18},{3,19},{18,2},{19,3},{4,20},{5,... | collective-permute-start | bytes 196616 | tf_op jit(solution)/shard_map/ppermute | solution.py:44
  113.2 5.7 %collective-permute-start.19 = (bf16[4,64,128]{2,1,0:T(8,128)(2,1)}, bf16[4,64,128]{2,1,0:T(8,128)(2,1)S(1)}, u32[]{:S(2)}, u32[]{:S(2)}) collective-permute-start(bf16[4,64,128]{2,1,0:T(8,128)(2,1)} %get-tuple-element.93), channel_id=1, source_target_pairs={{0,17},{1,16},{16,1},{17,0},{2,19},{3,18},{18,3},{19,2},{4,21},{5,... | collective-permute-start | bytes 196616 | tf_op jit(solution)/shard_map/ppermute | solution.py:44
  113.6 5.3 %copy-start.16 = (bf16[4,64,128]{2,1,0:T(8,128)(2,1)}, bf16[4,64,128]{2,1,0:T(8,128)(2,1)S(1)}, u32[]{:S(2)}) copy-start(bf16[4,64,128]{2,1,0:T(8,128)(2,1)S(1)} %collective-permute-done.17.refs_1_) | copy-start | bytes 196612
  116.7 2.2 %copy-start.17 = (bf16[4,64,128]{2,1,0:T(8,128)(2,1)}, bf16[4,64,128]{2,1,0:T(8,128)(2,1)S(1)}, u32[]{:S(2)}) copy-start(bf16[4,64,128]{2,1,0:T(8,128)(2,1)S(1)} %collective-permute-done.18.refs_2_) | copy-start | bytes 196612
  118.9 0.6 copy-start.18
  121.1 6.5 %collective-permute-start.20 = (bf16[64,128]{1,0:T(8,128)(2,1)}, bf16[64,128]{1,0:T(8,128)(2,1)S(1)}, u32[]{:S(2)}, u32[]{:S(2)}) collective-permute-start(bf16[64,128]{1,0:T(8,128)(2,1)} %get-tuple-element.95), channel_id=1, source_target_pairs={{0,2},{2,4},{4,6},{6,0},{1,3},{3,5},{5,7},{7,1},{8,10},{10,12},{12... | collective-permute-start | bytes 49160 | tf_op jit(solution)/shard_map/ppermute | solution.py:49
  122.6 5.5 %collective-permute-start.21 = (bf16[64,128]{1,0:T(8,128)(2,1)}, bf16[64,128]{1,0:T(8,128)(2,1)S(1)}, u32[]{:S(2)}, u32[]{:S(2)}) collective-permute-start(bf16[64,128]{1,0:T(8,128)(2,1)} %get-tuple-element.96), channel_id=1, source_target_pairs={{0,4},{2,6},{4,0},{6,2},{1,5},{3,7},{5,1},{7,3},{8,12},{10,14},{12... | collective-permute-start | bytes 49160 | tf_op jit(solution)/shard_map/ppermute | solution.py:49
  125.3 3.9 %collective-permute-start.22 = (bf16[64,128]{1,0:T(8,128)(2,1)}, bf16[64,128]{1,0:T(8,128)(2,1)S(1)}, u32[]{:S(2)}, u32[]{:S(2)}) collective-permute-start(bf16[64,128]{1,0:T(8,128)(2,1)} %get-tuple-element.97), channel_id=1, source_target_pairs={{0,6},{2,0},{4,2},{6,4},{1,7},{3,1},{5,3},{7,5},{8,14},{10,8},{12,... | collective-permute-start | bytes 49160 | tf_op jit(solution)/shard_map/ppermute | solution.py:49
  129.2 0.7 copy-start.4

commit v5 on v4

v5 whole, which is shorter than its diff:
```python
import math

import jax
import jax.numpy as jnp
from jax import lax
from jax.experimental import pallas as pl
from jax.experimental.pallas import tpu as pltpu
from jax.sharding import Mesh, PartitionSpec as P

EPSILON = 1e-05
LOG2E = math.log2(math.e)
IA = ("z", "xh", "core")
JA = ("y", "xl")
F32 = jnp.float32
BF16 = jnp.bfloat16
LANES = 128
PARAMS = pltpu.CompilerParams(vmem_limit_bytes=48 * 1024 * 1024)


def normalize(values, norm_gain, norm_shift):
    mean_val = jnp.mean(values, axis=-1, keepdims=True)
    centred = values - mean_val
    variance = jnp.mean(centred * centred, axis=-1, keepdims=True)
    return centred * lax.rsqrt(variance + EPSILON) * norm_gain + norm_shift


def mm(a, b):
    return lax.dot_general(a, b, (((1,), (0,)), ((), ())), preferred_element_type=F32)


def mm_nt(a, b):
    return lax.dot_general(a, b, (((1,), (1,)), ((), ())), preferred_element_type=F32)


def mm_tn(a, b):
    return lax.dot_general(a, b, (((0,), (0,)), ((), ())), preferred_element_type=F32)


def swap(a):
    return lax.ppermute(a, "core", [(0, 1), (1, 0)])


def cross(a, bits):
    return lax.ppermute(a, ("xh", "xl"), [(s, s ^ bits) for s in range(4)])


def shift(a, axis, by):
    size = lax.axis_size(axis)
    return lax.ppermute(a, axis, [(s, (s + by) % size) for s in range(size)])


def whole(a):
    return pl.BlockSpec(a.shape, lambda *_: (0,) * len(a.shape))


def line_mask(block, width):
    lane = lax.broadcasted_iota(jnp.int32, (block, width), 1)
    return lax.broadcasted_iota(jnp.int32, (block, width), 0) == lane % block


def spread_heads(w_ref, block):
    w = w_ref[...].astype(F32)
    shape = (w.shape[0], block)
    cols = [jnp.broadcast_to(w[:, h : h + 1], shape) for h in range(w.shape[1])]
    return jnp.concatenate(cols, axis=1).astype(BF16)


def prep_kernel(pair_ref, gain_ref, shift_ref, w_ref, out_ref):
    rows, block, channels = pair_ref.shape
    n_ja = out_ref.shape[0]
    own = rows // n_ja
    split = (n_ja, own, block, channels)
    out_ref[:, :own] = pair_ref[...].reshape(split)
    x = pair_ref[...].reshape(rows * block, channels).astype(F32)
    normed = normalize(x, gain_ref[...], shift_ref[...]).astype(BF16)
    every = mm(normed, spread_heads(w_ref, block))
    width = every.shape[1]
    keep = line_mask(block, width)
    lines = []
    for i in range(rows):
        part = jnp.where(keep, every[i * block : (i + 1) * block], 0.0)
        lines.append(jnp.sum(part, axis=0, keepdims=True))
    tile = jnp.concatenate(lines, axis=0).astype(BF16)
    tile = jnp.concatenate([tile[:, :LANES], tile[:, LANES:]], axis=0)
    for d in range(n_ja):
        out_ref[d, own] = tile


def prep(pair, gain, shift_row, bias_weight, n_ja):
    rows, block, channels = pair.shape
    out = jax.ShapeDtypeStruct((n_ja, rows // n_ja + 1, block, channels), BF16)
    return pl.pallas_call(
        prep_kernel,
        out_shape=out,
        compiler_params=PARAMS,
        cost_estimate=pl.CostEstimate(
            flops=2**27, bytes_accessed=2**21, transcendentals=2**12
        ),
    )(pair, gain, shift_row, bias_weight)


def project_kernel(
    pair_ref, gain_ref, shift_ref, w_q_ref, w_k_ref, w_v_ref, w_g_ref, out_n_ref, out_t_ref, gate_ref
):
    n_blocks, _, block, channels = pair_ref.shape
    n = n_blocks * block
    inner = w_q_ref.shape[1]
    x = pair_ref[...].reshape(n, channels).astype(F32)
    normed = normalize(x, gain_ref[...], shift_ref[...]).astype(BF16)
    weights = [ref[...] for ref in (w_q_ref, w_k_ref, w_v_ref, w_g_ref)]
    out_n_ref[0] = mm(normed, jnp.concatenate(weights[:3], axis=1)).astype(BF16)
    proj_t = mm_nt(jnp.concatenate([w.T for w in weights], axis=0), normed)
    out_t_ref[0] = proj_t[: 3 * inner].astype(BF16)
    gate_ref[0] = jax.nn.sigmoid(proj_t[3 * inner :])


def project(both, gain, shift_row, weights):
    n_blocks, slabs, block, channels = both.shape
    rows = slabs - 1
    n = n_blocks * block
    inner = weights[0].shape[1]
    out_n = jax.ShapeDtypeStruct((rows, n, 3 * inner), BF16)
    out_t = jax.ShapeDtypeStruct((rows, 3 * inner, n), BF16)
    gate = jax.ShapeDtypeStruct((rows, inner, n), F32)
    return pl.pallas_call(
        project_kernel,
        grid=(rows,),
        in_specs=[pl.BlockSpec((n_blocks, 1, block, channels), lambda i: (0, i, 0, 0))]
        + [whole(a) for a in (gain, shift_row, *weights)],
        out_specs=[
            pl.BlockSpec((1,) + a.shape[1:], lambda i: (i, 0, 0)) for a in (out_n, out_t, gate)
        ],
        out_shape=[out_n, out_t, gate],
        compiler_params=PARAMS,
        cost_estimate=pl.CostEstimate(
            flops=2**31, bytes_accessed=8 * 2**20, transcendentals=2**18
        ),
    )(both, gain, shift_row, *weights)


def z_lanes(ahead):
    at = lax.rem(lax.axis_index("z") + ahead, lax.axis_size("z"))
    return pl.ds(pl.multiple_of(at * LANES, LANES), LANES)


def attend_kernel(
    heads,
    ahead,
    n_own,
    n_ref,
    t_ref,
    gate_ref,
    cot_ref,
    w_o_ref,
    *refs,
):
    bias_refs = refs[: n_own * 2]
    att_ref, dq_ref, dk_ref, dv_ref, mine_ref, theirs_ref = refs[n_own * 2 : n_own * 2 + 6]
    bias_s, gb_s, s_s, p_s, ds_s, tile_s, line_s = refs[n_own * 2 + 6 :]
    row = pl.program_id(0)
    n = n_ref.shape[1]
    inner = n_ref.shape[2] // 3
    head_dim = inner // heads
    scale = 1.0 / math.sqrt(head_dim)
    n_ja = tile_s.shape[0]
    block = n // n_ja
    rows_i = LANES // 4
    pairs = heads // 2
    core = lax.axis_index("core")
    xh = lax.axis_index("xh")

    @pl.when(row == 0)
    def _():
        for which in range(2):
            far = 0
            for ref in bias_refs[which * n_own : (which + 1) * n_own]:
                for e in range(ref.shape[0]):
                    at = (xh ^ far) * 2 + (core ^ which)
                    at = pl.ds(pl.multiple_of(at * rows_i, rows_i), rows_i)
                    for owner in range(n_ja):
                        for p in range(pairs):
                            tile_s[owner, at, p * LANES : (p + 1) * LANES] = ref[
                                e, owner, p * rows_i : (p + 1) * rows_i, :
                            ]
                    far += 1
        for owner in range(n_ja):
            for p in range(pairs):
                t = tile_s[owner, :, p * LANES : (p + 1) * LANES].astype(F32).T * LOG2E
                for e in range(2):
                    h = p * 2 + e
                    bias_s[
                        owner * block : (owner + 1) * block, h * LANES : (h + 1) * LANES
                    ] = t[e * block : (e + 1) * block]
        gb_s[...] = jnp.zeros_like(gb_s)

    at = z_lanes(ahead)
    nil = jnp.zeros((), BF16)
    row_head = lax.broadcasted_iota(jnp.int32, (inner, LANES), 0) // head_dim
    lane_head = lax.broadcasted_iota(jnp.int32, (LANES, inner), 1) // head_dim
    q_t = t_ref[0, :inner, at]
    q_n = n_ref[0, at, :inner]
    z = lax.rem(lax.axis_index("z") + ahead, lax.axis_size("z"))
    span = LANES // block
    cot = cot_ref[pl.ds(z * span, span), 0].reshape(LANES, cot_ref.shape[3])
    d_att = mm_nt(w_o_ref[...], cot) * gate_ref[0, :, at]
    q_row = jnp.concatenate([jnp.where(lane_head == h, q_n, nil) for h in range(heads)], 0)
    step = 16
    chunk = 128
    wide = 2 * LANES
    a_rows = []
    invs = []
    for p in range(pairs):
        cols = slice(p * wide, (p + 1) * wide)
        q_blk = jnp.concatenate(
            [jnp.where(row_head == h, q_t, nil) for h in (2 * p, 2 * p + 1)], axis=1
        )
        top = jnp.full((8, wide), -jnp.inf, F32)
        for k in range(0, n, chunk):
            t = mm(n_ref[0, k : k + chunk, inner : 2 * inner], q_blk) * (scale * LOG2E)
            t = t + bias_s[k : k + chunk, cols]
            s_s[k : k + chunk, cols] = t
            for e in range(0, chunk, 8):
                top = jnp.maximum(top, t[e : e + 8])
        top = jnp.max(top, axis=0, keepdims=True)
        total = jnp.zeros((8, wide), F32)
        for k in range(0, n, step):
            e = jnp.exp2(s_s[k : k + step, cols] - top)
            s_s[k : k + step, cols] = e
            p_s[k : k + step, cols] = e.astype(BF16)
            total = total + (e[:8] + e[8:])
        invs.append(1.0 / jnp.sum(total, axis=0, keepdims=True))
    for p in range(pairs):
        cols = slice(p * wide, (p + 1) * wide)
        first = 2 * p * head_dim
        rows = slice(first, first + 2 * head_dim)
        inv = invs[p]
        att = mm(t_ref[0, 2 * inner + first : 2 * inner + first + 2 * head_dim, :], p_s[:, cols])
        att = att * inv
        a_two = jnp.concatenate([d_att[rows], d_att[rows]], axis=1) * inv
        lane = lax.broadcasted_iota(jnp.int32, a_two.shape, 1) // LANES
        sub = lax.broadcasted_iota(jnp.int32, a_two.shape, 0) // head_dim
        a_two = jnp.where(lane == sub, a_two, 0.0).astype(BF16)
        diag = jnp.sum(a_two.astype(F32) * att, axis=0, keepdims=True)
        for e in range(2):
            h = 2 * p + e
            own = slice(h * head_dim, (h + 1) * head_dim)
            att_ref[0, own, :] = att[
                e * head_dim : (e + 1) * head_dim, e * LANES : (e + 1) * LANES
            ]
        lead = [jnp.zeros((first, wide), BF16)] if p else []
        tail = [jnp.zeros((inner - first - 2 * head_dim, wide), BF16)] if p + 1 < pairs else []
        a_blk = jnp.concatenate(lead + [a_two] + tail, axis=0)
        a_rows.append(a_blk.T)
        for k in range(0, n, chunk):
            dp = mm(n_ref[0, k : k + chunk, 2 * inner :], a_blk)
            ds = s_s[k : k + chunk, cols] * (dp - diag)
            gb_s[k : k + chunk, cols] += ds
            ds_s[k : k + chunk, cols] = ds.astype(BF16)
        dq = mm(t_ref[0, inner + first : inner + first + 2 * head_dim, :], ds_s[:, cols]) * scale
        for e in range(2):
            h = 2 * p + e
            dq_ref[0, h * head_dim : (h + 1) * head_dim, :] = dq[
                e * head_dim : (e + 1) * head_dim, e * LANES : (e + 1) * LANES
            ].astype(BF16)
    dk_ref[0] = (mm(ds_s[...], q_row) * scale).astype(BF16)
    dv_ref[0] = mm(p_s[...], jnp.concatenate(a_rows, axis=0)).astype(BF16)

    @pl.when(row == pl.num_programs(0) - 1)
    def _():
        for owner in range(n_ja):
            for p in range(pairs):
                t = jnp.concatenate(
                    [
                        gb_s[owner * block : (owner + 1) * block, h * LANES : (h + 1) * LANES]
                        for h in (2 * p, 2 * p + 1)
                    ],
                    axis=0,
                )
                line_s[:, p * LANES : (p + 1) * LANES] = t.T.astype(BF16)
            for far in range(2):
                for ref, which in ((mine_ref, core), (theirs_ref, 1 - core)):
                    at = pl.multiple_of((far * 2 + which) * rows_i, rows_i)
                    for p in range(pairs):
                        ref[far, owner, p * rows_i : (p + 1) * rows_i, :] = line_s[
                            pl.ds(at, rows_i), p * LANES : (p + 1) * LANES
                        ]


def attend(heads, ahead, by_n, by_t, gate, cot, w_o, own, other):
    rows, n, _ = by_n.shape
    inner = gate.shape[1]
    n_ja, slab, _ = own[0].shape[1:]
    lines = heads * n // n_ja
    att = jax.ShapeDtypeStruct((rows, inner, LANES), F32)
    dq = jax.ShapeDtypeStruct((rows, inner, LANES), BF16)
    grad = jax.ShapeDtypeStruct((rows, n, inner), BF16)
    gb = jax.ShapeDtypeStruct((2, n_ja, slab, LANES), BF16)

    def by_row(a):
        return pl.BlockSpec((1,) + a.shape[1:], lambda i: (i, 0, 0))

    cot_spec = pl.BlockSpec((cot.shape[0], 1) + cot.shape[2:], lambda i: (0, i, 0, 0))
    return pl.pallas_call(
        lambda *refs: attend_kernel(heads, ahead, len(own), *refs),
        grid=(rows,),
        in_specs=[by_row(by_n), by_row(by_t), by_row(gate), cot_spec, whole(w_o)]
        + [whole(a) for a in (*own, *other)],
        out_specs=[by_row(a) for a in (att, dq, grad, grad)] + [whole(gb)] * 2,
        out_shape=[att, dq, grad, grad, gb, gb],
        scratch_shapes=[
            pltpu.VMEM((n, heads * LANES), F32),
            pltpu.VMEM((n, heads * LANES), F32),
            pltpu.VMEM((n, heads * LANES), F32),
            pltpu.VMEM((n, heads * LANES), BF16),
            pltpu.VMEM((n, heads * LANES), BF16),
            pltpu.VMEM((n_ja, LANES, lines), BF16),
            pltpu.VMEM((LANES, lines), BF16),
        ],
        compiler_params=PARAMS,
        cost_estimate=pl.CostEstimate(
            flops=2**32, bytes_accessed=2**23, transcendentals=2**20
        ),
    )(by_n, by_t, gate, cot, w_o, *own, *other)


def finish_kernel(aheads, gate_ref, cot_ref, w_o_ref, w_q_ref, w_k_ref, w_v_ref, w_g_ref, *refs):
    count = len(aheads)
    att_refs, dq_refs = refs[:count], refs[count : 2 * count]
    dk_refs, dv_refs = refs[2 * count : 3 * count], refs[3 * count : 4 * count]
    out_ref, att_s, dq_s = refs[4 * count :]
    for ahead, att_ref, dq_ref in zip(aheads, att_refs, dq_refs):
        at = z_lanes(ahead)
        att_s[:, at] = att_ref[0]
        dq_s[:, at] = dq_ref[0]
    half = (out_ref.shape[0],) + out_ref.shape[2:]
    gate = gate_ref[0]
    cot = cot_ref[...].reshape(gate.shape[1], cot_ref.shape[3])
    d_gated = mm_nt(w_o_ref[...], cot)
    att = att_s[...]
    update = mm_tn((gate * att).astype(BF16), w_o_ref[...])
    out_ref[:, 0] = update.astype(BF16).reshape(half)
    d_gate = (d_gated * att * gate * (1.0 - gate)).astype(BF16)
    left_t = jnp.concatenate([dq_s[...], d_gate], axis=0)
    dk = sum(ref[0].astype(F32) for ref in dk_refs).astype(BF16)
    dv = sum(ref[0].astype(F32) for ref in dv_refs).astype(BF16)
    dn = mm_tn(left_t, jnp.concatenate([w_q_ref[...].T, w_g_ref[...].T], axis=0))
    dn = dn + mm(
        jnp.concatenate([dk, dv], axis=1),
        jnp.concatenate([w_k_ref[...].T, w_v_ref[...].T], axis=0),
    )
    out_ref[:, 1] = dn.astype(BF16).reshape(half)


def finish(aheads, gate, cot, w_o, weights, att, dq, dk, dv):
    n_blocks, rows, block, channels = cot.shape
    inner = w_o.shape[0]
    arrays = (*att, *dq, *dk, *dv)

    def by_row(a):
        return pl.BlockSpec((1,) + a.shape[1:], lambda i: (i, 0, 0))

    cot_spec = pl.BlockSpec((n_blocks, 1, block, channels), lambda i: (0, i, 0, 0))
    return pl.pallas_call(
        lambda *refs: finish_kernel(aheads, *refs),
        grid=(rows,),
        in_specs=[by_row(gate), cot_spec, whole(w_o)]
        + [whole(a) for a in weights]
        + [by_row(a) for a in arrays],
        out_specs=pl.BlockSpec(
            (n_blocks, 2, 1, block, channels), lambda i: (0, 0, i, 0, 0)
        ),
        out_shape=jax.ShapeDtypeStruct((n_blocks, 2, rows, block, channels), BF16),
        scratch_shapes=[
            pltpu.VMEM((inner, n_blocks * block), F32),
            pltpu.VMEM((inner, n_blocks * block), BF16),
        ],
        compiler_params=PARAMS,
        cost_estimate=pl.CostEstimate(flops=2**31, bytes_accessed=2**23, transcendentals=0),
    )(gate, cot, w_o, *weights, *arrays)


def arrange_x_kernel(*refs):
    ins, outs = refs[:4], refs[4:]
    xh = lax.axis_index("xh")
    xl = lax.axis_index("xl")
    for bits, out in enumerate(outs):
        for y in range(out.shape[0]):
            at = (xh ^ (bits >> 1), y * 2 + (xl ^ (bits & 1)))
            out[y] = sum(ref[at].astype(F32) for ref in ins).astype(BF16)


def arrange_y_kernel(*refs):
    ins, outs = refs[:4], refs[4:]
    size = ins[0].shape[0]
    y = lax.axis_index("y")
    for ahead, out in enumerate(outs):
        at = lax.rem(y + ahead, size)
        out[...] = sum(ref[at].astype(F32) for ref in ins).astype(BF16)


def arrange(kernel, arrays, shape):
    out = jax.ShapeDtypeStruct(shape, BF16)
    return pl.pallas_call(
        kernel,
        out_shape=[out] * 4,
        cost_estimate=pl.CostEstimate(flops=2**18, bytes_accessed=2**20, transcendentals=0),
    )(*arrays)


def final_kernel(
    pair_ref, both_ref, gain_ref, shift_ref, w_ref, g0_ref, g1_ref, g2_ref, g3_ref, out_ref
):
    rows, block, channels = pair_ref.shape
    tile = sum(ref[...].astype(F32) for ref in (g0_ref, g1_ref, g2_ref, g3_ref))
    tile = jnp.concatenate([tile[:rows], tile[rows:]], axis=1).astype(BF16).astype(F32)
    keep = line_mask(block, tile.shape[1])
    spread = jnp.concatenate(
        [
            jnp.where(keep, jnp.broadcast_to(tile[i : i + 1], keep.shape), 0.0).astype(BF16)
            for i in range(rows)
        ],
        axis=0,
    )
    w_back = spread_heads(w_ref, block)
    dn = both_ref[:, 1].reshape(rows * block, channels).astype(F32) + mm_nt(spread, w_back)
    x = pair_ref[...].reshape(rows * block, channels).astype(F32)
    centred = x - jnp.mean(x, axis=-1, keepdims=True)
    rstd = lax.rsqrt(jnp.mean(centred * centred, axis=-1, keepdims=True) + EPSILON)
    unit = centred * rstd
    push = dn * gain_ref[...]
    along = jnp.mean(push * unit, axis=-1, keepdims=True)
    level = jnp.mean(push, axis=-1, keepdims=True)
    out_ref[...] = ((push - level - unit * along) * rstd).reshape(out_ref.shape)


def final(pair, both, gain, shift_row, bias_weight, gb):
    return pl.pallas_call(
        final_kernel,
        out_shape=jax.ShapeDtypeStruct(pair.shape, F32),
        compiler_params=PARAMS,
        cost_estimate=pl.CostEstimate(
            flops=2**27, bytes_accessed=2**21, transcendentals=2**12
        ),
    )(pair, both, gain, shift_row, bias_weight, *gb)


def shards(
    pair,
    cotangent,
    norm_gain,
    norm_shift,
    query_weight,
    key_weight,
    value_weight,
    gate_weight,
    bias_weight,
    out_weight,
):
    rows_i, rows_j, channels = pair.shape
    heads = bias_weight.shape[1]
    n_ja = lax.axis_size(JA)
    own_i = rows_i // n_ja
    gain = norm_gain.reshape(1, channels)
    shift_row = norm_shift.reshape(1, channels)
    weights = (query_weight, key_weight, value_weight, gate_weight)
    tie = lax.optimization_barrier

    both = lax.all_to_all(
        prep(pair, gain, shift_row, bias_weight, n_ja), JA, 0, 0, tiled=True
    )
    cotangent, both = tie((cotangent, both))
    cot = lax.all_to_all(
        cotangent.reshape(n_ja, own_i, rows_j, channels), JA, 0, 0, tiled=True
    )

    near = both[:, own_i]
    far = lax.ppermute(near, "xh", [(0, 1), (1, 0)])
    by_n, by_t, gate = project(both, gain, shift_row, weights)
    far, by_n = tie((far, by_n))
    near = jnp.stack([near, far])
    prev, after = shift(near, "z", 1), shift(near, "z", 3)
    att, dq, dk, dv, total = [], [], [], [], []

    def slice_of(ahead, own, other):
        att_a, dq_a, dk_a, dv_a, mine, theirs = attend(
            heads, ahead, by_n, by_t, gate, cot, out_weight, own, other
        )
        att.append(att_a)
        dq.append(dq_a)
        dk.append(dk_a)
        dv.append(dv_a)
        return mine, swap(theirs)

    def joined(mine, theirs):
        return (mine.astype(F32) + theirs.astype(F32)).astype(BF16)

    mine0, theirs0 = slice_of(0, [near], [swap(near)])
    prev, after, dk[0] = tie((prev, after, dk[0]))
    opp0, opp1 = shift(prev[0], "z", 1)[None], shift(after[1], "z", 3)[None]
    mine1, theirs1 = slice_of(3, [prev], [swap(prev)])
    after_swap = swap(after)
    after, after_swap, opp0, opp1, dk[1] = tie((after, after_swap, opp0, opp1, dk[1]))
    mine2, theirs2 = slice_of(1, [after], [after_swap])
    opp_swap = [swap(opp0), swap(opp1)]
    opp0, opp1, opp_swap, theirs0, theirs1, dk[2] = tie(
        (opp0, opp1, opp_swap, theirs0, theirs1, dk[2])
    )
    part0 = joined(mine0, theirs0)
    part1 = joined(mine1, theirs1)
    opp0, part1 = tie((opp0, part1))
    part1 = shift(part1, "z", 3)
    mine3, theirs3 = slice_of(2, [opp0, opp1], opp_swap)
    part1, theirs2, dk[3] = tie((part1, theirs2, dk[3]))
    part2 = joined(mine2, theirs2)
    part3 = joined(mine3, theirs3)
    part2, part3, dk[3] = tie((part2, part3, dk[3]))
    part2, part3 = shift(part2, "z", 1), shift(part3, "z", 2)
    done = finish((0, 3, 1, 2), gate, cot, out_weight, weights, att, dq, dk, dv)
    part2, part3, done = tie((part2, part3, done))
    total = [part0, part1, part2, part3]

    slab = total[0].shape[2:]
    by_x = list(arrange(arrange_x_kernel, total, (lax.axis_size("y"),) + slab))
    by_x[1], done = tie((by_x[1], done))
    done = lax.all_to_all(done, JA, 0, 0, tiled=True)
    by_x = [by_x[0]] + [cross(by_x[bits], bits) for bits in (1, 2, 3)]
    by_y = arrange(arrange_y_kernel, by_x, slab)
    by_y = [by_y[0]] + [shift(by_y[d], "y", d) for d in (1, 2, 3)]

    update = done[:, 0].reshape(pair.shape)
    pair_grad = final(pair, done, gain, shift_row, bias_weight, by_y)
    return (update, pair_grad)


def solution(mesh):
    fine = Mesh(mesh.devices.reshape(4, 2, 2, 4, 2), IA + JA)
    spec = P(IA, JA, None)
    in_specs = (spec, spec) + (P(),) * 8
    return jax.shard_map(
        shards, mesh=fine, in_specs=in_specs, out_specs=(spec, spec), check_vma=False
    )
```

time: 133 us -> 135 us (1.015)
  blocking collectives: 22.6 us -> 17 us
  starting transfers between devices: 30.9 us -> 34.5 us
  waiting for transfers between devices: 23.7 us -> 26.2 us
  local copies, waits for them, and re-layouts: 9.74 us -> 11.4 us
    ppermute x3, waiting for transfers between devices: 5.33 us -> 11.3 us  [cross(): return lax.ppermute(a, ('xh', 'xl'), [(s, s ^ bits) for s in range(4)])]
    all_to_all x1, blocking collectives: 22.6 us -> 17 us  [shards(): lax.all_to_all(prep(pair, gain, shift_row, bias_weight, n_ja), JA, 0, 0,...]
    ppermute x10, waiting for transfers between devices: 14.1 us -> 10.6 us  [shift(): return lax.ppermute(a, axis, [(s, (s + by) % size) for s in range(size)])]
    all_to_all x0 -> x1, starting transfers between devices: none -> 3.5 us  [shards(): lax.all_to_all(cotangent.reshape(n_ja, own_i, rows_j, channels), JA, 0, 0...]
    unnamed x44 -> x53, local copies, waits for them, and re-layouts: 8.03 us -> 10.5 us
  transfers between devices with their start and end apart: 24 -> 25, of which waited for: 8 -> 8; matrix products, arithmetic and copies ran while one was open for 2% -> 1% of each run, Pallas kernels for 25% -> 28%
where the time goes in v5:
time: 135 us; the launch traced here: 134 us
  Pallas kernels  43.2 us (32%)
  starting transfers between devices  34.5 us (26%)
  waiting for transfers between devices  26.2 us (19%)
  blocking collectives  17 us (13%)
  local copies, waits for them, and re-layouts  11.4 us (8%)
    pallas_call x4, Pallas kernels, attend(): pl.pallas_call(lambda *refs: attend_kernel(heads, ahead, len(own), *refs)...  29.2 us
    all_to_all x1, blocking collectives, shards(): lax.all_to_all(prep(pair, gain, shift_row, bias_weight, n_ja), JA, 0, 0,...  17 us
    ppermute x10, starting transfers between devices, shift(): return lax.ppermute(a, axis, [(s, (s + by) % size) for s in range(size)])  16.4 us
    ppermute x3, waiting for transfers between devices, cross(): return lax.ppermute(a, ('xh', 'xl'), [(s, s ^ bits) for s in range(4)])  11.3 us
    ppermute x10, waiting for transfers between devices, shift(): return lax.ppermute(a, axis, [(s, (s + by) % size) for s in range(size)])  10.6 us
    unnamed x53, local copies, waits for them, and re-layouts  10.5 us
    all_to_all x1, starting transfers between devices, shards(): done = lax.all_to_all(done, JA, 0, 0, tiled=True)  4.89 us
    ppermute x3, starting transfers between devices, cross(): return lax.ppermute(a, ('xh', 'xl'), [(s, s ^ bits) for s in range(4)])  4.78 us
  transfers between devices with their start and end apart: 25, of which 8 were waited for; matrix products, arithmetic and copies ran while one was open for 1% of the time, Pallas kernels for 28%

profile of v5, /device:TPU:0, one launch (start us, length us, event | category | flops | bytes accessed | tf_op | source)
XLA Modules:
  0.0 134.3 jit_solution(18207638839717251660)
XLA Ops:
  0.6 0.8 copy.16.w_ref
  1.4 1.0 copy-done
  2.5 0.7 copy-done.10
  3.1 0.7 copy-done.12
  3.8 1.1 shard_map.113
  4.9 0.0 copy-start.5
  4.9 0.0 copy-start.6
  5.0 0.0 copy-start.11
  5.0 0.0 copy-start.13
  5.0 17.0 %all_to_all.15.pair_ref = bf16[8,5,64,128]{3,2,1,0:T(8,128)(2,1)S(1)} all-to-all(bf16[8,5,64,128]{3,2,1,0:T(8,128)(2,1)S(1)} %shard_map.113), channel_id=1, replica_groups=mesh['z'=4,'xh'=2,'core'=2,'y'=4,'xl'=2] {'y','xl'}, dimensions={0} | all-to-all | bytes 1310720 | tf_op jit(solution)/shard_map/all_to_all | solution.py:468
  22.0 3.5 %all-to-all-start.1 = ((bf16[8,4,64,128]{3,2,1,0:T(8,128)(2,1)}), bf16[8,4,64,128]{3,2,1,0:T(8,128)(2,1)S(1)}, u32[]{:S(2)}, u32[]{:S(2)}) async-start(bf16[8,4,64,128]{3,2,1,0:T(8,128)(2,1)} %bitcast.3), calls=%async_computation.1 | async-start | bytes 1048576 | tf_op jit(solution)/shard_map/all_to_all | solution.py:472
  25.6 2.8 %collective-permute-start = (bf16[8,64,128]{2,1,0:T(8,128)(2,1)S(1)}, bf16[8,64,128]{2,1,0:T(8,128)(2,1)S(1)}, u32[]{:S(2)}, u32[]{:S(2)}) collective-permute-start(bf16[8,64,128]{2,1,0:T(8,128)(2,1)S(1)} %get-tuple-element.137), channel_id=1, source_target_pairs={{0,16},{16,0},{1,17},{17,1},{2,18},{18,2},{3,19},{19,3},{4,20},{20... | collective-permute-start | bytes 393224 | tf_op jit(solution)/shard_map/ppermute | solution.py:477
  28.4 2.6 %shard_map.114 = (bf16[4,512,384]{2,1,0:T(8,128)(2,1)S(1)}, bf16[4,384,512]{2,1,0:T(8,128)(2,1)S(1)}, f32[4,128,512]{2,1,0:T(8,128)S(1)}) custom-call(bf16[8,5,64,128]{3,2,1,0:T(8,128)(2,1)S(1)} %all_to_all.15.pair_ref, f32[1,128]{1,0:T(1,128)S(1)} %bitcast.16, f32[1,128]{1,0:T(1,128)S(1)} %bitcast.19, bf16[128,128]{1,0:T(8,128)(2,1)S(1)} %copy-done.4, ...), custom_call_target="tpu_custom_call" | custom-call | flops 2147483648 | bytes 8388608 | tf_op jit(solution)/shard_map/pallas_call | solution.py:125
  31.0 1.2 copy-done.14
  32.2 1.1 copy-done.16
  33.3 3.0 %collective-permute-done = bf16[8,64,128]{2,1,0:T(8,128)(2,1)S(1)} collective-permute-done((bf16[8,64,128]{2,1,0:T(8,128)(2,1)S(1)}, bf16[8,64,128]{2,1,0:T(8,128)(2,1)S(1)}, u32[]{:S(2)}, u32[]{:S(2)}) %collective-permute-start) | collective-permute-done | bytes 131104 | tf_op jit(solution)/shard_map/ppermute | solution.py:477
  36.3 0.1 collective-permute-start.1
  36.4 4.1 %collective-permute-start.3 = (bf16[2,8,64,128]{3,2,1,0:T(8,128)(2,1)S(1)}, bf16[2,8,64,128]{3,2,1,0:T(8,128)(2,1)S(1)}, u32[]{:S(2)}, u32[]{:S(2)}) collective-permute-start(bf16[2,8,64,128]{3,2,1,0:T(8,128)(2,1)S(1)} %pad_maximum_fusion.refs_5_), channel_id=1, source_target_pairs={{0,96},{32,0},{64,32},{96,64},{1,97},{33,1},{65,33},{97,65},{2,98}... | collective-permute-start | bytes 786440 | tf_op jit(solution)/shard_map/ppermute | solution.py:49
  40.6 1.4 %copy-done.15 = bf16[4,512,384]{2,1,0:T(8,128)(2,1)S(1)} copy-done((bf16[4,512,384]{2,1,0:T(8,128)(2,1)S(1)}, bf16[4,512,384]{2,1,0:T(8,128)(2,1)}, u32[]{:S(2)}) %copy-start.15) | copy-done | bytes 1572888
  42.0 7.3 %shard_map.115 = (f32[4,128,128]{2,1,0:T(8,128)S(1)}, bf16[4,128,128]{2,1,0:T(8,128)(2,1)S(1)}, bf16[4,512,128]{2,1,0:T(8,128)(2,1)S(1)}, bf16[4,512,128]{2,1,0:...) custom-call(bf16[4,512,384]{2,1,0:T(8,128)(2,1)S(1)} %copy-done.15, ...), custom_call_target="tpu_custom_call" | custom-call | flops 4294967296 | bytes 8388608 | tf_op jit(solution)/shard_map/pallas_call | solution.py:303
  49.3 0.8 collective-permute-done.2.refs_5_
  50.1 0.1 collective-permute-start.5
  50.2 0.6 collective-permute-start.4
  50.8 2.9 %collective-permute-start.6 = (bf16[8,64,128]{2,1,0:T(8,128)(2,1)S(1)}, bf16[8,64,128]{2,1,0:T(8,128)(2,1)S(1)}, u32[]{:S(2)}, u32[]{:S(2)}) collective-permute-start(bf16[8,64,128]{2,1,0:T(8,128)(2,1)S(1)} %slice_bitcast_fusion), channel_id=1, source_target_pairs={{0,96},{32,0},{64,32},{96,64},{1,97},{33,1},{65,33},{97,65},{2,98}... | collective-permute-start | bytes 393224 | tf_op jit(solution)/shard_map/ppermute | solution.py:49
  53.7 7.3 %shard_map.116 = (f32[4,128,128]{2,1,0:T(8,128)S(1)}, bf16[4,128,128]{2,1,0:T(8,128)(2,1)S(1)}, bf16[4,512,128]{2,1,0:T(8,128)(2,1)S(1)}, bf16[4,512,128]{2,1,0:...) custom-call(bf16[4,512,384]{2,1,0:T(8,128)(2,1)S(1)} %copy-done.15, ...), custom_call_target="tpu_custom_call" | custom-call | flops 4294967296 | bytes 8388608 | tf_op jit(solution)/shard_map/pallas_call | solution.py:303
  61.1 0.6 collective-permute-start.8
  61.7 0.1 collective-permute-start.9
  61.8 0.4 collective-permute-start.11
  62.2 7.3 %shard_map.117 = (f32[4,128,128]{2,1,0:T(8,128)S(1)}, bf16[4,128,128]{2,1,0:T(8,128)(2,1)S(1)}, bf16[4,512,128]{2,1,0:T(8,128)(2,1)S(1)}, bf16[4,512,128]{2,1,0:...) custom-call(bf16[4,512,384]{2,1,0:T(8,128)(2,1)S(1)} %copy-done.15, ...), custom_call_target="tpu_custom_call" | custom-call | flops 4294967296 | bytes 8388608 | tf_op jit(solution)/shard_map/pallas_call | solution.py:303
  69.5 0.2 collective-permute-start.13
  69.7 0.1 add_convert_fusion.2
  69.8 1.5 %collective-permute-start.12 = (bf16[2,8,64,128]{3,2,1,0:T(8,128)(2,1)S(1)}, bf16[2,8,64,128]{3,2,1,0:T(8,128)(2,1)S(1)}, u32[]{:S(2)}, u32[]{:S(2)}) collective-permute-start(bf16[2,8,64,128]{3,2,1,0:T(8,128)(2,1)S(1)} %add_convert_fusion.2), channel_id=1, source_target_pairs={{0,96},{32,0},{64,32},{96,64},{1,97},{33,1},{65,33},{97,65},{2,98}... | collective-permute-start | bytes 786440 | tf_op jit(solution)/shard_map/ppermute | solution.py:49
  71.3 7.3 %shard_map.118 = (f32[4,128,128]{2,1,0:T(8,128)S(1)}, bf16[4,128,128]{2,1,0:T(8,128)(2,1)S(1)}, bf16[4,512,128]{2,1,0:T(8,128)(2,1)S(1)}, bf16[4,512,128]{2,1,0:...) custom-call(bf16[4,512,384]{2,1,0:T(8,128)(2,1)S(1)} %copy-done.15, ...), custom_call_target="tpu_custom_call" | custom-call | flops 4294967296 | bytes 8388608 | tf_op jit(solution)/shard_map/pallas_call | solution.py:303
  78.6 0.0 copy-start.3
  78.6 0.8 copy-done.3
  79.4 0.2 collective-permute-start.14
  79.6 0.1 add_convert_fusion.1
  79.6 1.3 collective-permute-done.14
  80.9 0.1 add_convert_fusion
  81.0 0.8 collective-permute-start.15
  81.9 1.0 collective-permute-start.16
  82.9 0.8 add_convert_fusion.3.refs_0_
  83.7 4.6 %shard_map.119 = bf16[8,2,4,64,128]{4,3,2,1,0:T(8,128)(2,1)} custom-call(f32[4,128,512]{2,1,0:T(8,128)} %copy-done.2, bf16[8,4,64,128]{3,2,1,0:T(8,128)(2,1)S(1)} %all-to-all-done.1.refs_3_.refs_1_, bf16[128,128]{1,0:T(8,128)(2,1)S(1)} %copy-done.8, bf16[128,128]{1,0:T(8,128)(2,1)S(1)} %copy-done.4, bf16[128,128]{1,0:T(8,128)(2,1)S(1)} %copy-done.5, ...), custom_call_target="tpu_custom_call" | custom-call | flops 2147483648 | bytes 8388608 | tf_op jit(solution)/shard_map/pallas_call | solution.py:363
  88.2 8.1 %collective-permute-done.15.refs_2_ = bf16[2,8,64,128]{3,2,1,0:T(8,128)(2,1)S(1)} collective-permute-done((bf16[2,8,64,128]{3,2,1,0:T(8,128)(2,1)S(1)}, bf16[2,8,64,128]{3,2,1,0:T(8,128)(2,1)S(1)}, u32[]{:S(2)}, u32[]{:S(2)}) %collective-permute-start.15) | collective-permute-done | bytes 262176 | tf_op jit(solution)/shard_map/ppermute | solution.py:49
  96.3 0.7 copy-done.18
  97.0 0.7 copy-done.19
  97.7 2.0 %shard_map.120 = (bf16[4,64,128]{2,1,0:T(8,128)(2,1)}, bf16[4,64,128]{2,1,0:T(8,128)(2,1)}, bf16[4,64,128]{2,1,0:T(8,128)(2,1)}, bf16[4,64,128]{2,1,0:T(8,128)(2,1)}) custom-call(bf16[2,8,64,128]{3,2,1,0:T(8,128)(2,1)} %add_convert_fusion.3.refs_0_, bf16[2,8,64,128]{3,2,1,0:T(8,128)(2,1)} %copy-done.17, bf16[2,8,64,128]{3,2,1,0:T(8,128)(2,1)} %copy-done.18, ...), custom_call_target="tpu_custom_call" | custom-call | flops 262144 | bytes 1048576 | tf_op jit(solution)/shard_map/pallas_call | solution.py:403
  99.7 4.9 %all-to-all-start.2 = ((bf16[8,2,4,64,128]{4,3,2,1,0:T(8,128)(2,1)}), bf16[8,2,4,64,128]{4,3,2,1,0:T(8,128)(2,1)S(1)}, u32[]{:S(2)}, u32[]{:S(2)}) async-start(bf16[8,2,4,64,128]{4,3,2,1,0:T(8,128)(2,1)} %shard_map.119), calls=%async_computation.2 | async-start | bytes 2097152 | tf_op jit(solution)/shard_map/all_to_all | solution.py:525
  104.6 2.0 %collective-permute-start.17 = (bf16[4,64,128]{2,1,0:T(8,128)(2,1)S(1)}, bf16[4,64,128]{2,1,0:T(8,128)(2,1)S(1)}, u32[]{:S(2)}, u32[]{:S(2)}) collective-permute-start(bf16[4,64,128]{2,1,0:T(8,128)(2,1)S(1)} %copy-done.25), channel_id=1, source_target_pairs={{0,1},{1,0},{16,17},{17,16},{2,3},{3,2},{18,19},{19,18},{4,5},{5,4... | collective-permute-start | bytes 196616 | tf_op jit(solution)/shard_map/ppermute | solution.py:44
  106.6 2.0 %collective-permute-start.18 = (bf16[4,64,128]{2,1,0:T(8,128)(2,1)S(1)}, bf16[4,64,128]{2,1,0:T(8,128)(2,1)S(1)}, u32[]{:S(2)}, u32[]{:S(2)}) collective-permute-start(bf16[4,64,128]{2,1,0:T(8,128)(2,1)S(1)} %copy-done.24), channel_id=1, source_target_pairs={{0,16},{1,17},{16,0},{17,1},{2,18},{3,19},{18,2},{19,3},{4,20},{5,... | collective-permute-start | bytes 196616 | tf_op jit(solution)/shard_map/ppermute | solution.py:44
  108.6 0.8 collective-permute-start.19
  109.3 10.4 %collective-permute-done.17.refs_1_ = bf16[4,64,128]{2,1,0:T(8,128)(2,1)S(1)} collective-permute-done((bf16[4,64,128]{2,1,0:T(8,128)(2,1)S(1)}, bf16[4,64,128]{2,1,0:T(8,128)(2,1)S(1)}, u32[]{:S(2)}, u32[]{:S(2)}) %collective-permute-start.17) | collective-permute-done | bytes 65568 | tf_op jit(solution)/shard_map/ppermute | solution.py:44
  119.8 0.9 collective-permute-done.18.refs_2_
  120.7 0.6 copy-done.21
  121.3 0.0 copy-done.22
  121.3 1.6 %shard_map.121 = (bf16[64,128]{1,0:T(8,128)(2,1)}, bf16[64,128]{1,0:T(8,128)(2,1)}, bf16[64,128]{1,0:T(8,128)(2,1)}, bf16[64,128]{1,0:T(8,128)(2,1)}) custom-call(bf16[4,64,128]{2,1,0:T(8,128)(2,1)} %get-tuple-element.128.refs_0_, bf16[4,64,128]{2,1,0:T(8,128)(2,1)} %copy-done.20, bf16[4,64,128]{2,1,0:T(8,128)(2,1)} %copy-done.21, bf16[4,64,128]{2,1,0:T(8,128)(2,1)} %copy-done.22), custom_call_target="tpu_custom_call" | custom-call | flops 262144 | bytes 1048576 | tf_op jit(solution)/shard_map/pallas_call | solution.py:403
  122.9 1.8 %collective-permute-start.20 = (bf16[64,128]{1,0:T(8,128)(2,1)}, bf16[64,128]{1,0:T(8,128)(2,1)S(1)}, u32[]{:S(2)}, u32[]{:S(2)}) collective-permute-start(bf16[64,128]{1,0:T(8,128)(2,1)} %get-tuple-element.133), channel_id=1, source_target_pairs={{0,2},{2,4},{4,6},{6,0},{1,3},{3,5},{5,7},{7,1},{8,10},{10,12},{12... | collective-permute-start | bytes 49160 | tf_op jit(solution)/shard_map/ppermute | solution.py:49
  124.7 2.7 %collective-permute-start.21 = (bf16[64,128]{1,0:T(8,128)(2,1)}, bf16[64,128]{1,0:T(8,128)(2,1)S(1)}, u32[]{:S(2)}, u32[]{:S(2)}) collective-permute-start(bf16[64,128]{1,0:T(8,128)(2,1)} %get-tuple-element.134), channel_id=1, source_target_pairs={{0,4},{2,6},{4,0},{6,2},{1,5},{3,7},{5,1},{7,3},{8,12},{10,14},{12... | collective-permute-start | bytes 49160 | tf_op jit(solution)/shard_map/ppermute | solution.py:49
  127.4 1.4 %collective-permute-start.22 = (bf16[64,128]{1,0:T(8,128)(2,1)}, bf16[64,128]{1,0:T(8,128)(2,1)S(1)}, u32[]{:S(2)}, u32[]{:S(2)}) collective-permute-start(bf16[64,128]{1,0:T(8,128)(2,1)} %get-tuple-element.135), channel_id=1, source_target_pairs={{0,6},{2,0},{4,2},{6,4},{1,7},{3,1},{5,3},{7,5},{8,14},{10,8},{12,... | collective-permute-start | bytes 49160 | tf_op jit(solution)/shard_map/ppermute | solution.py:49
  128.8 0.8 slice.17
  129.7 0.5 collective-permute-done.21.g2_ref
  130.2 1.2 collective-permute-done.22.g3_ref
  131.3 0.7 copy-done.9
  132.1 2.2 %shard_map.122 = f32[32,64,128]{2,1,0:T(8,128)} custom-call(bf16[32,64,128]{2,1,0:T(8,128)(2,1)S(1)} %copy-done.1, bf16[8,2,4,64,128]{4,3,2,1,0:T(8,128)(2,1)S(1)} %all-to-all-done.2.both_ref, f32[1,128]{1,0:T(1,128)S(1)} %bitcast.17, f32[1,128]{1,0:T(1,128)S(1)} %bitcast.20, bf16[128,4]{1,0:T(8,128)(2,1)S(1)} %copy.16.w_ref, bf16[64,128]{1,0:T(8,128)(2,1)S(1)} %copy-done.9, ...), custom_call_target="tpu_custom_call" | custom-call | flops 134217728 | bytes 2097152 | tf_op jit(solution)/shard_map/pallas_call | solution.py:437
  (59 shorter events, 0.2 us)
Async XLA Ops:
  1.4 1.0 copy-start
  2.5 0.7 copy-start.10
  3.1 0.7 copy-start.12
  4.9 23.5 %copy-start.4 = (bf16[128,128]{1,0:T(8,128)(2,1)S(1)}, bf16[128,128]{1,0:T(8,128)(2,1)}, u32[]{:S(2)}) copy-start(bf16[128,128]{1,0:T(8,128)(2,1)} %refs_3_.1) | copy-start | bytes 98308
  4.9 23.5 %copy-start.5 = (bf16[128,128]{1,0:T(8,128)(2,1)S(1)}, bf16[128,128]{1,0:T(8,128)(2,1)}, u32[]{:S(2)}) copy-start(bf16[128,128]{1,0:T(8,128)(2,1)} %refs_4_.9) | copy-start | bytes 98308
  4.9 23.4 %copy-start.6 = (bf16[128,128]{1,0:T(8,128)(2,1)S(1)}, bf16[128,128]{1,0:T(8,128)(2,1)}, u32[]{:S(2)}) copy-start(bf16[128,128]{1,0:T(8,128)(2,1)} %refs_5_.1) | copy-start | bytes 98308
  5.0 23.4 %copy-start.7 = (bf16[128,128]{1,0:T(8,128)(2,1)S(1)}, bf16[128,128]{1,0:T(8,128)(2,1)}, u32[]{:S(2)}) copy-start(bf16[128,128]{1,0:T(8,128)(2,1)} %refs_6_.1) | copy-start | bytes 98308
  5.0 23.4 %copy-start.11 = (f32[128]{0:T(128)S(1)}, f32[128]{0:T(128)}, u32[]{:S(2)}) copy-start(f32[128]{0:T(128)} %param.12) | copy-start | bytes 1540
  5.0 23.4 %copy-start.13 = (f32[128]{0:T(128)S(1)}, f32[128]{0:T(128)}, u32[]{:S(2)}) copy-start(f32[128]{0:T(128)} %param.13) | copy-start | bytes 1540
  22.0 18.5 %all-to-all-start.1 = ((bf16[8,4,64,128]{3,2,1,0:T(8,128)(2,1)}), bf16[8,4,64,128]{3,2,1,0:T(8,128)(2,1)S(1)}, u32[]{:S(2)}, u32[]{:S(2)}) async-start(bf16[8,4,64,128]{3,2,1,0:T(8,128)(2,1)} %bitcast.3), calls=%async_computation.1 | async-start | bytes 1048576 | tf_op jit(solution)/shard_map/all_to_all | solution.py:472
  25.6 15.0 %copy-start.8 = (bf16[128,128]{1,0:T(8,128)(2,1)S(1)}, bf16[128,128]{1,0:T(8,128)(2,1)}, u32[]{:S(2)}) copy-start(bf16[128,128]{1,0:T(8,128)(2,1)} %refs_2_.1) | copy-start | bytes 98308
  25.6 10.7 %collective-permute-start = (bf16[8,64,128]{2,1,0:T(8,128)(2,1)S(1)}, bf16[8,64,128]{2,1,0:T(8,128)(2,1)S(1)}, u32[]{:S(2)}, u32[]{:S(2)}) collective-permute-start(bf16[8,64,128]{2,1,0:T(8,128)(2,1)S(1)} %get-tuple-element.137), channel_id=1, source_target_pairs={{0,16},{16,0},{1,17},{17,1},{2,18},{18,2},{3,19},{19,3},{4,20},{20... | collective-permute-start | bytes 393224 | tf_op jit(solution)/shard_map/ppermute | solution.py:477
  31.0 1.2 copy-start.14
  32.2 1.1 copy-start.16
  33.3 38.0 %copy-start.2 = (f32[4,128,512]{2,1,0:T(8,128)}, f32[4,128,512]{2,1,0:T(8,128)S(1)}, u32[]{:S(2)}) copy-start(f32[4,128,512]{2,1,0:T(8,128)S(1)} %get-tuple-element.73.refs_2_.refs_0_) | copy-start | bytes 3145732
  36.3 4.2 %collective-permute-start.1 = (bf16[2,8,64,128]{3,2,1,0:T(8,128)(2,1)S(1)}, bf16[2,8,64,128]{3,2,1,0:T(8,128)(2,1)S(1)}, u32[]{:S(2)}, u32[]{:S(2)}) collective-permute-start(bf16[2,8,64,128]{3,2,1,0:T(8,128)(2,1)S(1)} %pad_maximum_fusion.refs_5_), channel_id=1, source_target_pairs={{0,8},{8,0},{1,9},{9,1},{2,10},{10,2},{3,11},{11,3},{4,12},{12,4},... | collective-permute-start | bytes 786440 | tf_op jit(solution)/shard_map/ppermute | solution.py:40
  36.4 12.9 %collective-permute-start.3 = (bf16[2,8,64,128]{3,2,1,0:T(8,128)(2,1)S(1)}, bf16[2,8,64,128]{3,2,1,0:T(8,128)(2,1)S(1)}, u32[]{:S(2)}, u32[]{:S(2)}) collective-permute-start(bf16[2,8,64,128]{3,2,1,0:T(8,128)(2,1)S(1)} %pad_maximum_fusion.refs_5_), channel_id=1, source_target_pairs={{0,96},{32,0},{64,32},{96,64},{1,97},{33,1},{65,33},{97,65},{2,98}... | collective-permute-start | bytes 786440 | tf_op jit(solution)/shard_map/ppermute | solution.py:49
  40.5 9.6 %collective-permute-start.2 = (bf16[2,8,64,128]{3,2,1,0:T(8,128)(2,1)S(1)}, bf16[2,8,64,128]{3,2,1,0:T(8,128)(2,1)S(1)}, u32[]{:S(2)}, u32[]{:S(2)}) collective-permute-start(bf16[2,8,64,128]{3,2,1,0:T(8,128)(2,1)S(1)} %pad_maximum_fusion.refs_5_), channel_id=1, source_target_pairs={{0,32},{32,64},{64,96},{96,0},{1,33},{33,65},{65,97},{97,1},{2,34}... | collective-permute-start | bytes 786440 | tf_op jit(solution)/shard_map/ppermute | solution.py:49
  40.5 1.4 %copy-start.15 = (bf16[4,512,384]{2,1,0:T(8,128)(2,1)S(1)}, bf16[4,512,384]{2,1,0:T(8,128)(2,1)}, u32[]{:S(2)}) copy-start(bf16[4,512,384]{2,1,0:T(8,128)(2,1)} %copy-done.14) | copy-start | bytes 4718596
  50.1 3.6 %collective-permute-start.7 = (bf16[2,8,64,128]{3,2,1,0:T(8,128)(2,1)S(1)}, bf16[2,8,64,128]{3,2,1,0:T(8,128)(2,1)S(1)}, u32[]{:S(2)}, u32[]{:S(2)}) collective-permute-start(bf16[2,8,64,128]{3,2,1,0:T(8,128)(2,1)S(1)} %collective-permute-done.2.refs_5_), channel_id=1, source_target_pairs={{0,8},{8,0},{1,9},{9,1},{2,10},{10,2},{3,11},{11,3},{4,12},{12,4},... | collective-permute-start | bytes 786440 | tf_op jit(solution)/shard_map/ppermute | solution.py:40
  50.1 10.9 %collective-permute-start.5 = (bf16[8,64,128]{2,1,0:T(8,128)(2,1)S(1)}, bf16[8,64,128]{2,1,0:T(8,128)(2,1)S(1)}, u32[]{:S(2)}, u32[]{:S(2)}) collective-permute-start(bf16[8,64,128]{2,1,0:T(8,128)(2,1)S(1)} %slice_bitcast_fusion.1), channel_id=1, source_target_pairs={{0,32},{32,64},{64,96},{96,0},{1,33},{33,65},{65,97},{97,1},{2,34}... | collective-permute-start | bytes 393224 | tf_op jit(solution)/shard_map/ppermute | solution.py:49
  50.2 10.9 %collective-permute-start.4 = (bf16[2,8,64,128]{3,2,1,0:T(8,128)(2,1)S(1)}, bf16[2,8,64,128]{3,2,1,0:T(8,128)(2,1)S(1)}, u32[]{:S(2)}, u32[]{:S(2)}) collective-permute-start(bf16[2,8,64,128]{3,2,1,0:T(8,128)(2,1)S(1)} %collective-permute-done.3.refs_5_), channel_id=1, source_target_pairs={{0,8},{8,0},{1,9},{9,1},{2,10},{10,2},{3,11},{11,3},{4,12},{12,4},... | collective-permute-start | bytes 786440 | tf_op jit(solution)/shard_map/ppermute | solution.py:40
  50.8 10.3 %collective-permute-start.6 = (bf16[8,64,128]{2,1,0:T(8,128)(2,1)S(1)}, bf16[8,64,128]{2,1,0:T(8,128)(2,1)S(1)}, u32[]{:S(2)}, u32[]{:S(2)}) collective-permute-start(bf16[8,64,128]{2,1,0:T(8,128)(2,1)S(1)} %slice_bitcast_fusion), channel_id=1, source_target_pairs={{0,96},{32,0},{64,32},{96,64},{1,97},{33,1},{65,33},{97,65},{2,98}... | collective-permute-start | bytes 393224 | tf_op jit(solution)/shard_map/ppermute | solution.py:49
  53.7 15.9 %collective-permute-start.10 = (bf16[2,8,64,128]{3,2,1,0:T(8,128)(2,1)S(1)}, bf16[2,8,64,128]{3,2,1,0:T(8,128)(2,1)S(1)}, u32[]{:S(2)}, u32[]{:S(2)}) collective-permute-start(bf16[2,8,64,128]{3,2,1,0:T(8,128)(2,1)S(1)} %get-tuple-element.83), channel_id=1, source_target_pairs={{0,8},{8,0},{1,9},{9,1},{2,10},{10,2},{3,11},{11,3},{4,12},{12,4},... | collective-permute-start | bytes 786440 | tf_op jit(solution)/shard_map/ppermute | solution.py:40
  61.1 8.6 %collective-permute-start.8 = (bf16[1,8,64,128]{3,2,1,0:T(8,128)(2,1)S(1)}, bf16[1,8,64,128]{3,2,1,0:T(8,128)(2,1)S(1)}, u32[]{:S(2)}, u32[]{:S(2)}) collective-permute-start(bf16[1,8,64,128]{3,2,1,0:T(8,128)(2,1)S(1)} %bitcast.21), channel_id=1, source_target_pairs={{0,8},{8,0},{1,9},{9,1},{2,10},{10,2},{3,11},{11,3},{4,12},{12,4},... | collective-permute-start | bytes 393224 | tf_op jit(solution)/shard_map/ppermute | solution.py:40
  61.7 8.0 %collective-permute-start.9 = (bf16[1,8,64,128]{3,2,1,0:T(8,128)(2,1)S(1)}, bf16[1,8,64,128]{3,2,1,0:T(8,128)(2,1)S(1)}, u32[]{:S(2)}, u32[]{:S(2)}) collective-permute-start(bf16[1,8,64,128]{3,2,1,0:T(8,128)(2,1)S(1)} %bitcast.23), channel_id=1, source_target_pairs={{0,8},{8,0},{1,9},{9,1},{2,10},{10,2},{3,11},{11,3},{4,12},{12,4},... | collective-permute-start | bytes 393224 | tf_op jit(solution)/shard_map/ppermute | solution.py:40
  61.8 7.9 %collective-permute-start.11 = (bf16[2,8,64,128]{3,2,1,0:T(8,128)(2,1)S(1)}, bf16[2,8,64,128]{3,2,1,0:T(8,128)(2,1)S(1)}, u32[]{:S(2)}, u32[]{:S(2)}) collective-permute-start(bf16[2,8,64,128]{3,2,1,0:T(8,128)(2,1)S(1)} %get-tuple-element.84), channel_id=1, source_target_pairs={{0,8},{8,0},{1,9},{9,1},{2,10},{10,2},{3,11},{11,3},{4,12},{12,4},... | collective-permute-start | bytes 786440 | tf_op jit(solution)/shard_map/ppermute | solution.py:40
  69.5 10.1 %collective-permute-start.13 = (bf16[2,8,64,128]{3,2,1,0:T(8,128)(2,1)S(1)}, bf16[2,8,64,128]{3,2,1,0:T(8,128)(2,1)S(1)}, u32[]{:S(2)}, u32[]{:S(2)}) collective-permute-start(bf16[2,8,64,128]{3,2,1,0:T(8,128)(2,1)S(1)} %get-tuple-element.93), channel_id=1, source_target_pairs={{0,8},{8,0},{1,9},{9,1},{2,10},{10,2},{3,11},{11,3},{4,12},{12,4},... | collective-permute-start | bytes 786440 | tf_op jit(solution)/shard_map/ppermute | solution.py:40
  69.8 9.8 %collective-permute-start.12 = (bf16[2,8,64,128]{3,2,1,0:T(8,128)(2,1)S(1)}, bf16[2,8,64,128]{3,2,1,0:T(8,128)(2,1)S(1)}, u32[]{:S(2)}, u32[]{:S(2)}) collective-permute-start(bf16[2,8,64,128]{3,2,1,0:T(8,128)(2,1)S(1)} %add_convert_fusion.2), channel_id=1, source_target_pairs={{0,96},{32,0},{64,32},{96,64},{1,97},{33,1},{65,33},{97,65},{2,98}... | collective-permute-start | bytes 786440 | tf_op jit(solution)/shard_map/ppermute | solution.py:49
  78.6 0.8 copy-start.3
  79.4 1.5 %collective-permute-start.14 = (bf16[2,8,64,128]{3,2,1,0:T(8,128)(2,1)S(1)}, bf16[2,8,64,128]{3,2,1,0:T(8,128)(2,1)S(1)}, u32[]{:S(2)}, u32[]{:S(2)}) collective-permute-start(bf16[2,8,64,128]{3,2,1,0:T(8,128)(2,1)S(1)} %get-tuple-element.103), channel_id=1, source_target_pairs={{0,8},{8,0},{1,9},{9,1},{2,10},{10,2},{3,11},{11,3},{4,12},{12,4},... | collective-permute-start | bytes 786440 | tf_op jit(solution)/shard_map/ppermute | solution.py:40
  79.6 8.7 %copy-start.17 = (bf16[2,8,64,128]{3,2,1,0:T(8,128)(2,1)}, bf16[2,8,64,128]{3,2,1,0:T(8,128)(2,1)S(1)}, u32[]{:S(2)}) copy-start(bf16[2,8,64,128]{3,2,1,0:T(8,128)(2,1)S(1)} %collective-permute-done.12.refs_1_) | copy-start | bytes 786436
  81.0 15.3 %collective-permute-start.15 = (bf16[2,8,64,128]{3,2,1,0:T(8,128)(2,1)S(1)}, bf16[2,8,64,128]{3,2,1,0:T(8,128)(2,1)S(1)}, u32[]{:S(2)}, u32[]{:S(2)}) collective-permute-start(bf16[2,8,64,128]{3,2,1,0:T(8,128)(2,1)S(1)} %add_convert_fusion.1), channel_id=1, source_target_pairs={{0,32},{32,64},{64,96},{96,0},{1,33},{33,65},{65,97},{97,1},{2,34}... | collective-permute-start | bytes 786440 | tf_op jit(solution)/shard_map/ppermute | solution.py:49
  81.9 14.4 %collective-permute-start.16 = (bf16[2,8,64,128]{3,2,1,0:T(8,128)(2,1)S(1)}, bf16[2,8,64,128]{3,2,1,0:T(8,128)(2,1)S(1)}, u32[]{:S(2)}, u32[]{:S(2)}) collective-permute-start(bf16[2,8,64,128]{3,2,1,0:T(8,128)(2,1)S(1)} %add_convert_fusion), channel_id=1, source_target_pairs={{0,64},{32,96},{64,0},{96,32},{1,65},{33,97},{65,1},{97,33},{2,66}... | collective-permute-start | bytes 786440 | tf_op jit(solution)/shard_map/ppermute | solution.py:49
  96.3 0.7 copy-start.18
  97.0 0.7 copy-start.19
  99.6 4.9 %copy-start.25 = (bf16[4,64,128]{2,1,0:T(8,128)(2,1)S(1)}, bf16[4,64,128]{2,1,0:T(8,128)(2,1)}, u32[]{:S(2)}) copy-start(bf16[4,64,128]{2,1,0:T(8,128)(2,1)} %get-tuple-element.129) | copy-start | bytes 196612
  99.6 6.9 %copy-start.24 = (bf16[4,64,128]{2,1,0:T(8,128)(2,1)S(1)}, bf16[4,64,128]{2,1,0:T(8,128)(2,1)}, u32[]{:S(2)}) copy-start(bf16[4,64,128]{2,1,0:T(8,128)(2,1)} %get-tuple-element.130) | copy-start | bytes 196612
  99.6 8.9 %copy-start.23 = (bf16[4,64,128]{2,1,0:T(8,128)(2,1)S(1)}, bf16[4,64,128]{2,1,0:T(8,128)(2,1)}, u32[]{:S(2)}) copy-start(bf16[4,64,128]{2,1,0:T(8,128)(2,1)} %get-tuple-element.131) | copy-start | bytes 196612
  99.6 31.7 %copy-start.1 = (bf16[32,64,128]{2,1,0:T(8,128)(2,1)S(1)}, bf16[32,64,128]{2,1,0:T(8,128)(2,1)}, u32[]{:S(2)}) copy-start(bf16[32,64,128]{2,1,0:T(8,128)(2,1)} %pair_ref.3) | copy-start | bytes 1572868
  99.7 29.1 %all-to-all-start.2 = ((bf16[8,2,4,64,128]{4,3,2,1,0:T(8,128)(2,1)}), bf16[8,2,4,64,128]{4,3,2,1,0:T(8,128)(2,1)S(1)}, u32[]{:S(2)}, u32[]{:S(2)}) async-start(bf16[8,2,4,64,128]{4,3,2,1,0:T(8,128)(2,1)} %shard_map.119), calls=%async_computation.2 | async-start | bytes 2097152 | tf_op jit(solution)/shard_map/all_to_all | solution.py:525
  104.6 15.2 %collective-permute-start.17 = (bf16[4,64,128]{2,1,0:T(8,128)(2,1)S(1)}, bf16[4,64,128]{2,1,0:T(8,128)(2,1)S(1)}, u32[]{:S(2)}, u32[]{:S(2)}) collective-permute-start(bf16[4,64,128]{2,1,0:T(8,128)(2,1)S(1)} %copy-done.25), channel_id=1, source_target_pairs={{0,1},{1,0},{16,17},{17,16},{2,3},{3,2},{18,19},{19,18},{4,5},{5,4... | collective-permute-start | bytes 196616 | tf_op jit(solution)/shard_map/ppermute | solution.py:44
  106.6 14.1 %collective-permute-start.18 = (bf16[4,64,128]{2,1,0:T(8,128)(2,1)S(1)}, bf16[4,64,128]{2,1,0:T(8,128)(2,1)S(1)}, u32[]{:S(2)}, u32[]{:S(2)}) collective-permute-start(bf16[4,64,128]{2,1,0:T(8,128)(2,1)S(1)} %copy-done.24), channel_id=1, source_target_pairs={{0,16},{1,17},{16,0},{17,1},{2,18},{3,19},{18,2},{19,3},{4,20},{5,... | collective-permute-start | bytes 196616 | tf_op jit(solution)/shard_map/ppermute | solution.py:44
  108.6 12.1 %collective-permute-start.19 = (bf16[4,64,128]{2,1,0:T(8,128)(2,1)S(1)}, bf16[4,64,128]{2,1,0:T(8,128)(2,1)S(1)}, u32[]{:S(2)}, u32[]{:S(2)}) collective-permute-start(bf16[4,64,128]{2,1,0:T(8,128)(2,1)S(1)} %copy-done.23), channel_id=1, source_target_pairs={{0,17},{1,16},{16,1},{17,0},{2,19},{3,18},{18,3},{19,2},{4,21},{5,... | collective-permute-start | bytes 196616 | tf_op jit(solution)/shard_map/ppermute | solution.py:44
  119.8 0.9 copy-start.20
  120.7 0.6 copy-start.21
  120.7 0.6 copy-start.22
  122.9 6.7 %collective-permute-start.20 = (bf16[64,128]{1,0:T(8,128)(2,1)}, bf16[64,128]{1,0:T(8,128)(2,1)S(1)}, u32[]{:S(2)}, u32[]{:S(2)}) collective-permute-start(bf16[64,128]{1,0:T(8,128)(2,1)} %get-tuple-element.133), channel_id=1, source_target_pairs={{0,2},{2,4},{4,6},{6,0},{1,3},{3,5},{5,7},{7,1},{8,10},{10,12},{12... | collective-permute-start | bytes 49160 | tf_op jit(solution)/shard_map/ppermute | solution.py:49
  124.7 5.5 %collective-permute-start.21 = (bf16[64,128]{1,0:T(8,128)(2,1)}, bf16[64,128]{1,0:T(8,128)(2,1)S(1)}, u32[]{:S(2)}, u32[]{:S(2)}) collective-permute-start(bf16[64,128]{1,0:T(8,128)(2,1)} %get-tuple-element.134), channel_id=1, source_target_pairs={{0,4},{2,6},{4,0},{6,2},{1,5},{3,7},{5,1},{7,3},{8,12},{10,14},{12... | collective-permute-start | bytes 49160 | tf_op jit(solution)/shard_map/ppermute | solution.py:49
  127.4 3.9 %collective-permute-start.22 = (bf16[64,128]{1,0:T(8,128)(2,1)}, bf16[64,128]{1,0:T(8,128)(2,1)S(1)}, u32[]{:S(2)}, u32[]{:S(2)}) collective-permute-start(bf16[64,128]{1,0:T(8,128)(2,1)} %get-tuple-element.135), channel_id=1, source_target_pairs={{0,6},{2,0},{4,2},{6,4},{1,7},{3,1},{5,3},{7,5},{8,14},{10,8},{12,... | collective-permute-start | bytes 49160 | tf_op jit(solution)/shard_map/ppermute | solution.py:49
  131.3 0.7 copy-start.9

commit v6 on v5

--- a/solution.py
+++ b/solution.py
@@ -14,7 +14,8 @@
 F32 = jnp.float32
 BF16 = jnp.bfloat16
 LANES = 128
-PARAMS = pltpu.CompilerParams(vmem_limit_bytes=48 * 1024 * 1024)
+PARAMS = pltpu.CompilerParams(vmem_limit_bytes=24 * 1024 * 1024)
+FIRST = pltpu.CompilerParams(vmem_limit_bytes=60 * 1024 * 1024)
 
 
 def normalize(values, norm_gain, norm_shift):
@@ -40,10 +41,6 @@
     return lax.ppermute(a, "core", [(0, 1), (1, 0)])
 
 
-def cross(a, bits):
-    return lax.ppermute(a, ("xh", "xl"), [(s, s ^ bits) for s in range(4)])
-
-
 def shift(a, axis, by):
     size = lax.axis_size(axis)
     return lax.ppermute(a, axis, [(s, (s + by) % size) for s in range(size)])
@@ -60,9 +57,9 @@
 
 def spread_heads(w_ref, block):
     w = w_ref[...].astype(F32)
-    shape = (w.shape[0], block)
-    cols = [jnp.broadcast_to(w[:, h : h + 1], shape) for h in range(w.shape[1])]
-    return jnp.concatenate(cols, axis=1).astype(BF16)
+    shape = (block, w.shape[1])
+    rows = [jnp.broadcast_to(w[h : h + 1], shape) for h in range(w.shape[0])]
+    return jnp.concatenate(rows, axis=0).astype(BF16)
 
 
 def prep_kernel(pair_ref, gain_ref, shift_ref, w_ref, out_ref):
@@ -73,7 +70,7 @@
     out_ref[:, :own] = pair_ref[...].reshape(split)
     x = pair_ref[...].reshape(rows * block, channels).astype(F32)
     normed = normalize(x, gain_ref[...], shift_ref[...]).astype(BF16)
-    every = mm(normed, spread_heads(w_ref, block))
+    every = mm_nt(normed, spread_heads(w_ref, block))
     width = every.shape[1]
     keep = line_mask(block, width)
     lines = []
@@ -92,7 +89,7 @@
     return pl.pallas_call(
         prep_kernel,
         out_shape=out,
-        compiler_params=PARAMS,
+        compiler_params=FIRST,
         cost_estimate=pl.CostEstimate(
             flops=2**27, bytes_accessed=2**21, transcendentals=2**12
         ),
@@ -379,39 +376,28 @@
     )(gate, cot, w_o, *weights, *arrays)
 
 
-def arrange_x_kernel(*refs):
-    ins, outs = refs[:4], refs[4:]
+def join_kernel(mine_ref, theirs_ref, back_ref, ahead_ref, opp_ref, keep_ref, send_ref):
     xh = lax.axis_index("xh")
-    xl = lax.axis_index("xl")
-    for bits, out in enumerate(outs):
-        for y in range(out.shape[0]):
-            at = (xh ^ (bits >> 1), y * 2 + (xl ^ (bits & 1)))
-            out[y] = sum(ref[at].astype(F32) for ref in ins).astype(BF16)
-
-
-def arrange_y_kernel(*refs):
-    ins, outs = refs[:4], refs[4:]
-    size = ins[0].shape[0]
-    y = lax.axis_index("y")
-    for ahead, out in enumerate(outs):
-        at = lax.rem(y + ahead, size)
-        out[...] = sum(ref[at].astype(F32) for ref in ins).astype(BF16)
-
-
-def arrange(kernel, arrays, shape):
-    out = jax.ShapeDtypeStruct(shape, BF16)
+    refs = (mine_ref, theirs_ref, back_ref, ahead_ref, opp_ref)
+    for far, out in ((0, keep_ref), (1, send_ref)):
+        out[...] = sum(ref[xh ^ far].astype(F32) for ref in refs).astype(BF16)
+
+
+def join(arrays):
+    out = jax.ShapeDtypeStruct(arrays[0].shape[1:], BF16)
     return pl.pallas_call(
-        kernel,
-        out_shape=[out] * 4,
+        join_kernel,
+        out_shape=[out] * 2,
+        compiler_params=PARAMS,
         cost_estimate=pl.CostEstimate(flops=2**18, bytes_accessed=2**20, transcendentals=0),
     )(*arrays)
 
 
 def final_kernel(
-    pair_ref, both_ref, gain_ref, shift_ref, w_ref, g0_ref, g1_ref, g2_ref, g3_ref, out_ref
+    pair_ref, both_ref, gain_ref, shift_ref, w_ref, gb_ref, out_ref
 ):
     rows, block, channels = pair_ref.shape
-    tile = sum(ref[...].astype(F32) for ref in (g0_ref, g1_ref, g2_ref, g3_ref))
+    tile = jnp.sum(gb_ref[...].astype(F32), axis=0)
     tile = jnp.concatenate([tile[:rows], tile[rows:]], axis=1).astype(BF16).astype(F32)
     keep = line_mask(block, tile.shape[1])
     spread = jnp.concatenate(
@@ -422,7 +408,7 @@
         axis=0,
     )
     w_back = spread_heads(w_ref, block)
-    dn = both_ref[:, 1].reshape(rows * block, channels).astype(F32) + mm_nt(spread, w_back)
+    dn = both_ref[:, 1].reshape(rows * block, channels).astype(F32) + mm(spread, w_back)
     x = pair_ref[...].reshape(rows * block, channels).astype(F32)
     centred = x - jnp.mean(x, axis=-1, keepdims=True)
     rstd = lax.rsqrt(jnp.mean(centred * centred, axis=-1, keepdims=True) + EPSILON)
@@ -441,7 +427,7 @@
         cost_estimate=pl.CostEstimate(
             flops=2**27, bytes_accessed=2**21, transcendentals=2**12
         ),
-    )(pair, both, gain, shift_row, bias_weight, *gb)
+    )(pair, both, gain, shift_row, bias_weight, gb)
 
 
 def shards(
@@ -462,11 +448,12 @@
     own_i = rows_i // n_ja
     gain = norm_gain.reshape(1, channels)
     shift_row = norm_shift.reshape(1, channels)
+    bias_rows = bias_weight.T
     weights = (query_weight, key_weight, value_weight, gate_weight)
     tie = lax.optimization_barrier
 
     both = lax.all_to_all(
-        prep(pair, gain, shift_row, bias_weight, n_ja), JA, 0, 0, tiled=True
+        prep(pair, gain, shift_row, bias_rows, n_ja), JA, 0, 0, tiled=True
     )
     cotangent, both = tie((cotangent, both))
     cot = lax.all_to_all(
@@ -505,30 +492,25 @@
     opp0, opp1, opp_swap, theirs0, theirs1, dk[2] = tie(
         (opp0, opp1, opp_swap, theirs0, theirs1, dk[2])
     )
-    part0 = joined(mine0, theirs0)
     part1 = joined(mine1, theirs1)
     opp0, part1 = tie((opp0, part1))
     part1 = shift(part1, "z", 3)
     mine3, theirs3 = slice_of(2, [opp0, opp1], opp_swap)
     part1, theirs2, dk[3] = tie((part1, theirs2, dk[3]))
     part2 = joined(mine2, theirs2)
+    done = finish((0, 3, 1, 2), gate, cot, out_weight, weights, att, dq, dk, dv)
+    theirs3, done = tie((theirs3, done))
     part3 = joined(mine3, theirs3)
-    part2, part3, dk[3] = tie((part2, part3, dk[3]))
+    part2, part3, done = tie((part2, part3, done))
     part2, part3 = shift(part2, "z", 1), shift(part3, "z", 2)
-    done = finish((0, 3, 1, 2), gate, cot, out_weight, weights, att, dq, dk, dv)
-    part2, part3, done = tie((part2, part3, done))
-    total = [part0, part1, part2, part3]
-
-    slab = total[0].shape[2:]
-    by_x = list(arrange(arrange_x_kernel, total, (lax.axis_size("y"),) + slab))
-    by_x[1], done = tie((by_x[1], done))
+
+    keep, send = join([mine0, theirs0, part1, part2, part3])
     done = lax.all_to_all(done, JA, 0, 0, tiled=True)
-    by_x = [by_x[0]] + [cross(by_x[bits], bits) for bits in (1, 2, 3)]
-    by_y = arrange(arrange_y_kernel, by_x, slab)
-    by_y = [by_y[0]] + [shift(by_y[d], "y", d) for d in (1, 2, 3)]
+    gb = joined(keep, lax.ppermute(send, "xh", [(0, 1), (1, 0)]))
+    gb = lax.all_to_all(gb, JA, 0, 0, tiled=True)
 
     update = done[:, 0].reshape(pair.shape)
-    pair_grad = final(pair, done, gain, shift_row, bias_weight, by_y)
+    pair_grad = final(pair, done, gain, shift_row, bias_rows, gb)
     return (update, pair_grad)
 
 

time: 135 us -> 121 us (0.90)
  Pallas kernels: 43.2 us -> 36.3 us
  local copies, waits for them, and re-layouts: 11.4 us -> 6.08 us
    ppermute x3 -> x1, waiting for transfers between devices: 11.3 us -> 4.46 us  [shards(): gb = joined(keep, lax.ppermute(send, 'xh', [(0, 1), (1, 0)]))]
    all_to_all x0 -> x1, waiting for transfers between devices: none -> 5.87 us  [shards(): gb = lax.all_to_all(gb, JA, 0, 0, tiled=True)]
    all_to_all x0 -> x1, starting transfers between devices: none -> 5.34 us  [shards(): gb = lax.all_to_all(gb, JA, 0, 0, tiled=True)]
    unnamed x53 -> x28, local copies, waits for them, and re-layouts: 10.5 us -> 5.19 us
    pallas_call x4, Pallas kernels: 29.2 us -> 25.3 us  [attend(): pl.pallas_call(lambda *refs: attend_kernel(heads, ahead, len(own), *refs)...]
    ppermute x10 -> x7, starting transfers between devices: 16.4 us -> 13.4 us  [shift(): return lax.ppermute(a, axis, [(s, (s + by) % size) for s in range(size)])]
    ppermute x3 -> x1, starting transfers between devices: 4.78 us -> 2.09 us  [shards(): gb = joined(keep, lax.ppermute(send, 'xh', [(0, 1), (1, 0)]))]
    pallas_call x3 -> x2, Pallas kernels: 4.66 us -> 2.99 us  [the longest x1 2.83 us: prep(): pl.pallas_call(prep_kernel, out_shape=out, compiler_params=FIRST, cost_es...]
  transfers between devices with their start and end apart: 25 -> 21, of which waited for: 8 -> 7; matrix products, arithmetic and copies ran while one was open for 1% -> 1% of each run, Pallas kernels for 28% -> 26%
where the time goes in v6:
time: 121 us
  Pallas kernels  36.3 us (30%)
  starting transfers between devices  34.1 us (28%)
  waiting for transfers between devices  25.3 us (21%)
  blocking collectives  17.2 us (14%)
  local copies, waits for them, and re-layouts  6.08 us (5%)
    pallas_call x4, Pallas kernels, attend(): pl.pallas_call(lambda *refs: attend_kernel(heads, ahead, len(own), *refs)...  25.3 us
    all_to_all x1, blocking collectives, shards(): lax.all_to_all(prep(pair, gain, shift_row, bias_rows, n_ja), JA, 0, 0, ti...  17.2 us
    ppermute x7, starting transfers between devices, shift(): return lax.ppermute(a, axis, [(s, (s + by) % size) for s in range(size)])  13.4 us
    ppermute x7, waiting for transfers between devices, shift(): return lax.ppermute(a, axis, [(s, (s + by) % size) for s in range(size)])  12 us
    all_to_all x1, waiting for transfers between devices, shards(): gb = lax.all_to_all(gb, JA, 0, 0, tiled=True)  5.87 us
    all_to_all x1, starting transfers between devices, shards(): gb = lax.all_to_all(gb, JA, 0, 0, tiled=True)  5.34 us
    unnamed x28, local copies, waits for them, and re-layouts  5.19 us
    all_to_all x1, starting transfers between devices, shards(): done = lax.all_to_all(done, JA, 0, 0, tiled=True)  4.77 us
  transfers between devices with their start and end apart: 21, of which 7 were waited for; matrix products, arithmetic and copies ran while one was open for 1% of the time, Pallas kernels for 26%

profile of v6, /device:TPU:0, one launch (start us, length us, event | category | flops | bytes accessed | tf_op | source)
XLA Modules:
  0.0 120.8 jit_solution(8942799896815769021)
XLA Ops:
  0.6 2.8 %shard_map.113 = bf16[8,5,64,128]{3,2,1,0:T(8,128)(2,1)} custom-call(bf16[32,64,128]{2,1,0:T(8,128)(2,1)} %pair_ref.3, f32[1,128]{1,0:T(1,128)} %bitcast.18, f32[1,128]{1,0:T(1,128)} %bitcast.21, bf16[4,128]{1,0:T(4,128)(2,1)} %bitcast.16), custom_call_target="tpu_custom_call" | custom-call | flops 134217728 | bytes 2097152 | tf_op jit(solution)/shard_map/pallas_call | solution.py:89
  3.5 0.0 copy-start.7
  3.5 0.0 copy-start.8
  3.5 17.2 %all_to_all.20.pair_ref = bf16[8,5,64,128]{3,2,1,0:T(8,128)(2,1)S(1)} all-to-all(bf16[8,5,64,128]{3,2,1,0:T(8,128)(2,1)} %shard_map.113), channel_id=1, replica_groups=mesh['z'=4,'xh'=2,'core'=2,'y'=4,'xl'=2] {'y','xl'}, dimensions={0} | all-to-all | bytes 1310720 | tf_op jit(solution)/shard_map/all_to_all | solution.py:455
  20.7 3.5 %all-to-all-start.1 = ((bf16[8,4,64,128]{3,2,1,0:T(8,128)(2,1)}), bf16[8,4,64,128]{3,2,1,0:T(8,128)(2,1)S(1)}, u32[]{:S(2)}, u32[]{:S(2)}) async-start(bf16[8,4,64,128]{3,2,1,0:T(8,128)(2,1)} %bitcast.4), calls=%async_computation.1 | async-start | bytes 1048576 | tf_op jit(solution)/shard_map/all_to_all | solution.py:459
  24.3 0.0 copy-start.5
  24.3 2.8 %collective-permute-start = (bf16[8,64,128]{2,1,0:T(8,128)(2,1)S(1)}, bf16[8,64,128]{2,1,0:T(8,128)(2,1)S(1)}, u32[]{:S(2)}, u32[]{:S(2)}) collective-permute-start(bf16[8,64,128]{2,1,0:T(8,128)(2,1)S(1)} %get-tuple-element.119), channel_id=1, source_target_pairs={{0,16},{16,0},{1,17},{17,1},{2,18},{18,2},{3,19},{19,3},{4,20},{20... | collective-permute-start | bytes 393224 | tf_op jit(solution)/shard_map/ppermute | solution.py:464
  27.1 2.6 %shard_map.114 = (bf16[4,512,384]{2,1,0:T(8,128)(2,1)S(1)}, bf16[4,384,512]{2,1,0:T(8,128)(2,1)S(1)}, f32[4,128,512]{2,1,0:T(8,128)S(1)}) custom-call(bf16[8,5,64,128]{3,2,1,0:T(8,128)(2,1)S(1)} %all_to_all.20.pair_ref, f32[1,128]{1,0:T(1,128)S(1)} %bitcast.19, f32[1,128]{1,0:T(1,128)S(1)} %bitcast.22, bf16[128,128]{1,0:T(8,128)(2,1)S(1)} %copy-done.1, ...), custom_call_target="tpu_custom_call" | custom-call | flops 2147483648 | bytes 8388608 | tf_op jit(solution)/shard_map/pallas_call | solution.py:122
  29.7 1.2 copy-done.9
  30.9 1.2 copy-done.11
  32.0 2.9 %collective-permute-done = bf16[8,64,128]{2,1,0:T(8,128)(2,1)S(1)} collective-permute-done((bf16[8,64,128]{2,1,0:T(8,128)(2,1)S(1)}, bf16[8,64,128]{2,1,0:T(8,128)(2,1)S(1)}, u32[]{:S(2)}, u32[]{:S(2)}) %collective-permute-start) | collective-permute-done | bytes 131104 | tf_op jit(solution)/shard_map/ppermute | solution.py:464
  35.0 0.1 collective-permute-start.3
  35.1 4.1 %collective-permute-start.2 = (bf16[2,8,64,128]{3,2,1,0:T(8,128)(2,1)S(1)}, bf16[2,8,64,128]{3,2,1,0:T(8,128)(2,1)S(1)}, u32[]{:S(2)}, u32[]{:S(2)}) collective-permute-start(bf16[2,8,64,128]{3,2,1,0:T(8,128)(2,1)S(1)} %pad_maximum_fusion.refs_5_), channel_id=1, source_target_pairs={{0,96},{32,0},{64,32},{96,64},{1,97},{33,1},{65,33},{97,65},{2,98}... | collective-permute-start | bytes 786440 | tf_op jit(solution)/shard_map/ppermute | solution.py:46
  39.2 0.0 collective-permute-start.1
  39.2 0.0 collective-permute-done.3.refs_6_
  39.2 0.0 all-to-all-done.1.refs_3_.refs_1_
  39.3 1.4 %copy-done.10 = bf16[4,512,384]{2,1,0:T(8,128)(2,1)S(1)} copy-done((bf16[4,512,384]{2,1,0:T(8,128)(2,1)S(1)}, bf16[4,512,384]{2,1,0:T(8,128)(2,1)}, u32[]{:S(2)}) %copy-start.10) | copy-done | bytes 1572888
  40.7 1.4 %copy-done.12 = bf16[4,384,512]{2,1,0:T(8,128)(2,1)S(1)} copy-done((bf16[4,384,512]{2,1,0:T(8,128)(2,1)S(1)}, bf16[4,384,512]{2,1,0:T(8,128)(2,1)}, u32[]{:S(2)}) %copy-start.12) | copy-done | bytes 1572888
  42.1 6.3 %shard_map.115 = (f32[4,128,128]{2,1,0:T(8,128)S(1)}, bf16[4,128,128]{2,1,0:T(8,128)(2,1)S(1)}, bf16[4,512,128]{2,1,0:T(8,128)(2,1)S(1)}, bf16[4,512,128]{2,1,0:...) custom-call(bf16[4,512,384]{2,1,0:T(8,128)(2,1)S(1)} %copy-done.10, ...), custom_call_target="tpu_custom_call" | custom-call | flops 4294967296 | bytes 8388608 | tf_op jit(solution)/shard_map/pallas_call | solution.py:300
  48.4 0.0 collective-permute-done.2.refs_5_
  48.4 0.4 collective-permute-done.1.refs_5_
  48.8 0.0 collective-permute-start.7
  48.8 0.1 collective-permute-start.5
  48.9 0.6 collective-permute-start.4
  49.5 3.0 %collective-permute-start.6 = (bf16[8,64,128]{2,1,0:T(8,128)(2,1)S(1)}, bf16[8,64,128]{2,1,0:T(8,128)(2,1)S(1)}, u32[]{:S(2)}, u32[]{:S(2)}) collective-permute-start(bf16[8,64,128]{2,1,0:T(8,128)(2,1)S(1)} %slice_bitcast_fusion), channel_id=1, source_target_pairs={{0,96},{32,0},{64,32},{96,64},{1,97},{33,1},{65,33},{97,65},{2,98}... | collective-permute-start | bytes 393224 | tf_op jit(solution)/shard_map/ppermute | solution.py:46
  52.5 0.0 collective-permute-start.10
  52.5 0.0 collective-permute-done.7.refs_6_
  52.5 6.4 %shard_map.116 = (f32[4,128,128]{2,1,0:T(8,128)S(1)}, bf16[4,128,128]{2,1,0:T(8,128)(2,1)S(1)}, bf16[4,512,128]{2,1,0:T(8,128)(2,1)S(1)}, bf16[4,512,128]{2,1,0:...) custom-call(bf16[4,512,384]{2,1,0:T(8,128)(2,1)S(1)} %copy-done.10, ...), custom_call_target="tpu_custom_call" | custom-call | flops 4294967296 | bytes 8388608 | tf_op jit(solution)/shard_map/pallas_call | solution.py:300
  58.9 0.0 collective-permute-done.5
  58.9 0.0 collective-permute-done.6
  58.9 0.0 collective-permute-done.4.refs_6_
  58.9 0.6 collective-permute-start.8
  59.5 0.1 collective-permute-start.9
  59.6 0.4 collective-permute-start.11
  60.0 6.3 %shard_map.117 = (f32[4,128,128]{2,1,0:T(8,128)S(1)}, bf16[4,128,128]{2,1,0:T(8,128)(2,1)S(1)}, bf16[4,512,128]{2,1,0:T(8,128)(2,1)S(1)}, bf16[4,512,128]{2,1,0:...) custom-call(bf16[4,512,384]{2,1,0:T(8,128)(2,1)S(1)} %copy-done.10, ...), custom_call_target="tpu_custom_call" | custom-call | flops 4294967296 | bytes 8388608 | tf_op jit(solution)/shard_map/pallas_call | solution.py:300
  66.3 0.2 collective-permute-start.13
  66.5 0.0 collective-permute-done.10.theirs_ref
  66.5 0.0 collective-permute-done.8.refs_7_
  66.5 0.0 collective-permute-done.9.refs_8_
  66.5 0.0 collective-permute-done.11
  66.5 0.1 add_convert_fusion.2
  66.6 1.9 %collective-permute-start.12 = (bf16[2,8,64,128]{3,2,1,0:T(8,128)(2,1)S(1)}, bf16[2,8,64,128]{3,2,1,0:T(8,128)(2,1)S(1)}, u32[]{:S(2)}, u32[]{:S(2)}) collective-permute-start(bf16[2,8,64,128]{3,2,1,0:T(8,128)(2,1)S(1)} %add_convert_fusion.2), channel_id=1, source_target_pairs={{0,96},{32,0},{64,32},{96,64},{1,97},{33,1},{65,33},{97,65},{2,98}... | collective-permute-start | bytes 786440 | tf_op jit(solution)/shard_map/ppermute | solution.py:46
  68.5 6.3 %shard_map.118 = (f32[4,128,128]{2,1,0:T(8,128)S(1)}, bf16[4,128,128]{2,1,0:T(8,128)(2,1)S(1)}, bf16[4,512,128]{2,1,0:T(8,128)(2,1)S(1)}, bf16[4,512,128]{2,1,0:...) custom-call(bf16[4,512,384]{2,1,0:T(8,128)(2,1)S(1)} %copy-done.10, ...), custom_call_target="tpu_custom_call" | custom-call | flops 4294967296 | bytes 8388608 | tf_op jit(solution)/shard_map/pallas_call | solution.py:300
  74.8 0.2 collective-permute-start.14
  75.1 0.0 collective-permute-done.13
  75.1 0.4 collective-permute-done.12.back_ref
  75.5 3.2 %shard_map.119 = bf16[8,2,4,64,128]{4,3,2,1,0:T(8,128)(2,1)} custom-call(f32[4,128,512]{2,1,0:T(8,128)S(1)} %get-tuple-element.64.refs_2_.refs_0_, bf16[8,4,64,128]{3,2,1,0:T(8,128)(2,1)S(1)} %all-to-all-done.1.refs_3_.refs_1_, bf16[128,128]{1,0:T(8,128)(2,1)S(1)} %copy-done.5, bf16[128,128]{1,0:T(8,128)(2,1)S(1)} %copy-done.1, ...), custom_call_target="tpu_custom_call" | custom-call | flops 2147483648 | bytes 8388608 | tf_op jit(solution)/shard_map/pallas_call | solution.py:360
  78.7 0.0 collective-permute-done.14
  78.7 0.2 add_convert_fusion
  78.9 4.8 %all-to-all-start.2 = ((bf16[8,2,4,64,128]{4,3,2,1,0:T(8,128)(2,1)}), bf16[8,2,4,64,128]{4,3,2,1,0:T(8,128)(2,1)S(1)}, u32[]{:S(2)}, u32[]{:S(2)}) async-start(bf16[8,2,4,64,128]{4,3,2,1,0:T(8,128)(2,1)} %shard_map.119), calls=%async_computation.2 | async-start | bytes 2097152 | tf_op jit(solution)/shard_map/all_to_all | solution.py:508
  83.7 0.0 copy-start.6
  83.7 0.1 collective-permute-start.15
  83.8 4.3 %collective-permute-start.16 = (bf16[2,8,64,128]{3,2,1,0:T(8,128)(2,1)S(1)}, bf16[2,8,64,128]{3,2,1,0:T(8,128)(2,1)S(1)}, u32[]{:S(2)}, u32[]{:S(2)}) collective-permute-start(bf16[2,8,64,128]{3,2,1,0:T(8,128)(2,1)S(1)} %get-tuple-element.115), channel_id=1, source_target_pairs={{0,64},{32,96},{64,0},{96,32},{1,65},{33,97},{65,1},{97,33},{2,66}... | collective-permute-start | bytes 786440 | tf_op jit(solution)/shard_map/ppermute | solution.py:46
  88.1 5.6 %collective-permute-done.15.ahead_ref = bf16[2,8,64,128]{3,2,1,0:T(8,128)(2,1)S(1)} collective-permute-done((bf16[2,8,64,128]{3,2,1,0:T(8,128)(2,1)S(1)}, bf16[2,8,64,128]{3,2,1,0:T(8,128)(2,1)S(1)}, u32[]{:S(2)}, u32[]{:S(2)}) %collective-permute-start.15) | collective-permute-done | bytes 262176 | tf_op jit(solution)/shard_map/ppermute | solution.py:46
  93.7 5.5 %collective-permute-done.16.opp_ref = bf16[2,8,64,128]{3,2,1,0:T(8,128)(2,1)S(1)} collective-permute-done((bf16[2,8,64,128]{3,2,1,0:T(8,128)(2,1)S(1)}, bf16[2,8,64,128]{3,2,1,0:T(8,128)(2,1)S(1)}, u32[]{:S(2)}, u32[]{:S(2)}) %collective-permute-start.16) | collective-permute-done | bytes 262176 | tf_op jit(solution)/shard_map/ppermute | solution.py:46
  99.2 0.2 shard_map.120
  99.4 2.1 %collective-permute-start.17 = (bf16[8,64,128]{2,1,0:T(8,128)(2,1)S(1)}, bf16[8,64,128]{2,1,0:T(8,128)(2,1)S(1)}, u32[]{:S(2)}, u32[]{:S(2)}) collective-permute-start(bf16[8,64,128]{2,1,0:T(8,128)(2,1)S(1)} %get-tuple-element.117), channel_id=1, source_target_pairs={{0,16},{16,0},{1,17},{17,1},{2,18},{18,2},{3,19},{19,3},{4,20},{20... | collective-permute-start | bytes 393224 | tf_op jit(solution)/shard_map/ppermute | solution.py:509
  101.5 4.5 %collective-permute-done.17 = bf16[8,64,128]{2,1,0:T(8,128)(2,1)S(1)} collective-permute-done((bf16[8,64,128]{2,1,0:T(8,128)(2,1)S(1)}, bf16[8,64,128]{2,1,0:T(8,128)(2,1)S(1)}, u32[]{:S(2)}, u32[]{:S(2)}) %collective-permute-start.17) | collective-permute-done | bytes 131104 | tf_op jit(solution)/shard_map/ppermute | solution.py:509
  105.9 0.7 add_convert_fusion.3
  106.6 0.0 all-to-all-done.2.both_ref
  106.6 5.3 %all-to-all-start.3 = ((bf16[8,64,128]{2,1,0:T(8,128)(2,1)}), bf16[8,64,128]{2,1,0:T(8,128)(2,1)S(1)}, u32[]{:S(2)}, u32[]{:S(2)}) async-start(bf16[8,64,128]{2,1,0:T(8,128)(2,1)} %add_convert_fusion.3), calls=%async_computation.3 | async-start | bytes 262144 | tf_op jit(solution)/shard_map/all_to_all | solution.py:510
  112.0 0.8 slice.17
  112.8 5.9 %all-to-all-done.3.gb_ref = bf16[8,64,128]{2,1,0:T(8,128)(2,1)S(1)} async-done(((bf16[8,64,128]{2,1,0:T(8,128)(2,1)}), bf16[8,64,128]{2,1,0:T(8,128)(2,1)S(1)}, u32[]{:S(2)}, u32[]{:S(2)}) %all-to-all-start.3) | async-done | bytes 131104 | tf_op jit(solution)/shard_map/all_to_all | solution.py:510
  118.7 2.2 %shard_map.121 = f32[32,64,128]{2,1,0:T(8,128)} custom-call(bf16[32,64,128]{2,1,0:T(8,128)(2,1)S(1)} %copy-done, bf16[8,2,4,64,128]{4,3,2,1,0:T(8,128)(2,1)S(1)} %all-to-all-done.2.both_ref, f32[1,128]{1,0:T(1,128)S(1)} %bitcast.20, f32[1,128]{1,0:T(1,128)S(1)} %bitcast.23, bf16[4,128]{1,0:T(4,128)(2,1)S(1)} %bitcast.17, ...), custom_call_target="tpu_custom_call" | custom-call | flops 134217728 | bytes 2097152 | tf_op jit(solution)/shard_map/pallas_call | solution.py:423
  (24 shorter events, 0.1 us)
Async XLA Ops:
  3.5 23.6 %copy-start.1 = (bf16[128,128]{1,0:T(8,128)(2,1)S(1)}, bf16[128,128]{1,0:T(8,128)(2,1)}, u32[]{:S(2)}) copy-start(bf16[128,128]{1,0:T(8,128)(2,1)} %refs_3_.1) | copy-start | bytes 98308
  3.5 23.6 %copy-start.2 = (bf16[128,128]{1,0:T(8,128)(2,1)S(1)}, bf16[128,128]{1,0:T(8,128)(2,1)}, u32[]{:S(2)}) copy-start(bf16[128,128]{1,0:T(8,128)(2,1)} %refs_4_.9) | copy-start | bytes 98308
  3.5 23.6 %copy-start.3 = (bf16[128,128]{1,0:T(8,128)(2,1)S(1)}, bf16[128,128]{1,0:T(8,128)(2,1)}, u32[]{:S(2)}) copy-start(bf16[128,128]{1,0:T(8,128)(2,1)} %refs_5_.1) | copy-start | bytes 98308
  3.5 23.6 %copy-start.4 = (bf16[128,128]{1,0:T(8,128)(2,1)S(1)}, bf16[128,128]{1,0:T(8,128)(2,1)}, u32[]{:S(2)}) copy-start(bf16[128,128]{1,0:T(8,128)(2,1)} %refs_6_.1) | copy-start | bytes 98308
  3.5 23.6 %copy-start.7 = (f32[128]{0:T(128)S(1)}, f32[128]{0:T(128)}, u32[]{:S(2)}) copy-start(f32[128]{0:T(128)} %param.12) | copy-start | bytes 1540
  3.5 23.6 %copy-start.8 = (f32[128]{0:T(128)S(1)}, f32[128]{0:T(128)}, u32[]{:S(2)}) copy-start(f32[128]{0:T(128)} %param.13) | copy-start | bytes 1540
  20.7 18.5 %all-to-all-start.1 = ((bf16[8,4,64,128]{3,2,1,0:T(8,128)(2,1)}), bf16[8,4,64,128]{3,2,1,0:T(8,128)(2,1)S(1)}, u32[]{:S(2)}, u32[]{:S(2)}) async-start(bf16[8,4,64,128]{3,2,1,0:T(8,128)(2,1)} %bitcast.4), calls=%async_computation.1 | async-start | bytes 1048576 | tf_op jit(solution)/shard_map/all_to_all | solution.py:459
  24.3 15.0 %copy-start.5 = (bf16[128,128]{1,0:T(8,128)(2,1)S(1)}, bf16[128,128]{1,0:T(8,128)(2,1)}, u32[]{:S(2)}) copy-start(bf16[128,128]{1,0:T(8,128)(2,1)} %refs_2_.1) | copy-start | bytes 98308
  24.3 10.7 %collective-permute-start = (bf16[8,64,128]{2,1,0:T(8,128)(2,1)S(1)}, bf16[8,64,128]{2,1,0:T(8,128)(2,1)S(1)}, u32[]{:S(2)}, u32[]{:S(2)}) collective-permute-start(bf16[8,64,128]{2,1,0:T(8,128)(2,1)S(1)} %get-tuple-element.119), channel_id=1, source_target_pairs={{0,16},{16,0},{1,17},{17,1},{2,18},{18,2},{3,19},{19,3},{4,20},{20... | collective-permute-start | bytes 393224 | tf_op jit(solution)/shard_map/ppermute | solution.py:464
  29.7 1.2 copy-start.9
  30.9 1.2 copy-start.11
  35.0 4.2 %collective-permute-start.3 = (bf16[2,8,64,128]{3,2,1,0:T(8,128)(2,1)S(1)}, bf16[2,8,64,128]{3,2,1,0:T(8,128)(2,1)S(1)}, u32[]{:S(2)}, u32[]{:S(2)}) collective-permute-start(bf16[2,8,64,128]{3,2,1,0:T(8,128)(2,1)S(1)} %pad_maximum_fusion.refs_5_), channel_id=1, source_target_pairs={{0,8},{8,0},{1,9},{9,1},{2,10},{10,2},{3,11},{11,3},{4,12},{12,4},... | collective-permute-start | bytes 786440 | tf_op jit(solution)/shard_map/ppermute | solution.py:41
  35.1 13.3 %collective-permute-start.2 = (bf16[2,8,64,128]{3,2,1,0:T(8,128)(2,1)S(1)}, bf16[2,8,64,128]{3,2,1,0:T(8,128)(2,1)S(1)}, u32[]{:S(2)}, u32[]{:S(2)}) collective-permute-start(bf16[2,8,64,128]{3,2,1,0:T(8,128)(2,1)S(1)} %pad_maximum_fusion.refs_5_), channel_id=1, source_target_pairs={{0,96},{32,0},{64,32},{96,64},{1,97},{33,1},{65,33},{97,65},{2,98}... | collective-permute-start | bytes 786440 | tf_op jit(solution)/shard_map/ppermute | solution.py:46
  39.2 9.6 %collective-permute-start.1 = (bf16[2,8,64,128]{3,2,1,0:T(8,128)(2,1)S(1)}, bf16[2,8,64,128]{3,2,1,0:T(8,128)(2,1)S(1)}, u32[]{:S(2)}, u32[]{:S(2)}) collective-permute-start(bf16[2,8,64,128]{3,2,1,0:T(8,128)(2,1)S(1)} %pad_maximum_fusion.refs_5_), channel_id=1, source_target_pairs={{0,32},{32,64},{64,96},{96,0},{1,33},{33,65},{65,97},{97,1},{2,34}... | collective-permute-start | bytes 786440 | tf_op jit(solution)/shard_map/ppermute | solution.py:46
  39.2 1.4 %copy-start.10 = (bf16[4,512,384]{2,1,0:T(8,128)(2,1)S(1)}, bf16[4,512,384]{2,1,0:T(8,128)(2,1)}, u32[]{:S(2)}) copy-start(bf16[4,512,384]{2,1,0:T(8,128)(2,1)} %copy-done.9) | copy-start | bytes 4718596
  40.7 1.4 %copy-start.12 = (bf16[4,384,512]{2,1,0:T(8,128)(2,1)S(1)}, bf16[4,384,512]{2,1,0:T(8,128)(2,1)}, u32[]{:S(2)}) copy-start(bf16[4,384,512]{2,1,0:T(8,128)(2,1)} %copy-done.11) | copy-start | bytes 4718596
  42.1 10.4 %copy-start.13 = (bf16[4,384,512]{2,1,0:T(8,128)(2,1)S(1)}, bf16[4,384,512]{2,1,0:T(8,128)(2,1)}, u32[]{:S(2)}) copy-start(bf16[4,384,512]{2,1,0:T(8,128)(2,1)} %copy-done.11) | copy-start | bytes 4718596
  48.8 3.7 %collective-permute-start.7 = (bf16[2,8,64,128]{3,2,1,0:T(8,128)(2,1)S(1)}, bf16[2,8,64,128]{3,2,1,0:T(8,128)(2,1)S(1)}, u32[]{:S(2)}, u32[]{:S(2)}) collective-permute-start(bf16[2,8,64,128]{3,2,1,0:T(8,128)(2,1)S(1)} %collective-permute-done.1.refs_5_), channel_id=1, source_target_pairs={{0,8},{8,0},{1,9},{9,1},{2,10},{10,2},{3,11},{11,3},{4,12},{12,4},... | collective-permute-start | bytes 786440 | tf_op jit(solution)/shard_map/ppermute | solution.py:41
  48.8 10.0 %collective-permute-start.5 = (bf16[8,64,128]{2,1,0:T(8,128)(2,1)S(1)}, bf16[8,64,128]{2,1,0:T(8,128)(2,1)S(1)}, u32[]{:S(2)}, u32[]{:S(2)}) collective-permute-start(bf16[8,64,128]{2,1,0:T(8,128)(2,1)S(1)} %slice_bitcast_fusion.1), channel_id=1, source_target_pairs={{0,32},{32,64},{64,96},{96,0},{1,33},{33,65},{65,97},{97,1},{2,34}... | collective-permute-start | bytes 393224 | tf_op jit(solution)/shard_map/ppermute | solution.py:46
  48.9 10.0 %collective-permute-start.4 = (bf16[2,8,64,128]{3,2,1,0:T(8,128)(2,1)S(1)}, bf16[2,8,64,128]{3,2,1,0:T(8,128)(2,1)S(1)}, u32[]{:S(2)}, u32[]{:S(2)}) collective-permute-start(bf16[2,8,64,128]{3,2,1,0:T(8,128)(2,1)S(1)} %collective-permute-done.2.refs_5_), channel_id=1, source_target_pairs={{0,8},{8,0},{1,9},{9,1},{2,10},{10,2},{3,11},{11,3},{4,12},{12,4},... | collective-permute-start | bytes 786440 | tf_op jit(solution)/shard_map/ppermute | solution.py:41
  49.5 9.4 %collective-permute-start.6 = (bf16[8,64,128]{2,1,0:T(8,128)(2,1)S(1)}, bf16[8,64,128]{2,1,0:T(8,128)(2,1)S(1)}, u32[]{:S(2)}, u32[]{:S(2)}) collective-permute-start(bf16[8,64,128]{2,1,0:T(8,128)(2,1)S(1)} %slice_bitcast_fusion), channel_id=1, source_target_pairs={{0,96},{32,0},{64,32},{96,64},{1,97},{33,1},{65,33},{97,65},{2,98}... | collective-permute-start | bytes 393224 | tf_op jit(solution)/shard_map/ppermute | solution.py:46
  52.5 14.0 %collective-permute-start.10 = (bf16[2,8,64,128]{3,2,1,0:T(8,128)(2,1)S(1)}, bf16[2,8,64,128]{3,2,1,0:T(8,128)(2,1)S(1)}, u32[]{:S(2)}, u32[]{:S(2)}) collective-permute-start(bf16[2,8,64,128]{3,2,1,0:T(8,128)(2,1)S(1)} %get-tuple-element.76), channel_id=1, source_target_pairs={{0,8},{8,0},{1,9},{9,1},{2,10},{10,2},{3,11},{11,3},{4,12},{12,4},... | collective-permute-start | bytes 786440 | tf_op jit(solution)/shard_map/ppermute | solution.py:41
  58.9 7.6 %collective-permute-start.8 = (bf16[1,8,64,128]{3,2,1,0:T(8,128)(2,1)S(1)}, bf16[1,8,64,128]{3,2,1,0:T(8,128)(2,1)S(1)}, u32[]{:S(2)}, u32[]{:S(2)}) collective-permute-start(bf16[1,8,64,128]{3,2,1,0:T(8,128)(2,1)S(1)} %bitcast.24), channel_id=1, source_target_pairs={{0,8},{8,0},{1,9},{9,1},{2,10},{10,2},{3,11},{11,3},{4,12},{12,4},... | collective-permute-start | bytes 393224 | tf_op jit(solution)/shard_map/ppermute | solution.py:41
  59.5 7.0 %collective-permute-start.9 = (bf16[1,8,64,128]{3,2,1,0:T(8,128)(2,1)S(1)}, bf16[1,8,64,128]{3,2,1,0:T(8,128)(2,1)S(1)}, u32[]{:S(2)}, u32[]{:S(2)}) collective-permute-start(bf16[1,8,64,128]{3,2,1,0:T(8,128)(2,1)S(1)} %bitcast.26), channel_id=1, source_target_pairs={{0,8},{8,0},{1,9},{9,1},{2,10},{10,2},{3,11},{11,3},{4,12},{12,4},... | collective-permute-start | bytes 393224 | tf_op jit(solution)/shard_map/ppermute | solution.py:41
  59.6 7.0 %collective-permute-start.11 = (bf16[2,8,64,128]{3,2,1,0:T(8,128)(2,1)S(1)}, bf16[2,8,64,128]{3,2,1,0:T(8,128)(2,1)S(1)}, u32[]{:S(2)}, u32[]{:S(2)}) collective-permute-start(bf16[2,8,64,128]{3,2,1,0:T(8,128)(2,1)S(1)} %get-tuple-element.77), channel_id=1, source_target_pairs={{0,8},{8,0},{1,9},{9,1},{2,10},{10,2},{3,11},{11,3},{4,12},{12,4},... | collective-permute-start | bytes 786440 | tf_op jit(solution)/shard_map/ppermute | solution.py:41
  66.3 8.7 %collective-permute-start.13 = (bf16[2,8,64,128]{3,2,1,0:T(8,128)(2,1)S(1)}, bf16[2,8,64,128]{3,2,1,0:T(8,128)(2,1)S(1)}, u32[]{:S(2)}, u32[]{:S(2)}) collective-permute-start(bf16[2,8,64,128]{3,2,1,0:T(8,128)(2,1)S(1)} %get-tuple-element.83), channel_id=1, source_target_pairs={{0,8},{8,0},{1,9},{9,1},{2,10},{10,2},{3,11},{11,3},{4,12},{12,4},... | collective-permute-start | bytes 786440 | tf_op jit(solution)/shard_map/ppermute | solution.py:41
  66.6 8.9 %collective-permute-start.12 = (bf16[2,8,64,128]{3,2,1,0:T(8,128)(2,1)S(1)}, bf16[2,8,64,128]{3,2,1,0:T(8,128)(2,1)S(1)}, u32[]{:S(2)}, u32[]{:S(2)}) collective-permute-start(bf16[2,8,64,128]{3,2,1,0:T(8,128)(2,1)S(1)} %add_convert_fusion.2), channel_id=1, source_target_pairs={{0,96},{32,0},{64,32},{96,64},{1,97},{33,1},{65,33},{97,65},{2,98}... | collective-permute-start | bytes 786440 | tf_op jit(solution)/shard_map/ppermute | solution.py:46
  74.8 3.9 %collective-permute-start.14 = (bf16[2,8,64,128]{3,2,1,0:T(8,128)(2,1)S(1)}, bf16[2,8,64,128]{3,2,1,0:T(8,128)(2,1)S(1)}, u32[]{:S(2)}, u32[]{:S(2)}) collective-permute-start(bf16[2,8,64,128]{3,2,1,0:T(8,128)(2,1)S(1)} %get-tuple-element.91), channel_id=1, source_target_pairs={{0,8},{8,0},{1,9},{9,1},{2,10},{10,2},{3,11},{11,3},{4,12},{12,4},... | collective-permute-start | bytes 786440 | tf_op jit(solution)/shard_map/ppermute | solution.py:41
  78.9 27.7 %all-to-all-start.2 = ((bf16[8,2,4,64,128]{4,3,2,1,0:T(8,128)(2,1)}), bf16[8,2,4,64,128]{4,3,2,1,0:T(8,128)(2,1)S(1)}, u32[]{:S(2)}, u32[]{:S(2)}) async-start(bf16[8,2,4,64,128]{4,3,2,1,0:T(8,128)(2,1)} %shard_map.119), calls=%async_computation.2 | async-start | bytes 2097152 | tf_op jit(solution)/shard_map/all_to_all | solution.py:508
  83.7 35.0 %copy-start = (bf16[32,64,128]{2,1,0:T(8,128)(2,1)S(1)}, bf16[32,64,128]{2,1,0:T(8,128)(2,1)}, u32[]{:S(2)}) copy-start(bf16[32,64,128]{2,1,0:T(8,128)(2,1)} %pair_ref.3) | copy-start | bytes 1572868
  83.7 35.0 %copy-start.6 = (bf16[128,4]{0,1:T(4,128)(2,1)S(1)}, bf16[128,4]{0,1:T(4,128)(2,1)}, u32[]{:S(2)}) copy-start(bf16[128,4]{0,1:T(4,128)(2,1)} %param.18) | copy-start | bytes 3076
  83.7 10.0 %collective-permute-start.15 = (bf16[2,8,64,128]{3,2,1,0:T(8,128)(2,1)S(1)}, bf16[2,8,64,128]{3,2,1,0:T(8,128)(2,1)S(1)}, u32[]{:S(2)}, u32[]{:S(2)}) collective-permute-start(bf16[2,8,64,128]{3,2,1,0:T(8,128)(2,1)S(1)} %get-tuple-element.114), channel_id=1, source_target_pairs={{0,32},{32,64},{64,96},{96,0},{1,33},{33,65},{65,97},{97,1},{2,34}... | collective-permute-start | bytes 786440 | tf_op jit(solution)/shard_map/ppermute | solution.py:46
  83.8 15.5 %collective-permute-start.16 = (bf16[2,8,64,128]{3,2,1,0:T(8,128)(2,1)S(1)}, bf16[2,8,64,128]{3,2,1,0:T(8,128)(2,1)S(1)}, u32[]{:S(2)}, u32[]{:S(2)}) collective-permute-start(bf16[2,8,64,128]{3,2,1,0:T(8,128)(2,1)S(1)} %get-tuple-element.115), channel_id=1, source_target_pairs={{0,64},{32,96},{64,0},{96,32},{1,65},{33,97},{65,1},{97,33},{2,66}... | collective-permute-start | bytes 786440 | tf_op jit(solution)/shard_map/ppermute | solution.py:46
  99.4 6.6 %collective-permute-start.17 = (bf16[8,64,128]{2,1,0:T(8,128)(2,1)S(1)}, bf16[8,64,128]{2,1,0:T(8,128)(2,1)S(1)}, u32[]{:S(2)}, u32[]{:S(2)}) collective-permute-start(bf16[8,64,128]{2,1,0:T(8,128)(2,1)S(1)} %get-tuple-element.117), channel_id=1, source_target_pairs={{0,16},{16,0},{1,17},{17,1},{2,18},{18,2},{3,19},{19,3},{4,20},{20... | collective-permute-start | bytes 393224 | tf_op jit(solution)/shard_map/ppermute | solution.py:509
  106.6 12.0 %all-to-all-start.3 = ((bf16[8,64,128]{2,1,0:T(8,128)(2,1)}), bf16[8,64,128]{2,1,0:T(8,128)(2,1)S(1)}, u32[]{:S(2)}, u32[]{:S(2)}) async-start(bf16[8,64,128]{2,1,0:T(8,128)(2,1)} %add_convert_fusion.3), calls=%async_computation.3 | async-start | bytes 262144 | tf_op jit(solution)/shard_map/all_to_all | solution.py:510

commit v7 on v6

--- a/solution.py
+++ b/solution.py
@@ -46,6 +46,10 @@
     return lax.ppermute(a, axis, [(s, (s + by) % size) for s in range(size)])
 
 
+def in_hbm(*arrays):
+    return [pltpu.with_memory_space_constraint(a, pltpu.HBM) for a in arrays]
+
+
 def whole(a):
     return pl.BlockSpec(a.shape, lambda *_: (0,) * len(a.shape))
 
@@ -62,12 +66,13 @@
     return jnp.concatenate(rows, axis=0).astype(BF16)
 
 
-def prep_kernel(pair_ref, gain_ref, shift_ref, w_ref, out_ref):
+def prep_kernel(pair_ref, cot_ref, gain_ref, shift_ref, w_ref, out_ref):
     rows, block, channels = pair_ref.shape
     n_ja = out_ref.shape[0]
     own = rows // n_ja
     split = (n_ja, own, block, channels)
     out_ref[:, :own] = pair_ref[...].reshape(split)
+    out_ref[:, own : 2 * own] = cot_ref[...].reshape(split)
     x = pair_ref[...].reshape(rows * block, channels).astype(F32)
     normed = normalize(x, gain_ref[...], shift_ref[...]).astype(BF16)
     every = mm_nt(normed, spread_heads(w_ref, block))
@@ -80,12 +85,12 @@
     tile = jnp.concatenate(lines, axis=0).astype(BF16)
     tile = jnp.concatenate([tile[:, :LANES], tile[:, LANES:]], axis=0)
     for d in range(n_ja):
-        out_ref[d, own] = tile
-
-
-def prep(pair, gain, shift_row, bias_weight, n_ja):
+        out_ref[d, 2 * own] = tile
+
+
+def prep(pair, cot, gain, shift_row, bias_weight, n_ja):
     rows, block, channels = pair.shape
-    out = jax.ShapeDtypeStruct((n_ja, rows // n_ja + 1, block, channels), BF16)
+    out = jax.ShapeDtypeStruct((n_ja, 2 * rows // n_ja + 1, block, channels), BF16)
     return pl.pallas_call(
         prep_kernel,
         out_shape=out,
@@ -93,11 +98,25 @@
         cost_estimate=pl.CostEstimate(
             flops=2**27, bytes_accessed=2**21, transcendentals=2**12
         ),
-    )(pair, gain, shift_row, bias_weight)
+    )(pair, cot, gain, shift_row, bias_weight)
 
 
 def project_kernel(
-    pair_ref, gain_ref, shift_ref, w_q_ref, w_k_ref, w_v_ref, w_g_ref, out_n_ref, out_t_ref, gate_ref
+    pair_ref,
+    cot_ref,
+    gain_ref,
+    shift_ref,
+    w_o_ref,
+    w_q_ref,
+    w_k_ref,
+    w_v_ref,
+    w_g_ref,
+    kv_n_ref,
+    kv_t_ref,
+    q_n_ref,
+    q_t_ref,
+    d_att_ref,
+    gate_ref,
 ):
     n_blocks, _, block, channels = pair_ref.shape
     n = n_blocks * block
@@ -105,34 +124,58 @@
     x = pair_ref[...].reshape(n, channels).astype(F32)
     normed = normalize(x, gain_ref[...], shift_ref[...]).astype(BF16)
     weights = [ref[...] for ref in (w_q_ref, w_k_ref, w_v_ref, w_g_ref)]
-    out_n_ref[0] = mm(normed, jnp.concatenate(weights[:3], axis=1)).astype(BF16)
+    proj = mm(normed, jnp.concatenate(weights[:3], axis=1)).astype(BF16)
+    kv_n_ref[0] = proj[:, inner:]
     proj_t = mm_nt(jnp.concatenate([w.T for w in weights], axis=0), normed)
-    out_t_ref[0] = proj_t[: 3 * inner].astype(BF16)
-    gate_ref[0] = jax.nn.sigmoid(proj_t[3 * inner :])
-
-
-def project(both, gain, shift_row, weights):
+    kv_t_ref[0] = proj_t[inner : 3 * inner].astype(BF16)
+    gate = jax.nn.sigmoid(proj_t[3 * inner :])
+    gate_ref[0] = gate
+    d_att = mm_nt(w_o_ref[...], cot_ref[...].reshape(n, channels)) * gate
+    size = lax.axis_size("z")
+    z = lax.axis_index("z")
+    for owner in range(n // LANES):
+        at = slice(owner * LANES, (owner + 1) * LANES)
+        ahead = lax.rem(owner + size - z, size)
+        q_n_ref[ahead, 0] = proj[at, :inner]
+        q_t_ref[ahead, 0] = proj_t[:inner, at].astype(BF16)
+        d_att_ref[ahead, 0] = d_att[:, at]
+
+
+def project(both, gain, shift_row, w_o, weights):
     n_blocks, slabs, block, channels = both.shape
-    rows = slabs - 1
+    rows = slabs // 2
     n = n_blocks * block
-    inner = weights[0].shape[1]
-    out_n = jax.ShapeDtypeStruct((rows, n, 3 * inner), BF16)
-    out_t = jax.ShapeDtypeStruct((rows, 3 * inner, n), BF16)
-    gate = jax.ShapeDtypeStruct((rows, inner, n), F32)
+    inner = w_o.shape[0]
+    kv_n = pltpu.HBM((rows, n, 2 * inner), BF16)
+    kv_t = pltpu.HBM((rows, 2 * inner, n), BF16)
+    gate = pltpu.HBM((rows, inner, n), F32)
+    q_n = pltpu.HBM((n // LANES, rows, LANES, inner), BF16)
+    q_t = pltpu.HBM((n // LANES, rows, inner, LANES), BF16)
+    d_att = pltpu.HBM((n // LANES, rows, inner, LANES), F32)
+
+    def by_row(a):
+        return pl.BlockSpec((1,) + a.shape[1:], lambda i: (i, 0, 0))
+
+    def sliced(a):
+        return pl.BlockSpec((a.shape[0], 1) + a.shape[2:], lambda i: (0, i, 0, 0))
+
     return pl.pallas_call(
         project_kernel,
         grid=(rows,),
-        in_specs=[pl.BlockSpec((n_blocks, 1, block, channels), lambda i: (0, i, 0, 0))]
-        + [whole(a) for a in (gain, shift_row, *weights)],
-        out_specs=[
-            pl.BlockSpec((1,) + a.shape[1:], lambda i: (i, 0, 0)) for a in (out_n, out_t, gate)
-        ],
-        out_shape=[out_n, out_t, gate],
+        in_specs=[
+            pl.BlockSpec((n_blocks, 1, block, channels), lambda i: (0, i, 0, 0)),
+            pl.BlockSpec((n_blocks, 1, block, channels), lambda i: (0, rows + i, 0, 0)),
+        ]
+        + [whole(a) for a in (gain, shift_row, w_o, *weights)],
+        out_specs=[by_row(kv_n), by_row(kv_t)]
+        + [sliced(a) for a in (q_n, q_t, d_att)]
+        + [by_row(gate)],
+        out_shape=[kv_n, kv_t, q_n, q_t, d_att, gate],
         compiler_params=PARAMS,
         cost_estimate=pl.CostEstimate(
             flops=2**31, bytes_accessed=8 * 2**20, transcendentals=2**18
         ),
-    )(both, gain, shift_row, *weights)
+    )(both, both, gain, shift_row, w_o, *weights)
 
 
 def z_lanes(ahead):
@@ -142,13 +185,12 @@
 
 def attend_kernel(
     heads,
-    ahead,
     n_own,
     n_ref,
     t_ref,
-    gate_ref,
-    cot_ref,
-    w_o_ref,
+    q_n_ref,
+    q_t_ref,
+    d_att_ref,
     *refs,
 ):
     bias_refs = refs[: n_own * 2]
@@ -156,7 +198,7 @@
     bias_s, gb_s, s_s, p_s, ds_s, tile_s, line_s = refs[n_own * 2 + 6 :]
     row = pl.program_id(0)
     n = n_ref.shape[1]
-    inner = n_ref.shape[2] // 3
+    inner = n_ref.shape[2] // 2
     head_dim = inner // heads
     scale = 1.0 / math.sqrt(head_dim)
     n_ja = tile_s.shape[0]
@@ -169,17 +211,17 @@
     @pl.when(row == 0)
     def _():
         for which in range(2):
-            far = 0
+            views = []
             for ref in bias_refs[which * n_own : (which + 1) * n_own]:
-                for e in range(ref.shape[0]):
-                    at = (xh ^ far) * 2 + (core ^ which)
-                    at = pl.ds(pl.multiple_of(at * rows_i, rows_i), rows_i)
-                    for owner in range(n_ja):
-                        for p in range(pairs):
-                            tile_s[owner, at, p * LANES : (p + 1) * LANES] = ref[
-                                e, owner, p * rows_i : (p + 1) * rows_i, :
-                            ]
-                    far += 1
+                views += [ref] if len(ref.shape) == 3 else [ref.at[e] for e in range(2)]
+            for far, ref in enumerate(views):
+                at = (xh ^ far) * 2 + (core ^ which)
+                at = pl.ds(pl.multiple_of(at * rows_i, rows_i), rows_i)
+                for owner in range(n_ja):
+                    for p in range(pairs):
+                        tile_s[owner, at, p * LANES : (p + 1) * LANES] = ref[
+                            owner, p * rows_i : (p + 1) * rows_i, :
+                        ]
         for owner in range(n_ja):
             for p in range(pairs):
                 t = tile_s[owner, :, p * LANES : (p + 1) * LANES].astype(F32).T * LOG2E
@@ -190,16 +232,12 @@
                     ] = t[e * block : (e + 1) * block]
         gb_s[...] = jnp.zeros_like(gb_s)
 
-    at = z_lanes(ahead)
     nil = jnp.zeros((), BF16)
     row_head = lax.broadcasted_iota(jnp.int32, (inner, LANES), 0) // head_dim
     lane_head = lax.broadcasted_iota(jnp.int32, (LANES, inner), 1) // head_dim
-    q_t = t_ref[0, :inner, at]
-    q_n = n_ref[0, at, :inner]
-    z = lax.rem(lax.axis_index("z") + ahead, lax.axis_size("z"))
-    span = LANES // block
-    cot = cot_ref[pl.ds(z * span, span), 0].reshape(LANES, cot_ref.shape[3])
-    d_att = mm_nt(w_o_ref[...], cot) * gate_ref[0, :, at]
+    q_n = q_n_ref[0, 0]
+    q_t = q_t_ref[0, 0]
+    d_att = d_att_ref[0, 0]
     q_row = jnp.concatenate([jnp.where(lane_head == h, q_n, nil) for h in range(heads)], 0)
     step = 16
     chunk = 128
@@ -213,7 +251,7 @@
         )
         top = jnp.full((8, wide), -jnp.inf, F32)
         for k in range(0, n, chunk):
-            t = mm(n_ref[0, k : k + chunk, inner : 2 * inner], q_blk) * (scale * LOG2E)
+            t = mm(n_ref[0, k : k + chunk, :inner], q_blk) * (scale * LOG2E)
             t = t + bias_s[k : k + chunk, cols]
             s_s[k : k + chunk, cols] = t
             for e in range(0, chunk, 8):
@@ -231,7 +269,7 @@
         first = 2 * p * head_dim
         rows = slice(first, first + 2 * head_dim)
         inv = invs[p]
-        att = mm(t_ref[0, 2 * inner + first : 2 * inner + first + 2 * head_dim, :], p_s[:, cols])
+        att = mm(t_ref[0, inner + first : inner + first + 2 * head_dim, :], p_s[:, cols])
         att = att * inv
         a_two = jnp.concatenate([d_att[rows], d_att[rows]], axis=1) * inv
         lane = lax.broadcasted_iota(jnp.int32, a_two.shape, 1) // LANES
@@ -249,11 +287,11 @@
         a_blk = jnp.concatenate(lead + [a_two] + tail, axis=0)
         a_rows.append(a_blk.T)
         for k in range(0, n, chunk):
-            dp = mm(n_ref[0, k : k + chunk, 2 * inner :], a_blk)
+            dp = mm(n_ref[0, k : k + chunk, inner:], a_blk)
             ds = s_s[k : k + chunk, cols] * (dp - diag)
             gb_s[k : k + chunk, cols] += ds
             ds_s[k : k + chunk, cols] = ds.astype(BF16)
-        dq = mm(t_ref[0, inner + first : inner + first + 2 * head_dim, :], ds_s[:, cols]) * scale
+        dq = mm(t_ref[0, first : first + 2 * head_dim, :], ds_s[:, cols]) * scale
         for e in range(2):
             h = 2 * p + e
             dq_ref[0, h * head_dim : (h + 1) * head_dim, :] = dq[
@@ -283,10 +321,10 @@
                         ]
 
 
-def attend(heads, ahead, by_n, by_t, gate, cot, w_o, own, other):
-    rows, n, _ = by_n.shape
-    inner = gate.shape[1]
-    n_ja, slab, _ = own[0].shape[1:]
+def attend(heads, ahead, projected, own, other):
+    rows, n, inner = projected[0].shape
+    inner = inner // 2
+    n_ja, slab, _ = own[0].shape[-3:]
     lines = heads * n // n_ja
     att = jax.ShapeDtypeStruct((rows, inner, LANES), F32)
     dq = jax.ShapeDtypeStruct((rows, inner, LANES), BF16)
@@ -296,11 +334,14 @@
     def by_row(a):
         return pl.BlockSpec((1,) + a.shape[1:], lambda i: (i, 0, 0))
 
-    cot_spec = pl.BlockSpec((cot.shape[0], 1) + cot.shape[2:], lambda i: (0, i, 0, 0))
-    return pl.pallas_call(
-        lambda *refs: attend_kernel(heads, ahead, len(own), *refs),
+    def sliced(a):
+        return pl.BlockSpec((1, 1) + a.shape[2:], lambda i: (ahead, i, 0, 0))
+
+    return pl.pallas_call(
+        lambda *refs: attend_kernel(heads, len(own), *refs),
         grid=(rows,),
-        in_specs=[by_row(by_n), by_row(by_t), by_row(gate), cot_spec, whole(w_o)]
+        in_specs=[by_row(a) for a in projected[:2]]
+        + [sliced(a) for a in projected[2:]]
         + [whole(a) for a in (*own, *other)],
         out_specs=[by_row(a) for a in (att, dq, grad, grad)] + [whole(gb)] * 2,
         out_shape=[att, dq, grad, grad, gb, gb],
@@ -317,7 +358,7 @@
         cost_estimate=pl.CostEstimate(
             flops=2**32, bytes_accessed=2**23, transcendentals=2**20
         ),
-    )(by_n, by_t, gate, cot, w_o, *own, *other)
+    )(*in_hbm(*projected), *own, *other)
 
 
 def finish_kernel(aheads, gate_ref, cot_ref, w_o_ref, w_q_ref, w_k_ref, w_v_ref, w_g_ref, *refs):
@@ -348,56 +389,77 @@
     out_ref[:, 1] = dn.astype(BF16).reshape(half)
 
 
-def finish(aheads, gate, cot, w_o, weights, att, dq, dk, dv):
-    n_blocks, rows, block, channels = cot.shape
-    inner = w_o.shape[0]
+def finish(aheads, gate, both, w_o, weights, att, dq, dk, dv):
+    n_blocks, _, block, channels = both.shape
+    rows, inner, _ = gate.shape
     arrays = (*att, *dq, *dk, *dv)
 
     def by_row(a):
         return pl.BlockSpec((1,) + a.shape[1:], lambda i: (i, 0, 0))
 
-    cot_spec = pl.BlockSpec((n_blocks, 1, block, channels), lambda i: (0, i, 0, 0))
+    cot_spec = pl.BlockSpec((n_blocks, 1, block, channels), lambda i: (0, rows + i, 0, 0))
     return pl.pallas_call(
         lambda *refs: finish_kernel(aheads, *refs),
         grid=(rows,),
         in_specs=[by_row(gate), cot_spec, whole(w_o)]
         + [whole(a) for a in weights]
         + [by_row(a) for a in arrays],
-        out_specs=pl.BlockSpec(
-            (n_blocks, 2, 1, block, channels), lambda i: (0, 0, i, 0, 0)
-        ),
-        out_shape=jax.ShapeDtypeStruct((n_blocks, 2, rows, block, channels), BF16),
+        out_specs=pl.BlockSpec((n_blocks, 2, block, channels), lambda i: (0, i, 0, 0)),
+        out_shape=jax.ShapeDtypeStruct((n_blocks, 2 * rows + 1, block, channels), BF16),
         scratch_shapes=[
             pltpu.VMEM((inner, n_blocks * block), F32),
             pltpu.VMEM((inner, n_blocks * block), BF16),
         ],
         compiler_params=PARAMS,
         cost_estimate=pl.CostEstimate(flops=2**31, bytes_accessed=2**23, transcendentals=0),
-    )(gate, cot, w_o, *weights, *arrays)
-
-
-def join_kernel(mine_ref, theirs_ref, back_ref, ahead_ref, opp_ref, keep_ref, send_ref):
+    )(*in_hbm(gate), both, w_o, *weights, *arrays)
+
+
+def halves_kernel(parts, *refs):
     xh = lax.axis_index("xh")
-    refs = (mine_ref, theirs_ref, back_ref, ahead_ref, opp_ref)
+    keep_ref, send_ref = refs[parts:]
     for far, out in ((0, keep_ref), (1, send_ref)):
-        out[...] = sum(ref[xh ^ far].astype(F32) for ref in refs).astype(BF16)
-
-
-def join(arrays):
+        out[...] = sum(ref[xh ^ far].astype(F32) for ref in refs[:parts]).astype(BF16)
+
+
+def halves(*arrays):
     out = jax.ShapeDtypeStruct(arrays[0].shape[1:], BF16)
     return pl.pallas_call(
-        join_kernel,
+        lambda *refs: halves_kernel(len(arrays), *refs),
         out_shape=[out] * 2,
         compiler_params=PARAMS,
         cost_estimate=pl.CostEstimate(flops=2**18, bytes_accessed=2**20, transcendentals=0),
     )(*arrays)
 
 
+def fill_kernel(done_ref, a_ref, b_ref, c_ref, d_ref, out_ref):
+    del done_ref
+    total = sum(ref[...].astype(F32) for ref in (a_ref, b_ref, c_ref, d_ref))
+    out_ref[:, 0] = total.astype(BF16)
+
+
+def fill(done, *parts):
+    n_ja, slabs, block, channels = done.shape
+    spec = pl.BlockSpec((n_ja, 1, block, channels), lambda i: (0, slabs - 1, 0, 0))
+    return pl.pallas_call(
+        fill_kernel,
+        grid=(1,),
+        in_specs=[pl.BlockSpec(memory_space=pl.ANY)] + [whole(a) for a in parts],
+        out_specs=spec,
+        out_shape=jax.ShapeDtypeStruct(done.shape, BF16),
+        input_output_aliases={0: 0},
+        compiler_params=PARAMS,
+        cost_estimate=pl.CostEstimate(flops=2**18, bytes_accessed=2**20, transcendentals=0),
+    )(done, *parts)
+
+
 def final_kernel(
-    pair_ref, both_ref, gain_ref, shift_ref, w_ref, gb_ref, out_ref
+    pair_ref, both_ref, gain_ref, shift_ref, w_ref, out_ref
 ):
     rows, block, channels = pair_ref.shape
-    tile = jnp.sum(gb_ref[...].astype(F32), axis=0)
+    n_ja = both_ref.shape[0]
+    own = rows // n_ja
+    tile = jnp.sum(both_ref[:, 2 * own].astype(F32), axis=0)
     tile = jnp.concatenate([tile[:rows], tile[rows:]], axis=1).astype(BF16).astype(F32)
     keep = line_mask(block, tile.shape[1])
     spread = jnp.concatenate(
@@ -408,7 +470,9 @@
         axis=0,
     )
     w_back = spread_heads(w_ref, block)
-    dn = both_ref[:, 1].reshape(rows * block, channels).astype(F32) + mm(spread, w_back)
+    dn = [both_ref[:, 2 * i + 1][:, None] for i in range(own)]
+    dn = jnp.concatenate(dn, axis=1).reshape(rows * block, channels).astype(F32)
+    dn = dn + mm(spread, w_back)
     x = pair_ref[...].reshape(rows * block, channels).astype(F32)
     centred = x - jnp.mean(x, axis=-1, keepdims=True)
     rstd = lax.rsqrt(jnp.mean(centred * centred, axis=-1, keepdims=True) + EPSILON)
@@ -419,7 +483,7 @@
     out_ref[...] = ((push - level - unit * along) * rstd).reshape(out_ref.shape)
 
 
-def final(pair, both, gain, shift_row, bias_weight, gb):
+def final(pair, both, gain, shift_row, bias_weight):
     return pl.pallas_call(
         final_kernel,
         out_shape=jax.ShapeDtypeStruct(pair.shape, F32),
@@ -427,7 +491,7 @@
         cost_estimate=pl.CostEstimate(
             flops=2**27, bytes_accessed=2**21, transcendentals=2**12
         ),
-    )(pair, both, gain, shift_row, bias_weight, gb)
+    )(pair, both, gain, shift_row, bias_weight)
 
 
 def shards(
@@ -453,64 +517,59 @@
     tie = lax.optimization_barrier
 
     both = lax.all_to_all(
-        prep(pair, gain, shift_row, bias_rows, n_ja), JA, 0, 0, tiled=True
+        prep(pair, cotangent, gain, shift_row, bias_rows, n_ja), JA, 0, 0, tiled=True
     )
-    cotangent, both = tie((cotangent, both))
-    cot = lax.all_to_all(
-        cotangent.reshape(n_ja, own_i, rows_j, channels), JA, 0, 0, tiled=True
-    )
-
-    near = both[:, own_i]
-    far = lax.ppermute(near, "xh", [(0, 1), (1, 0)])
-    by_n, by_t, gate = project(both, gain, shift_row, weights)
-    far, by_n = tie((far, by_n))
-    near = jnp.stack([near, far])
+
+    def cross(a, bits):
+        return lax.ppermute(a, ("xh", "core"), [(s, s ^ bits) for s in range(4)])
+
+    own = both[:, 2 * own_i]
+    far, own_swap, far_swap = cross(own, 2), cross(own, 1), cross(own, 3)
+    projected = project(both, gain, shift_row, out_weight, weights)
+    far, own_swap, far_swap, projected = tie((far, own_swap, far_swap, projected))
+    *projected, gate = projected
+    near = jnp.stack([own, far])
     prev, after = shift(near, "z", 1), shift(near, "z", 3)
-    att, dq, dk, dv, total = [], [], [], [], []
 
     def slice_of(ahead, own, other):
-        att_a, dq_a, dk_a, dv_a, mine, theirs = attend(
-            heads, ahead, by_n, by_t, gate, cot, out_weight, own, other
-        )
-        att.append(att_a)
-        dq.append(dq_a)
-        dk.append(dk_a)
-        dv.append(dv_a)
-        return mine, swap(theirs)
-
-    def joined(mine, theirs):
-        return (mine.astype(F32) + theirs.astype(F32)).astype(BF16)
-
-    mine0, theirs0 = slice_of(0, [near], [swap(near)])
-    prev, after, dk[0] = tie((prev, after, dk[0]))
-    opp0, opp1 = shift(prev[0], "z", 1)[None], shift(after[1], "z", 3)[None]
-    mine1, theirs1 = slice_of(3, [prev], [swap(prev)])
-    after_swap = swap(after)
-    after, after_swap, opp0, opp1, dk[1] = tie((after, after_swap, opp0, opp1, dk[1]))
-    mine2, theirs2 = slice_of(1, [after], [after_swap])
-    opp_swap = [swap(opp0), swap(opp1)]
-    opp0, opp1, opp_swap, theirs0, theirs1, dk[2] = tie(
-        (opp0, opp1, opp_swap, theirs0, theirs1, dk[2])
-    )
-    part1 = joined(mine1, theirs1)
-    opp0, part1 = tie((opp0, part1))
-    part1 = shift(part1, "z", 3)
-    mine3, theirs3 = slice_of(2, [opp0, opp1], opp_swap)
-    part1, theirs2, dk[3] = tie((part1, theirs2, dk[3]))
-    part2 = joined(mine2, theirs2)
-    done = finish((0, 3, 1, 2), gate, cot, out_weight, weights, att, dq, dk, dv)
-    theirs3, done = tie((theirs3, done))
-    part3 = joined(mine3, theirs3)
-    part2, part3, done = tie((part2, part3, done))
-    part2, part3 = shift(part2, "z", 1), shift(part3, "z", 2)
-
-    keep, send = join([mine0, theirs0, part1, part2, part3])
+        return attend(heads, ahead, projected, own, other)
+
+    def joined(out, theirs):
+        return (out[4].astype(F32) + theirs.astype(F32)).astype(BF16)
+
+    out0 = slice_of(0, [own, far], [own_swap, far_swap])
+    out0, prev, after = tie((out0, prev, after))
+    opp0, opp1 = shift(prev[0], "z", 1), shift(after[1], "z", 3)
+    prev_swap, after_swap, theirs0 = swap(prev), swap(after), swap(out0[5])
+    out0, prev, prev_swap = tie((out0, prev, prev_swap))
+    out1 = slice_of(3, [prev], [prev_swap])
+    out1, opp0, opp1, after_swap, theirs0 = tie((out1, opp0, opp1, after_swap, theirs0))
+    opp0_swap, opp1_swap, theirs1 = swap(opp0), swap(opp1), swap(out1[5])
+    out2 = slice_of(1, [after], [after_swap])
+    out2, opp0_swap, opp1_swap, theirs1 = tie((out2, opp0_swap, opp1_swap, theirs1))
+    theirs2 = swap(out2[5])
+    part1 = joined(out1, theirs1)
+    theirs2, part1, opp0 = tie((theirs2, part1, opp0))
+    part2 = joined(out2, theirs2)
+    part2, opp0 = tie((part2, opp0))
+    part1, part2 = shift(part1, "z", 3), shift(part2, "z", 1)
+    out3 = slice_of(2, [opp0, opp1], [opp0_swap, opp1_swap])
+    out3, part1, part2 = tie((out3, part1, part2))
+    theirs3 = swap(out3[5])
+    keep, send = halves(out0[4], theirs0, part1, part2)
+    theirs3, keep, send = tie((theirs3, keep, send))
+    opp_keep, opp_send = halves(out3[4], theirs3)
+    flips = [(s, s ^ 5) for s in range(8)]
+    opp_keep = shift(opp_keep, "z", 2)
+    opp_send = lax.ppermute(opp_send, ("z", "xh"), flips)
+    send = lax.ppermute(send, "xh", [(0, 1), (1, 0)])
+    att, dq, dk, dv = zip(out0[:4], out1[:4], out2[:4], out3[:4])
+    done = finish((0, 3, 1, 2), gate, both, out_weight, weights, att, dq, dk, dv)
+    done, opp_keep, opp_send, send = tie((done, opp_keep, opp_send, send))
+    done = fill(done, keep, send, opp_keep, opp_send)
     done = lax.all_to_all(done, JA, 0, 0, tiled=True)
-    gb = joined(keep, lax.ppermute(send, "xh", [(0, 1), (1, 0)]))
-    gb = lax.all_to_all(gb, JA, 0, 0, tiled=True)
-
-    update = done[:, 0].reshape(pair.shape)
-    pair_grad = final(pair, done, gain, shift_row, bias_rows, gb)
+    update = jnp.stack([done[:, 2 * i] for i in range(own_i)], axis=1).reshape(pair.shape)
+    pair_grad = final(pair, done, gain, shift_row, bias_rows)
     return (update, pair_grad)
 
 

time: 121 us -> 117 us (0.967)
  blocking collectives: 17.2 us -> 42.2 us
  waiting for transfers between devices: 25.3 us -> 8.56 us
  starting transfers between devices: 34.1 us -> 22 us
  local copies, waits for them, and re-layouts: 6.08 us -> 0.35 us
  Pallas kernels: 36.3 us -> 41.8 us
    all_to_all x1 -> x2, blocking collectives: 17.2 us -> 42.2 us  [the longest x1 22.9 us: shards(): lax.all_to_all(prep(pair, cotangent, gain, shift_row, bias_rows, n_ja), J...]
    all_to_all x3 -> x0, starting transfers between devices: 13.6 us -> none  [the longest x1 5.34 us: shards(): gb = lax.all_to_all(gb, JA, 0, 0, tiled=True)]
    ppermute x7, waiting for transfers between devices: 12 us -> 1.26 us  [shift(): return lax.ppermute(a, axis, [(s, (s + by) % size) for s in range(size)])]
    all_to_all x3 -> x0, waiting for transfers between devices: 5.87 us -> none  [the longest x1 5.87 us: shards(): gb = lax.all_to_all(gb, JA, 0, 0, tiled=True)]
    unnamed x28 -> x18, local copies, waits for them, and re-layouts: 5.19 us -> 0.25 us
    pallas_call x5 -> x7, Pallas kernels: 25.5 us -> 28.7 us  [the longest x4 28.4 us: attend(): pl.pallas_call(lambda *refs: attend_kernel(heads, len(own), *refs), grid=...]
    ppermute x2 -> x5, starting transfers between devices: 4.9 us -> 7.99 us  [the longest x3 3.72 us: cross(): return lax.ppermute(a, ('xh', 'core'), [(s, s ^ bits) for s in range(4)])]
    ppermute x2 -> x5, waiting for transfers between devices: 7.41 us -> 4.55 us  [the longest x3 2.38 us: cross(): return lax.ppermute(a, ('xh', 'core'), [(s, s ^ bits) for s in range(4)])]
  transfers between devices with their start and end apart: 21 -> 20, of which waited for: 7 -> 5; matrix products, arithmetic and copies ran while one was open for 1% -> 0% of each run, Pallas kernels for 26% -> 31%
where the time goes in v7:
time: 117 us
  blocking collectives  42.2 us (36%)
  Pallas kernels  41.8 us (36%)
  starting transfers between devices  22 us (19%)
  waiting for transfers between devices  8.56 us (7%)
    pallas_call x4, Pallas kernels, attend(): pl.pallas_call(lambda *refs: attend_kernel(heads, len(own), *refs), grid=...  28.4 us
    all_to_all x1, blocking collectives, shards(): lax.all_to_all(prep(pair, cotangent, gain, shift_row, bias_rows, n_ja), J...  22.9 us
    all_to_all x1, blocking collectives, shards(): done = lax.all_to_all(done, JA, 0, 0, tiled=True)  19.4 us
    ppermute x7, starting transfers between devices, shift(): return lax.ppermute(a, axis, [(s, (s + by) % size) for s in range(size)])  12.1 us
    pallas_call x1, Pallas kernels, finish(): pl.pallas_call(lambda *refs: finish_kernel(aheads, *refs), grid=(rows,),...  3.86 us
    pallas_call x1, Pallas kernels, project(): pl.pallas_call(project_kernel, grid=(rows,), in_specs=[pl.BlockSpec((n_bl...  3.81 us
    ppermute x3, starting transfers between devices, cross(): return lax.ppermute(a, ('xh', 'core'), [(s, s ^ bits) for s in range(4)])  3.72 us
    pallas_call x1, Pallas kernels, prep(): pl.pallas_call(prep_kernel, out_shape=out, compiler_params=FIRST, cost_es...  3.19 us
  transfers between devices with their start and end apart: 20, of which 5 were waited for; matrix products, arithmetic and copies ran while one was open for 0% of the time, Pallas kernels for 31%

profile of v7, /device:TPU:0, one launch (start us, length us, event | category | flops | bytes accessed | tf_op | source)
XLA Modules:
  0.0 116.9 jit_solution(4837848224623622654)
XLA Ops:
  0.6 3.2 %shard_map.113 = bf16[8,9,64,128]{3,2,1,0:T(8,128)(2,1)} custom-call(bf16[32,64,128]{2,1,0:T(8,128)(2,1)} %pair_ref.3, bf16[32,64,128]{2,1,0:T(8,128)(2,1)} %cot_ref.1, f32[1,128]{1,0:T(1,128)} %bitcast.16, f32[1,128]{1,0:T(1,128)} %bitcast.19, bf16[4,128]{1,0:T(4,128)(2,1)} %bitcast.14), custom_call_target="tpu_custom_call" | custom-call | flops 134217728 | bytes 2097152 | tf_op jit(solution)/shard_map/pallas_call | solution.py:94
  3.8 0.0 copy-start.5
  3.8 0.0 copy-start.7
  3.9 0.0 copy-start.8
  3.9 22.9 %all_to_all.10.pair_ref.cot_ref.refs_1_ = bf16[8,9,64,128]{3,2,1,0:T(8,128)(2,1)S(1)} all-to-all(bf16[8,9,64,128]{3,2,1,0:T(8,128)(2,1)} %shard_map.113), channel_id=1, replica_groups=mesh['z'=4,'xh'=2,'core'=2,'y'=4,'xl'=2] {'y','xl'}, dimensions={0} | all-to-all | bytes 2359296 | tf_op jit(solution)/shard_map/all_to_all | solution.py:519
  26.8 1.1 collective-permute-start.2
  27.8 1.9 %collective-permute-start.1 = (bf16[8,64,128]{2,1,0:T(8,128)(2,1)S(1)}, bf16[8,64,128]{2,1,0:T(8,128)(2,1)S(1)}, u32[]{:S(2)}, u32[]{:S(2)}) collective-permute-start(bf16[8,64,128]{2,1,0:T(8,128)(2,1)S(1)} %get-tuple-element.201.refs_5_), channel_id=1, source_target_pairs={{0,8},{8,0},{16,24},{24,16},{1,9},{9,1},{17,25},{25,17},{2,10},{10... | collective-permute-start | bytes 393224 | tf_op jit(solution)/shard_map/ppermute | solution.py:524
  29.7 0.8 collective-permute-start
  30.5 0.0 copy-done.1
  30.5 0.0 copy-done.2
  30.5 0.0 copy-done.3
  30.5 0.0 copy-done.4
  30.5 3.8 %shard_map.114 = (bf16[4,512,256]{2,1,0:T(8,128)(2,1)}, bf16[4,256,512]{2,1,0:T(8,128)(2,1)}, bf16[4,4,128,128]{3,2,1,0:T(8,128)(2,1)}, bf16[4,4,128,128]{3,2,1,...) custom-call(bf16[8,9,64,128]{3,2,1,0:T(8,128)(2,1)S(1)} %all_to_all.10.pair_ref.cot_ref.refs_1_, ...), custom_call_target="tpu_custom_call" | custom-call | flops 2147483648 | bytes 8388608 | tf_op jit(solution)/shard_map/pallas_call | solution.py:162
  34.4 0.0 collective-permute-done.2.refs_8_
  34.4 0.0 collective-permute-done.1.refs_7_
  34.4 2.4 %collective-permute-done.refs_6_ = bf16[8,64,128]{2,1,0:T(8,128)(2,1)S(1)} collective-permute-done((bf16[8,64,128]{2,1,0:T(8,128)(2,1)S(1)}, bf16[8,64,128]{2,1,0:T(8,128)(2,1)S(1)}, u32[]{:S(2)}, u32[]{:S(2)}) %collective-permute-start) | collective-permute-done | bytes 131104 | tf_op jit(solution)/shard_map/ppermute | solution.py:524
  36.8 4.1 %collective-permute-start.4 = (bf16[2,8,64,128]{3,2,1,0:T(8,128)(2,1)S(1)}, bf16[2,8,64,128]{3,2,1,0:T(8,128)(2,1)S(1)}, u32[]{:S(2)}, u32[]{:S(2)}) collective-permute-start(bf16[2,8,64,128]{3,2,1,0:T(8,128)(2,1)S(1)} %pad_maximum_fusion.1), channel_id=1, source_target_pairs={{0,96},{32,0},{64,32},{96,64},{1,97},{33,1},{65,33},{97,65},{2,98}... | collective-permute-start | bytes 786440 | tf_op jit(solution)/shard_map/ppermute | solution.py:46
  40.9 0.0 collective-permute-start.3
  40.9 7.1 %shard_map.115 = (f32[4,128,128]{2,1,0:T(8,128)S(1)}, bf16[4,128,128]{2,1,0:T(8,128)(2,1)S(1)}, bf16[4,512,128]{2,1,0:T(8,128)(2,1)S(1)}, bf16[4,512,128]{2,1,0:...) custom-call(bf16[4,512,256]{2,1,0:T(8,128)(2,1)} %get-tuple-element.106.refs_0_, ...), custom_call_target="tpu_custom_call" | custom-call | flops 4294967296 | bytes 8388608 | tf_op jit(solution)/shard_map/pallas_call | solution.py:340
  48.0 0.0 collective-permute-done.4.refs_5_
  48.0 1.2 %collective-permute-done.3.refs_5_ = bf16[2,8,64,128]{3,2,1,0:T(8,128)(2,1)S(1)} collective-permute-done((bf16[2,8,64,128]{3,2,1,0:T(8,128)(2,1)S(1)}, bf16[2,8,64,128]{3,2,1,0:T(8,128)(2,1)S(1)}, u32[]{:S(2)}, u32[]{:S(2)}) %collective-permute-start.3) | collective-permute-done | bytes 262176 | tf_op jit(solution)/shard_map/ppermute | solution.py:46
  49.2 0.0 collective-permute-start.5
  49.3 0.6 collective-permute-start.8
  49.8 2.1 %collective-permute-start.7 = (bf16[8,64,128]{2,1,0:T(8,128)(2,1)S(1)}, bf16[8,64,128]{2,1,0:T(8,128)(2,1)S(1)}, u32[]{:S(2)}, u32[]{:S(2)}) collective-permute-start(bf16[8,64,128]{2,1,0:T(8,128)(2,1)S(1)} %slice_bitcast_fusion), channel_id=1, source_target_pairs={{0,96},{32,0},{64,32},{96,64},{1,97},{33,1},{65,33},{97,65},{2,98}... | collective-permute-start | bytes 393224 | tf_op jit(solution)/shard_map/ppermute | solution.py:46
  51.9 0.1 collective-permute-start.6
  52.0 0.1 collective-permute-start.9
  52.1 0.0 collective-permute-done.5.refs_6_
  52.1 7.1 %shard_map.116 = (f32[4,128,128]{2,1,0:T(8,128)S(1)}, bf16[4,128,128]{2,1,0:T(8,128)(2,1)S(1)}, bf16[4,512,128]{2,1,0:T(8,128)(2,1)S(1)}, bf16[4,512,128]{2,1,0:...) custom-call(bf16[4,512,256]{2,1,0:T(8,128)(2,1)} %get-tuple-element.106.refs_0_, ...), custom_call_target="tpu_custom_call" | custom-call | flops 4294967296 | bytes 8388608 | tf_op jit(solution)/shard_map/pallas_call | solution.py:340
  59.3 0.0 collective-permute-done.7.refs_6_
  59.3 0.0 collective-permute-done.6.refs_5_
  59.3 0.0 collective-permute-done.9.refs_1_
  59.3 0.0 collective-permute-done.8.refs_6_
  59.3 0.5 collective-permute-start.10
  59.8 0.1 collective-permute-start.11
  59.9 0.4 collective-permute-start.12
  60.4 7.1 %shard_map.117 = (f32[4,128,128]{2,1,0:T(8,128)S(1)}, bf16[4,128,128]{2,1,0:T(8,128)(2,1)S(1)}, bf16[4,512,128]{2,1,0:T(8,128)(2,1)S(1)}, bf16[4,512,128]{2,1,0:...) custom-call(bf16[4,512,256]{2,1,0:T(8,128)(2,1)} %get-tuple-element.106.refs_0_, ...), custom_call_target="tpu_custom_call" | custom-call | flops 4294967296 | bytes 8388608 | tf_op jit(solution)/shard_map/pallas_call | solution.py:340
  67.5 0.0 collective-permute-done.10.refs_7_
  67.5 0.0 collective-permute-done.11.refs_8_
  67.5 0.0 collective-permute-done.12
  67.5 0.2 collective-permute-start.13
  67.7 0.1 add_convert_fusion.1
  67.7 1.4 %collective-permute-done.13 = bf16[2,8,64,128]{3,2,1,0:T(8,128)(2,1)S(1)} collective-permute-done((bf16[2,8,64,128]{3,2,1,0:T(8,128)(2,1)S(1)}, bf16[2,8,64,128]{3,2,1,0:T(8,128)(2,1)S(1)}, u32[]{:S(2)}, u32[]{:S(2)}) %collective-permute-start.13) | collective-permute-done | bytes 262176 | tf_op jit(solution)/shard_map/ppermute | solution.py:41
  69.1 0.1 add_convert_fusion
  69.2 0.3 collective-permute-start.15
  69.5 3.2 %collective-permute-start.14 = (bf16[2,8,64,128]{3,2,1,0:T(8,128)(2,1)S(1)}, bf16[2,8,64,128]{3,2,1,0:T(8,128)(2,1)S(1)}, u32[]{:S(2)}, u32[]{:S(2)}) collective-permute-start(bf16[2,8,64,128]{3,2,1,0:T(8,128)(2,1)S(1)} %add_convert_fusion.1), channel_id=1, source_target_pairs={{0,96},{32,0},{64,32},{96,64},{1,97},{33,1},{65,33},{97,65},{2,98}... | collective-permute-start | bytes 786440 | tf_op jit(solution)/shard_map/ppermute | solution.py:46
  72.7 7.1 %shard_map.118 = (f32[4,128,128]{2,1,0:T(8,128)S(1)}, bf16[4,128,128]{2,1,0:T(8,128)(2,1)S(1)}, bf16[4,512,128]{2,1,0:T(8,128)(2,1)S(1)}, bf16[4,512,128]{2,1,0:...) custom-call(bf16[4,512,256]{2,1,0:T(8,128)(2,1)} %get-tuple-element.106.refs_0_, ...), custom_call_target="tpu_custom_call" | custom-call | flops 4294967296 | bytes 8388608 | tf_op jit(solution)/shard_map/pallas_call | solution.py:340
  79.8 0.0 collective-permute-done.15.refs_3_
  79.8 0.0 collective-permute-done.14.refs_2_
  79.8 0.1 collective-permute-start.16
  79.9 0.1 shard_map.120
  80.0 1.4 %collective-permute-done.16.refs_1_ = bf16[2,8,64,128]{3,2,1,0:T(8,128)(2,1)S(1)} collective-permute-done((bf16[2,8,64,128]{3,2,1,0:T(8,128)(2,1)S(1)}, bf16[2,8,64,128]{3,2,1,0:T(8,128)(2,1)S(1)}, u32[]{:S(2)}, u32[]{:S(2)}) %collective-permute-start.16) | collective-permute-done | bytes 262176 | tf_op jit(solution)/shard_map/ppermute | solution.py:41
  81.4 0.1 shard_map.121
  81.5 2.3 %collective-permute-start.17 = (bf16[8,64,128]{2,1,0:T(8,128)(2,1)S(1)}, bf16[8,64,128]{2,1,0:T(8,128)(2,1)S(1)}, u32[]{:S(2)}, u32[]{:S(2)}) collective-permute-start(bf16[8,64,128]{2,1,0:T(8,128)(2,1)S(1)} %get-tuple-element.188), channel_id=1, source_target_pairs={{0,64},{32,96},{64,0},{96,32},{1,65},{33,97},{65,1},{97,33},{2,66}... | collective-permute-start | bytes 393224 | tf_op jit(solution)/shard_map/ppermute | solution.py:46
  83.8 3.2 %collective-permute-start.18 = (bf16[8,64,128]{2,1,0:T(8,128)(2,1)S(1)}, bf16[8,64,128]{2,1,0:T(8,128)(2,1)S(1)}, u32[]{:S(2)}, u32[]{:S(2)}) collective-permute-start(bf16[8,64,128]{2,1,0:T(8,128)(2,1)S(1)} %get-tuple-element.189), channel_id=1, source_target_pairs={{0,80},{16,64},{32,112},{48,96},{64,16},{80,0},{96,48},{112,32},{1... | collective-permute-start | bytes 393224 | tf_op jit(solution)/shard_map/ppermute | solution.py:564
  87.0 1.1 collective-permute-start.19
  88.1 3.9 %shard_map.119.done_ref = bf16[8,9,64,128]{3,2,1,0:T(8,128)(2,1)S(1)} custom-call(f32[4,128,512]{2,1,0:T(8,128)} %get-tuple-element.105.refs_0_, bf16[8,9,64,128]{3,2,1,0:T(8,128)(2,1)S(1)} %all_to_all.10.pair_ref.cot_ref.refs_1_, bf16[128,128]{1,0:T(8,128)(2,1)S(1)} %copy-done.1, bf16[128,128]{1,0:T(8,128)(2,1)S(1)} %copy-done.2, ...), custom_call_target="tpu_custom_call" | custom-call | flops 2147483648 | bytes 8388608 | tf_op jit(solution)/shard_map/pallas_call | solution.py:401
  91.9 0.0 collective-permute-done.17.c_ref
  91.9 2.1 %collective-permute-done.18.d_ref = bf16[8,64,128]{2,1,0:T(8,128)(2,1)S(1)} collective-permute-done((bf16[8,64,128]{2,1,0:T(8,128)(2,1)S(1)}, bf16[8,64,128]{2,1,0:T(8,128)(2,1)S(1)}, u32[]{:S(2)}, u32[]{:S(2)}) %collective-permute-start.18) | collective-permute-done | bytes 131104 | tf_op jit(solution)/shard_map/ppermute | solution.py:564
  94.1 0.0 collective-permute-done.19.b_ref
  94.1 0.1 shard_map.122
  94.2 19.4 %all_to_all.11.both_ref = bf16[8,9,64,128]{3,2,1,0:T(8,128)(2,1)S(1)} all-to-all(bf16[8,9,64,128]{3,2,1,0:T(8,128)(2,1)S(1)} %shard_map.122), channel_id=1, replica_groups=mesh['z'=4,'xh'=2,'core'=2,'y'=4,'xl'=2] {'y','xl'}, dimensions={0} | all-to-all | bytes 2359296 | tf_op jit(solution)/shard_map/all_to_all | solution.py:570
  113.6 0.9 pad_maximum_fusion
  114.5 0.2 copy-done
  114.7 2.2 %shard_map.123 = f32[32,64,128]{2,1,0:T(8,128)} custom-call(bf16[32,64,128]{2,1,0:T(8,128)(2,1)S(1)} %copy-done, bf16[8,9,64,128]{3,2,1,0:T(8,128)(2,1)S(1)} %all_to_all.11.both_ref, f32[1,128]{1,0:T(1,128)S(1)} %bitcast.18, f32[1,128]{1,0:T(1,128)S(1)} %bitcast.21, bf16[4,128]{1,0:T(4,128)(2,1)S(1)} %bitcast.15), custom_call_target="tpu_custom_call" | custom-call | flops 134217728 | bytes 2097152 | tf_op jit(solution)/shard_map/pallas_call | solution.py:487
  (15 shorter events, 0.1 us)
Async XLA Ops:
  3.8 26.7 %copy-start.1 = (bf16[128,128]{1,0:T(8,128)(2,1)S(1)}, bf16[128,128]{1,0:T(8,128)(2,1)}, u32[]{:S(2)}) copy-start(bf16[128,128]{1,0:T(8,128)(2,1)} %refs_2_.1) | copy-start | bytes 98308
  3.8 26.7 %copy-start.2 = (bf16[128,128]{1,0:T(8,128)(2,1)S(1)}, bf16[128,128]{1,0:T(8,128)(2,1)}, u32[]{:S(2)}) copy-start(bf16[128,128]{1,0:T(8,128)(2,1)} %refs_3_.1) | copy-start | bytes 98308
  3.8 26.7 %copy-start.3 = (bf16[128,128]{1,0:T(8,128)(2,1)S(1)}, bf16[128,128]{1,0:T(8,128)(2,1)}, u32[]{:S(2)}) copy-start(bf16[128,128]{1,0:T(8,128)(2,1)} %refs_4_.1) | copy-start | bytes 98308
  3.8 26.7 %copy-start.4 = (bf16[128,128]{1,0:T(8,128)(2,1)S(1)}, bf16[128,128]{1,0:T(8,128)(2,1)}, u32[]{:S(2)}) copy-start(bf16[128,128]{1,0:T(8,128)(2,1)} %refs_5_.1) | copy-start | bytes 98308
  3.8 26.7 %copy-start.5 = (bf16[128,128]{1,0:T(8,128)(2,1)S(1)}, bf16[128,128]{1,0:T(8,128)(2,1)}, u32[]{:S(2)}) copy-start(bf16[128,128]{1,0:T(8,128)(2,1)} %refs_6_.1) | copy-start | bytes 98308
  3.8 26.7 %copy-start.7 = (f32[128]{0:T(128)S(1)}, f32[128]{0:T(128)}, u32[]{:S(2)}) copy-start(f32[128]{0:T(128)} %param.12) | copy-start | bytes 1540
  3.9 26.7 %copy-start.8 = (f32[128]{0:T(128)S(1)}, f32[128]{0:T(128)}, u32[]{:S(2)}) copy-start(f32[128]{0:T(128)} %param.13) | copy-start | bytes 1540
  26.8 7.6 %collective-permute-start.2 = (bf16[8,64,128]{2,1,0:T(8,128)(2,1)S(1)}, bf16[8,64,128]{2,1,0:T(8,128)(2,1)S(1)}, u32[]{:S(2)}, u32[]{:S(2)}) collective-permute-start(bf16[8,64,128]{2,1,0:T(8,128)(2,1)S(1)} %get-tuple-element.201.refs_5_), channel_id=1, source_target_pairs={{0,24},{8,16},{16,8},{24,0},{1,25},{9,17},{17,9},{25,1},{2,26},{10... | collective-permute-start | bytes 393224 | tf_op jit(solution)/shard_map/ppermute | solution.py:524
  27.8 6.5 %collective-permute-start.1 = (bf16[8,64,128]{2,1,0:T(8,128)(2,1)S(1)}, bf16[8,64,128]{2,1,0:T(8,128)(2,1)S(1)}, u32[]{:S(2)}, u32[]{:S(2)}) collective-permute-start(bf16[8,64,128]{2,1,0:T(8,128)(2,1)S(1)} %get-tuple-element.201.refs_5_), channel_id=1, source_target_pairs={{0,8},{8,0},{16,24},{24,16},{1,9},{9,1},{17,25},{25,17},{2,10},{10... | collective-permute-start | bytes 393224 | tf_op jit(solution)/shard_map/ppermute | solution.py:524
  29.7 7.0 %collective-permute-start = (bf16[8,64,128]{2,1,0:T(8,128)(2,1)S(1)}, bf16[8,64,128]{2,1,0:T(8,128)(2,1)S(1)}, u32[]{:S(2)}, u32[]{:S(2)}) collective-permute-start(bf16[8,64,128]{2,1,0:T(8,128)(2,1)S(1)} %get-tuple-element.201.refs_5_), channel_id=1, source_target_pairs={{0,16},{8,24},{16,0},{24,8},{1,17},{9,25},{17,1},{25,9},{2,18},{10... | collective-permute-start | bytes 393224 | tf_op jit(solution)/shard_map/ppermute | solution.py:524
  36.8 11.2 %collective-permute-start.4 = (bf16[2,8,64,128]{3,2,1,0:T(8,128)(2,1)S(1)}, bf16[2,8,64,128]{3,2,1,0:T(8,128)(2,1)S(1)}, u32[]{:S(2)}, u32[]{:S(2)}) collective-permute-start(bf16[2,8,64,128]{3,2,1,0:T(8,128)(2,1)S(1)} %pad_maximum_fusion.1), channel_id=1, source_target_pairs={{0,96},{32,0},{64,32},{96,64},{1,97},{33,1},{65,33},{97,65},{2,98}... | collective-permute-start | bytes 786440 | tf_op jit(solution)/shard_map/ppermute | solution.py:46
  40.9 8.4 %collective-permute-start.3 = (bf16[2,8,64,128]{3,2,1,0:T(8,128)(2,1)S(1)}, bf16[2,8,64,128]{3,2,1,0:T(8,128)(2,1)S(1)}, u32[]{:S(2)}, u32[]{:S(2)}) collective-permute-start(bf16[2,8,64,128]{3,2,1,0:T(8,128)(2,1)S(1)} %pad_maximum_fusion.1), channel_id=1, source_target_pairs={{0,32},{32,64},{64,96},{96,0},{1,33},{33,65},{65,97},{97,1},{2,34}... | collective-permute-start | bytes 786440 | tf_op jit(solution)/shard_map/ppermute | solution.py:46
  49.2 2.9 %collective-permute-start.5 = (bf16[2,8,64,128]{3,2,1,0:T(8,128)(2,1)S(1)}, bf16[2,8,64,128]{3,2,1,0:T(8,128)(2,1)S(1)}, u32[]{:S(2)}, u32[]{:S(2)}) collective-permute-start(bf16[2,8,64,128]{3,2,1,0:T(8,128)(2,1)S(1)} %collective-permute-done.3.refs_5_), channel_id=1, source_target_pairs={{0,8},{8,0},{1,9},{9,1},{2,10},{10,2},{3,11},{11,3},{4,12},{12,4},... | collective-permute-start | bytes 786440 | tf_op jit(solution)/shard_map/ppermute | solution.py:41
  49.3 10.0 %collective-permute-start.8 = (bf16[2,8,64,128]{3,2,1,0:T(8,128)(2,1)S(1)}, bf16[2,8,64,128]{3,2,1,0:T(8,128)(2,1)S(1)}, u32[]{:S(2)}, u32[]{:S(2)}) collective-permute-start(bf16[2,8,64,128]{3,2,1,0:T(8,128)(2,1)S(1)} %collective-permute-done.4.refs_5_), channel_id=1, source_target_pairs={{0,8},{8,0},{1,9},{9,1},{2,10},{10,2},{3,11},{11,3},{4,12},{12,4},... | collective-permute-start | bytes 786440 | tf_op jit(solution)/shard_map/ppermute | solution.py:41
  49.8 9.4 %collective-permute-start.7 = (bf16[8,64,128]{2,1,0:T(8,128)(2,1)S(1)}, bf16[8,64,128]{2,1,0:T(8,128)(2,1)S(1)}, u32[]{:S(2)}, u32[]{:S(2)}) collective-permute-start(bf16[8,64,128]{2,1,0:T(8,128)(2,1)S(1)} %slice_bitcast_fusion), channel_id=1, source_target_pairs={{0,96},{32,0},{64,32},{96,64},{1,97},{33,1},{65,33},{97,65},{2,98}... | collective-permute-start | bytes 393224 | tf_op jit(solution)/shard_map/ppermute | solution.py:46
  51.9 7.3 %collective-permute-start.6 = (bf16[8,64,128]{2,1,0:T(8,128)(2,1)S(1)}, bf16[8,64,128]{2,1,0:T(8,128)(2,1)S(1)}, u32[]{:S(2)}, u32[]{:S(2)}) collective-permute-start(bf16[8,64,128]{2,1,0:T(8,128)(2,1)S(1)} %slice_bitcast_fusion.1), channel_id=1, source_target_pairs={{0,32},{32,64},{64,96},{96,0},{1,33},{33,65},{65,97},{97,1},{2,34}... | collective-permute-start | bytes 393224 | tf_op jit(solution)/shard_map/ppermute | solution.py:46
  52.0 7.3 %collective-permute-start.9 = (bf16[2,8,64,128]{3,2,1,0:T(8,128)(2,1)S(1)}, bf16[2,8,64,128]{3,2,1,0:T(8,128)(2,1)S(1)}, u32[]{:S(2)}, u32[]{:S(2)}) collective-permute-start(bf16[2,8,64,128]{3,2,1,0:T(8,128)(2,1)S(1)} %get-tuple-element.125), channel_id=1, source_target_pairs={{0,8},{8,0},{1,9},{9,1},{2,10},{10,2},{3,11},{11,3},{4,12},{12,4},... | collective-permute-start | bytes 786440 | tf_op jit(solution)/shard_map/ppermute | solution.py:41
  59.3 8.2 %collective-permute-start.10 = (bf16[8,64,128]{2,1,0:T(8,128)(2,1)S(1)}, bf16[8,64,128]{2,1,0:T(8,128)(2,1)S(1)}, u32[]{:S(2)}, u32[]{:S(2)}) collective-permute-start(bf16[8,64,128]{2,1,0:T(8,128)(2,1)S(1)} %collective-permute-done.6.refs_5_), channel_id=1, source_target_pairs={{0,8},{8,0},{1,9},{9,1},{2,10},{10,2},{3,11},{11,3},{4,12},{12,4},... | collective-permute-start | bytes 393224 | tf_op jit(solution)/shard_map/ppermute | solution.py:41
  59.8 7.6 %collective-permute-start.11 = (bf16[8,64,128]{2,1,0:T(8,128)(2,1)S(1)}, bf16[8,64,128]{2,1,0:T(8,128)(2,1)S(1)}, u32[]{:S(2)}, u32[]{:S(2)}) collective-permute-start(bf16[8,64,128]{2,1,0:T(8,128)(2,1)S(1)} %collective-permute-done.7.refs_6_), channel_id=1, source_target_pairs={{0,8},{8,0},{1,9},{9,1},{2,10},{10,2},{3,11},{11,3},{4,12},{12,4},... | collective-permute-start | bytes 393224 | tf_op jit(solution)/shard_map/ppermute | solution.py:41
  59.9 7.5 %collective-permute-start.12 = (bf16[2,8,64,128]{3,2,1,0:T(8,128)(2,1)S(1)}, bf16[2,8,64,128]{3,2,1,0:T(8,128)(2,1)S(1)}, u32[]{:S(2)}, u32[]{:S(2)}) collective-permute-start(bf16[2,8,64,128]{3,2,1,0:T(8,128)(2,1)S(1)} %get-tuple-element.147), channel_id=1, source_target_pairs={{0,8},{8,0},{1,9},{9,1},{2,10},{10,2},{3,11},{11,3},{4,12},{12,4},... | collective-permute-start | bytes 786440 | tf_op jit(solution)/shard_map/ppermute | solution.py:41
  67.5 1.6 %collective-permute-start.13 = (bf16[2,8,64,128]{3,2,1,0:T(8,128)(2,1)S(1)}, bf16[2,8,64,128]{3,2,1,0:T(8,128)(2,1)S(1)}, u32[]{:S(2)}, u32[]{:S(2)}) collective-permute-start(bf16[2,8,64,128]{3,2,1,0:T(8,128)(2,1)S(1)} %get-tuple-element.150), channel_id=1, source_target_pairs={{0,8},{8,0},{1,9},{9,1},{2,10},{10,2},{3,11},{11,3},{4,12},{12,4},... | collective-permute-start | bytes 786440 | tf_op jit(solution)/shard_map/ppermute | solution.py:41
  69.2 10.6 %collective-permute-start.15 = (bf16[2,8,64,128]{3,2,1,0:T(8,128)(2,1)S(1)}, bf16[2,8,64,128]{3,2,1,0:T(8,128)(2,1)S(1)}, u32[]{:S(2)}, u32[]{:S(2)}) collective-permute-start(bf16[2,8,64,128]{3,2,1,0:T(8,128)(2,1)S(1)} %add_convert_fusion), channel_id=1, source_target_pairs={{0,32},{32,64},{64,96},{96,0},{1,33},{33,65},{65,97},{97,1},{2,34}... | collective-permute-start | bytes 786440 | tf_op jit(solution)/shard_map/ppermute | solution.py:46
  69.5 10.3 %collective-permute-start.14 = (bf16[2,8,64,128]{3,2,1,0:T(8,128)(2,1)S(1)}, bf16[2,8,64,128]{3,2,1,0:T(8,128)(2,1)S(1)}, u32[]{:S(2)}, u32[]{:S(2)}) collective-permute-start(bf16[2,8,64,128]{3,2,1,0:T(8,128)(2,1)S(1)} %add_convert_fusion.1), channel_id=1, source_target_pairs={{0,96},{32,0},{64,32},{96,64},{1,97},{33,1},{65,33},{97,65},{2,98}... | collective-permute-start | bytes 786440 | tf_op jit(solution)/shard_map/ppermute | solution.py:46
  79.8 1.6 %collective-permute-start.16 = (bf16[2,8,64,128]{3,2,1,0:T(8,128)(2,1)S(1)}, bf16[2,8,64,128]{3,2,1,0:T(8,128)(2,1)S(1)}, u32[]{:S(2)}, u32[]{:S(2)}) collective-permute-start(bf16[2,8,64,128]{3,2,1,0:T(8,128)(2,1)S(1)} %get-tuple-element.180), channel_id=1, source_target_pairs={{0,8},{8,0},{1,9},{9,1},{2,10},{10,2},{3,11},{11,3},{4,12},{12,4},... | collective-permute-start | bytes 786440 | tf_op jit(solution)/shard_map/ppermute | solution.py:41
  81.5 10.4 %collective-permute-start.17 = (bf16[8,64,128]{2,1,0:T(8,128)(2,1)S(1)}, bf16[8,64,128]{2,1,0:T(8,128)(2,1)S(1)}, u32[]{:S(2)}, u32[]{:S(2)}) collective-permute-start(bf16[8,64,128]{2,1,0:T(8,128)(2,1)S(1)} %get-tuple-element.188), channel_id=1, source_target_pairs={{0,64},{32,96},{64,0},{96,32},{1,65},{33,97},{65,1},{97,33},{2,66}... | collective-permute-start | bytes 393224 | tf_op jit(solution)/shard_map/ppermute | solution.py:46
  83.8 10.3 %collective-permute-start.18 = (bf16[8,64,128]{2,1,0:T(8,128)(2,1)S(1)}, bf16[8,64,128]{2,1,0:T(8,128)(2,1)S(1)}, u32[]{:S(2)}, u32[]{:S(2)}) collective-permute-start(bf16[8,64,128]{2,1,0:T(8,128)(2,1)S(1)} %get-tuple-element.189), channel_id=1, source_target_pairs={{0,80},{16,64},{32,112},{48,96},{64,16},{80,0},{96,48},{112,32},{1... | collective-permute-start | bytes 393224 | tf_op jit(solution)/shard_map/ppermute | solution.py:564
  87.0 7.1 %collective-permute-start.19 = (bf16[8,64,128]{2,1,0:T(8,128)(2,1)S(1)}, bf16[8,64,128]{2,1,0:T(8,128)(2,1)S(1)}, u32[]{:S(2)}, u32[]{:S(2)}) collective-permute-start(bf16[8,64,128]{2,1,0:T(8,128)(2,1)S(1)} %get-tuple-element.190), channel_id=1, source_target_pairs={{0,16},{16,0},{1,17},{17,1},{2,18},{18,2},{3,19},{19,3},{4,20},{20... | collective-permute-start | bytes 393224 | tf_op jit(solution)/shard_map/ppermute | solution.py:565
  113.6 1.1 copy-start
  113.6 1.1 copy-start.6

commit v8 on v7

--- a/solution.py
+++ b/solution.py
@@ -15,6 +15,7 @@
 BF16 = jnp.bfloat16
 LANES = 128
 PARAMS = pltpu.CompilerParams(vmem_limit_bytes=24 * 1024 * 1024)
+WIDE = pltpu.CompilerParams(vmem_limit_bytes=36 * 1024 * 1024)
 FIRST = pltpu.CompilerParams(vmem_limit_bytes=60 * 1024 * 1024)
 
 
@@ -183,38 +184,43 @@
     return pl.ds(pl.multiple_of(at * LANES, LANES), LANES)
 
 
-def attend_kernel(
-    heads,
-    n_own,
-    n_ref,
-    t_ref,
-    q_n_ref,
-    q_t_ref,
-    d_att_ref,
-    *refs,
-):
-    bias_refs = refs[: n_own * 2]
-    att_ref, dq_ref, dk_ref, dv_ref, mine_ref, theirs_ref = refs[n_own * 2 : n_own * 2 + 6]
-    bias_s, gb_s, s_s, p_s, ds_s, tile_s, line_s = refs[n_own * 2 + 6 :]
-    row = pl.program_id(0)
-    n = n_ref.shape[1]
-    inner = n_ref.shape[2] // 2
+def attend_kernel(heads, count, views, kv_n_hbm, kv_t_hbm, q_n_ref, q_t_ref, d_att_ref, *refs):
+    bias_refs = refs[: count * 2 * views]
+    refs = refs[count * 2 * views :]
+    att_ref, dq_ref, dk_ref, dv_ref, mine_ref, theirs_ref = refs[:6]
+    n_ref, t_ref, bias_s, gb_s, s_s, p_s, ds_s, tile_s, line_s, dk_s, dv_s, sems = refs[6:]
+    at_slice = pl.program_id(0)
+    row_count, n, wide_kv = n_ref.shape
+    inner = wide_kv // 2
     head_dim = inner // heads
     scale = 1.0 / math.sqrt(head_dim)
     n_ja = tile_s.shape[0]
     block = n // n_ja
     rows_i = LANES // 4
     pairs = heads // 2
+    wide = 2 * LANES
     core = lax.axis_index("core")
     xh = lax.axis_index("xh")
-
-    @pl.when(row == 0)
+    copies = [
+        pltpu.make_async_copy(src, dst, sems.at[e])
+        for e, (src, dst) in enumerate(((kv_n_hbm, n_ref), (kv_t_hbm, t_ref)))
+    ]
+
+    @pl.when(at_slice == 0)
     def _():
+        for copy in copies:
+            copy.start()
+        if count > 1:
+            dk_s[...] = jnp.zeros_like(dk_s)
+            dv_s[...] = jnp.zeros_like(dv_s)
+
+    def sort_tiles(c):
         for which in range(2):
-            views = []
-            for ref in bias_refs[which * n_own : (which + 1) * n_own]:
-                views += [ref] if len(ref.shape) == 3 else [ref.at[e] for e in range(2)]
-            for far, ref in enumerate(views):
+            base = (c * 2 + which) * views
+            parts = []
+            for ref in bias_refs[base : base + views]:
+                parts += [ref] if len(ref.shape) == 3 else [ref.at[e] for e in range(2)]
+            for far, ref in enumerate(parts):
                 at = (xh ^ far) * 2 + (core ^ which)
                 at = pl.ds(pl.multiple_of(at * rows_i, rows_i), rows_i)
                 for owner in range(n_ja):
@@ -222,154 +228,217 @@
                         tile_s[owner, at, p * LANES : (p + 1) * LANES] = ref[
                             owner, p * rows_i : (p + 1) * rows_i, :
                         ]
-        for owner in range(n_ja):
-            for p in range(pairs):
-                t = tile_s[owner, :, p * LANES : (p + 1) * LANES].astype(F32).T * LOG2E
-                for e in range(2):
-                    h = p * 2 + e
-                    bias_s[
-                        owner * block : (owner + 1) * block, h * LANES : (h + 1) * LANES
-                    ] = t[e * block : (e + 1) * block]
-        gb_s[...] = jnp.zeros_like(gb_s)
+
+    for c in range(count):
+        pl.when(at_slice == c)(lambda c=c: sort_tiles(c))
+    for owner in range(n_ja):
+        for p in range(pairs):
+            t = tile_s[owner, :, p * LANES : (p + 1) * LANES].astype(F32).T * LOG2E
+            for e in range(2):
+                h = p * 2 + e
+                bias_s[owner * block : (owner + 1) * block, h * LANES : (h + 1) * LANES] = t[
+                    e * block : (e + 1) * block
+                ]
+
+    @pl.when(at_slice == 0)
+    def _():
+        for copy in copies:
+            copy.wait()
 
     nil = jnp.zeros((), BF16)
     row_head = lax.broadcasted_iota(jnp.int32, (inner, LANES), 0) // head_dim
     lane_head = lax.broadcasted_iota(jnp.int32, (LANES, inner), 1) // head_dim
-    q_n = q_n_ref[0, 0]
-    q_t = q_t_ref[0, 0]
-    d_att = d_att_ref[0, 0]
-    q_row = jnp.concatenate([jnp.where(lane_head == h, q_n, nil) for h in range(heads)], 0)
     step = 16
-    chunk = 128
-    wide = 2 * LANES
-    a_rows = []
-    invs = []
-    for p in range(pairs):
-        cols = slice(p * wide, (p + 1) * wide)
+    held = {}
+
+    def cols_of(p):
+        return slice(p * wide, (p + 1) * wide)
+
+    def scores(r, p):
         q_blk = jnp.concatenate(
-            [jnp.where(row_head == h, q_t, nil) for h in (2 * p, 2 * p + 1)], axis=1
+            [jnp.where(row_head == h, q_t_ref[0, r], nil) for h in (2 * p, 2 * p + 1)], axis=1
         )
-        top = jnp.full((8, wide), -jnp.inf, F32)
-        for k in range(0, n, chunk):
-            t = mm(n_ref[0, k : k + chunk, :inner], q_blk) * (scale * LOG2E)
-            t = t + bias_s[k : k + chunk, cols]
-            s_s[k : k + chunk, cols] = t
-            for e in range(0, chunk, 8):
-                top = jnp.maximum(top, t[e : e + 8])
-        top = jnp.max(top, axis=0, keepdims=True)
+        t = mm(n_ref[r, :, :inner], q_blk) * (scale * LOG2E) + bias_s[:, cols_of(p)]
+        s_s[r, :, cols_of(p)] = t
+        top = t[:8]
+        for e in range(8, n, 8):
+            top = jnp.maximum(top, t[e : e + 8])
+        held["top", r, p] = jnp.max(top, axis=0, keepdims=True)
+
+    def weights(r, p):
         total = jnp.zeros((8, wide), F32)
         for k in range(0, n, step):
-            e = jnp.exp2(s_s[k : k + step, cols] - top)
-            s_s[k : k + step, cols] = e
-            p_s[k : k + step, cols] = e.astype(BF16)
+            e = jnp.exp2(s_s[r, k : k + step, cols_of(p)] - held["top", r, p])
+            s_s[r, k : k + step, cols_of(p)] = e
+            p_s[r, k : k + step, cols_of(p)] = e.astype(BF16)
             total = total + (e[:8] + e[8:])
-        invs.append(1.0 / jnp.sum(total, axis=0, keepdims=True))
-    for p in range(pairs):
-        cols = slice(p * wide, (p + 1) * wide)
+        held["inv", r, p] = 1.0 / jnp.sum(total, axis=0, keepdims=True)
+
+    def attended(r, p):
         first = 2 * p * head_dim
         rows = slice(first, first + 2 * head_dim)
-        inv = invs[p]
-        att = mm(t_ref[0, inner + first : inner + first + 2 * head_dim, :], p_s[:, cols])
+        inv = held["inv", r, p]
+        att = mm(t_ref[r, inner + first : inner + first + 2 * head_dim, :], p_s[r, :, cols_of(p)])
         att = att * inv
-        a_two = jnp.concatenate([d_att[rows], d_att[rows]], axis=1) * inv
+        d_att = d_att_ref[0, r, rows, :]
+        a_two = jnp.concatenate([d_att, d_att], axis=1) * inv
         lane = lax.broadcasted_iota(jnp.int32, a_two.shape, 1) // LANES
         sub = lax.broadcasted_iota(jnp.int32, a_two.shape, 0) // head_dim
         a_two = jnp.where(lane == sub, a_two, 0.0).astype(BF16)
-        diag = jnp.sum(a_two.astype(F32) * att, axis=0, keepdims=True)
+        held["diag", r, p] = jnp.sum(a_two.astype(F32) * att, axis=0, keepdims=True)
         for e in range(2):
             h = 2 * p + e
-            own = slice(h * head_dim, (h + 1) * head_dim)
-            att_ref[0, own, :] = att[
+            att_ref[0, r, h * head_dim : (h + 1) * head_dim, :] = att[
                 e * head_dim : (e + 1) * head_dim, e * LANES : (e + 1) * LANES
             ]
         lead = [jnp.zeros((first, wide), BF16)] if p else []
         tail = [jnp.zeros((inner - first - 2 * head_dim, wide), BF16)] if p + 1 < pairs else []
-        a_blk = jnp.concatenate(lead + [a_two] + tail, axis=0)
-        a_rows.append(a_blk.T)
-        for k in range(0, n, chunk):
-            dp = mm(n_ref[0, k : k + chunk, inner:], a_blk)
-            ds = s_s[k : k + chunk, cols] * (dp - diag)
-            gb_s[k : k + chunk, cols] += ds
-            ds_s[k : k + chunk, cols] = ds.astype(BF16)
-        dq = mm(t_ref[0, first : first + 2 * head_dim, :], ds_s[:, cols]) * scale
+        held["a", r, p] = jnp.concatenate(lead + [a_two] + tail, axis=0)
+
+    def d_scores(r, p):
+        dp = mm(n_ref[r, :, inner:], held["a", r, p])
+        for k in range(0, n, step):
+            ds = s_s[r, k : k + step, cols_of(p)] * (dp[k : k + step] - held["diag", r, p])
+            if r == 0:
+                gb_s[k : k + step, cols_of(p)] = ds
+            else:
+                gb_s[k : k + step, cols_of(p)] += ds
+            ds_s[r, k : k + step, cols_of(p)] = ds.astype(BF16)
+
+    def d_query(r, p):
+        first = 2 * p * head_dim
+        dq = mm(t_ref[r, first : first + 2 * head_dim, :], ds_s[r, :, cols_of(p)]) * scale
         for e in range(2):
             h = 2 * p + e
-            dq_ref[0, h * head_dim : (h + 1) * head_dim, :] = dq[
+            dq_ref[0, r, h * head_dim : (h + 1) * head_dim, :] = dq[
                 e * head_dim : (e + 1) * head_dim, e * LANES : (e + 1) * LANES
             ].astype(BF16)
-    dk_ref[0] = (mm(ds_s[...], q_row) * scale).astype(BF16)
-    dv_ref[0] = mm(p_s[...], jnp.concatenate(a_rows, axis=0)).astype(BF16)
-
-    @pl.when(row == pl.num_programs(0) - 1)
-    def _():
-        for owner in range(n_ja):
-            for p in range(pairs):
-                t = jnp.concatenate(
-                    [
-                        gb_s[owner * block : (owner + 1) * block, h * LANES : (h + 1) * LANES]
-                        for h in (2 * p, 2 * p + 1)
-                    ],
-                    axis=0,
-                )
-                line_s[:, p * LANES : (p + 1) * LANES] = t.T.astype(BF16)
-            for far in range(2):
-                for ref, which in ((mine_ref, core), (theirs_ref, 1 - core)):
-                    at = pl.multiple_of((far * 2 + which) * rows_i, rows_i)
-                    for p in range(pairs):
-                        ref[far, owner, p * rows_i : (p + 1) * rows_i, :] = line_s[
-                            pl.ds(at, rows_i), p * LANES : (p + 1) * LANES
-                        ]
-
-
-def attend(heads, ahead, projected, own, other):
+
+    def gather(r, p, name, part, sum_s, out_ref, factor):
+        if p:
+            part = part + held.pop((name, r))
+        if p + 1 < pairs:
+            held[name, r] = part
+            return
+        if count > 1:
+            part = part + sum_s[r]
+            sum_s[r] = part
+        out_ref[r] = (part * factor).astype(BF16)
+
+    def d_key(r, p):
+        q_row = jnp.concatenate(
+            [jnp.where(lane_head == h, q_n_ref[0, r], nil) for h in (2 * p, 2 * p + 1)], axis=0
+        )
+        gather(r, p, "dk", mm(ds_s[r, :, cols_of(p)], q_row), dk_s, dk_ref, scale)
+
+    def d_value(r, p):
+        part = mm(p_s[r, :, cols_of(p)], held["a", r, p].T)
+        gather(r, p, "dv", part, dv_s, dv_ref, 1.0)
+
+    order = [
+        (scores, 0),
+        (scores, 1),
+        (weights, 0),
+        (attended, 0),
+        (weights, 1),
+        (d_scores, 0),
+        (attended, 1),
+        (d_value, 0),
+        (d_scores, 1),
+        (d_query, 0),
+        (d_key, 0),
+        (d_value, 1),
+        (d_query, 1),
+        (d_key, 1),
+    ]
+    lag = 5
+    for t in range(len(order) + lag * (row_count - 1)):
+        for r in range(row_count):
+            if 0 <= t - lag * r < len(order):
+                phase, p = order[t - lag * r]
+                phase(r, p)
+
+    for owner in range(n_ja):
+        for p in range(pairs):
+            t = jnp.concatenate(
+                [
+                    gb_s[owner * block : (owner + 1) * block, h * LANES : (h + 1) * LANES]
+                    for h in (2 * p, 2 * p + 1)
+                ],
+                axis=0,
+            )
+            line_s[:, p * LANES : (p + 1) * LANES] = t.T.astype(BF16)
+        for far in range(2):
+            for ref, which in ((mine_ref, core), (theirs_ref, 1 - core)):
+                at = pl.multiple_of((far * 2 + which) * rows_i, rows_i)
+                for p in range(pairs):
+                    ref[0, far, owner, p * rows_i : (p + 1) * rows_i, :] = line_s[
+                        pl.ds(at, rows_i), p * LANES : (p + 1) * LANES
+                    ]
+
+
+def attend(heads, aheads, projected, bias):
     rows, n, inner = projected[0].shape
     inner = inner // 2
-    n_ja, slab, _ = own[0].shape[-3:]
+    count = len(aheads)
+    leap = aheads[1] - aheads[0] if count > 1 else 0
+    views = len(bias[0][0])
+    flat = [a for slice_of in bias for side in slice_of for a in side]
+    n_ja, slab, _ = flat[0].shape[-3:]
     lines = heads * n // n_ja
-    att = jax.ShapeDtypeStruct((rows, inner, LANES), F32)
-    dq = jax.ShapeDtypeStruct((rows, inner, LANES), BF16)
+    att = jax.ShapeDtypeStruct((count, rows, inner, LANES), F32)
+    dq = jax.ShapeDtypeStruct((count, rows, inner, LANES), BF16)
     grad = jax.ShapeDtypeStruct((rows, n, inner), BF16)
-    gb = jax.ShapeDtypeStruct((2, n_ja, slab, LANES), BF16)
-
-    def by_row(a):
-        return pl.BlockSpec((1,) + a.shape[1:], lambda i: (i, 0, 0))
+    gb = jax.ShapeDtypeStruct((count, 2, n_ja, slab, LANES), BF16)
+    sums = (rows, n, inner) if count > 1 else (1, 8, LANES)
+
+    def by_slice(a):
+        return pl.BlockSpec((1,) + a.shape[1:], lambda i: (i,) + (0,) * (len(a.shape) - 1))
 
     def sliced(a):
-        return pl.BlockSpec((1, 1) + a.shape[2:], lambda i: (ahead, i, 0, 0))
+        return pl.BlockSpec((1,) + a.shape[1:], lambda i: (aheads[0] + leap * i, 0, 0, 0))
 
     return pl.pallas_call(
-        lambda *refs: attend_kernel(heads, len(own), *refs),
-        grid=(rows,),
-        in_specs=[by_row(a) for a in projected[:2]]
+        lambda *refs: attend_kernel(heads, count, views, *refs),
+        grid=(count,),
+        in_specs=[pl.BlockSpec(memory_space=pl.ANY)] * 2
         + [sliced(a) for a in projected[2:]]
-        + [whole(a) for a in (*own, *other)],
-        out_specs=[by_row(a) for a in (att, dq, grad, grad)] + [whole(gb)] * 2,
+        + [whole(a) for a in flat],
+        out_specs=[by_slice(att), by_slice(dq), whole(grad), whole(grad)] + [by_slice(gb)] * 2,
         out_shape=[att, dq, grad, grad, gb, gb],
         scratch_shapes=[
+            pltpu.VMEM((rows, n, 2 * inner), BF16),
+            pltpu.VMEM((rows, 2 * inner, n), BF16),
             pltpu.VMEM((n, heads * LANES), F32),
             pltpu.VMEM((n, heads * LANES), F32),
-            pltpu.VMEM((n, heads * LANES), F32),
-            pltpu.VMEM((n, heads * LANES), BF16),
-            pltpu.VMEM((n, heads * LANES), BF16),
+            pltpu.VMEM((rows, n, heads * LANES), F32),
+            pltpu.VMEM((rows, n, heads * LANES), BF16),
+            pltpu.VMEM((rows, n, heads * LANES), BF16),
             pltpu.VMEM((n_ja, LANES, lines), BF16),
             pltpu.VMEM((LANES, lines), BF16),
+            pltpu.VMEM(sums, F32),
+            pltpu.VMEM(sums, F32),
+            pltpu.SemaphoreType.DMA((2,)),
         ],
-        compiler_params=PARAMS,
+        compiler_params=WIDE,
         cost_estimate=pl.CostEstimate(
-            flops=2**32, bytes_accessed=2**23, transcendentals=2**20
+            flops=count * 2**32, bytes_accessed=2**23, transcendentals=count * 2**20
         ),
-    )(*in_hbm(*projected), *own, *other)
-
-
-def finish_kernel(aheads, gate_ref, cot_ref, w_o_ref, w_q_ref, w_k_ref, w_v_ref, w_g_ref, *refs):
+    )(*in_hbm(*projected), *flat)
+
+
+def finish_kernel(
+    aheads, gate_ref, cot_ref, w_o_ref, w_q_ref, w_k_ref, w_v_ref, w_g_ref, *refs
+):
     count = len(aheads)
     att_refs, dq_refs = refs[:count], refs[count : 2 * count]
     dk_refs, dv_refs = refs[2 * count : 3 * count], refs[3 * count : 4 * count]
     out_ref, att_s, dq_s = refs[4 * count :]
-    for ahead, att_ref, dq_ref in zip(aheads, att_refs, dq_refs):
-        at = z_lanes(ahead)
-        att_s[:, at] = att_ref[0]
-        dq_s[:, at] = dq_ref[0]
+    for group, att_ref, dq_ref in zip(aheads, att_refs, dq_refs):
+        for c, ahead in enumerate(group):
+            at = z_lanes(ahead)
+            att_s[:, at] = att_ref[c, 0]
+            dq_s[:, at] = dq_ref[c, 0]
     half = (out_ref.shape[0],) + out_ref.shape[2:]
     gate = gate_ref[0]
     cot = cot_ref[...].reshape(gate.shape[1], cot_ref.shape[3])
@@ -397,13 +466,17 @@
     def by_row(a):
         return pl.BlockSpec((1,) + a.shape[1:], lambda i: (i, 0, 0))
 
+    def by_slices(a):
+        return pl.BlockSpec((a.shape[0], 1) + a.shape[2:], lambda i: (0, i, 0, 0))
+
     cot_spec = pl.BlockSpec((n_blocks, 1, block, channels), lambda i: (0, rows + i, 0, 0))
     return pl.pallas_call(
         lambda *refs: finish_kernel(aheads, *refs),
         grid=(rows,),
         in_specs=[by_row(gate), cot_spec, whole(w_o)]
         + [whole(a) for a in weights]
-        + [by_row(a) for a in arrays],
+        + [by_slices(a) for a in (*att, *dq)]
+        + [by_row(a) for a in (*dk, *dv)],
         out_specs=pl.BlockSpec((n_blocks, 2, block, channels), lambda i: (0, i, 0, 0)),
         out_shape=jax.ShapeDtypeStruct((n_blocks, 2 * rows + 1, block, channels), BF16),
         scratch_shapes=[
@@ -520,51 +593,46 @@
         prep(pair, cotangent, gain, shift_row, bias_rows, n_ja), JA, 0, 0, tiled=True
     )
 
-    def cross(a, bits):
-        return lax.ppermute(a, ("xh", "core"), [(s, s ^ bits) for s in range(4)])
+    def joined(mine, theirs):
+        return (mine.astype(F32) + theirs.astype(F32)).astype(BF16)
 
     own = both[:, 2 * own_i]
-    far, own_swap, far_swap = cross(own, 2), cross(own, 1), cross(own, 3)
+    far = lax.ppermute(own, "xh", [(0, 1), (1, 0)])
     projected = project(both, gain, shift_row, out_weight, weights)
-    far, own_swap, far_swap, projected = tie((far, own_swap, far_swap, projected))
+    far, projected = tie((far, projected))
     *projected, gate = projected
     near = jnp.stack([own, far])
+    near_swap = swap(near)
     prev, after = shift(near, "z", 1), shift(near, "z", 3)
 
-    def slice_of(ahead, own, other):
-        return attend(heads, ahead, projected, own, other)
-
-    def joined(out, theirs):
-        return (out[4].astype(F32) + theirs.astype(F32)).astype(BF16)
-
-    out0 = slice_of(0, [own, far], [own_swap, far_swap])
+    groups = ((0,), (3, 1), (2,))
+    out0 = attend(heads, groups[0], projected, [([near], [near_swap])])
     out0, prev, after = tie((out0, prev, after))
+    prev_swap, after_swap = swap(prev), swap(after)
     opp0, opp1 = shift(prev[0], "z", 1), shift(after[1], "z", 3)
-    prev_swap, after_swap, theirs0 = swap(prev), swap(after), swap(out0[5])
-    out0, prev, prev_swap = tie((out0, prev, prev_swap))
-    out1 = slice_of(3, [prev], [prev_swap])
-    out1, opp0, opp1, after_swap, theirs0 = tie((out1, opp0, opp1, after_swap, theirs0))
+    theirs0 = swap(out0[5])
+    out0, prev, prev_swap, after, after_swap = tie((out0, prev, prev_swap, after, after_swap))
+    out1 = attend(
+        heads, groups[1], projected, [([prev], [prev_swap]), ([after], [after_swap])]
+    )
+    out1, opp0, opp1, theirs0 = tie((out1, opp0, opp1, theirs0))
     opp0_swap, opp1_swap, theirs1 = swap(opp0), swap(opp1), swap(out1[5])
-    out2 = slice_of(1, [after], [after_swap])
-    out2, opp0_swap, opp1_swap, theirs1 = tie((out2, opp0_swap, opp1_swap, theirs1))
-    theirs2 = swap(out2[5])
-    part1 = joined(out1, theirs1)
-    theirs2, part1, opp0 = tie((theirs2, part1, opp0))
-    part2 = joined(out2, theirs2)
-    part2, opp0 = tie((part2, opp0))
-    part1, part2 = shift(part1, "z", 3), shift(part2, "z", 1)
-    out3 = slice_of(2, [opp0, opp1], [opp0_swap, opp1_swap])
+    theirs1, opp0_swap, opp1_swap = tie((theirs1, opp0_swap, opp1_swap))
+    part1 = joined(out1[4], theirs1)
+    part1, opp0 = tie((part1, opp0))
+    part1, part2 = shift(part1[0], "z", 3), shift(part1[1], "z", 1)
+    out3 = attend(heads, groups[2], projected, [([opp0, opp1], [opp0_swap, opp1_swap])])
     out3, part1, part2 = tie((out3, part1, part2))
     theirs3 = swap(out3[5])
-    keep, send = halves(out0[4], theirs0, part1, part2)
+    keep, send = halves(out0[4][0], theirs0[0], part1, part2)
     theirs3, keep, send = tie((theirs3, keep, send))
-    opp_keep, opp_send = halves(out3[4], theirs3)
+    opp_keep, opp_send = halves(out3[4][0], theirs3[0])
     flips = [(s, s ^ 5) for s in range(8)]
     opp_keep = shift(opp_keep, "z", 2)
     opp_send = lax.ppermute(opp_send, ("z", "xh"), flips)
     send = lax.ppermute(send, "xh", [(0, 1), (1, 0)])
-    att, dq, dk, dv = zip(out0[:4], out1[:4], out2[:4], out3[:4])
-    done = finish((0, 3, 1, 2), gate, both, out_weight, weights, att, dq, dk, dv)
+    att, dq, dk, dv = zip(out0[:4], out1[:4], out3[:4])
+    done = finish(groups, gate, both, out_weight, weights, att, dq, dk, dv)
     done, opp_keep, opp_send, send = tie((done, opp_keep, opp_send, send))
     done = fill(done, keep, send, opp_keep, opp_send)
     done = lax.all_to_all(done, JA, 0, 0, tiled=True)

time: 117 us -> 111 us (0.949)
  Pallas kernels: 41.8 us -> 37.2 us
  starting transfers between devices: 22 us -> 20.7 us
    pallas_call x4 -> x3, Pallas kernels: 28.4 us -> 23.8 us  [attend(): pl.pallas_call(lambda *refs: attend_kernel(heads, count, views, *refs), g...]
    ppermute x3 -> x1, waiting for transfers between devices: 2.38 us -> 0.01 us  [shards(): far = lax.ppermute(own, 'xh', [(0, 1), (1, 0)])]
    ppermute x7, waiting for transfers between devices: 1.26 us -> 3.23 us  [shift(): return lax.ppermute(a, axis, [(s, (s + by) % size) for s in range(size)])]
    ppermute x1, waiting for transfers between devices: 2.15 us -> 0.74 us  [shards(): opp_send = lax.ppermute(opp_send, ('z', 'xh'), flips)]
    ppermute x1, waiting for transfers between devices: 0.02 us -> 1.42 us  [shards(): send = lax.ppermute(send, 'xh', [(0, 1), (1, 0)])]
    ppermute x3 -> x1, starting transfers between devices: 3.72 us -> 2.81 us  [shards(): far = lax.ppermute(own, 'xh', [(0, 1), (1, 0)])]
  transfers between devices with their start and end apart: 20 -> 18, of which waited for: 5 -> 7; matrix products, arithmetic and copies ran while one was open for 0% -> 0% of each run, Pallas kernels for 31% -> 29%
where the time goes in v8:
time: 111 us; the launch traced here: 110 us
  blocking collectives  42.1 us (38%)
  Pallas kernels  37.2 us (34%)
  starting transfers between devices  20.7 us (19%)
  waiting for transfers between devices  8.18 us (7%)
    pallas_call x3, Pallas kernels, attend(): pl.pallas_call(lambda *refs: attend_kernel(heads, count, views, *refs), g...  23.8 us
    all_to_all x1, blocking collectives, shards(): lax.all_to_all(prep(pair, cotangent, gain, shift_row, bias_rows, n_ja), J...  22.9 us
    all_to_all x1, blocking collectives, shards(): done = lax.all_to_all(done, JA, 0, 0, tiled=True)  19.3 us
    ppermute x7, starting transfers between devices, shift(): return lax.ppermute(a, axis, [(s, (s + by) % size) for s in range(size)])  11.1 us
    ppermute x1, starting transfers between devices, shards(): opp_send = lax.ppermute(opp_send, ('z', 'xh'), flips)  4.08 us
    pallas_call x1, Pallas kernels, finish(): pl.pallas_call(lambda *refs: finish_kernel(aheads, *refs), grid=(rows,),...  3.87 us
    pallas_call x1, Pallas kernels, project(): pl.pallas_call(project_kernel, grid=(rows,), in_specs=[pl.BlockSpec((n_bl...  3.84 us
    ppermute x7, waiting for transfers between devices, shift(): return lax.ppermute(a, axis, [(s, (s + by) % size) for s in range(size)])  3.23 us
  transfers between devices with their start and end apart: 18, of which 7 were waited for; matrix products, arithmetic and copies ran while one was open for 0% of the time, Pallas kernels for 29%

profile of v8, /device:TPU:0, one launch (start us, length us, event | category | flops | bytes accessed | tf_op | source)
XLA Modules:
  0.0 110.4 jit_solution(12628459446202401492)
XLA Ops:
  0.6 3.2 %shard_map.113 = bf16[8,9,64,128]{3,2,1,0:T(8,128)(2,1)} custom-call(bf16[32,64,128]{2,1,0:T(8,128)(2,1)} %pair_ref.3, bf16[32,64,128]{2,1,0:T(8,128)(2,1)} %cot_ref.1, f32[1,128]{1,0:T(1,128)} %bitcast.27, f32[1,128]{1,0:T(1,128)} %bitcast.30, bf16[4,128]{1,0:T(4,128)(2,1)} %bitcast.25), custom_call_target="tpu_custom_call" | custom-call | flops 134217728 | bytes 2097152 | tf_op jit(solution)/shard_map/pallas_call | solution.py:95
  3.8 0.0 copy-start.1
  3.8 0.0 copy-start.2
  3.8 0.0 copy-start.5
  3.8 0.0 copy-start.7
  3.8 0.0 copy-start.8
  3.9 22.9 %all_to_all.10.pair_ref.cot_ref.refs_1_ = bf16[8,9,64,128]{3,2,1,0:T(8,128)(2,1)S(1)} all-to-all(bf16[8,9,64,128]{3,2,1,0:T(8,128)(2,1)} %shard_map.113), channel_id=1, replica_groups=mesh['z'=4,'xh'=2,'core'=2,'y'=4,'xl'=2] {'y','xl'}, dimensions={0} | all-to-all | bytes 2359296 | tf_op jit(solution)/shard_map/all_to_all | solution.py:592
  26.8 2.8 %collective-permute-start = (bf16[8,64,128]{2,1,0:T(8,128)(2,1)S(1)}, bf16[8,64,128]{2,1,0:T(8,128)(2,1)S(1)}, u32[]{:S(2)}, u32[]{:S(2)}) collective-permute-start(bf16[8,64,128]{2,1,0:T(8,128)(2,1)S(1)} %get-tuple-element.169), channel_id=1, source_target_pairs={{0,16},{16,0},{1,17},{17,1},{2,18},{18,2},{3,19},{19,3},{4,20},{20... | collective-permute-start | bytes 393224 | tf_op jit(solution)/shard_map/ppermute | solution.py:600
  29.6 0.0 copy-done.1
  29.6 0.0 copy-done.2
  29.6 0.0 copy-done.3
  29.6 0.0 copy-done.4
  29.6 0.0 copy-done.5
  29.6 0.0 copy-done.7
  29.6 0.0 copy-done.8
  29.6 3.8 %shard_map.114 = (bf16[4,512,256]{2,1,0:T(8,128)(2,1)}, bf16[4,256,512]{2,1,0:T(8,128)(2,1)}, bf16[4,4,128,128]{3,2,1,0:T(8,128)(2,1)}, bf16[4,4,128,128]{3,2,1,...) custom-call(bf16[8,9,64,128]{3,2,1,0:T(8,128)(2,1)S(1)} %all_to_all.10.pair_ref.cot_ref.refs_1_, ...), custom_call_target="tpu_custom_call" | custom-call | flops 2147483648 | bytes 8388608 | tf_op jit(solution)/shard_map/pallas_call | solution.py:163
  33.5 0.0 collective-permute-done
  33.5 0.1 collective-permute-start.1
  33.6 4.1 %collective-permute-start.3 = (bf16[2,8,64,128]{3,2,1,0:T(8,128)(2,1)S(1)}, bf16[2,8,64,128]{3,2,1,0:T(8,128)(2,1)S(1)}, u32[]{:S(2)}, u32[]{:S(2)}) collective-permute-start(bf16[2,8,64,128]{3,2,1,0:T(8,128)(2,1)S(1)} %pad_maximum_fusion.1.refs_5_), channel_id=1, source_target_pairs={{0,96},{32,0},{64,32},{96,64},{1,97},{33,1},{65,33},{97,65},{2,98}... | collective-permute-start | bytes 786440 | tf_op jit(solution)/shard_map/ppermute | solution.py:47
  37.7 0.0 collective-permute-start.2
  37.7 0.0 collective-permute-done.1.refs_6_
  37.7 6.4 %shard_map.115 = (f32[1,4,128,128]{3,2,1,0:T(8,128)S(1)}, bf16[1,4,128,128]{3,2,1,0:T(8,128)(2,1)S(1)}, bf16[4,512,128]{2,1,0:T(8,128)(2,1)S(1)}, bf16[4,512,128...) custom-call(bf16[4,512,256]{2,1,0:T(8,128)(2,1)} %get-tuple-element.90.refs_0_, ...), custom_call_target="tpu_custom_call" | custom-call | flops 4294967296 | bytes 8388608 | tf_op jit(solution)/shard_map/pallas_call | solution.py:401
  44.2 0.0 collective-permute-done.3.refs_7_
  44.2 3.1 %collective-permute-done.2.refs_5_ = bf16[2,8,64,128]{3,2,1,0:T(8,128)(2,1)S(1)} collective-permute-done((bf16[2,8,64,128]{3,2,1,0:T(8,128)(2,1)S(1)}, bf16[2,8,64,128]{3,2,1,0:T(8,128)(2,1)S(1)}, u32[]{:S(2)}, u32[]{:S(2)}) %collective-permute-start.2) | collective-permute-done | bytes 262176 | tf_op jit(solution)/shard_map/ppermute | solution.py:47
  47.3 0.0 collective-permute-start.4
  47.3 0.5 collective-permute-start.5
  47.8 0.4 collective-permute-start.7
  48.2 1.8 %collective-permute-start.6 = (bf16[8,64,128]{2,1,0:T(8,128)(2,1)S(1)}, bf16[8,64,128]{2,1,0:T(8,128)(2,1)S(1)}, u32[]{:S(2)}, u32[]{:S(2)}) collective-permute-start(bf16[8,64,128]{2,1,0:T(8,128)(2,1)S(1)} %slice_bitcast_fusion.3), channel_id=1, source_target_pairs={{0,32},{32,64},{64,96},{96,0},{1,33},{33,65},{65,97},{97,1},{2,34}... | collective-permute-start | bytes 393224 | tf_op jit(solution)/shard_map/ppermute | solution.py:47
  50.0 0.0 collective-permute-start.8
  50.0 0.0 collective-permute-done.4.refs_6_
  50.0 0.0 collective-permute-done.5.refs_8_
  50.0 11.0 %shard_map.116 = (f32[2,4,128,128]{3,2,1,0:T(8,128)S(1)}, bf16[2,4,128,128]{3,2,1,0:T(8,128)(2,1)S(1)}, bf16[4,512,128]{2,1,0:T(8,128)(2,1)S(1)}, bf16[4,512,128...) custom-call(bf16[4,512,256]{2,1,0:T(8,128)(2,1)} %get-tuple-element.90.refs_0_, ...), custom_call_target="tpu_custom_call" | custom-call | flops 8589934592 | bytes 8388608 | tf_op jit(solution)/shard_map/pallas_call | solution.py:401
  61.0 0.0 collective-permute-done.7.refs_6_
  61.0 0.0 collective-permute-done.6.refs_5_
  61.0 0.0 collective-permute-done.8
  61.0 0.6 collective-permute-start.9
  61.6 0.1 collective-permute-start.10
  61.7 0.4 collective-permute-start.11
  62.1 1.2 %collective-permute-done.10.refs_7_ = bf16[8,64,128]{2,1,0:T(8,128)(2,1)S(1)} collective-permute-done((bf16[8,64,128]{2,1,0:T(8,128)(2,1)S(1)}, bf16[8,64,128]{2,1,0:T(8,128)(2,1)S(1)}, u32[]{:S(2)}, u32[]{:S(2)}) %collective-permute-start.10) | collective-permute-done | bytes 131104 | tf_op jit(solution)/shard_map/ppermute | solution.py:42
  63.3 0.2 collective-permute-done.11.refs_8_
  63.5 0.0 collective-permute-done.9
  63.5 0.2 add_convert_fusion
  63.7 0.3 collective-permute-start.13
  64.1 3.0 %collective-permute-start.12 = (bf16[2,8,64,128]{3,2,1,0:T(8,128)(2,1)S(1)}, bf16[2,8,64,128]{3,2,1,0:T(8,128)(2,1)S(1)}, u32[]{:S(2)}, u32[]{:S(2)}) collective-permute-start(bf16[2,8,64,128]{3,2,1,0:T(8,128)(2,1)S(1)} %get-tuple-element.171), channel_id=1, source_target_pairs={{0,96},{32,0},{64,32},{96,64},{1,97},{33,1},{65,33},{97,65},{2,98}... | collective-permute-start | bytes 786440 | tf_op jit(solution)/shard_map/ppermute | solution.py:47
  67.0 6.4 %shard_map.117 = (f32[1,4,128,128]{3,2,1,0:T(8,128)S(1)}, bf16[1,4,128,128]{3,2,1,0:T(8,128)(2,1)S(1)}, bf16[4,512,128]{2,1,0:T(8,128)(2,1)S(1)}, bf16[4,512,128...) custom-call(bf16[4,512,256]{2,1,0:T(8,128)(2,1)} %get-tuple-element.90.refs_0_, ...), custom_call_target="tpu_custom_call" | custom-call | flops 4294967296 | bytes 8388608 | tf_op jit(solution)/shard_map/pallas_call | solution.py:401
  73.5 0.1 collective-permute-done.13.refs_3_
  73.6 0.0 collective-permute-done.12.refs_2_
  73.6 0.0 collective-permute-start.14
  73.6 0.1 shard_map.119
  73.8 1.4 %collective-permute-done.14 = bf16[1,2,8,64,128]{4,3,2,1,0:T(8,128)(2,1)S(1)} collective-permute-done((bf16[1,2,8,64,128]{4,3,2,1,0:T(8,128)(2,1)S(1)}, bf16[1,2,8,64,128]{4,3,2,1,0:T(8,128)(2,1)S(1)}, u32[]{:S(2)}, u32[]{:S(2)}) %collective-permute-start.14) | collective-permute-done | bytes 262176 | tf_op jit(solution)/shard_map/ppermute | solution.py:42
  75.1 0.1 shard_map.120
  75.2 1.5 %collective-permute-start.15 = (bf16[8,64,128]{2,1,0:T(8,128)(2,1)S(1)}, bf16[8,64,128]{2,1,0:T(8,128)(2,1)S(1)}, u32[]{:S(2)}, u32[]{:S(2)}) collective-permute-start(bf16[8,64,128]{2,1,0:T(8,128)(2,1)S(1)} %get-tuple-element.156), channel_id=1, source_target_pairs={{0,64},{32,96},{64,0},{96,32},{1,65},{33,97},{65,1},{97,33},{2,66}... | collective-permute-start | bytes 393224 | tf_op jit(solution)/shard_map/ppermute | solution.py:47
  76.7 4.1 %collective-permute-start.16 = (bf16[8,64,128]{2,1,0:T(8,128)(2,1)S(1)}, bf16[8,64,128]{2,1,0:T(8,128)(2,1)S(1)}, u32[]{:S(2)}, u32[]{:S(2)}) collective-permute-start(bf16[8,64,128]{2,1,0:T(8,128)(2,1)S(1)} %get-tuple-element.157), channel_id=1, source_target_pairs={{0,80},{16,64},{32,112},{48,96},{64,16},{80,0},{96,48},{112,32},{1... | collective-permute-start | bytes 393224 | tf_op jit(solution)/shard_map/ppermute | solution.py:632
  80.8 1.0 collective-permute-start.17
  81.8 3.9 %shard_map.118.done_ref = bf16[8,9,64,128]{3,2,1,0:T(8,128)(2,1)S(1)} custom-call(f32[4,128,512]{2,1,0:T(8,128)} %get-tuple-element.89.refs_0_, bf16[8,9,64,128]{3,2,1,0:T(8,128)(2,1)S(1)} %all_to_all.10.pair_ref.cot_ref.refs_1_, bf16[128,128]{1,0:T(8,128)(2,1)S(1)} %copy-done.1, bf16[128,128]{1,0:T(8,128)(2,1)S(1)} %copy-done.2, ...), custom_call_target="tpu_custom_call" | custom-call | flops 2147483648 | bytes 8388608 | tf_op jit(solution)/shard_map/pallas_call | solution.py:473
  85.6 0.0 collective-permute-done.15.c_ref
  85.7 0.7 collective-permute-done.16.d_ref
  86.4 1.4 %collective-permute-done.17.b_ref = bf16[8,64,128]{2,1,0:T(8,128)(2,1)S(1)} collective-permute-done((bf16[8,64,128]{2,1,0:T(8,128)(2,1)S(1)}, bf16[8,64,128]{2,1,0:T(8,128)(2,1)S(1)}, u32[]{:S(2)}, u32[]{:S(2)}) %collective-permute-start.17) | collective-permute-done | bytes 131104 | tf_op jit(solution)/shard_map/ppermute | solution.py:633
  87.8 0.1 shard_map.121
  87.9 19.3 %all_to_all.11.both_ref = bf16[8,9,64,128]{3,2,1,0:T(8,128)(2,1)S(1)} all-to-all(bf16[8,9,64,128]{3,2,1,0:T(8,128)(2,1)S(1)} %shard_map.121), channel_id=1, replica_groups=mesh['z'=4,'xh'=2,'core'=2,'y'=4,'xl'=2] {'y','xl'}, dimensions={0} | all-to-all | bytes 2359296 | tf_op jit(solution)/shard_map/all_to_all | solution.py:638
  107.2 0.9 pad_maximum_fusion
  108.1 0.2 copy-done
  108.3 0.0 copy-done.6
  108.3 2.2 %shard_map.122 = f32[32,64,128]{2,1,0:T(8,128)} custom-call(bf16[32,64,128]{2,1,0:T(8,128)(2,1)S(1)} %copy-done, bf16[8,9,64,128]{3,2,1,0:T(8,128)(2,1)S(1)} %all_to_all.11.both_ref, f32[1,128]{1,0:T(1,128)S(1)} %bitcast.29, f32[1,128]{1,0:T(1,128)S(1)} %bitcast.32, bf16[4,128]{1,0:T(4,128)(2,1)S(1)} %bitcast.26), custom_call_target="tpu_custom_call" | custom-call | flops 134217728 | bytes 2097152 | tf_op jit(solution)/shard_map/pallas_call | solution.py:560
  (10 shorter events, 0.2 us)
Async XLA Ops:
  3.8 25.8 %copy-start.1 = (bf16[128,128]{1,0:T(8,128)(2,1)S(1)}, bf16[128,128]{1,0:T(8,128)(2,1)}, u32[]{:S(2)}) copy-start(bf16[128,128]{1,0:T(8,128)(2,1)} %refs_2_.1) | copy-start | bytes 98308
  3.8 25.8 %copy-start.2 = (bf16[128,128]{1,0:T(8,128)(2,1)S(1)}, bf16[128,128]{1,0:T(8,128)(2,1)}, u32[]{:S(2)}) copy-start(bf16[128,128]{1,0:T(8,128)(2,1)} %refs_3_.1) | copy-start | bytes 98308
  3.8 25.8 %copy-start.3 = (bf16[128,128]{1,0:T(8,128)(2,1)S(1)}, bf16[128,128]{1,0:T(8,128)(2,1)}, u32[]{:S(2)}) copy-start(bf16[128,128]{1,0:T(8,128)(2,1)} %refs_4_.1) | copy-start | bytes 98308
  3.8 25.8 %copy-start.4 = (bf16[128,128]{1,0:T(8,128)(2,1)S(1)}, bf16[128,128]{1,0:T(8,128)(2,1)}, u32[]{:S(2)}) copy-start(bf16[128,128]{1,0:T(8,128)(2,1)} %refs_5_.1) | copy-start | bytes 98308
  3.8 25.8 %copy-start.5 = (bf16[128,128]{1,0:T(8,128)(2,1)S(1)}, bf16[128,128]{1,0:T(8,128)(2,1)}, u32[]{:S(2)}) copy-start(bf16[128,128]{1,0:T(8,128)(2,1)} %refs_6_.1) | copy-start | bytes 98308
  3.8 25.8 %copy-start.7 = (f32[128]{0:T(128)S(1)}, f32[128]{0:T(128)}, u32[]{:S(2)}) copy-start(f32[128]{0:T(128)} %param.12) | copy-start | bytes 1540
  3.8 25.8 %copy-start.8 = (f32[128]{0:T(128)S(1)}, f32[128]{0:T(128)}, u32[]{:S(2)}) copy-start(f32[128]{0:T(128)} %param.13) | copy-start | bytes 1540
  26.8 6.7 %collective-permute-start = (bf16[8,64,128]{2,1,0:T(8,128)(2,1)S(1)}, bf16[8,64,128]{2,1,0:T(8,128)(2,1)S(1)}, u32[]{:S(2)}, u32[]{:S(2)}) collective-permute-start(bf16[8,64,128]{2,1,0:T(8,128)(2,1)S(1)} %get-tuple-element.169), channel_id=1, source_target_pairs={{0,16},{16,0},{1,17},{17,1},{2,18},{18,2},{3,19},{19,3},{4,20},{20... | collective-permute-start | bytes 393224 | tf_op jit(solution)/shard_map/ppermute | solution.py:600
  33.5 4.2 %collective-permute-start.1 = (bf16[2,8,64,128]{3,2,1,0:T(8,128)(2,1)S(1)}, bf16[2,8,64,128]{3,2,1,0:T(8,128)(2,1)S(1)}, u32[]{:S(2)}, u32[]{:S(2)}) collective-permute-start(bf16[2,8,64,128]{3,2,1,0:T(8,128)(2,1)S(1)} %pad_maximum_fusion.1.refs_5_), channel_id=1, source_target_pairs={{0,8},{8,0},{1,9},{9,1},{2,10},{10,2},{3,11},{11,3},{4,12},{12,4},... | collective-permute-start | bytes 786440 | tf_op jit(solution)/shard_map/ppermute | solution.py:42
  33.6 10.6 %collective-permute-start.3 = (bf16[2,8,64,128]{3,2,1,0:T(8,128)(2,1)S(1)}, bf16[2,8,64,128]{3,2,1,0:T(8,128)(2,1)S(1)}, u32[]{:S(2)}, u32[]{:S(2)}) collective-permute-start(bf16[2,8,64,128]{3,2,1,0:T(8,128)(2,1)S(1)} %pad_maximum_fusion.1.refs_5_), channel_id=1, source_target_pairs={{0,96},{32,0},{64,32},{96,64},{1,97},{33,1},{65,33},{97,65},{2,98}... | collective-permute-start | bytes 786440 | tf_op jit(solution)/shard_map/ppermute | solution.py:47
  37.7 9.6 %collective-permute-start.2 = (bf16[2,8,64,128]{3,2,1,0:T(8,128)(2,1)S(1)}, bf16[2,8,64,128]{3,2,1,0:T(8,128)(2,1)S(1)}, u32[]{:S(2)}, u32[]{:S(2)}) collective-permute-start(bf16[2,8,64,128]{3,2,1,0:T(8,128)(2,1)S(1)} %pad_maximum_fusion.1.refs_5_), channel_id=1, source_target_pairs={{0,32},{32,64},{64,96},{96,0},{1,33},{33,65},{65,97},{97,1},{2,34}... | collective-permute-start | bytes 786440 | tf_op jit(solution)/shard_map/ppermute | solution.py:47
  47.3 2.7 %collective-permute-start.4 = (bf16[2,8,64,128]{3,2,1,0:T(8,128)(2,1)S(1)}, bf16[2,8,64,128]{3,2,1,0:T(8,128)(2,1)S(1)}, u32[]{:S(2)}, u32[]{:S(2)}) collective-permute-start(bf16[2,8,64,128]{3,2,1,0:T(8,128)(2,1)S(1)} %collective-permute-done.2.refs_5_), channel_id=1, source_target_pairs={{0,8},{8,0},{1,9},{9,1},{2,10},{10,2},{3,11},{11,3},{4,12},{12,4},... | collective-permute-start | bytes 786440 | tf_op jit(solution)/shard_map/ppermute | solution.py:42
  47.3 2.7 %collective-permute-start.5 = (bf16[2,8,64,128]{3,2,1,0:T(8,128)(2,1)S(1)}, bf16[2,8,64,128]{3,2,1,0:T(8,128)(2,1)S(1)}, u32[]{:S(2)}, u32[]{:S(2)}) collective-permute-start(bf16[2,8,64,128]{3,2,1,0:T(8,128)(2,1)S(1)} %collective-permute-done.3.refs_7_), channel_id=1, source_target_pairs={{0,8},{8,0},{1,9},{9,1},{2,10},{10,2},{3,11},{11,3},{4,12},{12,4},... | collective-permute-start | bytes 786440 | tf_op jit(solution)/shard_map/ppermute | solution.py:42
  47.8 13.2 %collective-permute-start.7 = (bf16[8,64,128]{2,1,0:T(8,128)(2,1)S(1)}, bf16[8,64,128]{2,1,0:T(8,128)(2,1)S(1)}, u32[]{:S(2)}, u32[]{:S(2)}) collective-permute-start(bf16[8,64,128]{2,1,0:T(8,128)(2,1)S(1)} %slice_bitcast_fusion.2), channel_id=1, source_target_pairs={{0,96},{32,0},{64,32},{96,64},{1,97},{33,1},{65,33},{97,65},{2,98}... | collective-permute-start | bytes 393224 | tf_op jit(solution)/shard_map/ppermute | solution.py:47
  48.2 12.8 %collective-permute-start.6 = (bf16[8,64,128]{2,1,0:T(8,128)(2,1)S(1)}, bf16[8,64,128]{2,1,0:T(8,128)(2,1)S(1)}, u32[]{:S(2)}, u32[]{:S(2)}) collective-permute-start(bf16[8,64,128]{2,1,0:T(8,128)(2,1)S(1)} %slice_bitcast_fusion.3), channel_id=1, source_target_pairs={{0,32},{32,64},{64,96},{96,0},{1,33},{33,65},{65,97},{97,1},{2,34}... | collective-permute-start | bytes 393224 | tf_op jit(solution)/shard_map/ppermute | solution.py:47
  50.0 11.0 %collective-permute-start.8 = (bf16[1,2,8,64,128]{4,3,2,1,0:T(8,128)(2,1)S(1)}, bf16[1,2,8,64,128]{4,3,2,1,0:T(8,128)(2,1)S(1)}, u32[]{:S(2)}, u32[]{:S(2)}) collective-permute-start(bf16[1,2,8,64,128]{4,3,2,1,0:T(8,128)(2,1)S(1)} %get-tuple-element.107), channel_id=1, source_target_pairs={{0,8},{8,0},{1,9},{9,1},{2,10},{10,2},{3,11},{11,3},{4,12},{12,4},... | collective-permute-start | bytes 786440 | tf_op jit(solution)/shard_map/ppermute | solution.py:42
  61.0 2.5 %collective-permute-start.9 = (bf16[2,2,8,64,128]{4,3,2,1,0:T(8,128)(2,1)S(1)}, bf16[2,2,8,64,128]{4,3,2,1,0:T(8,128)(2,1)S(1)}, u32[]{:S(2)}, u32[]{:S(2)}) collective-permute-start(bf16[2,2,8,64,128]{4,3,2,1,0:T(8,128)(2,1)S(1)} %get-tuple-element.123), channel_id=1, source_target_pairs={{0,8},{8,0},{1,9},{9,1},{2,10},{10,2},{3,11},{11,3},{4,12},{12,4},... | collective-permute-start | bytes 1572872 | tf_op jit(solution)/shard_map/ppermute | solution.py:42
  61.6 1.7 %collective-permute-start.10 = (bf16[8,64,128]{2,1,0:T(8,128)(2,1)S(1)}, bf16[8,64,128]{2,1,0:T(8,128)(2,1)S(1)}, u32[]{:S(2)}, u32[]{:S(2)}) collective-permute-start(bf16[8,64,128]{2,1,0:T(8,128)(2,1)S(1)} %collective-permute-done.6.refs_5_), channel_id=1, source_target_pairs={{0,8},{8,0},{1,9},{9,1},{2,10},{10,2},{3,11},{11,3},{4,12},{12,4},... | collective-permute-start | bytes 393224 | tf_op jit(solution)/shard_map/ppermute | solution.py:42
  61.7 1.8 %collective-permute-start.11 = (bf16[8,64,128]{2,1,0:T(8,128)(2,1)S(1)}, bf16[8,64,128]{2,1,0:T(8,128)(2,1)S(1)}, u32[]{:S(2)}, u32[]{:S(2)}) collective-permute-start(bf16[8,64,128]{2,1,0:T(8,128)(2,1)S(1)} %collective-permute-done.7.refs_6_), channel_id=1, source_target_pairs={{0,8},{8,0},{1,9},{9,1},{2,10},{10,2},{3,11},{11,3},{4,12},{12,4},... | collective-permute-start | bytes 393224 | tf_op jit(solution)/shard_map/ppermute | solution.py:42
  63.7 9.9 %collective-permute-start.13 = (bf16[2,8,64,128]{3,2,1,0:T(8,128)(2,1)S(1)}, bf16[2,8,64,128]{3,2,1,0:T(8,128)(2,1)S(1)}, u32[]{:S(2)}, u32[]{:S(2)}) collective-permute-start(bf16[2,8,64,128]{3,2,1,0:T(8,128)(2,1)S(1)} %get-tuple-element.170), channel_id=1, source_target_pairs={{0,32},{32,64},{64,96},{96,0},{1,33},{33,65},{65,97},{97,1},{2,34}... | collective-permute-start | bytes 786440 | tf_op jit(solution)/shard_map/ppermute | solution.py:47
  64.1 9.5 %collective-permute-start.12 = (bf16[2,8,64,128]{3,2,1,0:T(8,128)(2,1)S(1)}, bf16[2,8,64,128]{3,2,1,0:T(8,128)(2,1)S(1)}, u32[]{:S(2)}, u32[]{:S(2)}) collective-permute-start(bf16[2,8,64,128]{3,2,1,0:T(8,128)(2,1)S(1)} %get-tuple-element.171), channel_id=1, source_target_pairs={{0,96},{32,0},{64,32},{96,64},{1,97},{33,1},{65,33},{97,65},{2,98}... | collective-permute-start | bytes 786440 | tf_op jit(solution)/shard_map/ppermute | solution.py:47
  73.6 1.5 %collective-permute-start.14 = (bf16[1,2,8,64,128]{4,3,2,1,0:T(8,128)(2,1)S(1)}, bf16[1,2,8,64,128]{4,3,2,1,0:T(8,128)(2,1)S(1)}, u32[]{:S(2)}, u32[]{:S(2)}) collective-permute-start(bf16[1,2,8,64,128]{4,3,2,1,0:T(8,128)(2,1)S(1)} %get-tuple-element.148), channel_id=1, source_target_pairs={{0,8},{8,0},{1,9},{9,1},{2,10},{10,2},{3,11},{11,3},{4,12},{12,4},... | collective-permute-start | bytes 786440 | tf_op jit(solution)/shard_map/ppermute | solution.py:42
  75.2 10.5 %collective-permute-start.15 = (bf16[8,64,128]{2,1,0:T(8,128)(2,1)S(1)}, bf16[8,64,128]{2,1,0:T(8,128)(2,1)S(1)}, u32[]{:S(2)}, u32[]{:S(2)}) collective-permute-start(bf16[8,64,128]{2,1,0:T(8,128)(2,1)S(1)} %get-tuple-element.156), channel_id=1, source_target_pairs={{0,64},{32,96},{64,0},{96,32},{1,65},{33,97},{65,1},{97,33},{2,66}... | collective-permute-start | bytes 393224 | tf_op jit(solution)/shard_map/ppermute | solution.py:47
  76.7 9.7 %collective-permute-start.16 = (bf16[8,64,128]{2,1,0:T(8,128)(2,1)S(1)}, bf16[8,64,128]{2,1,0:T(8,128)(2,1)S(1)}, u32[]{:S(2)}, u32[]{:S(2)}) collective-permute-start(bf16[8,64,128]{2,1,0:T(8,128)(2,1)S(1)} %get-tuple-element.157), channel_id=1, source_target_pairs={{0,80},{16,64},{32,112},{48,96},{64,16},{80,0},{96,48},{112,32},{1... | collective-permute-start | bytes 393224 | tf_op jit(solution)/shard_map/ppermute | solution.py:632
  80.8 7.0 %collective-permute-start.17 = (bf16[8,64,128]{2,1,0:T(8,128)(2,1)S(1)}, bf16[8,64,128]{2,1,0:T(8,128)(2,1)S(1)}, u32[]{:S(2)}, u32[]{:S(2)}) collective-permute-start(bf16[8,64,128]{2,1,0:T(8,128)(2,1)S(1)} %get-tuple-element.158), channel_id=1, source_target_pairs={{0,16},{16,0},{1,17},{17,1},{2,18},{18,2},{3,19},{19,3},{4,20},{20... | collective-permute-start | bytes 393224 | tf_op jit(solution)/shard_map/ppermute | solution.py:633
  107.2 1.1 copy-start
  107.2 1.1 copy-start.6

commit v9 on v8

--- a/solution.py
+++ b/solution.py
@@ -19,13 +19,6 @@
 FIRST = pltpu.CompilerParams(vmem_limit_bytes=60 * 1024 * 1024)
 
 
-def normalize(values, norm_gain, norm_shift):
-    mean_val = jnp.mean(values, axis=-1, keepdims=True)
-    centred = values - mean_val
-    variance = jnp.mean(centred * centred, axis=-1, keepdims=True)
-    return centred * lax.rsqrt(variance + EPSILON) * norm_gain + norm_shift
-
-
 def mm(a, b):
     return lax.dot_general(a, b, (((1,), (0,)), ((), ())), preferred_element_type=F32)
 
@@ -36,6 +29,19 @@
 
 def mm_tn(a, b):
     return lax.dot_general(a, b, (((0,), (0,)), ((), ())), preferred_element_type=F32)
+
+
+def centre(rows):
+    channels = rows.shape[1]
+    share = jnp.full((channels, channels), 1.0 / channels, BF16)
+    centred = rows.astype(F32) - mm(rows, share)
+    variance = jnp.mean(centred * centred, axis=-1, keepdims=True)
+    return centred, lax.rsqrt(variance + EPSILON)
+
+
+def normalize(rows, norm_gain, norm_shift):
+    centred, rstd = centre(rows)
+    return (centred * rstd * norm_gain + norm_shift).astype(BF16)
 
 
 def swap(a):
@@ -67,15 +73,10 @@
     return jnp.concatenate(rows, axis=0).astype(BF16)
 
 
-def prep_kernel(pair_ref, cot_ref, gain_ref, shift_ref, w_ref, out_ref):
+def prep_kernel(pair_ref, gain_ref, shift_ref, w_ref, tile_ref):
     rows, block, channels = pair_ref.shape
-    n_ja = out_ref.shape[0]
-    own = rows // n_ja
-    split = (n_ja, own, block, channels)
-    out_ref[:, :own] = pair_ref[...].reshape(split)
-    out_ref[:, own : 2 * own] = cot_ref[...].reshape(split)
-    x = pair_ref[...].reshape(rows * block, channels).astype(F32)
-    normed = normalize(x, gain_ref[...], shift_ref[...]).astype(BF16)
+    x = pair_ref[...].reshape(rows * block, channels)
+    normed = normalize(x, gain_ref[...], shift_ref[...])
     every = mm_nt(normed, spread_heads(w_ref, block))
     width = every.shape[1]
     keep = line_mask(block, width)
@@ -85,21 +86,43 @@
         lines.append(jnp.sum(part, axis=0, keepdims=True))
     tile = jnp.concatenate(lines, axis=0).astype(BF16)
     tile = jnp.concatenate([tile[:, :LANES], tile[:, LANES:]], axis=0)
-    for d in range(n_ja):
-        out_ref[d, 2 * own] = tile
-
-
-def prep(pair, cot, gain, shift_row, bias_weight, n_ja):
+    for d in range(tile_ref.shape[0]):
+        tile_ref[d] = tile
+
+
+def prep(pair, gain, shift_row, bias_weight, copies):
     rows, block, channels = pair.shape
-    out = jax.ShapeDtypeStruct((n_ja, 2 * rows // n_ja + 1, block, channels), BF16)
     return pl.pallas_call(
         prep_kernel,
-        out_shape=out,
+        out_shape=jax.ShapeDtypeStruct((copies, block, channels), BF16),
         compiler_params=FIRST,
         cost_estimate=pl.CostEstimate(
-            flops=2**27, bytes_accessed=2**21, transcendentals=2**12
+            flops=2**27, bytes_accessed=2**20, transcendentals=2**12
         ),
-    )(pair, cot, gain, shift_row, bias_weight)
+    )(pair, gain, shift_row, bias_weight)
+
+
+def pack_kernel(pair_ref, cot_ref, out_ref):
+    group, slabs, block, channels = out_ref.shape
+    own = slabs // 2
+    out_ref[:, :own] = pair_ref[...].reshape(group, own, block, channels)
+    out_ref[:, own:] = cot_ref[...].reshape(group, own, block, channels)
+
+
+def pack(pair, cot, n_ja):
+    rows, block, channels = pair.shape
+    own = rows // n_ja
+    group = n_ja // 2
+    part = pl.BlockSpec((group * own, block, channels), lambda d: (d, 0, 0))
+    return pl.pallas_call(
+        pack_kernel,
+        grid=(n_ja // group,),
+        in_specs=[part, part],
+        out_specs=pl.BlockSpec((group, 2 * own, block, channels), lambda d: (d, 0, 0, 0)),
+        out_shape=jax.ShapeDtypeStruct((n_ja, 2 * own, block, channels), BF16),
+        compiler_params=FIRST,
+        cost_estimate=pl.CostEstimate(flops=2**10, bytes_accessed=2**21, transcendentals=0),
+    )(pair, cot)
 
 
 def project_kernel(
@@ -119,32 +142,35 @@
     d_att_ref,
     gate_ref,
 ):
-    n_blocks, _, block, channels = pair_ref.shape
+    n_blocks, group, block, channels = pair_ref.shape
     n = n_blocks * block
     inner = w_q_ref.shape[1]
-    x = pair_ref[...].reshape(n, channels).astype(F32)
-    normed = normalize(x, gain_ref[...], shift_ref[...]).astype(BF16)
     weights = [ref[...] for ref in (w_q_ref, w_k_ref, w_v_ref, w_g_ref)]
-    proj = mm(normed, jnp.concatenate(weights[:3], axis=1)).astype(BF16)
-    kv_n_ref[0] = proj[:, inner:]
-    proj_t = mm_nt(jnp.concatenate([w.T for w in weights], axis=0), normed)
-    kv_t_ref[0] = proj_t[inner : 3 * inner].astype(BF16)
-    gate = jax.nn.sigmoid(proj_t[3 * inner :])
-    gate_ref[0] = gate
-    d_att = mm_nt(w_o_ref[...], cot_ref[...].reshape(n, channels)) * gate
+    w_n = jnp.concatenate(weights[:3], axis=1)
+    w_t = jnp.concatenate([w.T for w in weights], axis=0)
     size = lax.axis_size("z")
     z = lax.axis_index("z")
-    for owner in range(n // LANES):
-        at = slice(owner * LANES, (owner + 1) * LANES)
-        ahead = lax.rem(owner + size - z, size)
-        q_n_ref[ahead, 0] = proj[at, :inner]
-        q_t_ref[ahead, 0] = proj_t[:inner, at].astype(BF16)
-        d_att_ref[ahead, 0] = d_att[:, at]
+    for r in range(group):
+        normed = normalize(pair_ref[:, r].reshape(n, channels), gain_ref[...], shift_ref[...])
+        proj = mm(normed, w_n).astype(BF16)
+        kv_n_ref[r] = proj[:, inner:]
+        proj_t = mm_nt(w_t, normed)
+        kv_t_ref[r] = proj_t[inner : 3 * inner].astype(BF16)
+        gate = jax.nn.sigmoid(proj_t[3 * inner :])
+        gate_ref[r] = gate
+        d_att = mm_nt(w_o_ref[...], cot_ref[:, r].reshape(n, channels)) * gate
+        for owner in range(n // LANES):
+            at = slice(owner * LANES, (owner + 1) * LANES)
+            ahead = lax.rem(owner + size - z, size)
+            q_n_ref[ahead, r] = proj[at, :inner]
+            q_t_ref[ahead, r] = proj_t[:inner, at].astype(BF16)
+            d_att_ref[ahead, r] = d_att[:, at]
 
 
 def project(both, gain, shift_row, w_o, weights):
     n_blocks, slabs, block, channels = both.shape
     rows = slabs // 2
+    group = 2
     n = n_blocks * block
     inner = w_o.shape[0]
     kv_n = pltpu.HBM((rows, n, 2 * inner), BF16)
@@ -155,17 +181,19 @@
     d_att = pltpu.HBM((n // LANES, rows, inner, LANES), F32)
 
     def by_row(a):
-        return pl.BlockSpec((1,) + a.shape[1:], lambda i: (i, 0, 0))
+        return pl.BlockSpec((group,) + a.shape[1:], lambda i: (i, 0, 0))
 
     def sliced(a):
-        return pl.BlockSpec((a.shape[0], 1) + a.shape[2:], lambda i: (0, i, 0, 0))
+        return pl.BlockSpec((a.shape[0], group) + a.shape[2:], lambda i: (0, i, 0, 0))
 
     return pl.pallas_call(
         project_kernel,
-        grid=(rows,),
+        grid=(rows // group,),
         in_specs=[
-            pl.BlockSpec((n_blocks, 1, block, channels), lambda i: (0, i, 0, 0)),
-            pl.BlockSpec((n_blocks, 1, block, channels), lambda i: (0, rows + i, 0, 0)),
+            pl.BlockSpec((n_blocks, group, block, channels), lambda i: (0, i, 0, 0)),
+            pl.BlockSpec(
+                (n_blocks, group, block, channels), lambda i: (0, rows // group + i, 0, 0)
+            ),
         ]
         + [whole(a) for a in (gain, shift_row, w_o, *weights)],
         out_specs=[by_row(kv_n), by_row(kv_t)]
@@ -200,7 +228,6 @@
     pairs = heads // 2
     wide = 2 * LANES
     core = lax.axis_index("core")
-    xh = lax.axis_index("xh")
     copies = [
         pltpu.make_async_copy(src, dst, sems.at[e])
         for e, (src, dst) in enumerate(((kv_n_hbm, n_ref), (kv_t_hbm, t_ref)))
@@ -221,7 +248,7 @@
             for ref in bias_refs[base : base + views]:
                 parts += [ref] if len(ref.shape) == 3 else [ref.at[e] for e in range(2)]
             for far, ref in enumerate(parts):
-                at = (xh ^ far) * 2 + (core ^ which)
+                at = far * 2 + (core ^ which)
                 at = pl.ds(pl.multiple_of(at * rows_i, rows_i), rows_i)
                 for owner in range(n_ja):
                     for p in range(pairs):
@@ -233,7 +260,7 @@
         pl.when(at_slice == c)(lambda c=c: sort_tiles(c))
     for owner in range(n_ja):
         for p in range(pairs):
-            t = tile_s[owner, :, p * LANES : (p + 1) * LANES].astype(F32).T * LOG2E
+            t = tile_s[owner, :, p * LANES : (p + 1) * LANES].T.astype(F32) * LOG2E
             for e in range(2):
                 h = p * 2 + e
                 bias_s[owner * block : (owner + 1) * block, h * LANES : (h + 1) * LANES] = t[
@@ -367,7 +394,7 @@
                 ],
                 axis=0,
             )
-            line_s[:, p * LANES : (p + 1) * LANES] = t.T.astype(BF16)
+            line_s[:, p * LANES : (p + 1) * LANES] = t.astype(BF16).T
         for far in range(2):
             for ref, which in ((mine_ref, core), (theirs_ref, 1 - core)):
                 at = pl.multiple_of((far * 2 + which) * rows_i, rows_i)
@@ -434,54 +461,60 @@
     att_refs, dq_refs = refs[:count], refs[count : 2 * count]
     dk_refs, dv_refs = refs[2 * count : 3 * count], refs[3 * count : 4 * count]
     out_ref, att_s, dq_s = refs[4 * count :]
-    for group, att_ref, dq_ref in zip(aheads, att_refs, dq_refs):
-        for c, ahead in enumerate(group):
+    group, inner, n = gate_ref.shape
+    for rows, att_ref, dq_ref in zip(aheads, att_refs, dq_refs):
+        for c, ahead in enumerate(rows):
             at = z_lanes(ahead)
-            att_s[:, at] = att_ref[c, 0]
-            dq_s[:, at] = dq_ref[c, 0]
+            for r in range(group):
+                att_s[r, :, at] = att_ref[c, r]
+                dq_s[r, :, at] = dq_ref[c, r]
+    w_t = jnp.concatenate([w_q_ref[...].T, w_g_ref[...].T], axis=0)
+    w_n = jnp.concatenate([w_k_ref[...].T, w_v_ref[...].T], axis=0)
     half = (out_ref.shape[0],) + out_ref.shape[2:]
-    gate = gate_ref[0]
-    cot = cot_ref[...].reshape(gate.shape[1], cot_ref.shape[3])
-    d_gated = mm_nt(w_o_ref[...], cot)
-    att = att_s[...]
-    update = mm_tn((gate * att).astype(BF16), w_o_ref[...])
-    out_ref[:, 0] = update.astype(BF16).reshape(half)
-    d_gate = (d_gated * att * gate * (1.0 - gate)).astype(BF16)
-    left_t = jnp.concatenate([dq_s[...], d_gate], axis=0)
-    dk = sum(ref[0].astype(F32) for ref in dk_refs).astype(BF16)
-    dv = sum(ref[0].astype(F32) for ref in dv_refs).astype(BF16)
-    dn = mm_tn(left_t, jnp.concatenate([w_q_ref[...].T, w_g_ref[...].T], axis=0))
-    dn = dn + mm(
-        jnp.concatenate([dk, dv], axis=1),
-        jnp.concatenate([w_k_ref[...].T, w_v_ref[...].T], axis=0),
-    )
-    out_ref[:, 1] = dn.astype(BF16).reshape(half)
+    for r in range(group):
+        gate = gate_ref[r]
+        d_gated = mm_nt(w_o_ref[...], cot_ref[:, r].reshape(n, cot_ref.shape[3]))
+        att = att_s[r]
+        update = mm_tn((gate * att).astype(BF16), w_o_ref[...])
+        out_ref[:, 2 * r] = update.astype(BF16).reshape(half)
+        d_gate = (d_gated * att * gate * (1.0 - gate)).astype(BF16)
+        left_t = jnp.concatenate([dq_s[r], d_gate], axis=0)
+        dk = sum(ref[r].astype(F32) for ref in dk_refs).astype(BF16)
+        dv = sum(ref[r].astype(F32) for ref in dv_refs).astype(BF16)
+        dn = mm_tn(left_t, w_t) + mm(jnp.concatenate([dk, dv], axis=1), w_n)
+        out_ref[:, 2 * r + 1] = dn.astype(BF16).reshape(half)
 
 
 def finish(aheads, gate, both, w_o, weights, att, dq, dk, dv):
     n_blocks, _, block, channels = both.shape
-    rows, inner, _ = gate.shape
+    rows, inner, n = gate.shape
+    group = 2
     arrays = (*att, *dq, *dk, *dv)
 
     def by_row(a):
-        return pl.BlockSpec((1,) + a.shape[1:], lambda i: (i, 0, 0))
+        return pl.BlockSpec((group,) + a.shape[1:], lambda i: (i, 0, 0))
 
     def by_slices(a):
-        return pl.BlockSpec((a.shape[0], 1) + a.shape[2:], lambda i: (0, i, 0, 0))
-
-    cot_spec = pl.BlockSpec((n_blocks, 1, block, channels), lambda i: (0, rows + i, 0, 0))
+        return pl.BlockSpec((a.shape[0], group) + a.shape[2:], lambda i: (0, i, 0, 0))
+
     return pl.pallas_call(
         lambda *refs: finish_kernel(aheads, *refs),
-        grid=(rows,),
-        in_specs=[by_row(gate), cot_spec, whole(w_o)]
+        grid=(rows // group,),
+        in_specs=[
+            by_row(gate),
+            pl.BlockSpec(
+                (n_blocks, group, block, channels), lambda i: (0, rows // group + i, 0, 0)
+            ),
+            whole(w_o),
+        ]
         + [whole(a) for a in weights]
         + [by_slices(a) for a in (*att, *dq)]
         + [by_row(a) for a in (*dk, *dv)],
-        out_specs=pl.BlockSpec((n_blocks, 2, block, channels), lambda i: (0, i, 0, 0)),
+        out_specs=pl.BlockSpec((n_blocks, 2 * group, block, channels), lambda i: (0, i, 0, 0)),
         out_shape=jax.ShapeDtypeStruct((n_blocks, 2 * rows + 1, block, channels), BF16),
         scratch_shapes=[
-            pltpu.VMEM((inner, n_blocks * block), F32),
-            pltpu.VMEM((inner, n_blocks * block), BF16),
+            pltpu.VMEM((group, inner, n), F32),
+            pltpu.VMEM((group, inner, n), BF16),
         ],
         compiler_params=PARAMS,
         cost_estimate=pl.CostEstimate(flops=2**31, bytes_accessed=2**23, transcendentals=0),
@@ -505,10 +538,9 @@
     )(*arrays)
 
 
-def fill_kernel(done_ref, a_ref, b_ref, c_ref, d_ref, out_ref):
+def fill_kernel(done_ref, a_ref, b_ref, out_ref):
     del done_ref
-    total = sum(ref[...].astype(F32) for ref in (a_ref, b_ref, c_ref, d_ref))
-    out_ref[:, 0] = total.astype(BF16)
+    out_ref[:, 0] = (a_ref[...].astype(F32) + b_ref[...].astype(F32)).astype(BF16)
 
 
 def fill(done, *parts):
@@ -527,13 +559,22 @@
 
 
 def final_kernel(
-    pair_ref, both_ref, gain_ref, shift_ref, w_ref, out_ref
+    pair_ref, both_ref, gb_ref, gain_ref, shift_ref, w_ref, update_ref, out_ref, tile_s
 ):
     rows, block, channels = pair_ref.shape
-    n_ja = both_ref.shape[0]
-    own = rows // n_ja
-    tile = jnp.sum(both_ref[:, 2 * own].astype(F32), axis=0)
-    tile = jnp.concatenate([tile[:rows], tile[rows:]], axis=1).astype(BF16).astype(F32)
+    group, slabs = both_ref.shape[:2]
+    own = slabs // 2
+    step = pl.program_id(0)
+
+    @pl.when(step == 0)
+    def _():
+        tile = jnp.sum(gb_ref[:, 0].astype(F32), axis=0)
+        half = tile.shape[0] // 2
+        tile = jnp.concatenate([tile[:half], tile[half:]], axis=1).astype(BF16).astype(F32)
+        for e in range(tile_s.shape[0]):
+            tile_s[e] = tile[e * rows : (e + 1) * rows]
+
+    tile = tile_s[step]
     keep = line_mask(block, tile.shape[1])
     spread = jnp.concatenate(
         [
@@ -542,13 +583,13 @@
         ],
         axis=0,
     )
-    w_back = spread_heads(w_ref, block)
-    dn = [both_ref[:, 2 * i + 1][:, None] for i in range(own)]
-    dn = jnp.concatenate(dn, axis=1).reshape(rows * block, channels).astype(F32)
-    dn = dn + mm(spread, w_back)
-    x = pair_ref[...].reshape(rows * block, channels).astype(F32)
-    centred = x - jnp.mean(x, axis=-1, keepdims=True)
-    rstd = lax.rsqrt(jnp.mean(centred * centred, axis=-1, keepdims=True) + EPSILON)
+    back = mm(spread, spread_heads(w_ref, block))
+    dn = [both_ref[d, 2 * i + 1] for d in range(group) for i in range(own)]
+    dn = jnp.concatenate(dn, axis=0).astype(F32) + back
+    for d in range(group):
+        for i in range(own):
+            update_ref[d * own + i] = both_ref[d, 2 * i]
+    centred, rstd = centre(pair_ref[...].reshape(rows * block, channels))
     unit = centred * rstd
     push = dn * gain_ref[...]
     along = jnp.mean(push * unit, axis=-1, keepdims=True)
@@ -557,14 +598,31 @@
 
 
 def final(pair, both, gain, shift_row, bias_weight):
+    n_ja, slabs, block, channels = both.shape
+    group = 2
+    steps = n_ja // group
+    rows = pair.shape[0] // steps
+    by_rows = pl.BlockSpec((rows, block, channels), lambda i: (i, 0, 0))
     return pl.pallas_call(
         final_kernel,
-        out_shape=jax.ShapeDtypeStruct(pair.shape, F32),
+        grid=(steps,),
+        in_specs=[
+            by_rows,
+            pl.BlockSpec((group, slabs, block, channels), lambda i: (i, 0, 0, 0)),
+            pl.BlockSpec((n_ja, 1, block, channels), lambda i: (0, slabs - 1, 0, 0)),
+        ]
+        + [whole(a) for a in (gain, shift_row, bias_weight)],
+        out_specs=[by_rows, by_rows],
+        out_shape=[
+            jax.ShapeDtypeStruct(pair.shape, BF16),
+            jax.ShapeDtypeStruct(pair.shape, F32),
+        ],
+        scratch_shapes=[pltpu.VMEM((steps, rows, bias_weight.shape[0] * block), F32)],
         compiler_params=PARAMS,
         cost_estimate=pl.CostEstimate(
             flops=2**27, bytes_accessed=2**21, transcendentals=2**12
         ),
-    )(pair, both, gain, shift_row, bias_weight)
+    )(pair, both, both, gain, shift_row, bias_weight)
 
 
 def shards(
@@ -589,55 +647,41 @@
     weights = (query_weight, key_weight, value_weight, gate_weight)
     tie = lax.optimization_barrier
 
-    both = lax.all_to_all(
-        prep(pair, cotangent, gain, shift_row, bias_rows, n_ja), JA, 0, 0, tiled=True
-    )
+    n_xh = lax.axis_size("xh")
+    tile = prep(pair, gain, shift_row, bias_rows, n_xh * n_ja)
+    both = pack(pair, cotangent, n_ja)
+    near = lax.all_to_all(tile, ("xh",) + JA, 0, 0, tiled=True)
+    near, both = tie((near, both))
+    near = near.reshape((n_xh, n_ja) + near.shape[1:])
+    both = lax.all_to_all(both, JA, 0, 0, tiled=True)
 
     def joined(mine, theirs):
         return (mine.astype(F32) + theirs.astype(F32)).astype(BF16)
 
-    own = both[:, 2 * own_i]
-    far = lax.ppermute(own, "xh", [(0, 1), (1, 0)])
+    slices = [shift(near, "z", 3), shift(near, "z", 2), shift(near, "z", 1)]
+    swaps = [swap(a) for a in slices]
+    near_swap = swap(near)
     projected = project(both, gain, shift_row, out_weight, weights)
-    far, projected = tie((far, projected))
+    projected, slices, swaps = tie((projected, slices, swaps))
     *projected, gate = projected
-    near = jnp.stack([own, far])
-    near_swap = swap(near)
-    prev, after = shift(near, "z", 1), shift(near, "z", 3)
-
-    groups = ((0,), (3, 1), (2,))
-    out0 = attend(heads, groups[0], projected, [([near], [near_swap])])
-    out0, prev, after = tie((out0, prev, after))
-    prev_swap, after_swap = swap(prev), swap(after)
-    opp0, opp1 = shift(prev[0], "z", 1), shift(after[1], "z", 3)
+
+    groups = ((1, 2, 3), (0,))
+    out1 = attend(heads, groups[0], projected, [([a], [b]) for a, b in zip(slices, swaps)])
+    theirs1 = swap(out1[5])
+    theirs1, near = tie((theirs1, near))
+    part = joined(out1[4], theirs1)
+    part, near = tie((part, near))
+    parts = [shift(part[e], "z", e + 1) for e in range(3)]
+    out0 = attend(heads, groups[1], projected, [([near], [near_swap])])
+    att, dq, dk, dv = zip(out1[:4], out0[:4])
+    done = finish(groups, gate, both, out_weight, weights, att, dq, dk, dv)
     theirs0 = swap(out0[5])
-    out0, prev, prev_swap, after, after_swap = tie((out0, prev, prev_swap, after, after_swap))
-    out1 = attend(
-        heads, groups[1], projected, [([prev], [prev_swap]), ([after], [after_swap])]
-    )
-    out1, opp0, opp1, theirs0 = tie((out1, opp0, opp1, theirs0))
-    opp0_swap, opp1_swap, theirs1 = swap(opp0), swap(opp1), swap(out1[5])
-    theirs1, opp0_swap, opp1_swap = tie((theirs1, opp0_swap, opp1_swap))
-    part1 = joined(out1[4], theirs1)
-    part1, opp0 = tie((part1, opp0))
-    part1, part2 = shift(part1[0], "z", 3), shift(part1[1], "z", 1)
-    out3 = attend(heads, groups[2], projected, [([opp0, opp1], [opp0_swap, opp1_swap])])
-    out3, part1, part2 = tie((out3, part1, part2))
-    theirs3 = swap(out3[5])
-    keep, send = halves(out0[4][0], theirs0[0], part1, part2)
-    theirs3, keep, send = tie((theirs3, keep, send))
-    opp_keep, opp_send = halves(out3[4][0], theirs3[0])
-    flips = [(s, s ^ 5) for s in range(8)]
-    opp_keep = shift(opp_keep, "z", 2)
-    opp_send = lax.ppermute(opp_send, ("z", "xh"), flips)
+    done, parts, theirs0 = tie((done, parts, theirs0))
+    keep, send = halves(out0[4][0], theirs0[0], *parts)
     send = lax.ppermute(send, "xh", [(0, 1), (1, 0)])
-    att, dq, dk, dv = zip(out0[:4], out1[:4], out3[:4])
-    done = finish(groups, gate, both, out_weight, weights, att, dq, dk, dv)
-    done, opp_keep, opp_send, send = tie((done, opp_keep, opp_send, send))
-    done = fill(done, keep, send, opp_keep, opp_send)
+    done = fill(done, keep, send)
     done = lax.all_to_all(done, JA, 0, 0, tiled=True)
-    update = jnp.stack([done[:, 2 * i] for i in range(own_i)], axis=1).reshape(pair.shape)
-    pair_grad = final(pair, done, gain, shift_row, bias_rows)
+    update, pair_grad = final(pair, done, gain, shift_row, bias_rows)
     return (update, pair_grad)
 
 

time: 111 us -> 109 us (0.982)
  blocking collectives: 42.1 us -> 20.7 us
  waiting for transfers between devices: 8.18 us -> 28.7 us
  Pallas kernels: 37.2 us -> 35.8 us
  starting transfers between devices: 20.7 us -> 21.9 us
    all_to_all x1 -> x0, blocking collectives: 22.9 us -> none  [shards(): lax.all_to_all(prep(pair, cotangent, gain, shift_row, bias_rows, n_ja), J...]
    ppermute x7 -> x6, waiting for transfers between devices: 3.23 us -> 15.2 us  [shift(): return lax.ppermute(a, axis, [(s, (s + by) % size) for s in range(size)])]
    all_to_all x0 -> x2, starting transfers between devices: none -> 10.7 us  [the longest x1 7.12 us: shards(): near = lax.all_to_all(tile, ('xh',) + JA, 0, 0, tiled=True)]
    ppermute x2 -> x0, starting transfers between devices: 6.89 us -> none  [the longest x1 4.08 us: shards(): opp_send = lax.ppermute(opp_send, ('z', 'xh'), flips)]
    all_to_all x0 -> x2, waiting for transfers between devices: none -> 6.59 us  [the longest x1 6.59 us: shards(): near = lax.all_to_all(tile, ('xh',) + JA, 0, 0, tiled=True)]
    ppermute x1, waiting for transfers between devices: 1.42 us -> 5.14 us  [shards(): send = lax.ppermute(send, 'xh', [(0, 1), (1, 0)])]
    pallas_call x3 -> x2, Pallas kernels: 23.8 us -> 21.3 us  [attend(): pl.pallas_call(lambda *refs: attend_kernel(heads, count, views, *refs), g...]
    ppermute x7 -> x6, starting transfers between devices: 11.1 us -> 9.02 us  [shift(): return lax.ppermute(a, axis, [(s, (s + by) % size) for s in range(size)])]
  transfers between devices with their start and end apart: 18 -> 15, of which waited for: 7 -> 8; matrix products, arithmetic and copies ran while one was open for 0% -> 0% of each run, Pallas kernels for 29% -> 14%
where the time goes in v9:
time: 109 us; the launch traced here: 108 us
  Pallas kernels  35.8 us (33%)
  waiting for transfers between devices  28.7 us (26%)
  starting transfers between devices  21.9 us (20%)
  blocking collectives  20.7 us (19%)
    pallas_call x2, Pallas kernels, attend(): pl.pallas_call(lambda *refs: attend_kernel(heads, count, views, *refs), g...  21.3 us
    all_to_all x1, blocking collectives, shards(): done = lax.all_to_all(done, JA, 0, 0, tiled=True)  20.7 us
    ppermute x6, waiting for transfers between devices, shift(): return lax.ppermute(a, axis, [(s, (s + by) % size) for s in range(size)])  15.2 us
    ppermute x6, starting transfers between devices, shift(): return lax.ppermute(a, axis, [(s, (s + by) % size) for s in range(size)])  9.02 us
    all_to_all x1, starting transfers between devices, shards(): near = lax.all_to_all(tile, ('xh',) + JA, 0, 0, tiled=True)  7.12 us
    all_to_all x1, waiting for transfers between devices, shards(): near = lax.all_to_all(tile, ('xh',) + JA, 0, 0, tiled=True)  6.59 us
    ppermute x1, waiting for transfers between devices, shards(): send = lax.ppermute(send, 'xh', [(0, 1), (1, 0)])  5.14 us
    pallas_call x1, Pallas kernels, project(): pl.pallas_call(project_kernel, grid=(rows // group,), in_specs=[pl.BlockS...  3.81 us
  transfers between devices with their start and end apart: 15, of which 8 were waited for; matrix products, arithmetic and copies ran while one was open for 0% of the time, Pallas kernels for 14%

profile of v9, /device:TPU:0, one launch (start us, length us, event | category | flops | bytes accessed | tf_op | source)
XLA Modules:
  0.0 108.3 jit_solution(7232471591144065791)
XLA Ops:
  0.6 2.6 %shard_map.113 = bf16[16,64,128]{2,1,0:T(8,128)(2,1)} custom-call(bf16[32,64,128]{2,1,0:T(8,128)(2,1)} %pair_ref.5, f32[1,128]{1,0:T(1,128)} %bitcast.21, f32[1,128]{1,0:T(1,128)} %bitcast.24, bf16[4,128]{1,0:T(4,128)(2,1)} %bitcast.19), custom_call_target="tpu_custom_call" | custom-call | flops 134217728 | bytes 1048576 | tf_op jit(solution)/shard_map/pallas_call | solution.py:95
  3.3 7.1 %all-to-all-start = ((bf16[16,64,128]{2,1,0:T(8,128)(2,1)}), bf16[16,64,128]{2,1,0:T(8,128)(2,1)S(1)}, u32[]{:S(2)}, u32[]{:S(2)}) async-start(bf16[16,64,128]{2,1,0:T(8,128)(2,1)} %shard_map.113), calls=%async_computation | async-start | bytes 524288 | tf_op jit(solution)/shard_map/all_to_all | solution.py:653
  10.4 2.0 %shard_map.114 = bf16[8,8,64,128]{3,2,1,0:T(8,128)(2,1)} custom-call(bf16[32,64,128]{2,1,0:T(8,128)(2,1)} %pair_ref.5, bf16[32,64,128]{2,1,0:T(8,128)(2,1)} %cot_ref.1), custom_call_target="tpu_custom_call" | custom-call | flops 1024 | bytes 2097152 | tf_op jit(solution)/shard_map/pallas_call | solution.py:117
  12.4 0.0 copy-start.2
  12.4 0.0 copy-start.3
  12.4 0.0 copy-start.4
  12.4 0.0 copy-start.5
  12.4 0.0 copy-start.6
  12.5 0.0 copy-start.7
  12.5 0.0 copy-start.8
  12.5 6.6 %all-to-all-done = bf16[16,64,128]{2,1,0:T(8,128)(2,1)S(1)} async-done(((bf16[16,64,128]{2,1,0:T(8,128)(2,1)}), bf16[16,64,128]{2,1,0:T(8,128)(2,1)S(1)}, u32[]{:S(2)}, u32[]{:S(2)}) %all-to-all-start) | async-done | bytes 262176 | tf_op jit(solution)/shard_map/all_to_all | solution.py:653
  19.1 3.6 %all-to-all-start.1 = ((bf16[8,8,64,128]{3,2,1,0:T(8,128)(2,1)}), bf16[8,8,64,128]{3,2,1,0:T(8,128)(2,1)S(1)}, u32[]{:S(2)}, u32[]{:S(2)}) async-start(bf16[8,8,64,128]{3,2,1,0:T(8,128)(2,1)} %shard_map.114), calls=%async_computation.1 | async-start | bytes 2097152 | tf_op jit(solution)/shard_map/all_to_all | solution.py:656
  22.6 4.1 %collective-permute-start = (bf16[2,8,64,128]{3,2,1,0:T(8,128)(2,1)S(1)}, bf16[2,8,64,128]{3,2,1,0:T(8,128)(2,1)S(1)}, u32[]{:S(2)}, u32[]{:S(2)}) collective-permute-start(bf16[2,8,64,128]{3,2,1,0:T(8,128)(2,1)S(1)} %bitcast.14), channel_id=1, source_target_pairs={{0,96},{32,0},{64,32},{96,64},{1,97},{33,1},{65,33},{97,65},{2,98}... | collective-permute-start | bytes 786440 | tf_op jit(solution)/shard_map/ppermute | solution.py:53
  26.7 0.0 collective-permute-start.1
  26.7 1.3 %collective-permute-start.2 = (bf16[2,8,64,128]{3,2,1,0:T(8,128)(2,1)S(1)}, bf16[2,8,64,128]{3,2,1,0:T(8,128)(2,1)S(1)}, u32[]{:S(2)}, u32[]{:S(2)}) collective-permute-start(bf16[2,8,64,128]{3,2,1,0:T(8,128)(2,1)S(1)} %bitcast.16), channel_id=1, source_target_pairs={{0,32},{32,64},{64,96},{96,0},{1,33},{33,65},{65,97},{97,1},{2,34}... | collective-permute-start | bytes 786440 | tf_op jit(solution)/shard_map/ppermute | solution.py:53
  28.0 8.7 %collective-permute-done.refs_5_ = bf16[2,8,64,128]{3,2,1,0:T(8,128)(2,1)S(1)} collective-permute-done((bf16[2,8,64,128]{3,2,1,0:T(8,128)(2,1)S(1)}, bf16[2,8,64,128]{3,2,1,0:T(8,128)(2,1)S(1)}, u32[]{:S(2)}, u32[]{:S(2)}) %collective-permute-start) | collective-permute-done | bytes 262176 | tf_op jit(solution)/shard_map/ppermute | solution.py:53
  36.7 0.0 collective-permute-start.3
  36.7 0.8 collective-permute-done.1.refs_7_
  37.5 0.0 collective-permute-start.4
  37.5 2.6 %collective-permute-done.2.refs_9_ = bf16[2,8,64,128]{3,2,1,0:T(8,128)(2,1)S(1)} collective-permute-done((bf16[2,8,64,128]{3,2,1,0:T(8,128)(2,1)S(1)}, bf16[2,8,64,128]{3,2,1,0:T(8,128)(2,1)S(1)}, u32[]{:S(2)}, u32[]{:S(2)}) %collective-permute-start.2) | collective-permute-done | bytes 262176 | tf_op jit(solution)/shard_map/ppermute | solution.py:53
  40.1 0.0 collective-permute-start.5
  40.1 0.0 all-to-all-done.1.pair_ref.cot_ref.refs_1_
  40.1 0.0 copy-done.2
  40.1 0.0 copy-done.3
  40.1 0.0 copy-done.4
  40.1 0.0 copy-done.5
  40.1 0.0 copy-done.6
  40.1 0.0 copy-done.7
  40.2 0.0 copy-done.8
  40.2 3.8 %shard_map.115 = (bf16[4,512,256]{2,1,0:T(8,128)(2,1)}, bf16[4,256,512]{2,1,0:T(8,128)(2,1)}, bf16[4,4,128,128]{3,2,1,0:T(8,128)(2,1)}, bf16[4,4,128,128]{3,2,1,...) custom-call(bf16[8,8,64,128]{3,2,1,0:T(8,128)(2,1)S(1)} %all-to-all-done.1.pair_ref.cot_ref.refs_1_, ...), custom_call_target="tpu_custom_call" | custom-call | flops 2147483648 | bytes 8388608 | tf_op jit(solution)/shard_map/pallas_call | solution.py:189
  44.0 0.0 collective-permute-done.3.refs_6_
  44.0 0.0 collective-permute-done.4.refs_8_
  44.0 0.0 collective-permute-done.5.refs_10_
  44.0 14.9 %shard_map.116 = (f32[3,4,128,128]{3,2,1,0:T(8,128)S(1)}, bf16[3,4,128,128]{3,2,1,0:T(8,128)(2,1)S(1)}, bf16[4,512,128]{2,1,0:T(8,128)(2,1)S(1)}, bf16[4,512,128...) custom-call(bf16[4,512,256]{2,1,0:T(8,128)(2,1)} %get-tuple-element.54.refs_0_, ...), custom_call_target="tpu_custom_call" | custom-call | flops 12884901888 | bytes 8388608 | tf_op jit(solution)/shard_map/pallas_call | solution.py:428
  58.9 0.6 collective-permute-start.6
  59.6 0.1 collective-permute-start.7
  59.7 1.8 %collective-permute-done.6 = bf16[3,2,8,64,128]{4,3,2,1,0:T(8,128)(2,1)S(1)} collective-permute-done((bf16[3,2,8,64,128]{4,3,2,1,0:T(8,128)(2,1)S(1)}, bf16[3,2,8,64,128]{4,3,2,1,0:T(8,128)(2,1)S(1)}, u32[]{:S(2)}, u32[]{:S(2)}) %collective-permute-start.6) | collective-permute-done | bytes 786464 | tf_op jit(solution)/shard_map/ppermute | solution.py:48
  61.5 0.3 add_convert_fusion
  61.8 0.1 slice_bitcast_fusion
  61.8 0.1 collective-permute-start.8
  61.9 2.6 %collective-permute-start.9 = (bf16[2,8,64,128]{3,2,1,0:T(8,128)(2,1)S(1)}, bf16[2,8,64,128]{3,2,1,0:T(8,128)(2,1)S(1)}, u32[]{:S(2)}, u32[]{:S(2)}) collective-permute-start(bf16[2,8,64,128]{3,2,1,0:T(8,128)(2,1)S(1)} %get-tuple-element.89), channel_id=1, source_target_pairs={{0,64},{32,96},{64,0},{96,32},{1,65},{33,97},{65,1},{97,33},{2,66}... | collective-permute-start | bytes 786440 | tf_op jit(solution)/shard_map/ppermute | solution.py:53
  64.5 1.0 collective-permute-start.10
  65.5 0.0 collective-permute-done.7.refs_6_
  65.5 6.3 %shard_map.117 = (f32[1,4,128,128]{3,2,1,0:T(8,128)S(1)}, bf16[1,4,128,128]{3,2,1,0:T(8,128)(2,1)S(1)}, bf16[4,512,128]{2,1,0:T(8,128)(2,1)S(1)}, bf16[4,512,128...) custom-call(bf16[4,512,256]{2,1,0:T(8,128)(2,1)} %get-tuple-element.54.refs_0_, ...), custom_call_target="tpu_custom_call" | custom-call | flops 4294967296 | bytes 8388608 | tf_op jit(solution)/shard_map/pallas_call | solution.py:428
  71.8 0.1 collective-permute-start.11
  71.9 2.9 %shard_map.118.done_ref = bf16[8,9,64,128]{3,2,1,0:T(8,128)(2,1)S(1)} custom-call(f32[4,128,512]{2,1,0:T(8,128)} %get-tuple-element.53.refs_0_, bf16[8,8,64,128]{3,2,1,0:T(8,128)(2,1)S(1)} %all-to-all-done.1.pair_ref.cot_ref.refs_1_, bf16[128,128]{1,0:T(8,128)(2,1)S(1)} %copy-done.4, bf16[128,128]{1,0:T(8,128)(2,1)S(1)} %copy-done.5, ...), custom_call_target="tpu_custom_call" | custom-call | flops 2147483648 | bytes 8388608 | tf_op jit(solution)/shard_map/pallas_call | solution.py:500
  74.8 2.5 %collective-permute-done.8.refs_2_ = bf16[2,8,64,128]{3,2,1,0:T(8,128)(2,1)S(1)} collective-permute-done((bf16[2,8,64,128]{3,2,1,0:T(8,128)(2,1)S(1)}, bf16[2,8,64,128]{3,2,1,0:T(8,128)(2,1)S(1)}, u32[]{:S(2)}, u32[]{:S(2)}) %collective-permute-start.8) | collective-permute-done | bytes 262176 | tf_op jit(solution)/shard_map/ppermute | solution.py:53
  77.3 0.0 collective-permute-done.9.refs_3_
  77.3 0.6 collective-permute-done.10.refs_4_
  77.9 0.0 collective-permute-done.11
  77.9 0.2 shard_map.119
  78.1 1.4 %collective-permute-start.12 = (bf16[8,64,128]{2,1,0:T(8,128)(2,1)S(1)}, bf16[8,64,128]{2,1,0:T(8,128)(2,1)S(1)}, u32[]{:S(2)}, u32[]{:S(2)}) collective-permute-start(bf16[8,64,128]{2,1,0:T(8,128)(2,1)S(1)} %get-tuple-element.87), channel_id=1, source_target_pairs={{0,16},{16,0},{1,17},{17,1},{2,18},{18,2},{3,19},{19,3},{4,20},{20... | collective-permute-start | bytes 393224 | tf_op jit(solution)/shard_map/ppermute | solution.py:681
  79.5 5.1 %collective-permute-done.12.b_ref = bf16[8,64,128]{2,1,0:T(8,128)(2,1)S(1)} collective-permute-done((bf16[8,64,128]{2,1,0:T(8,128)(2,1)S(1)}, bf16[8,64,128]{2,1,0:T(8,128)(2,1)S(1)}, u32[]{:S(2)}, u32[]{:S(2)}) %collective-permute-start.12) | collective-permute-done | bytes 131104 | tf_op jit(solution)/shard_map/ppermute | solution.py:681
  84.7 0.1 shard_map.120
  84.7 0.0 copy-start
  84.7 0.0 copy-start.1
  84.7 20.7 %all_to_all.15.both_ref.gb_ref = bf16[8,9,64,128]{3,2,1,0:T(8,128)(2,1)S(1)} all-to-all(bf16[8,9,64,128]{3,2,1,0:T(8,128)(2,1)S(1)} %shard_map.120), channel_id=1, replica_groups=mesh['z'=4,'xh'=2,'core'=2,'y'=4,'xl'=2] {'y','xl'}, dimensions={0} | all-to-all | bytes 2359296 | tf_op jit(solution)/shard_map/all_to_all | solution.py:683
  105.4 0.0 copy-done
  105.4 0.0 copy-done.1
  105.4 2.9 %shard_map.121 = (bf16[32,64,128]{2,1,0:T(8,128)(2,1)}, f32[32,64,128]{2,1,0:T(8,128)}) custom-call(bf16[32,64,128]{2,1,0:T(8,128)(2,1)S(1)} %copy-done, bf16[8,9,64,128]{3,2,1,0:T(8,128)(2,1)S(1)} %all_to_all.15.both_ref.gb_ref, bf16[8,9,64,128]{3,2,1,0:T(8,128)(2,1)S(1)} %all_to_all.15.both_ref.gb_ref, f32[1,128]{1,0:T(1,128)S(1)} %bitcast.23, ...), custom_call_target="tpu_custom_call" | custom-call | flops 134217728 | bytes 2097152 | tf_op jit(solution)/shard_map/pallas_call | solution.py:606
Async XLA Ops:
  3.3 15.8 %all-to-all-start = ((bf16[16,64,128]{2,1,0:T(8,128)(2,1)}), bf16[16,64,128]{2,1,0:T(8,128)(2,1)S(1)}, u32[]{:S(2)}, u32[]{:S(2)}) async-start(bf16[16,64,128]{2,1,0:T(8,128)(2,1)} %shard_map.113), calls=%async_computation | async-start | bytes 524288 | tf_op jit(solution)/shard_map/all_to_all | solution.py:653
  12.4 27.7 %copy-start.2 = (f32[128]{0:T(128)S(1)}, f32[128]{0:T(128)}, u32[]{:S(2)}) copy-start(f32[128]{0:T(128)} %param.12) | copy-start | bytes 1540
  12.4 27.7 %copy-start.3 = (f32[128]{0:T(128)S(1)}, f32[128]{0:T(128)}, u32[]{:S(2)}) copy-start(f32[128]{0:T(128)} %param.13) | copy-start | bytes 1540
  12.4 27.7 %copy-start.4 = (bf16[128,128]{1,0:T(8,128)(2,1)S(1)}, bf16[128,128]{1,0:T(8,128)(2,1)}, u32[]{:S(2)}) copy-start(bf16[128,128]{1,0:T(8,128)(2,1)} %refs_2_.1) | copy-start | bytes 98308
  12.4 27.7 %copy-start.5 = (bf16[128,128]{1,0:T(8,128)(2,1)S(1)}, bf16[128,128]{1,0:T(8,128)(2,1)}, u32[]{:S(2)}) copy-start(bf16[128,128]{1,0:T(8,128)(2,1)} %refs_3_.1) | copy-start | bytes 98308
  12.4 27.7 %copy-start.6 = (bf16[128,128]{1,0:T(8,128)(2,1)S(1)}, bf16[128,128]{1,0:T(8,128)(2,1)}, u32[]{:S(2)}) copy-start(bf16[128,128]{1,0:T(8,128)(2,1)} %refs_4_.1) | copy-start | bytes 98308
  12.5 27.7 %copy-start.7 = (bf16[128,128]{1,0:T(8,128)(2,1)S(1)}, bf16[128,128]{1,0:T(8,128)(2,1)}, u32[]{:S(2)}) copy-start(bf16[128,128]{1,0:T(8,128)(2,1)} %refs_5_.1) | copy-start | bytes 98308
  12.5 27.7 %copy-start.8 = (bf16[128,128]{1,0:T(8,128)(2,1)S(1)}, bf16[128,128]{1,0:T(8,128)(2,1)}, u32[]{:S(2)}) copy-start(bf16[128,128]{1,0:T(8,128)(2,1)} %refs_6_.1) | copy-start | bytes 98308
  19.1 21.0 %all-to-all-start.1 = ((bf16[8,8,64,128]{3,2,1,0:T(8,128)(2,1)}), bf16[8,8,64,128]{3,2,1,0:T(8,128)(2,1)S(1)}, u32[]{:S(2)}, u32[]{:S(2)}) async-start(bf16[8,8,64,128]{3,2,1,0:T(8,128)(2,1)} %shard_map.114), calls=%async_computation.1 | async-start | bytes 2097152 | tf_op jit(solution)/shard_map/all_to_all | solution.py:656
  22.6 14.0 %collective-permute-start = (bf16[2,8,64,128]{3,2,1,0:T(8,128)(2,1)S(1)}, bf16[2,8,64,128]{3,2,1,0:T(8,128)(2,1)S(1)}, u32[]{:S(2)}, u32[]{:S(2)}) collective-permute-start(bf16[2,8,64,128]{3,2,1,0:T(8,128)(2,1)S(1)} %bitcast.14), channel_id=1, source_target_pairs={{0,96},{32,0},{64,32},{96,64},{1,97},{33,1},{65,33},{97,65},{2,98}... | collective-permute-start | bytes 786440 | tf_op jit(solution)/shard_map/ppermute | solution.py:53
  26.7 10.7 %collective-permute-start.1 = (bf16[2,8,64,128]{3,2,1,0:T(8,128)(2,1)S(1)}, bf16[2,8,64,128]{3,2,1,0:T(8,128)(2,1)S(1)}, u32[]{:S(2)}, u32[]{:S(2)}) collective-permute-start(bf16[2,8,64,128]{3,2,1,0:T(8,128)(2,1)S(1)} %bitcast.15), channel_id=1, source_target_pairs={{0,64},{32,96},{64,0},{96,32},{1,65},{33,97},{65,1},{97,33},{2,66}... | collective-permute-start | bytes 786440 | tf_op jit(solution)/shard_map/ppermute | solution.py:53
  26.7 13.3 %collective-permute-start.2 = (bf16[2,8,64,128]{3,2,1,0:T(8,128)(2,1)S(1)}, bf16[2,8,64,128]{3,2,1,0:T(8,128)(2,1)S(1)}, u32[]{:S(2)}, u32[]{:S(2)}) collective-permute-start(bf16[2,8,64,128]{3,2,1,0:T(8,128)(2,1)S(1)} %bitcast.16), channel_id=1, source_target_pairs={{0,32},{32,64},{64,96},{96,0},{1,33},{33,65},{65,97},{97,1},{2,34}... | collective-permute-start | bytes 786440 | tf_op jit(solution)/shard_map/ppermute | solution.py:53
  36.7 7.3 %collective-permute-start.3 = (bf16[2,8,64,128]{3,2,1,0:T(8,128)(2,1)S(1)}, bf16[2,8,64,128]{3,2,1,0:T(8,128)(2,1)S(1)}, u32[]{:S(2)}, u32[]{:S(2)}) collective-permute-start(bf16[2,8,64,128]{3,2,1,0:T(8,128)(2,1)S(1)} %collective-permute-done.refs_5_), channel_id=1, source_target_pairs={{0,8},{8,0},{1,9},{9,1},{2,10},{10,2},{3,11},{11,3},{4,12},{12,4},... | collective-permute-start | bytes 786440 | tf_op jit(solution)/shard_map/ppermute | solution.py:48
  37.5 6.5 %collective-permute-start.4 = (bf16[2,8,64,128]{3,2,1,0:T(8,128)(2,1)S(1)}, bf16[2,8,64,128]{3,2,1,0:T(8,128)(2,1)S(1)}, u32[]{:S(2)}, u32[]{:S(2)}) collective-permute-start(bf16[2,8,64,128]{3,2,1,0:T(8,128)(2,1)S(1)} %collective-permute-done.1.refs_7_), channel_id=1, source_target_pairs={{0,8},{8,0},{1,9},{9,1},{2,10},{10,2},{3,11},{11,3},{4,12},{12,4},... | collective-permute-start | bytes 786440 | tf_op jit(solution)/shard_map/ppermute | solution.py:48
  40.1 3.9 %collective-permute-start.5 = (bf16[2,8,64,128]{3,2,1,0:T(8,128)(2,1)S(1)}, bf16[2,8,64,128]{3,2,1,0:T(8,128)(2,1)S(1)}, u32[]{:S(2)}, u32[]{:S(2)}) collective-permute-start(bf16[2,8,64,128]{3,2,1,0:T(8,128)(2,1)S(1)} %collective-permute-done.2.refs_9_), channel_id=1, source_target_pairs={{0,8},{8,0},{1,9},{9,1},{2,10},{10,2},{3,11},{11,3},{4,12},{12,4},... | collective-permute-start | bytes 786440 | tf_op jit(solution)/shard_map/ppermute | solution.py:48
  58.9 2.5 %collective-permute-start.6 = (bf16[3,2,8,64,128]{4,3,2,1,0:T(8,128)(2,1)S(1)}, bf16[3,2,8,64,128]{4,3,2,1,0:T(8,128)(2,1)S(1)}, u32[]{:S(2)}, u32[]{:S(2)}) collective-permute-start(bf16[3,2,8,64,128]{4,3,2,1,0:T(8,128)(2,1)S(1)} %get-tuple-element.67), channel_id=1, source_target_pairs={{0,8},{8,0},{1,9},{9,1},{2,10},{10,2},{3,11},{11,3},{4,12},{12,4},... | collective-permute-start | bytes 2359304 | tf_op jit(solution)/shard_map/ppermute | solution.py:48
  59.6 5.9 %collective-permute-start.7 = (bf16[2,8,64,128]{3,2,1,0:T(8,128)(2,1)S(1)}, bf16[2,8,64,128]{3,2,1,0:T(8,128)(2,1)S(1)}, u32[]{:S(2)}, u32[]{:S(2)}) collective-permute-start(bf16[2,8,64,128]{3,2,1,0:T(8,128)(2,1)S(1)} %bitcast.17), channel_id=1, source_target_pairs={{0,8},{8,0},{1,9},{9,1},{2,10},{10,2},{3,11},{11,3},{4,12},{12,4},... | collective-permute-start | bytes 786440 | tf_op jit(solution)/shard_map/ppermute | solution.py:48
  61.8 15.5 %collective-permute-start.8 = (bf16[2,8,64,128]{3,2,1,0:T(8,128)(2,1)S(1)}, bf16[2,8,64,128]{3,2,1,0:T(8,128)(2,1)S(1)}, u32[]{:S(2)}, u32[]{:S(2)}) collective-permute-start(bf16[2,8,64,128]{3,2,1,0:T(8,128)(2,1)S(1)} %get-tuple-element.90), channel_id=1, source_target_pairs={{0,32},{32,64},{64,96},{96,0},{1,33},{33,65},{65,97},{97,1},{2,34}... | collective-permute-start | bytes 786440 | tf_op jit(solution)/shard_map/ppermute | solution.py:53
  61.9 15.4 %collective-permute-start.9 = (bf16[2,8,64,128]{3,2,1,0:T(8,128)(2,1)S(1)}, bf16[2,8,64,128]{3,2,1,0:T(8,128)(2,1)S(1)}, u32[]{:S(2)}, u32[]{:S(2)}) collective-permute-start(bf16[2,8,64,128]{3,2,1,0:T(8,128)(2,1)S(1)} %get-tuple-element.89), channel_id=1, source_target_pairs={{0,64},{32,96},{64,0},{96,32},{1,65},{33,97},{65,1},{97,33},{2,66}... | collective-permute-start | bytes 786440 | tf_op jit(solution)/shard_map/ppermute | solution.py:53
  64.5 13.5 %collective-permute-start.10 = (bf16[2,8,64,128]{3,2,1,0:T(8,128)(2,1)S(1)}, bf16[2,8,64,128]{3,2,1,0:T(8,128)(2,1)S(1)}, u32[]{:S(2)}, u32[]{:S(2)}) collective-permute-start(bf16[2,8,64,128]{3,2,1,0:T(8,128)(2,1)S(1)} %get-tuple-element.88), channel_id=1, source_target_pairs={{0,96},{32,0},{64,32},{96,64},{1,97},{33,1},{65,33},{97,65},{2,98}... | collective-permute-start | bytes 786440 | tf_op jit(solution)/shard_map/ppermute | solution.py:53
  71.8 6.1 %collective-permute-start.11 = (bf16[1,2,8,64,128]{4,3,2,1,0:T(8,128)(2,1)S(1)}, bf16[1,2,8,64,128]{4,3,2,1,0:T(8,128)(2,1)S(1)}, u32[]{:S(2)}, u32[]{:S(2)}) collective-permute-start(bf16[1,2,8,64,128]{4,3,2,1,0:T(8,128)(2,1)S(1)} %get-tuple-element.79), channel_id=1, source_target_pairs={{0,8},{8,0},{1,9},{9,1},{2,10},{10,2},{3,11},{11,3},{4,12},{12,4},... | collective-permute-start | bytes 786440 | tf_op jit(solution)/shard_map/ppermute | solution.py:48
  78.1 6.6 %collective-permute-start.12 = (bf16[8,64,128]{2,1,0:T(8,128)(2,1)S(1)}, bf16[8,64,128]{2,1,0:T(8,128)(2,1)S(1)}, u32[]{:S(2)}, u32[]{:S(2)}) collective-permute-start(bf16[8,64,128]{2,1,0:T(8,128)(2,1)S(1)} %get-tuple-element.87), channel_id=1, source_target_pairs={{0,16},{16,0},{1,17},{17,1},{2,18},{18,2},{3,19},{19,3},{4,20},{20... | collective-permute-start | bytes 393224 | tf_op jit(solution)/shard_map/ppermute | solution.py:681
  84.7 20.7 %copy-start = (bf16[32,64,128]{2,1,0:T(8,128)(2,1)S(1)}, bf16[32,64,128]{2,1,0:T(8,128)(2,1)}, u32[]{:S(2)}) copy-start(bf16[32,64,128]{2,1,0:T(8,128)(2,1)} %pair_ref.5) | copy-start | bytes 1572868
  84.7 20.7 %copy-start.1 = (bf16[128,4]{0,1:T(4,128)(2,1)S(1)}, bf16[128,4]{0,1:T(4,128)(2,1)}, u32[]{:S(2)}) copy-start(bf16[128,4]{0,1:T(4,128)(2,1)} %param.18) | copy-start | bytes 3076

commit v10 on v9

--- a/solution.py
+++ b/solution.py
@@ -164,7 +164,7 @@
             ahead = lax.rem(owner + size - z, size)
             q_n_ref[ahead, r] = proj[at, :inner]
             q_t_ref[ahead, r] = proj_t[:inner, at].astype(BF16)
-            d_att_ref[ahead, r] = d_att[:, at]
+            d_att_ref[ahead, r] = d_att[:, at].astype(BF16)
 
 
 def project(both, gain, shift_row, w_o, weights):
@@ -178,7 +178,7 @@
     gate = pltpu.HBM((rows, inner, n), F32)
     q_n = pltpu.HBM((n // LANES, rows, LANES, inner), BF16)
     q_t = pltpu.HBM((n // LANES, rows, inner, LANES), BF16)
-    d_att = pltpu.HBM((n // LANES, rows, inner, LANES), F32)
+    d_att = pltpu.HBM((n // LANES, rows, inner, LANES), BF16)
 
     def by_row(a):
         return pl.BlockSpec((group,) + a.shape[1:], lambda i: (i, 0, 0))
@@ -307,7 +307,7 @@
         inv = held["inv", r, p]
         att = mm(t_ref[r, inner + first : inner + first + 2 * head_dim, :], p_s[r, :, cols_of(p)])
         att = att * inv
-        d_att = d_att_ref[0, r, rows, :]
+        d_att = d_att_ref[0, r, rows, :].astype(F32)
         a_two = jnp.concatenate([d_att, d_att], axis=1) * inv
         lane = lax.broadcasted_iota(jnp.int32, a_two.shape, 1) // LANES
         sub = lax.broadcasted_iota(jnp.int32, a_two.shape, 0) // head_dim

time: 109 us -> 109 us (level)
  no operation moved by 1% of the time
where the time goes in v10:
time: 109 us; the launch traced here: 108 us
  Pallas kernels  35.5 us (33%)
  waiting for transfers between devices  28.8 us (26%)
  starting transfers between devices  21.9 us (20%)
  blocking collectives  20.7 us (19%)
    pallas_call x2, Pallas kernels, attend(): pl.pallas_call(lambda *refs: attend_kernel(heads, count, views, *refs), g...  21.1 us
    all_to_all x1, blocking collectives, shards(): done = lax.all_to_all(done, JA, 0, 0, tiled=True)  20.7 us
    ppermute x6, waiting for transfers between devices, shift(): return lax.ppermute(a, axis, [(s, (s + by) % size) for s in range(size)])  15.2 us
    ppermute x6, starting transfers between devices, shift(): return lax.ppermute(a, axis, [(s, (s + by) % size) for s in range(size)])  9.02 us
    all_to_all x1, starting transfers between devices, shards(): near = lax.all_to_all(tile, ('xh',) + JA, 0, 0, tiled=True)  7.12 us
    all_to_all x1, waiting for transfers between devices, shards(): near = lax.all_to_all(tile, ('xh',) + JA, 0, 0, tiled=True)  6.59 us
    ppermute x1, waiting for transfers between devices, shards(): send = lax.ppermute(send, 'xh', [(0, 1), (1, 0)])  5.14 us
    pallas_call x1, Pallas kernels, project(): pl.pallas_call(project_kernel, grid=(rows // group,), in_specs=[pl.BlockS...  3.73 us
  transfers between devices with their start and end apart: 15, of which 8 were waited for; matrix products, arithmetic and copies ran while one was open for 0% of the time, Pallas kernels for 14%

profile of v10, /device:TPU:0, one launch (start us, length us, event | category | flops | bytes accessed | tf_op | source)
XLA Modules:
  0.0 108.1 jit_solution(17438810362985969178)
XLA Ops:
  0.6 2.6 %shard_map.113 = bf16[16,64,128]{2,1,0:T(8,128)(2,1)} custom-call(bf16[32,64,128]{2,1,0:T(8,128)(2,1)} %pair_ref.5, f32[1,128]{1,0:T(1,128)} %bitcast.21, f32[1,128]{1,0:T(1,128)} %bitcast.24, bf16[4,128]{1,0:T(4,128)(2,1)} %bitcast.19), custom_call_target="tpu_custom_call" | custom-call | flops 134217728 | bytes 1048576 | tf_op jit(solution)/shard_map/pallas_call | solution.py:95
  3.3 7.1 %all-to-all-start = ((bf16[16,64,128]{2,1,0:T(8,128)(2,1)}), bf16[16,64,128]{2,1,0:T(8,128)(2,1)S(1)}, u32[]{:S(2)}, u32[]{:S(2)}) async-start(bf16[16,64,128]{2,1,0:T(8,128)(2,1)} %shard_map.113), calls=%async_computation | async-start | bytes 524288 | tf_op jit(solution)/shard_map/all_to_all | solution.py:653
  10.4 2.0 %shard_map.114 = bf16[8,8,64,128]{3,2,1,0:T(8,128)(2,1)} custom-call(bf16[32,64,128]{2,1,0:T(8,128)(2,1)} %pair_ref.5, bf16[32,64,128]{2,1,0:T(8,128)(2,1)} %cot_ref.1), custom_call_target="tpu_custom_call" | custom-call | flops 1024 | bytes 2097152 | tf_op jit(solution)/shard_map/pallas_call | solution.py:117
  12.4 0.0 copy-start.2
  12.4 0.0 copy-start.3
  12.4 0.0 copy-start.4
  12.4 0.0 copy-start.5
  12.4 0.0 copy-start.6
  12.5 0.0 copy-start.7
  12.5 0.0 copy-start.8
  12.5 6.6 %all-to-all-done = bf16[16,64,128]{2,1,0:T(8,128)(2,1)S(1)} async-done(((bf16[16,64,128]{2,1,0:T(8,128)(2,1)}), bf16[16,64,128]{2,1,0:T(8,128)(2,1)S(1)}, u32[]{:S(2)}, u32[]{:S(2)}) %all-to-all-start) | async-done | bytes 262176 | tf_op jit(solution)/shard_map/all_to_all | solution.py:653
  19.1 3.6 %all-to-all-start.1 = ((bf16[8,8,64,128]{3,2,1,0:T(8,128)(2,1)}), bf16[8,8,64,128]{3,2,1,0:T(8,128)(2,1)S(1)}, u32[]{:S(2)}, u32[]{:S(2)}) async-start(bf16[8,8,64,128]{3,2,1,0:T(8,128)(2,1)} %shard_map.114), calls=%async_computation.1 | async-start | bytes 2097152 | tf_op jit(solution)/shard_map/all_to_all | solution.py:656
  22.6 4.1 %collective-permute-start = (bf16[2,8,64,128]{3,2,1,0:T(8,128)(2,1)S(1)}, bf16[2,8,64,128]{3,2,1,0:T(8,128)(2,1)S(1)}, u32[]{:S(2)}, u32[]{:S(2)}) collective-permute-start(bf16[2,8,64,128]{3,2,1,0:T(8,128)(2,1)S(1)} %bitcast.14), channel_id=1, source_target_pairs={{0,96},{32,0},{64,32},{96,64},{1,97},{33,1},{65,33},{97,65},{2,98}... | collective-permute-start | bytes 786440 | tf_op jit(solution)/shard_map/ppermute | solution.py:53
  26.7 0.0 collective-permute-start.1
  26.7 1.3 %collective-permute-start.2 = (bf16[2,8,64,128]{3,2,1,0:T(8,128)(2,1)S(1)}, bf16[2,8,64,128]{3,2,1,0:T(8,128)(2,1)S(1)}, u32[]{:S(2)}, u32[]{:S(2)}) collective-permute-start(bf16[2,8,64,128]{3,2,1,0:T(8,128)(2,1)S(1)} %bitcast.16), channel_id=1, source_target_pairs={{0,32},{32,64},{64,96},{96,0},{1,33},{33,65},{65,97},{97,1},{2,34}... | collective-permute-start | bytes 786440 | tf_op jit(solution)/shard_map/ppermute | solution.py:53
  28.0 8.7 %collective-permute-done.refs_5_ = bf16[2,8,64,128]{3,2,1,0:T(8,128)(2,1)S(1)} collective-permute-done((bf16[2,8,64,128]{3,2,1,0:T(8,128)(2,1)S(1)}, bf16[2,8,64,128]{3,2,1,0:T(8,128)(2,1)S(1)}, u32[]{:S(2)}, u32[]{:S(2)}) %collective-permute-start) | collective-permute-done | bytes 262176 | tf_op jit(solution)/shard_map/ppermute | solution.py:53
  36.7 0.0 collective-permute-start.3
  36.7 0.8 collective-permute-done.1.refs_7_
  37.5 0.0 collective-permute-start.4
  37.5 2.6 %collective-permute-done.2.refs_9_ = bf16[2,8,64,128]{3,2,1,0:T(8,128)(2,1)S(1)} collective-permute-done((bf16[2,8,64,128]{3,2,1,0:T(8,128)(2,1)S(1)}, bf16[2,8,64,128]{3,2,1,0:T(8,128)(2,1)S(1)}, u32[]{:S(2)}, u32[]{:S(2)}) %collective-permute-start.2) | collective-permute-done | bytes 262176 | tf_op jit(solution)/shard_map/ppermute | solution.py:53
  40.1 0.0 collective-permute-start.5
  40.1 0.0 all-to-all-done.1.pair_ref.cot_ref.refs_1_
  40.1 0.0 copy-done.2
  40.1 0.0 copy-done.3
  40.1 0.0 copy-done.4
  40.1 0.0 copy-done.5
  40.1 0.0 copy-done.6
  40.1 0.0 copy-done.7
  40.2 0.0 copy-done.8
  40.2 3.7 %shard_map.115 = (bf16[4,512,256]{2,1,0:T(8,128)(2,1)}, bf16[4,256,512]{2,1,0:T(8,128)(2,1)}, bf16[4,4,128,128]{3,2,1,0:T(8,128)(2,1)}, bf16[4,4,128,128]{3,2,1,...) custom-call(bf16[8,8,64,128]{3,2,1,0:T(8,128)(2,1)S(1)} %all-to-all-done.1.pair_ref.cot_ref.refs_1_, ...), custom_call_target="tpu_custom_call" | custom-call | flops 2147483648 | bytes 8388608 | tf_op jit(solution)/shard_map/pallas_call | solution.py:189
  43.9 0.0 collective-permute-done.3.refs_6_
  43.9 0.0 collective-permute-done.4.refs_8_
  43.9 0.0 collective-permute-done.5.refs_10_
  43.9 14.8 %shard_map.116 = (f32[3,4,128,128]{3,2,1,0:T(8,128)S(1)}, bf16[3,4,128,128]{3,2,1,0:T(8,128)(2,1)S(1)}, bf16[4,512,128]{2,1,0:T(8,128)(2,1)S(1)}, bf16[4,512,128...) custom-call(bf16[4,512,256]{2,1,0:T(8,128)(2,1)} %get-tuple-element.54.refs_0_, ...), custom_call_target="tpu_custom_call" | custom-call | flops 12884901888 | bytes 8388608 | tf_op jit(solution)/shard_map/pallas_call | solution.py:428
  58.8 0.6 collective-permute-start.6
  59.4 0.1 collective-permute-start.7
  59.5 1.8 %collective-permute-done.6 = bf16[3,2,8,64,128]{4,3,2,1,0:T(8,128)(2,1)S(1)} collective-permute-done((bf16[3,2,8,64,128]{4,3,2,1,0:T(8,128)(2,1)S(1)}, bf16[3,2,8,64,128]{4,3,2,1,0:T(8,128)(2,1)S(1)}, u32[]{:S(2)}, u32[]{:S(2)}) %collective-permute-start.6) | collective-permute-done | bytes 786464 | tf_op jit(solution)/shard_map/ppermute | solution.py:48
  61.3 0.3 add_convert_fusion
  61.6 0.1 slice_bitcast_fusion
  61.6 0.1 collective-permute-start.8
  61.7 2.6 %collective-permute-start.9 = (bf16[2,8,64,128]{3,2,1,0:T(8,128)(2,1)S(1)}, bf16[2,8,64,128]{3,2,1,0:T(8,128)(2,1)S(1)}, u32[]{:S(2)}, u32[]{:S(2)}) collective-permute-start(bf16[2,8,64,128]{3,2,1,0:T(8,128)(2,1)S(1)} %get-tuple-element.89), channel_id=1, source_target_pairs={{0,64},{32,96},{64,0},{96,32},{1,65},{33,97},{65,1},{97,33},{2,66}... | collective-permute-start | bytes 786440 | tf_op jit(solution)/shard_map/ppermute | solution.py:53
  64.3 1.0 collective-permute-start.10
  65.3 0.0 collective-permute-done.7.refs_6_
  65.3 6.3 %shard_map.117 = (f32[1,4,128,128]{3,2,1,0:T(8,128)S(1)}, bf16[1,4,128,128]{3,2,1,0:T(8,128)(2,1)S(1)}, bf16[4,512,128]{2,1,0:T(8,128)(2,1)S(1)}, bf16[4,512,128...) custom-call(bf16[4,512,256]{2,1,0:T(8,128)(2,1)} %get-tuple-element.54.refs_0_, ...), custom_call_target="tpu_custom_call" | custom-call | flops 4294967296 | bytes 8388608 | tf_op jit(solution)/shard_map/pallas_call | solution.py:428
  71.6 0.1 collective-permute-start.11
  71.7 2.9 %shard_map.118.done_ref = bf16[8,9,64,128]{3,2,1,0:T(8,128)(2,1)S(1)} custom-call(f32[4,128,512]{2,1,0:T(8,128)} %get-tuple-element.53.refs_0_, bf16[8,8,64,128]{3,2,1,0:T(8,128)(2,1)S(1)} %all-to-all-done.1.pair_ref.cot_ref.refs_1_, bf16[128,128]{1,0:T(8,128)(2,1)S(1)} %copy-done.4, bf16[128,128]{1,0:T(8,128)(2,1)S(1)} %copy-done.5, ...), custom_call_target="tpu_custom_call" | custom-call | flops 2147483648 | bytes 8388608 | tf_op jit(solution)/shard_map/pallas_call | solution.py:500
  74.6 2.5 %collective-permute-done.8.refs_2_ = bf16[2,8,64,128]{3,2,1,0:T(8,128)(2,1)S(1)} collective-permute-done((bf16[2,8,64,128]{3,2,1,0:T(8,128)(2,1)S(1)}, bf16[2,8,64,128]{3,2,1,0:T(8,128)(2,1)S(1)}, u32[]{:S(2)}, u32[]{:S(2)}) %collective-permute-start.8) | collective-permute-done | bytes 262176 | tf_op jit(solution)/shard_map/ppermute | solution.py:53
  77.1 0.0 collective-permute-done.9.refs_3_
  77.1 0.6 collective-permute-done.10.refs_4_
  77.7 0.0 collective-permute-done.11
  77.7 0.2 shard_map.119
  77.9 1.4 %collective-permute-start.12 = (bf16[8,64,128]{2,1,0:T(8,128)(2,1)S(1)}, bf16[8,64,128]{2,1,0:T(8,128)(2,1)S(1)}, u32[]{:S(2)}, u32[]{:S(2)}) collective-permute-start(bf16[8,64,128]{2,1,0:T(8,128)(2,1)S(1)} %get-tuple-element.87), channel_id=1, source_target_pairs={{0,16},{16,0},{1,17},{17,1},{2,18},{18,2},{3,19},{19,3},{4,20},{20... | collective-permute-start | bytes 393224 | tf_op jit(solution)/shard_map/ppermute | solution.py:681
  79.3 5.1 %collective-permute-done.12.b_ref = bf16[8,64,128]{2,1,0:T(8,128)(2,1)S(1)} collective-permute-done((bf16[8,64,128]{2,1,0:T(8,128)(2,1)S(1)}, bf16[8,64,128]{2,1,0:T(8,128)(2,1)S(1)}, u32[]{:S(2)}, u32[]{:S(2)}) %collective-permute-start.12) | collective-permute-done | bytes 131104 | tf_op jit(solution)/shard_map/ppermute | solution.py:681
  84.5 0.1 shard_map.120
  84.5 0.0 copy-start
  84.5 0.0 copy-start.1
  84.5 20.7 %all_to_all.15.both_ref.gb_ref = bf16[8,9,64,128]{3,2,1,0:T(8,128)(2,1)S(1)} all-to-all(bf16[8,9,64,128]{3,2,1,0:T(8,128)(2,1)S(1)} %shard_map.120), channel_id=1, replica_groups=mesh['z'=4,'xh'=2,'core'=2,'y'=4,'xl'=2] {'y','xl'}, dimensions={0} | all-to-all | bytes 2359296 | tf_op jit(solution)/shard_map/all_to_all | solution.py:683
  105.2 0.0 copy-done
  105.2 0.0 copy-done.1
  105.2 2.9 %shard_map.121 = (bf16[32,64,128]{2,1,0:T(8,128)(2,1)}, f32[32,64,128]{2,1,0:T(8,128)}) custom-call(bf16[32,64,128]{2,1,0:T(8,128)(2,1)S(1)} %copy-done, bf16[8,9,64,128]{3,2,1,0:T(8,128)(2,1)S(1)} %all_to_all.15.both_ref.gb_ref, bf16[8,9,64,128]{3,2,1,0:T(8,128)(2,1)S(1)} %all_to_all.15.both_ref.gb_ref, f32[1,128]{1,0:T(1,128)S(1)} %bitcast.23, ...), custom_call_target="tpu_custom_call" | custom-call | flops 134217728 | bytes 2097152 | tf_op jit(solution)/shard_map/pallas_call | solution.py:606
Async XLA Ops:
  3.3 15.8 %all-to-all-start = ((bf16[16,64,128]{2,1,0:T(8,128)(2,1)}), bf16[16,64,128]{2,1,0:T(8,128)(2,1)S(1)}, u32[]{:S(2)}, u32[]{:S(2)}) async-start(bf16[16,64,128]{2,1,0:T(8,128)(2,1)} %shard_map.113), calls=%async_computation | async-start | bytes 524288 | tf_op jit(solution)/shard_map/all_to_all | solution.py:653
  12.4 27.7 %copy-start.2 = (f32[128]{0:T(128)S(1)}, f32[128]{0:T(128)}, u32[]{:S(2)}) copy-start(f32[128]{0:T(128)} %param.12) | copy-start | bytes 1540
  12.4 27.7 %copy-start.3 = (f32[128]{0:T(128)S(1)}, f32[128]{0:T(128)}, u32[]{:S(2)}) copy-start(f32[128]{0:T(128)} %param.13) | copy-start | bytes 1540
  12.4 27.7 %copy-start.4 = (bf16[128,128]{1,0:T(8,128)(2,1)S(1)}, bf16[128,128]{1,0:T(8,128)(2,1)}, u32[]{:S(2)}) copy-start(bf16[128,128]{1,0:T(8,128)(2,1)} %refs_2_.1) | copy-start | bytes 98308
  12.4 27.7 %copy-start.5 = (bf16[128,128]{1,0:T(8,128)(2,1)S(1)}, bf16[128,128]{1,0:T(8,128)(2,1)}, u32[]{:S(2)}) copy-start(bf16[128,128]{1,0:T(8,128)(2,1)} %refs_3_.1) | copy-start | bytes 98308
  12.4 27.7 %copy-start.6 = (bf16[128,128]{1,0:T(8,128)(2,1)S(1)}, bf16[128,128]{1,0:T(8,128)(2,1)}, u32[]{:S(2)}) copy-start(bf16[128,128]{1,0:T(8,128)(2,1)} %refs_4_.1) | copy-start | bytes 98308
  12.5 27.7 %copy-start.7 = (bf16[128,128]{1,0:T(8,128)(2,1)S(1)}, bf16[128,128]{1,0:T(8,128)(2,1)}, u32[]{:S(2)}) copy-start(bf16[128,128]{1,0:T(8,128)(2,1)} %refs_5_.1) | copy-start | bytes 98308
  12.5 27.7 %copy-start.8 = (bf16[128,128]{1,0:T(8,128)(2,1)S(1)}, bf16[128,128]{1,0:T(8,128)(2,1)}, u32[]{:S(2)}) copy-start(bf16[128,128]{1,0:T(8,128)(2,1)} %refs_6_.1) | copy-start | bytes 98308
  19.1 21.0 %all-to-all-start.1 = ((bf16[8,8,64,128]{3,2,1,0:T(8,128)(2,1)}), bf16[8,8,64,128]{3,2,1,0:T(8,128)(2,1)S(1)}, u32[]{:S(2)}, u32[]{:S(2)}) async-start(bf16[8,8,64,128]{3,2,1,0:T(8,128)(2,1)} %shard_map.114), calls=%async_computation.1 | async-start | bytes 2097152 | tf_op jit(solution)/shard_map/all_to_all | solution.py:656
  22.6 14.0 %collective-permute-start = (bf16[2,8,64,128]{3,2,1,0:T(8,128)(2,1)S(1)}, bf16[2,8,64,128]{3,2,1,0:T(8,128)(2,1)S(1)}, u32[]{:S(2)}, u32[]{:S(2)}) collective-permute-start(bf16[2,8,64,128]{3,2,1,0:T(8,128)(2,1)S(1)} %bitcast.14), channel_id=1, source_target_pairs={{0,96},{32,0},{64,32},{96,64},{1,97},{33,1},{65,33},{97,65},{2,98}... | collective-permute-start | bytes 786440 | tf_op jit(solution)/shard_map/ppermute | solution.py:53
  26.7 10.7 %collective-permute-start.1 = (bf16[2,8,64,128]{3,2,1,0:T(8,128)(2,1)S(1)}, bf16[2,8,64,128]{3,2,1,0:T(8,128)(2,1)S(1)}, u32[]{:S(2)}, u32[]{:S(2)}) collective-permute-start(bf16[2,8,64,128]{3,2,1,0:T(8,128)(2,1)S(1)} %bitcast.15), channel_id=1, source_target_pairs={{0,64},{32,96},{64,0},{96,32},{1,65},{33,97},{65,1},{97,33},{2,66}... | collective-permute-start | bytes 786440 | tf_op jit(solution)/shard_map/ppermute | solution.py:53
  26.7 13.3 %collective-permute-start.2 = (bf16[2,8,64,128]{3,2,1,0:T(8,128)(2,1)S(1)}, bf16[2,8,64,128]{3,2,1,0:T(8,128)(2,1)S(1)}, u32[]{:S(2)}, u32[]{:S(2)}) collective-permute-start(bf16[2,8,64,128]{3,2,1,0:T(8,128)(2,1)S(1)} %bitcast.16), channel_id=1, source_target_pairs={{0,32},{32,64},{64,96},{96,0},{1,33},{33,65},{65,97},{97,1},{2,34}... | collective-permute-start | bytes 786440 | tf_op jit(solution)/shard_map/ppermute | solution.py:53
  36.7 7.2 %collective-permute-start.3 = (bf16[2,8,64,128]{3,2,1,0:T(8,128)(2,1)S(1)}, bf16[2,8,64,128]{3,2,1,0:T(8,128)(2,1)S(1)}, u32[]{:S(2)}, u32[]{:S(2)}) collective-permute-start(bf16[2,8,64,128]{3,2,1,0:T(8,128)(2,1)S(1)} %collective-permute-done.refs_5_), channel_id=1, source_target_pairs={{0,8},{8,0},{1,9},{9,1},{2,10},{10,2},{3,11},{11,3},{4,12},{12,4},... | collective-permute-start | bytes 786440 | tf_op jit(solution)/shard_map/ppermute | solution.py:48
  37.5 6.4 %collective-permute-start.4 = (bf16[2,8,64,128]{3,2,1,0:T(8,128)(2,1)S(1)}, bf16[2,8,64,128]{3,2,1,0:T(8,128)(2,1)S(1)}, u32[]{:S(2)}, u32[]{:S(2)}) collective-permute-start(bf16[2,8,64,128]{3,2,1,0:T(8,128)(2,1)S(1)} %collective-permute-done.1.refs_7_), channel_id=1, source_target_pairs={{0,8},{8,0},{1,9},{9,1},{2,10},{10,2},{3,11},{11,3},{4,12},{12,4},... | collective-permute-start | bytes 786440 | tf_op jit(solution)/shard_map/ppermute | solution.py:48
  40.1 3.8 %collective-permute-start.5 = (bf16[2,8,64,128]{3,2,1,0:T(8,128)(2,1)S(1)}, bf16[2,8,64,128]{3,2,1,0:T(8,128)(2,1)S(1)}, u32[]{:S(2)}, u32[]{:S(2)}) collective-permute-start(bf16[2,8,64,128]{3,2,1,0:T(8,128)(2,1)S(1)} %collective-permute-done.2.refs_9_), channel_id=1, source_target_pairs={{0,8},{8,0},{1,9},{9,1},{2,10},{10,2},{3,11},{11,3},{4,12},{12,4},... | collective-permute-start | bytes 786440 | tf_op jit(solution)/shard_map/ppermute | solution.py:48
  58.8 2.5 %collective-permute-start.6 = (bf16[3,2,8,64,128]{4,3,2,1,0:T(8,128)(2,1)S(1)}, bf16[3,2,8,64,128]{4,3,2,1,0:T(8,128)(2,1)S(1)}, u32[]{:S(2)}, u32[]{:S(2)}) collective-permute-start(bf16[3,2,8,64,128]{4,3,2,1,0:T(8,128)(2,1)S(1)} %get-tuple-element.67), channel_id=1, source_target_pairs={{0,8},{8,0},{1,9},{9,1},{2,10},{10,2},{3,11},{11,3},{4,12},{12,4},... | collective-permute-start | bytes 2359304 | tf_op jit(solution)/shard_map/ppermute | solution.py:48
  59.4 5.9 %collective-permute-start.7 = (bf16[2,8,64,128]{3,2,1,0:T(8,128)(2,1)S(1)}, bf16[2,8,64,128]{3,2,1,0:T(8,128)(2,1)S(1)}, u32[]{:S(2)}, u32[]{:S(2)}) collective-permute-start(bf16[2,8,64,128]{3,2,1,0:T(8,128)(2,1)S(1)} %bitcast.17), channel_id=1, source_target_pairs={{0,8},{8,0},{1,9},{9,1},{2,10},{10,2},{3,11},{11,3},{4,12},{12,4},... | collective-permute-start | bytes 786440 | tf_op jit(solution)/shard_map/ppermute | solution.py:48
  61.6 15.5 %collective-permute-start.8 = (bf16[2,8,64,128]{3,2,1,0:T(8,128)(2,1)S(1)}, bf16[2,8,64,128]{3,2,1,0:T(8,128)(2,1)S(1)}, u32[]{:S(2)}, u32[]{:S(2)}) collective-permute-start(bf16[2,8,64,128]{3,2,1,0:T(8,128)(2,1)S(1)} %get-tuple-element.90), channel_id=1, source_target_pairs={{0,32},{32,64},{64,96},{96,0},{1,33},{33,65},{65,97},{97,1},{2,34}... | collective-permute-start | bytes 786440 | tf_op jit(solution)/shard_map/ppermute | solution.py:53
  61.7 15.4 %collective-permute-start.9 = (bf16[2,8,64,128]{3,2,1,0:T(8,128)(2,1)S(1)}, bf16[2,8,64,128]{3,2,1,0:T(8,128)(2,1)S(1)}, u32[]{:S(2)}, u32[]{:S(2)}) collective-permute-start(bf16[2,8,64,128]{3,2,1,0:T(8,128)(2,1)S(1)} %get-tuple-element.89), channel_id=1, source_target_pairs={{0,64},{32,96},{64,0},{96,32},{1,65},{33,97},{65,1},{97,33},{2,66}... | collective-permute-start | bytes 786440 | tf_op jit(solution)/shard_map/ppermute | solution.py:53
  64.3 13.5 %collective-permute-start.10 = (bf16[2,8,64,128]{3,2,1,0:T(8,128)(2,1)S(1)}, bf16[2,8,64,128]{3,2,1,0:T(8,128)(2,1)S(1)}, u32[]{:S(2)}, u32[]{:S(2)}) collective-permute-start(bf16[2,8,64,128]{3,2,1,0:T(8,128)(2,1)S(1)} %get-tuple-element.88), channel_id=1, source_target_pairs={{0,96},{32,0},{64,32},{96,64},{1,97},{33,1},{65,33},{97,65},{2,98}... | collective-permute-start | bytes 786440 | tf_op jit(solution)/shard_map/ppermute | solution.py:53
  71.6 6.2 %collective-permute-start.11 = (bf16[1,2,8,64,128]{4,3,2,1,0:T(8,128)(2,1)S(1)}, bf16[1,2,8,64,128]{4,3,2,1,0:T(8,128)(2,1)S(1)}, u32[]{:S(2)}, u32[]{:S(2)}) collective-permute-start(bf16[1,2,8,64,128]{4,3,2,1,0:T(8,128)(2,1)S(1)} %get-tuple-element.79), channel_id=1, source_target_pairs={{0,8},{8,0},{1,9},{9,1},{2,10},{10,2},{3,11},{11,3},{4,12},{12,4},... | collective-permute-start | bytes 786440 | tf_op jit(solution)/shard_map/ppermute | solution.py:48
  77.9 6.6 %collective-permute-start.12 = (bf16[8,64,128]{2,1,0:T(8,128)(2,1)S(1)}, bf16[8,64,128]{2,1,0:T(8,128)(2,1)S(1)}, u32[]{:S(2)}, u32[]{:S(2)}) collective-permute-start(bf16[8,64,128]{2,1,0:T(8,128)(2,1)S(1)} %get-tuple-element.87), channel_id=1, source_target_pairs={{0,16},{16,0},{1,17},{17,1},{2,18},{18,2},{3,19},{19,3},{4,20},{20... | collective-permute-start | bytes 393224 | tf_op jit(solution)/shard_map/ppermute | solution.py:681
  84.5 20.7 %copy-start = (bf16[32,64,128]{2,1,0:T(8,128)(2,1)S(1)}, bf16[32,64,128]{2,1,0:T(8,128)(2,1)}, u32[]{:S(2)}) copy-start(bf16[32,64,128]{2,1,0:T(8,128)(2,1)} %pair_ref.5) | copy-start | bytes 1572868
  84.5 20.7 %copy-start.1 = (bf16[128,4]{0,1:T(4,128)(2,1)S(1)}, bf16[128,4]{0,1:T(4,128)(2,1)}, u32[]{:S(2)}) copy-start(bf16[128,4]{0,1:T(4,128)(2,1)} %param.18) | copy-start | bytes 3076

commit v11 on v9

--- a/solution.py
+++ b/solution.py
@@ -599,7 +599,7 @@
 
 def final(pair, both, gain, shift_row, bias_weight):
     n_ja, slabs, block, channels = both.shape
-    group = 2
+    group = 4
     steps = n_ja // group
     rows = pair.shape[0] // steps
     by_rows = pl.BlockSpec((rows, block, channels), lambda i: (i, 0, 0))

time: 109 us -> 108 us (level)
  no operation moved by 1% of the time
where the time goes in v11:
time: 108 us
  Pallas kernels  35.1 us (32%)
  waiting for transfers between devices  28.7 us (27%)
  starting transfers between devices  21.9 us (20%)
  blocking collectives  20.7 us (19%)
    pallas_call x2, Pallas kernels, attend(): pl.pallas_call(lambda *refs: attend_kernel(heads, count, views, *refs), g...  21.3 us
    all_to_all x1, blocking collectives, shards(): done = lax.all_to_all(done, JA, 0, 0, tiled=True)  20.7 us
    ppermute x6, waiting for transfers between devices, shift(): return lax.ppermute(a, axis, [(s, (s + by) % size) for s in range(size)])  15.2 us
    ppermute x6, starting transfers between devices, shift(): return lax.ppermute(a, axis, [(s, (s + by) % size) for s in range(size)])  9.02 us
    all_to_all x1, starting transfers between devices, shards(): near = lax.all_to_all(tile, ('xh',) + JA, 0, 0, tiled=True)  7.12 us
    all_to_all x1, waiting for transfers between devices, shards(): near = lax.all_to_all(tile, ('xh',) + JA, 0, 0, tiled=True)  6.59 us
    ppermute x1, waiting for transfers between devices, shards(): send = lax.ppermute(send, 'xh', [(0, 1), (1, 0)])  5.14 us
    pallas_call x1, Pallas kernels, project(): pl.pallas_call(project_kernel, grid=(rows // group,), in_specs=[pl.BlockS...  3.81 us
  transfers between devices with their start and end apart: 15, of which 8 were waited for; matrix products, arithmetic and copies ran while one was open for 0% of the time, Pallas kernels for 14%

profile of v11, /device:TPU:0, one launch (start us, length us, event | category | flops | bytes accessed | tf_op | source)
XLA Modules:
  0.0 107.7 jit_solution(9277948791712234190)
XLA Ops:
  0.6 2.6 %shard_map.113 = bf16[16,64,128]{2,1,0:T(8,128)(2,1)} custom-call(bf16[32,64,128]{2,1,0:T(8,128)(2,1)} %pair_ref.5, f32[1,128]{1,0:T(1,128)} %bitcast.21, f32[1,128]{1,0:T(1,128)} %bitcast.24, bf16[4,128]{1,0:T(4,128)(2,1)} %bitcast.19), custom_call_target="tpu_custom_call" | custom-call | flops 134217728 | bytes 1048576 | tf_op jit(solution)/shard_map/pallas_call | solution.py:95
  3.3 7.1 %all-to-all-start = ((bf16[16,64,128]{2,1,0:T(8,128)(2,1)}), bf16[16,64,128]{2,1,0:T(8,128)(2,1)S(1)}, u32[]{:S(2)}, u32[]{:S(2)}) async-start(bf16[16,64,128]{2,1,0:T(8,128)(2,1)} %shard_map.113), calls=%async_computation | async-start | bytes 524288 | tf_op jit(solution)/shard_map/all_to_all | solution.py:653
  10.4 2.0 %shard_map.114 = bf16[8,8,64,128]{3,2,1,0:T(8,128)(2,1)} custom-call(bf16[32,64,128]{2,1,0:T(8,128)(2,1)} %pair_ref.5, bf16[32,64,128]{2,1,0:T(8,128)(2,1)} %cot_ref.1), custom_call_target="tpu_custom_call" | custom-call | flops 1024 | bytes 2097152 | tf_op jit(solution)/shard_map/pallas_call | solution.py:117
  12.4 0.0 copy-start.2
  12.4 0.0 copy-start.3
  12.4 0.0 copy-start.4
  12.4 0.0 copy-start.5
  12.4 0.0 copy-start.6
  12.5 0.0 copy-start.7
  12.5 0.0 copy-start.8
  12.5 6.6 %all-to-all-done = bf16[16,64,128]{2,1,0:T(8,128)(2,1)S(1)} async-done(((bf16[16,64,128]{2,1,0:T(8,128)(2,1)}), bf16[16,64,128]{2,1,0:T(8,128)(2,1)S(1)}, u32[]{:S(2)}, u32[]{:S(2)}) %all-to-all-start) | async-done | bytes 262176 | tf_op jit(solution)/shard_map/all_to_all | solution.py:653
  19.1 3.6 %all-to-all-start.1 = ((bf16[8,8,64,128]{3,2,1,0:T(8,128)(2,1)}), bf16[8,8,64,128]{3,2,1,0:T(8,128)(2,1)S(1)}, u32[]{:S(2)}, u32[]{:S(2)}) async-start(bf16[8,8,64,128]{3,2,1,0:T(8,128)(2,1)} %shard_map.114), calls=%async_computation.1 | async-start | bytes 2097152 | tf_op jit(solution)/shard_map/all_to_all | solution.py:656
  22.6 4.1 %collective-permute-start = (bf16[2,8,64,128]{3,2,1,0:T(8,128)(2,1)S(1)}, bf16[2,8,64,128]{3,2,1,0:T(8,128)(2,1)S(1)}, u32[]{:S(2)}, u32[]{:S(2)}) collective-permute-start(bf16[2,8,64,128]{3,2,1,0:T(8,128)(2,1)S(1)} %bitcast.14), channel_id=1, source_target_pairs={{0,96},{32,0},{64,32},{96,64},{1,97},{33,1},{65,33},{97,65},{2,98}... | collective-permute-start | bytes 786440 | tf_op jit(solution)/shard_map/ppermute | solution.py:53
  26.7 0.0 collective-permute-start.1
  26.7 1.3 %collective-permute-start.2 = (bf16[2,8,64,128]{3,2,1,0:T(8,128)(2,1)S(1)}, bf16[2,8,64,128]{3,2,1,0:T(8,128)(2,1)S(1)}, u32[]{:S(2)}, u32[]{:S(2)}) collective-permute-start(bf16[2,8,64,128]{3,2,1,0:T(8,128)(2,1)S(1)} %bitcast.16), channel_id=1, source_target_pairs={{0,32},{32,64},{64,96},{96,0},{1,33},{33,65},{65,97},{97,1},{2,34}... | collective-permute-start | bytes 786440 | tf_op jit(solution)/shard_map/ppermute | solution.py:53
  28.0 8.7 %collective-permute-done.refs_5_ = bf16[2,8,64,128]{3,2,1,0:T(8,128)(2,1)S(1)} collective-permute-done((bf16[2,8,64,128]{3,2,1,0:T(8,128)(2,1)S(1)}, bf16[2,8,64,128]{3,2,1,0:T(8,128)(2,1)S(1)}, u32[]{:S(2)}, u32[]{:S(2)}) %collective-permute-start) | collective-permute-done | bytes 262176 | tf_op jit(solution)/shard_map/ppermute | solution.py:53
  36.7 0.0 collective-permute-start.3
  36.7 0.8 collective-permute-done.1.refs_7_
  37.5 0.0 collective-permute-start.4
  37.5 2.6 %collective-permute-done.2.refs_9_ = bf16[2,8,64,128]{3,2,1,0:T(8,128)(2,1)S(1)} collective-permute-done((bf16[2,8,64,128]{3,2,1,0:T(8,128)(2,1)S(1)}, bf16[2,8,64,128]{3,2,1,0:T(8,128)(2,1)S(1)}, u32[]{:S(2)}, u32[]{:S(2)}) %collective-permute-start.2) | collective-permute-done | bytes 262176 | tf_op jit(solution)/shard_map/ppermute | solution.py:53
  40.1 0.0 collective-permute-start.5
  40.1 0.0 all-to-all-done.1.pair_ref.cot_ref.refs_1_
  40.1 0.0 copy-done.2
  40.1 0.0 copy-done.3
  40.1 0.0 copy-done.4
  40.1 0.0 copy-done.5
  40.1 0.0 copy-done.6
  40.1 0.0 copy-done.7
  40.2 0.0 copy-done.8
  40.2 3.8 %shard_map.115 = (bf16[4,512,256]{2,1,0:T(8,128)(2,1)}, bf16[4,256,512]{2,1,0:T(8,128)(2,1)}, bf16[4,4,128,128]{3,2,1,0:T(8,128)(2,1)}, bf16[4,4,128,128]{3,2,1,...) custom-call(bf16[8,8,64,128]{3,2,1,0:T(8,128)(2,1)S(1)} %all-to-all-done.1.pair_ref.cot_ref.refs_1_, ...), custom_call_target="tpu_custom_call" | custom-call | flops 2147483648 | bytes 8388608 | tf_op jit(solution)/shard_map/pallas_call | solution.py:189
  44.0 0.0 collective-permute-done.3.refs_6_
  44.0 0.0 collective-permute-done.4.refs_8_
  44.0 0.0 collective-permute-done.5.refs_10_
  44.0 14.9 %shard_map.116 = (f32[3,4,128,128]{3,2,1,0:T(8,128)S(1)}, bf16[3,4,128,128]{3,2,1,0:T(8,128)(2,1)S(1)}, bf16[4,512,128]{2,1,0:T(8,128)(2,1)S(1)}, bf16[4,512,128...) custom-call(bf16[4,512,256]{2,1,0:T(8,128)(2,1)} %get-tuple-element.54.refs_0_, ...), custom_call_target="tpu_custom_call" | custom-call | flops 12884901888 | bytes 8388608 | tf_op jit(solution)/shard_map/pallas_call | solution.py:428
  58.9 0.6 collective-permute-start.6
  59.6 0.1 collective-permute-start.7
  59.7 1.8 %collective-permute-done.6 = bf16[3,2,8,64,128]{4,3,2,1,0:T(8,128)(2,1)S(1)} collective-permute-done((bf16[3,2,8,64,128]{4,3,2,1,0:T(8,128)(2,1)S(1)}, bf16[3,2,8,64,128]{4,3,2,1,0:T(8,128)(2,1)S(1)}, u32[]{:S(2)}, u32[]{:S(2)}) %collective-permute-start.6) | collective-permute-done | bytes 786464 | tf_op jit(solution)/shard_map/ppermute | solution.py:48
  61.5 0.3 add_convert_fusion
  61.8 0.1 slice_bitcast_fusion
  61.8 0.1 collective-permute-start.8
  61.9 2.6 %collective-permute-start.9 = (bf16[2,8,64,128]{3,2,1,0:T(8,128)(2,1)S(1)}, bf16[2,8,64,128]{3,2,1,0:T(8,128)(2,1)S(1)}, u32[]{:S(2)}, u32[]{:S(2)}) collective-permute-start(bf16[2,8,64,128]{3,2,1,0:T(8,128)(2,1)S(1)} %get-tuple-element.89), channel_id=1, source_target_pairs={{0,64},{32,96},{64,0},{96,32},{1,65},{33,97},{65,1},{97,33},{2,66}... | collective-permute-start | bytes 786440 | tf_op jit(solution)/shard_map/ppermute | solution.py:53
  64.5 1.0 collective-permute-start.10
  65.5 0.0 collective-permute-done.7.refs_6_
  65.5 6.3 %shard_map.117 = (f32[1,4,128,128]{3,2,1,0:T(8,128)S(1)}, bf16[1,4,128,128]{3,2,1,0:T(8,128)(2,1)S(1)}, bf16[4,512,128]{2,1,0:T(8,128)(2,1)S(1)}, bf16[4,512,128...) custom-call(bf16[4,512,256]{2,1,0:T(8,128)(2,1)} %get-tuple-element.54.refs_0_, ...), custom_call_target="tpu_custom_call" | custom-call | flops 4294967296 | bytes 8388608 | tf_op jit(solution)/shard_map/pallas_call | solution.py:428
  71.8 0.1 collective-permute-start.11
  71.9 2.9 %shard_map.118.done_ref = bf16[8,9,64,128]{3,2,1,0:T(8,128)(2,1)S(1)} custom-call(f32[4,128,512]{2,1,0:T(8,128)} %get-tuple-element.53.refs_0_, bf16[8,8,64,128]{3,2,1,0:T(8,128)(2,1)S(1)} %all-to-all-done.1.pair_ref.cot_ref.refs_1_, bf16[128,128]{1,0:T(8,128)(2,1)S(1)} %copy-done.4, bf16[128,128]{1,0:T(8,128)(2,1)S(1)} %copy-done.5, ...), custom_call_target="tpu_custom_call" | custom-call | flops 2147483648 | bytes 8388608 | tf_op jit(solution)/shard_map/pallas_call | solution.py:500
  74.8 2.5 %collective-permute-done.8.refs_2_ = bf16[2,8,64,128]{3,2,1,0:T(8,128)(2,1)S(1)} collective-permute-done((bf16[2,8,64,128]{3,2,1,0:T(8,128)(2,1)S(1)}, bf16[2,8,64,128]{3,2,1,0:T(8,128)(2,1)S(1)}, u32[]{:S(2)}, u32[]{:S(2)}) %collective-permute-start.8) | collective-permute-done | bytes 262176 | tf_op jit(solution)/shard_map/ppermute | solution.py:53
  77.3 0.0 collective-permute-done.9.refs_3_
  77.3 0.6 collective-permute-done.10.refs_4_
  77.9 0.0 collective-permute-done.11
  77.9 0.2 shard_map.119
  78.1 1.4 %collective-permute-start.12 = (bf16[8,64,128]{2,1,0:T(8,128)(2,1)S(1)}, bf16[8,64,128]{2,1,0:T(8,128)(2,1)S(1)}, u32[]{:S(2)}, u32[]{:S(2)}) collective-permute-start(bf16[8,64,128]{2,1,0:T(8,128)(2,1)S(1)} %get-tuple-element.87), channel_id=1, source_target_pairs={{0,16},{16,0},{1,17},{17,1},{2,18},{18,2},{3,19},{19,3},{4,20},{20... | collective-permute-start | bytes 393224 | tf_op jit(solution)/shard_map/ppermute | solution.py:681
  79.5 5.1 %collective-permute-done.12.b_ref = bf16[8,64,128]{2,1,0:T(8,128)(2,1)S(1)} collective-permute-done((bf16[8,64,128]{2,1,0:T(8,128)(2,1)S(1)}, bf16[8,64,128]{2,1,0:T(8,128)(2,1)S(1)}, u32[]{:S(2)}, u32[]{:S(2)}) %collective-permute-start.12) | collective-permute-done | bytes 131104 | tf_op jit(solution)/shard_map/ppermute | solution.py:681
  84.7 0.1 shard_map.120
  84.7 0.0 copy-start
  84.7 0.0 copy-start.1
  84.7 20.7 %all_to_all.15.both_ref.gb_ref = bf16[8,9,64,128]{3,2,1,0:T(8,128)(2,1)S(1)} all-to-all(bf16[8,9,64,128]{3,2,1,0:T(8,128)(2,1)S(1)} %shard_map.120), channel_id=1, replica_groups=mesh['z'=4,'xh'=2,'core'=2,'y'=4,'xl'=2] {'y','xl'}, dimensions={0} | all-to-all | bytes 2359296 | tf_op jit(solution)/shard_map/all_to_all | solution.py:683
  105.4 0.0 copy-done
  105.4 0.0 copy-done.1
  105.4 2.3 %shard_map.121 = (bf16[32,64,128]{2,1,0:T(8,128)(2,1)}, f32[32,64,128]{2,1,0:T(8,128)}) custom-call(bf16[32,64,128]{2,1,0:T(8,128)(2,1)S(1)} %copy-done, bf16[8,9,64,128]{3,2,1,0:T(8,128)(2,1)S(1)} %all_to_all.15.both_ref.gb_ref, bf16[8,9,64,128]{3,2,1,0:T(8,128)(2,1)S(1)} %all_to_all.15.both_ref.gb_ref, f32[1,128]{1,0:T(1,128)S(1)} %bitcast.23, ...), custom_call_target="tpu_custom_call" | custom-call | flops 134217728 | bytes 2097152 | tf_op jit(solution)/shard_map/pallas_call | solution.py:606
Async XLA Ops:
  3.3 15.8 %all-to-all-start = ((bf16[16,64,128]{2,1,0:T(8,128)(2,1)}), bf16[16,64,128]{2,1,0:T(8,128)(2,1)S(1)}, u32[]{:S(2)}, u32[]{:S(2)}) async-start(bf16[16,64,128]{2,1,0:T(8,128)(2,1)} %shard_map.113), calls=%async_computation | async-start | bytes 524288 | tf_op jit(solution)/shard_map/all_to_all | solution.py:653
  12.4 27.7 %copy-start.2 = (f32[128]{0:T(128)S(1)}, f32[128]{0:T(128)}, u32[]{:S(2)}) copy-start(f32[128]{0:T(128)} %param.12) | copy-start | bytes 1540
  12.4 27.7 %copy-start.3 = (f32[128]{0:T(128)S(1)}, f32[128]{0:T(128)}, u32[]{:S(2)}) copy-start(f32[128]{0:T(128)} %param.13) | copy-start | bytes 1540
  12.4 27.7 %copy-start.4 = (bf16[128,128]{1,0:T(8,128)(2,1)S(1)}, bf16[128,128]{1,0:T(8,128)(2,1)}, u32[]{:S(2)}) copy-start(bf16[128,128]{1,0:T(8,128)(2,1)} %refs_2_.1) | copy-start | bytes 98308
  12.4 27.7 %copy-start.5 = (bf16[128,128]{1,0:T(8,128)(2,1)S(1)}, bf16[128,128]{1,0:T(8,128)(2,1)}, u32[]{:S(2)}) copy-start(bf16[128,128]{1,0:T(8,128)(2,1)} %refs_3_.1) | copy-start | bytes 98308
  12.4 27.7 %copy-start.6 = (bf16[128,128]{1,0:T(8,128)(2,1)S(1)}, bf16[128,128]{1,0:T(8,128)(2,1)}, u32[]{:S(2)}) copy-start(bf16[128,128]{1,0:T(8,128)(2,1)} %refs_4_.1) | copy-start | bytes 98308
  12.5 27.7 %copy-start.7 = (bf16[128,128]{1,0:T(8,128)(2,1)S(1)}, bf16[128,128]{1,0:T(8,128)(2,1)}, u32[]{:S(2)}) copy-start(bf16[128,128]{1,0:T(8,128)(2,1)} %refs_5_.1) | copy-start | bytes 98308
  12.5 27.7 %copy-start.8 = (bf16[128,128]{1,0:T(8,128)(2,1)S(1)}, bf16[128,128]{1,0:T(8,128)(2,1)}, u32[]{:S(2)}) copy-start(bf16[128,128]{1,0:T(8,128)(2,1)} %refs_6_.1) | copy-start | bytes 98308
  19.1 21.0 %all-to-all-start.1 = ((bf16[8,8,64,128]{3,2,1,0:T(8,128)(2,1)}), bf16[8,8,64,128]{3,2,1,0:T(8,128)(2,1)S(1)}, u32[]{:S(2)}, u32[]{:S(2)}) async-start(bf16[8,8,64,128]{3,2,1,0:T(8,128)(2,1)} %shard_map.114), calls=%async_computation.1 | async-start | bytes 2097152 | tf_op jit(solution)/shard_map/all_to_all | solution.py:656
  22.6 14.0 %collective-permute-start = (bf16[2,8,64,128]{3,2,1,0:T(8,128)(2,1)S(1)}, bf16[2,8,64,128]{3,2,1,0:T(8,128)(2,1)S(1)}, u32[]{:S(2)}, u32[]{:S(2)}) collective-permute-start(bf16[2,8,64,128]{3,2,1,0:T(8,128)(2,1)S(1)} %bitcast.14), channel_id=1, source_target_pairs={{0,96},{32,0},{64,32},{96,64},{1,97},{33,1},{65,33},{97,65},{2,98}... | collective-permute-start | bytes 786440 | tf_op jit(solution)/shard_map/ppermute | solution.py:53
  26.7 10.7 %collective-permute-start.1 = (bf16[2,8,64,128]{3,2,1,0:T(8,128)(2,1)S(1)}, bf16[2,8,64,128]{3,2,1,0:T(8,128)(2,1)S(1)}, u32[]{:S(2)}, u32[]{:S(2)}) collective-permute-start(bf16[2,8,64,128]{3,2,1,0:T(8,128)(2,1)S(1)} %bitcast.15), channel_id=1, source_target_pairs={{0,64},{32,96},{64,0},{96,32},{1,65},{33,97},{65,1},{97,33},{2,66}... | collective-permute-start | bytes 786440 | tf_op jit(solution)/shard_map/ppermute | solution.py:53
  26.7 13.3 %collective-permute-start.2 = (bf16[2,8,64,128]{3,2,1,0:T(8,128)(2,1)S(1)}, bf16[2,8,64,128]{3,2,1,0:T(8,128)(2,1)S(1)}, u32[]{:S(2)}, u32[]{:S(2)}) collective-permute-start(bf16[2,8,64,128]{3,2,1,0:T(8,128)(2,1)S(1)} %bitcast.16), channel_id=1, source_target_pairs={{0,32},{32,64},{64,96},{96,0},{1,33},{33,65},{65,97},{97,1},{2,34}... | collective-permute-start | bytes 786440 | tf_op jit(solution)/shard_map/ppermute | solution.py:53
  36.7 7.3 %collective-permute-start.3 = (bf16[2,8,64,128]{3,2,1,0:T(8,128)(2,1)S(1)}, bf16[2,8,64,128]{3,2,1,0:T(8,128)(2,1)S(1)}, u32[]{:S(2)}, u32[]{:S(2)}) collective-permute-start(bf16[2,8,64,128]{3,2,1,0:T(8,128)(2,1)S(1)} %collective-permute-done.refs_5_), channel_id=1, source_target_pairs={{0,8},{8,0},{1,9},{9,1},{2,10},{10,2},{3,11},{11,3},{4,12},{12,4},... | collective-permute-start | bytes 786440 | tf_op jit(solution)/shard_map/ppermute | solution.py:48
  37.5 6.5 %collective-permute-start.4 = (bf16[2,8,64,128]{3,2,1,0:T(8,128)(2,1)S(1)}, bf16[2,8,64,128]{3,2,1,0:T(8,128)(2,1)S(1)}, u32[]{:S(2)}, u32[]{:S(2)}) collective-permute-start(bf16[2,8,64,128]{3,2,1,0:T(8,128)(2,1)S(1)} %collective-permute-done.1.refs_7_), channel_id=1, source_target_pairs={{0,8},{8,0},{1,9},{9,1},{2,10},{10,2},{3,11},{11,3},{4,12},{12,4},... | collective-permute-start | bytes 786440 | tf_op jit(solution)/shard_map/ppermute | solution.py:48
  40.1 3.9 %collective-permute-start.5 = (bf16[2,8,64,128]{3,2,1,0:T(8,128)(2,1)S(1)}, bf16[2,8,64,128]{3,2,1,0:T(8,128)(2,1)S(1)}, u32[]{:S(2)}, u32[]{:S(2)}) collective-permute-start(bf16[2,8,64,128]{3,2,1,0:T(8,128)(2,1)S(1)} %collective-permute-done.2.refs_9_), channel_id=1, source_target_pairs={{0,8},{8,0},{1,9},{9,1},{2,10},{10,2},{3,11},{11,3},{4,12},{12,4},... | collective-permute-start | bytes 786440 | tf_op jit(solution)/shard_map/ppermute | solution.py:48
  58.9 2.5 %collective-permute-start.6 = (bf16[3,2,8,64,128]{4,3,2,1,0:T(8,128)(2,1)S(1)}, bf16[3,2,8,64,128]{4,3,2,1,0:T(8,128)(2,1)S(1)}, u32[]{:S(2)}, u32[]{:S(2)}) collective-permute-start(bf16[3,2,8,64,128]{4,3,2,1,0:T(8,128)(2,1)S(1)} %get-tuple-element.67), channel_id=1, source_target_pairs={{0,8},{8,0},{1,9},{9,1},{2,10},{10,2},{3,11},{11,3},{4,12},{12,4},... | collective-permute-start | bytes 2359304 | tf_op jit(solution)/shard_map/ppermute | solution.py:48
  59.6 5.9 %collective-permute-start.7 = (bf16[2,8,64,128]{3,2,1,0:T(8,128)(2,1)S(1)}, bf16[2,8,64,128]{3,2,1,0:T(8,128)(2,1)S(1)}, u32[]{:S(2)}, u32[]{:S(2)}) collective-permute-start(bf16[2,8,64,128]{3,2,1,0:T(8,128)(2,1)S(1)} %bitcast.17), channel_id=1, source_target_pairs={{0,8},{8,0},{1,9},{9,1},{2,10},{10,2},{3,11},{11,3},{4,12},{12,4},... | collective-permute-start | bytes 786440 | tf_op jit(solution)/shard_map/ppermute | solution.py:48
  61.8 15.5 %collective-permute-start.8 = (bf16[2,8,64,128]{3,2,1,0:T(8,128)(2,1)S(1)}, bf16[2,8,64,128]{3,2,1,0:T(8,128)(2,1)S(1)}, u32[]{:S(2)}, u32[]{:S(2)}) collective-permute-start(bf16[2,8,64,128]{3,2,1,0:T(8,128)(2,1)S(1)} %get-tuple-element.90), channel_id=1, source_target_pairs={{0,32},{32,64},{64,96},{96,0},{1,33},{33,65},{65,97},{97,1},{2,34}... | collective-permute-start | bytes 786440 | tf_op jit(solution)/shard_map/ppermute | solution.py:53
  61.9 15.4 %collective-permute-start.9 = (bf16[2,8,64,128]{3,2,1,0:T(8,128)(2,1)S(1)}, bf16[2,8,64,128]{3,2,1,0:T(8,128)(2,1)S(1)}, u32[]{:S(2)}, u32[]{:S(2)}) collective-permute-start(bf16[2,8,64,128]{3,2,1,0:T(8,128)(2,1)S(1)} %get-tuple-element.89), channel_id=1, source_target_pairs={{0,64},{32,96},{64,0},{96,32},{1,65},{33,97},{65,1},{97,33},{2,66}... | collective-permute-start | bytes 786440 | tf_op jit(solution)/shard_map/ppermute | solution.py:53
  64.5 13.5 %collective-permute-start.10 = (bf16[2,8,64,128]{3,2,1,0:T(8,128)(2,1)S(1)}, bf16[2,8,64,128]{3,2,1,0:T(8,128)(2,1)S(1)}, u32[]{:S(2)}, u32[]{:S(2)}) collective-permute-start(bf16[2,8,64,128]{3,2,1,0:T(8,128)(2,1)S(1)} %get-tuple-element.88), channel_id=1, source_target_pairs={{0,96},{32,0},{64,32},{96,64},{1,97},{33,1},{65,33},{97,65},{2,98}... | collective-permute-start | bytes 786440 | tf_op jit(solution)/shard_map/ppermute | solution.py:53
  71.8 6.1 %collective-permute-start.11 = (bf16[1,2,8,64,128]{4,3,2,1,0:T(8,128)(2,1)S(1)}, bf16[1,2,8,64,128]{4,3,2,1,0:T(8,128)(2,1)S(1)}, u32[]{:S(2)}, u32[]{:S(2)}) collective-permute-start(bf16[1,2,8,64,128]{4,3,2,1,0:T(8,128)(2,1)S(1)} %get-tuple-element.79), channel_id=1, source_target_pairs={{0,8},{8,0},{1,9},{9,1},{2,10},{10,2},{3,11},{11,3},{4,12},{12,4},... | collective-permute-start | bytes 786440 | tf_op jit(solution)/shard_map/ppermute | solution.py:48
  78.1 6.6 %collective-permute-start.12 = (bf16[8,64,128]{2,1,0:T(8,128)(2,1)S(1)}, bf16[8,64,128]{2,1,0:T(8,128)(2,1)S(1)}, u32[]{:S(2)}, u32[]{:S(2)}) collective-permute-start(bf16[8,64,128]{2,1,0:T(8,128)(2,1)S(1)} %get-tuple-element.87), channel_id=1, source_target_pairs={{0,16},{16,0},{1,17},{17,1},{2,18},{18,2},{3,19},{19,3},{4,20},{20... | collective-permute-start | bytes 393224 | tf_op jit(solution)/shard_map/ppermute | solution.py:681
  84.7 20.7 %copy-start = (bf16[32,64,128]{2,1,0:T(8,128)(2,1)S(1)}, bf16[32,64,128]{2,1,0:T(8,128)(2,1)}, u32[]{:S(2)}) copy-start(bf16[32,64,128]{2,1,0:T(8,128)(2,1)} %pair_ref.5) | copy-start | bytes 1572868
  84.7 20.7 %copy-start.1 = (bf16[128,4]{0,1:T(4,128)(2,1)S(1)}, bf16[128,4]{0,1:T(4,128)(2,1)}, u32[]{:S(2)}) copy-start(bf16[128,4]{0,1:T(4,128)(2,1)} %param.18) | copy-start | bytes 3076
